TPU v7x, 32 devices: a whole 2x2x4 slice. The times are simulated.
32 devices in a mesh: section: 2 (over x), row: 4 (over z), col: 4 (over y, core).
Axes of the slice: x: 2, y: 2, z: 4, core: 2. Of those that a mesh axis runs over, the one named last changes fastest.
Arguments:
- tokens: bfloat16 [8192, 1280], P('row', 'col'), may hold values from -6 to 6
- cotangent: bfloat16 [8192, 1280], P('row', 'col'), may hold values from -6 to 6
- first_gain: bfloat16 [2, 1280], P('section', 'col'), may hold values from 0.5 to 1.5
- first_shift: bfloat16 [2, 1280], P('section', 'col'), may hold values from -1.1953125 to 1.1953125
- attend_weight: bfloat16 [2, 1280, 3, 1280], P('section', 'row', None, 'col'), may hold values from -0.15625 to 0.15625
- attend_bias: bfloat16 [2, 2, 1280], P('section', None, 'col'), may hold values from -1.1953125 to 1.1953125
- output_weight: bfloat16 [2, 1280, 1280], P('section', 'col', 'row'), may hold values from -2.5 to 2.5
- output_bias: bfloat16 [2, 1280], P('section', 'col'), may hold values from -1.1953125 to 1.1953125
- second_gain: bfloat16 [2, 1280], P('section', 'col'), may hold values from 0.5 to 1.5
- second_shift: bfloat16 [2, 1280], P('section', 'col'), may hold values from -1.1953125 to 1.1953125
- expand_weight: bfloat16 [2, 1280, 5120], P('section', 'row', 'col'), may hold values from -0.15625 to 0.15625
- expand_bias: bfloat16 [2, 5120], P('section', 'col'), may hold values from -1.1953125 to 1.1953125
- contract_weight: bfloat16 [2, 5120, 1280], P('section', 'col', 'row'), may hold values from -0.078125 to 0.078125
- contract_bias: bfloat16 [2, 1280], P('section', 'col'), may hold values from -1.1953125 to 1.1953125
Outputs:
- layer_outputs: bfloat16 [2, 8192, 1280], P('section', 'row', 'col')
- input_grads: float32 [2, 8192, 1280], P('section', 'row', 'col')
- grad_first_gain: float32 [2, 1280], P('section', 'col')
- grad_first_shift: float32 [2, 1280], P('section', 'col')
- grad_attend_weight: float32 [2, 1280, 3, 1280], P('section', 'row', None, 'col')
- grad_attend_bias: float32 [2, 2, 1280], P('section', None, 'col')
- grad_output_weight: float32 [2, 1280, 1280], P('section', 'col', 'row')
- grad_output_bias: float32 [2, 1280], P('section', 'col')
- grad_second_gain: float32 [2, 1280], P('section', 'col')
- grad_second_shift: float32 [2, 1280], P('section', 'col')
- grad_expand_weight: float32 [2, 1280, 5120], P('section', 'row', 'col')
- grad_expand_bias: float32 [2, 5120], P('section', 'col')
- grad_contract_weight: float32 [2, 5120, 1280], P('section', 'col', 'row')
- grad_contract_bias: float32 [2, 1280], P('section', 'col')
All inputs are finite; a program needn't handle non-finite values.
Results may differ from a plain program's by a relative error of at most 0.019.
Values may be sent and summed in bfloat16 or wider, within the bound.
A program may use at most 256 MiB of HBM per device.

v0:
```python
import jax
import jax.numpy as jnp
from jax import lax
from jax.sharding import PartitionSpec as P

D = 1280
HEAD = 64
LENGTH = 1024


eps = 1e-05


def from_behind(x, axis, by):
    peers = lax.axis_size(axis)
    pairs = [(i, i + by) for i in range(peers) if 0 <= i + by < peers]
    return lax.ppermute(x, axis, pairs)


def gelu(values):
    return (
        0.5
        * values
        * (1.0 + jnp.tanh(0.7978845608028654 * (values + 0.044715 * values * values * values)))
    )


def product(left, right):
    return jnp.dot(left, right, preferred_element_type=jnp.float32)


def cross_last(left, right):
    return lax.dot_general(
        left, right, (((1,), (1,)), ((), ())), preferred_element_type=jnp.float32
    )


def cross_first(left, right):
    return lax.dot_general(
        left, right, (((0,), (0,)), ((), ())), preferred_element_type=jnp.float32
    )


def row_totals(first_sum, second_sum):
    return lax.psum((first_sum, second_sum), "col")


def gather_cols(values):
    return lax.all_gather(values, "col", axis=1, tiled=True)


def gather_grads(values):
    return lax.all_gather(values, "col", axis=1, tiled=True)


def branch_sum(partial_terms):
    return lax.psum_scatter(partial_terms, "col", scatter_dimension=1, tiled=True)


def input_sum(partial_terms):
    return lax.psum_scatter(
        partial_terms.astype(jnp.bfloat16), "col", scatter_dimension=1, tiled=True
    ).astype(jnp.float32)


def fetch_forward(attend_block, expand_block, output_block, contract_block):
    attend_full, expand_full = (
        lax.all_gather(attend_block, "row", axis=0, tiled=True),
        lax.all_gather(expand_block, "row", axis=0, tiled=True),
    )
    output_full, contract_full = (
        lax.all_gather(output_block, "row", axis=1, tiled=True),
        lax.all_gather(contract_block, "row", axis=1, tiled=True),
    )
    return (attend_full.reshape(attend_full.shape[0], -1), expand_full, output_full, contract_full)


def fetch_backward(attend_block, expand_block, output_block, contract_block):
    attend_full, expand_full = (
        lax.all_gather(attend_block, "row", axis=0, tiled=True),
        lax.all_gather(expand_block, "row", axis=0, tiled=True),
    )
    output_full, contract_full = (
        lax.all_gather(output_block, "row", axis=1, tiled=True),
        lax.all_gather(contract_block, "row", axis=1, tiled=True),
    )
    return (attend_full.reshape(attend_full.shape[0], -1), expand_full, output_full, contract_full)


def reduce_weights(mat_grads):
    attend_grad, expand_grad, output_grad, contract_grad = mat_grads
    attend_part, expand_part = (
        lax.psum_scatter(
            attend_grad.astype(jnp.bfloat16), "row", scatter_dimension=0, tiled=True
        ).astype(jnp.float32),
        lax.psum_scatter(
            expand_grad.astype(jnp.bfloat16), "row", scatter_dimension=0, tiled=True
        ).astype(jnp.float32),
    )
    output_part, contract_part = (
        lax.psum_scatter(
            output_grad.astype(jnp.bfloat16), "row", scatter_dimension=1, tiled=True
        ).astype(jnp.float32),
        lax.psum_scatter(
            contract_grad.astype(jnp.bfloat16), "row", scatter_dimension=1, tiled=True
        ).astype(jnp.float32),
    )
    return (attend_part, expand_part, output_part, contract_part)


def norm_forward(values, gain, shift):
    row_sum, square_sum = row_totals(jnp.sum(values, axis=1), jnp.sum(values * values, axis=1))
    center = row_sum / D
    norm_scale = lax.rsqrt(square_sum / D - center * center + eps)
    centred = (values - center[:, None]) * norm_scale[:, None]
    return ((centred * gain + shift).astype(jnp.bfloat16), centred, norm_scale)


def norm_backward(grad_normed, centred, norm_scale, gain):
    scaled = grad_normed * gain
    row_sum, cross_sum = row_totals(jnp.sum(scaled, axis=1), jnp.sum(scaled * centred, axis=1))
    grad_values = norm_scale[:, None] * (
        scaled - row_sum[:, None] / D - centred * (cross_sum[:, None] / D)
    )
    return (grad_values, jnp.sum(grad_normed * centred, axis=0), jnp.sum(grad_normed, axis=0))


def causal_mask(row_begin, block_rows, finish):
    query_pos = row_begin + lax.broadcasted_iota(jnp.int32, (block_rows, finish), 0)
    key_pos = lax.broadcasted_iota(jnp.int32, (block_rows, finish), 1)
    return (query_pos >= key_pos)[None]


def split_heads(values):
    return values.reshape(values.shape[0], values.shape[1] // HEAD, HEAD)


def block_scores(query_heads, key_heads, row_begin, block_rows, finish):
    scores = jnp.einsum(
        "qhd,khd->hqk",
        query_heads[row_begin:finish],
        key_heads[:finish],
        preferred_element_type=jnp.float32,
    ) * HEAD ** (-0.5)
    return jnp.where(causal_mask(row_begin, block_rows, finish), scores, -1000000000.0)


def attention_forward(queries, key_rows, value_rows):
    length = queries.shape[0]
    block_rows = min(512, length)
    query_heads, key_heads, value_heads = (
        split_heads(queries),
        split_heads(key_rows),
        split_heads(value_rows),
    )
    outputs, totals = ([], [])
    for row_begin in range(0, length, block_rows):
        finish = row_begin + block_rows
        scores = block_scores(query_heads, key_heads, row_begin, block_rows, finish)
        highest = jnp.max(scores, axis=-1, keepdims=True)
        powers = jnp.exp(scores - highest)
        summed = jnp.sum(powers, axis=-1, keepdims=True)
        weights_low = (powers / summed).astype(jnp.bfloat16)
        outputs.append(
            jnp.einsum(
                "hqk,khd->qhd",
                weights_low,
                value_heads[:finish],
                preferred_element_type=jnp.float32,
            )
        )
        totals.append((highest + jnp.log(summed))[:, :, 0])
    return (
        jnp.concatenate(outputs, 0).astype(jnp.bfloat16).reshape(length, -1),
        jnp.concatenate(totals, 1),
    )


def attention_backward(queries, key_rows, value_rows, log_totals, grad_attended):
    length = queries.shape[0]
    block_rows = min(512, length)
    query_heads, key_heads, value_heads = (
        split_heads(queries),
        split_heads(key_rows),
        split_heads(value_rows),
    )
    grad_heads = split_heads(grad_attended)
    query_grads = []
    key_grad = jnp.zeros(key_heads.shape, jnp.float32)
    value_grad = jnp.zeros(value_heads.shape, jnp.float32)
    for row_begin in range(0, length, block_rows):
        finish = row_begin + block_rows
        scores = block_scores(query_heads, key_heads, row_begin, block_rows, finish)
        probs = jnp.exp(scores - log_totals[:, row_begin:finish, None])
        grad_probs = jnp.einsum(
            "qhd,khd->hqk",
            grad_heads[row_begin:finish],
            value_heads[:finish],
            preferred_element_type=jnp.float32,
        )
        grad_scores = (
            probs
            * (grad_probs - jnp.sum(probs * grad_probs, axis=-1, keepdims=True))
            * HEAD ** (-0.5)
        ).astype(jnp.bfloat16)
        query_grads.append(
            jnp.einsum(
                "hqk,khd->qhd", grad_scores, key_heads[:finish], preferred_element_type=jnp.float32
            )
        )
        padding = ((0, length - finish), (0, 0), (0, 0))
        key_grad = key_grad + jnp.pad(
            jnp.einsum(
                "hqk,qhd->khd",
                grad_scores,
                query_heads[row_begin:finish],
                preferred_element_type=jnp.float32,
            ),
            padding,
        )
        value_grad = value_grad + jnp.pad(
            jnp.einsum(
                "hqk,qhd->khd",
                probs.astype(jnp.bfloat16),
                grad_heads[row_begin:finish],
                preferred_element_type=jnp.float32,
            ),
            padding,
        )
    query_grad = jnp.concatenate(query_grads, 0).astype(jnp.bfloat16).reshape(length, -1)
    return (
        query_grad,
        key_grad.astype(jnp.bfloat16).reshape(length, -1),
        value_grad.astype(jnp.bfloat16).reshape(length, -1),
    )


def layer_forward(inputs, small, mats):
    (
        gain_one,
        shift_one,
        query_bias,
        value_bias,
        output_shift,
        gain_two,
        shift_two,
        expand_shift,
        contract_shift,
    ) = small
    attend_full, expand_full, output_full, contract_full = mats
    residual = inputs.astype(jnp.float32)
    normed_one, centred_one, scale_one = norm_forward(residual, gain_one, shift_one)
    full_one = gather_cols(normed_one)
    projected = product(full_one, attend_full).reshape(residual.shape[0], 3, -1)
    queries = (projected[:, 0] + query_bias).astype(jnp.bfloat16)
    key_rows = projected[:, 1].astype(jnp.bfloat16)
    value_rows = (projected[:, 2] + value_bias).astype(jnp.bfloat16)
    attended, log_totals = attention_forward(queries, key_rows, value_rows)
    hidden = residual + branch_sum(product(attended, output_full)) + output_shift
    normed_two, centred_two, scale_two = norm_forward(hidden, gain_two, shift_two)
    full_two = gather_cols(normed_two)
    before_gelu = product(full_two, expand_full) + expand_shift
    activations = gelu(before_gelu).astype(jnp.bfloat16)
    result = hidden + branch_sum(product(activations, contract_full)) + contract_shift
    kept = (
        full_one,
        queries,
        key_rows,
        value_rows,
        attended,
        log_totals,
        centred_one,
        scale_one,
        centred_two,
        scale_two,
        full_two,
        before_gelu,
        activations,
    )
    return (result, kept)


def layer_backward(grad_result, kept, small, mats):
    (
        gain_one,
        shift_one,
        query_bias,
        value_bias,
        output_shift,
        gain_two,
        shift_two,
        expand_shift,
        contract_shift,
    ) = small
    attend_full, expand_full, output_full, contract_full = mats
    (
        full_one,
        queries,
        key_rows,
        value_rows,
        attended,
        log_totals,
        centred_one,
        scale_one,
        centred_two,
        scale_two,
        full_two,
        before_gelu,
        activations,
    ) = kept
    grad_full = gather_grads(grad_result.astype(jnp.bfloat16))
    grad_activations = cross_last(grad_full, contract_full)
    contract_grad = cross_first(activations, grad_full)
    contract_shift_grad = jnp.sum(grad_result, axis=0)
    unused, pullback = jax.vjp(gelu, before_gelu)
    grad_before = pullback(grad_activations)[0].astype(jnp.bfloat16)
    expand_grad = cross_first(full_two, grad_before)
    expand_shift_grad = jnp.sum(grad_before.astype(jnp.float32), axis=0)
    grad_normed_two = input_sum(cross_last(grad_before, expand_full))
    grad_norm_two, gain_two_grad, shift_two_grad = norm_backward(
        grad_normed_two, centred_two, scale_two, gain_two
    )
    grad_hidden = grad_result + grad_norm_two
    hidden_full = gather_grads(grad_hidden.astype(jnp.bfloat16))
    grad_attended = cross_last(hidden_full, output_full).astype(jnp.bfloat16)
    output_grad = cross_first(attended, hidden_full)
    output_shift_grad = jnp.sum(grad_hidden, axis=0)
    grad_query, grad_key, grad_value = attention_backward(
        queries, key_rows, value_rows, log_totals, grad_attended
    )
    grad_mixed = jnp.concatenate([grad_query, grad_key, grad_value], 1)
    attend_grad = cross_first(full_one, grad_mixed)
    bias_grad = jnp.stack(
        [
            jnp.sum(grad_query.astype(jnp.float32), axis=0),
            jnp.sum(grad_value.astype(jnp.float32), axis=0),
        ]
    )
    grad_normed_one = input_sum(cross_last(grad_mixed, attend_full))
    grad_norm_one, gain_one_grad, shift_one_grad = norm_backward(
        grad_normed_one, centred_one, scale_one, gain_one
    )
    grad_input = grad_hidden + grad_norm_one
    mat_grads = (attend_grad, expand_grad, output_grad, contract_grad)
    small_grads = (
        gain_one_grad,
        shift_one_grad,
        bias_grad,
        output_shift_grad,
        gain_two_grad,
        shift_two_grad,
        expand_shift_grad,
        contract_shift_grad,
    )
    return (grad_input, mat_grads, small_grads)


def on_device(
    tokens,
    cotangent,
    first_gain,
    first_shift,
    attend_weight,
    attend_bias,
    output_weight,
    output_bias,
    second_gain,
    second_shift,
    expand_weight,
    expand_bias,
    contract_weight,
    contract_bias,
):
    first_section = lax.axis_index("section") == 0
    length = LENGTH
    micro_count = tokens.shape[0] // length
    column_count = tokens.shape[1]
    small = (
        first_gain[0].astype(jnp.float32),
        first_shift[0].astype(jnp.float32),
        attend_bias[0, 0].astype(jnp.float32),
        attend_bias[0, 1].astype(jnp.float32),
        output_bias[0].astype(jnp.float32),
        second_gain[0].astype(jnp.float32),
        second_shift[0].astype(jnp.float32),
        expand_bias[0].astype(jnp.float32),
        contract_bias[0].astype(jnp.float32),
    )
    forward_mats = fetch_forward(
        attend_weight[0], expand_weight[0], output_weight[0], contract_weight[0]
    )

    def pick(early, later):
        return jnp.where(first_section, early, later)

    received = jnp.zeros((length, column_count), jnp.bfloat16)
    results = []
    kept_list = []
    for slot_index in range(micro_count + 1):
        own_index = min(slot_index, micro_count - 1)
        own_rows = tokens[own_index * length : (own_index + 1) * length]
        result, kept = layer_forward(pick(own_rows, received), small, forward_mats)
        result_low = result.astype(jnp.bfloat16)
        results.append(result_low)
        kept_list.append(kept)
        if slot_index < micro_count:
            received = from_behind(result_low, "section", 1)
    backward_mats = fetch_backward(
        attend_weight[0], expand_weight[0], output_weight[0], contract_weight[0]
    )
    back_received = jnp.zeros((length, column_count), jnp.bfloat16)
    grad_inputs = []
    mat_sums = None
    small_sums = None
    for slot_index in range(micro_count + 1):
        later_index = min(slot_index, micro_count - 1)
        earlier_index = max(slot_index - 1, 0)
        if slot_index < micro_count:
            own_grad = cotangent[later_index * length : (later_index + 1) * length].astype(
                jnp.float32
            )
        else:
            own_grad = jnp.zeros((length, column_count), jnp.float32)
        incoming = pick(back_received.astype(jnp.float32), own_grad)
        kept = jax.tree.map(pick, kept_list[earlier_index], kept_list[later_index + 1])
        grad_input, mat_grads, small_grads = layer_backward(incoming, kept, small, backward_mats)
        grad_inputs.append(grad_input)
        if slot_index < micro_count:
            back_received = from_behind(grad_input.astype(jnp.bfloat16), "section", -1)
        mat_grads = reduce_weights(mat_grads)
        mat_sums = mat_grads if mat_sums is None else jax.tree.map(jnp.add, mat_sums, mat_grads)
        small_sums = (
            small_grads if small_sums is None else jax.tree.map(jnp.add, small_sums, small_grads)
        )
    (
        gain_one_grad,
        shift_one_grad,
        bias_grad,
        output_shift_grad,
        gain_two_grad,
        shift_two_grad,
        expand_shift_grad,
        contract_shift_grad,
    ) = small_sums
    summed_small = lax.psum(
        (
            gain_one_grad,
            shift_one_grad,
            bias_grad,
            output_shift_grad,
            gain_two_grad,
            shift_two_grad,
            expand_shift_grad,
            contract_shift_grad,
        ),
        "row",
    )
    attend_part, expand_part, output_part, contract_part = mat_sums
    layer_outputs = jnp.concatenate(
        [
            pick(results[micro_index], results[micro_index + 1])
            for micro_index in range(micro_count)
        ],
        0,
    )
    input_grads = jnp.concatenate(
        [
            pick(grad_inputs[micro_index + 1], grad_inputs[micro_index])
            for micro_index in range(micro_count)
        ],
        0,
    )
    attend_out = attend_part.reshape(attend_part.shape[0], 3, -1)
    return (
        layer_outputs[None],
        input_grads[None],
        summed_small[0][None],
        summed_small[1][None],
        attend_out[None],
        summed_small[2][None],
        output_part[None],
        summed_small[3][None],
        summed_small[4][None],
        summed_small[5][None],
        expand_part[None],
        summed_small[6][None],
        contract_part[None],
        summed_small[7][None],
    )


def solution(mesh):
    return jax.shard_map(
        on_device,
        mesh=mesh,
        in_specs=(
            P("row", "col"),
            P("row", "col"),
            P("section", "col"),
            P("section", "col"),
            P("section", "row", None, "col"),
            P("section", None, "col"),
            P("section", "col", "row"),
            P("section", "col"),
            P("section", "col"),
            P("section", "col"),
            P("section", "row", "col"),
            P("section", "col"),
            P("section", "col", "row"),
            P("section", "col"),
        ),
        out_specs=(
            P("section", "row", "col"),
            P("section", "row", "col"),
            P("section", "col"),
            P("section", "col"),
            P("section", "row", None, "col"),
            P("section", None, "col"),
            P("section", "col", "row"),
            P("section", "col"),
            P("section", "col"),
            P("section", "col"),
            P("section", "row", "col"),
            P("section", "col"),
            P("section", "col", "row"),
            P("section", "col"),
        ),
        check_vma=False,
    )
```

profile of v0, /device:TPU:0, one launch (start us, length us, event | category | flops | bytes accessed | tf_op | source)
XLA Modules:
  0.0 2220.2 jit_solution(9722988755792266035)
XLA Ops:
  22.4 67.9 %all-gather.1 = bf16[1,320,1280]{1,0,2:T(2,128)(2,1)} all-gather(bf16[1,320,320]{1,0,2:T(2,128)(2,1)S(1)} %copy.103), channel_id=3, replica_groups=mesh['section'=2,'row'=4,'col'=4] {'row'}, dimensions={2}, use_global_device_ids=true | all-gather | bytes 1024000 | tf_op jit(solution)/shard_map/all_gather | solution.py:72
  95.6 25.1 %all-gather.44.cloned.1.call-done = bf16[1,1280,3,320]{3,2,0,1:T(4,128)(2,1)} async-done(((bf16[1,320,3,320]{3,2,0,1:T(4,128)(2,1)}), bf16[1,1280,3,320]{3,2,0,1:T(4,128)(2,1)}) %all-gather.44.cloned.1.call-update) | async-done | bytes 2457616 | tf_op jit(solution)/shard_map/all_gather | solution.py:68
  128.2 18.9 all-gather.20.cloned.1.call-done
  172.7 50.8 %reduce-scatter.31.cloned.1.call-done = f32[1024,320]{0,1:T(8,128)} async-done(((f32[1024,1280]{0,1:T(8,128)}), f32[1024,320]{0,1:T(8,128)}) %reduce-scatter.31.cloned.1.call-update) | async-done | bytes 1310736 | tf_op jit(solution)/shard_map/reduce_scatter | solution.py:57
  232.9 57.8 %all-gather.46.cloned.1.call-done = bf16[1,1280,1280]{2,1,0:T(8,128)(2,1)} async-done(((bf16[1,320,1280]{2,1,0:T(8,128)(2,1)}), bf16[1,1280,1280]{2,1,0:T(8,128)(2,1)}) %all-gather.46.cloned.1.call-update) | async-done | bytes 3276816 | tf_op jit(solution)/shard_map/all_gather | solution.py:69
  290.7 26.3 %all-gather.22.cloned.1.call-done = bf16[1024,1280]{0,1:T(8,128)(2,1)} async-done(((bf16[1024,320]{0,1:T(8,128)(2,1)}), bf16[1024,1280]{0,1:T(8,128)(2,1)}) %all-gather.22.cloned.1.call-update) | async-done | bytes 2621456 | tf_op jit(solution)/shard_map/all_gather | solution.py:49
  325.6 58.6 %all-gather.48.cloned.1.call-done = bf16[1,1280,1280]{1,2,0:T(8,128)(2,1)} async-done(((bf16[1,1280,320]{1,2,0:T(8,128)(2,1)}), bf16[1,1280,1280]{1,2,0:T(8,128)(2,1)}) %all-gather.48.cloned.1.call-update) | async-done | bytes 3276816 | tf_op jit(solution)/shard_map/all_gather | solution.py:73
  394.6 49.5 %reduce-scatter.33.cloned.1.call-done = f32[1024,320]{0,1:T(8,128)} async-done(((f32[1024,1280]{0,1:T(8,128)}), f32[1024,320]{0,1:T(8,128)}) %reduce-scatter.33.cloned.1.call-update) | async-done | bytes 1310736 | tf_op jit(solution)/shard_map/reduce_scatter | solution.py:57
  449.0 13.9 collective-permute-done
  471.0 26.2 %all-gather.24.cloned.1.call-done = bf16[1024,1280]{0,1:T(8,128)(2,1)} async-done(((bf16[1024,320]{0,1:T(8,128)(2,1)}), bf16[1024,1280]{0,1:T(8,128)(2,1)}) %all-gather.24.cloned.1.call-update) | async-done | bytes 2621456 | tf_op jit(solution)/shard_map/all_gather | solution.py:49
  522.9 51.5 %reduce-scatter.35.cloned.1.call-done = f32[1024,320]{0,1:T(8,128)} async-done(((f32[1024,1280]{0,1:T(8,128)}), f32[1024,320]{0,1:T(8,128)}) %reduce-scatter.35.cloned.1.call-update) | async-done | bytes 1310736 | tf_op jit(solution)/shard_map/reduce_scatter | solution.py:57
  587.9 24.7 %all-gather.26.cloned.1.call-done = bf16[1024,1280]{0,1:T(8,128)(2,1)} async-done(((bf16[1024,320]{0,1:T(8,128)(2,1)}), bf16[1024,1280]{0,1:T(8,128)(2,1)}) %all-gather.26.cloned.1.call-update) | async-done | bytes 2621456 | tf_op jit(solution)/shard_map/all_gather | solution.py:49
  627.2 13.2 all-gather.32.cloned.1.call-done
  640.4 14.0 convert_reduce_fusion.2
  660.9 33.5 %reduce-scatter.37.cloned.1.call-done = f32[1024,320]{0,1:T(8,128)} async-done(((f32[1024,1280]{0,1:T(8,128)}), f32[1024,320]{0,1:T(8,128)}) %reduce-scatter.37.cloned.1.call-update) | async-done | bytes 1310736 | tf_op jit(solution)/shard_map/reduce_scatter | solution.py:57
  701.3 30.9 %reduce-scatter.43.cloned.1.call-done = bf16[1024,320]{0,1:T(8,128)(2,1)} async-done(((bf16[1024,1280]{0,1:T(8,128)(2,1)}), bf16[1024,320]{0,1:T(8,128)(2,1)}) %reduce-scatter.43.cloned.1.call-update) | async-done | bytes 655376 | tf_op jit(solution)/shard_map/reduce_scatter | solution.py:61
  764.0 12.8 all-gather.28.cloned.1.call-done
  785.6 18.3 all-gather.34.cloned.1.call-done
  861.6 22.6 %fusion.410 = bf16[5,64,512]{2,1,0:T(8,128)(2,1)} fusion(f32[5,512,1024]{2,1,0:T(8,128)} %fusion.438, f32[5,512,1024]{2,1,0:T(8,128)} %fusion.446, f32[5,512]{1,0:T(8,128)S(1)} %get-tuple-element.205, pred[512,1024]{1,0:T(8,128)(4,1)S(1)} %copy-done.18, bf16[1024,5,64]{0,2,1:T(8,128)(2,1)S(1)} %bitcast.333, bf16[1024,5,64]{0,2,1:T(8,128)(2,1)S(1)} %bitcast.327, ...), kind=kOutput, calls=%fused_computation.430 | convolution fusion | flops 364875264 | bytes 23144448 | tf_op jit(solution)/shard_map/hqk,khd->qhd/dot_general | solution.py:207
  884.3 23.6 %fusion.297 = bf16[1024,5,64]{0,2,1:T(8,128)(2,1)} fusion(bf16[512,5,64]{0,2,1:T(8,128)(2,1)S(1)} %bitcast.362, f32[5,512,1024]{2,1,0:T(8,128)} %fusion.438, f32[5,512,1024]{2,1,0:T(8,128)} %fusion.446, f32[5,512]{1,0:T(8,128)S(1)} %get-tuple-element.205, pred[512,1024]{1,0:T(8,128)(4,1)S(1)} %copy-done.18, f32[512,5,64]{0,2,1:T(8,128)} %fusion.389), kind=kOutput, calls=%fused_computation.309 | convolution fusion | flops 365039104 | bytes 23144448 | tf_op jit(solution)/shard_map/hqk,qhd->khd/dot_general | solution.py:213
  930.5 18.6 reduce-scatter.45.cloned.1.call-done
  951.7 51.2 %reduce-scatter.39.cloned.1.call-done = f32[1024,320]{0,1:T(8,128)} async-done(((f32[1024,1280]{0,1:T(8,128)}), f32[1024,320]{0,1:T(8,128)}) %reduce-scatter.39.cloned.1.call-update) | async-done | bytes 1310736 | tf_op jit(solution)/shard_map/reduce_scatter | solution.py:57
  1026.2 16.7 collective-permute-done.2
  1055.6 18.6 all-gather.36.cloned.1.call-done
  1074.2 13.8 convert_reduce_fusion.1
  1094.4 34.8 %reduce-scatter.47.cloned.1.call-done = bf16[1024,320]{0,1:T(8,128)(2,1)} async-done(((bf16[1024,1280]{0,1:T(8,128)(2,1)}), bf16[1024,320]{0,1:T(8,128)(2,1)}) %reduce-scatter.47.cloned.1.call-update) | async-done | bytes 655376 | tf_op jit(solution)/shard_map/reduce_scatter | solution.py:61
  1155.3 14.6 all-gather.38.cloned.1.call-done
  1214.1 22.2 %fusion.407 = bf16[5,64,512]{2,1,0:T(8,128)(2,1)} fusion(f32[5,512,1024]{2,1,0:T(8,128)} %fusion.436, f32[5,512,1024]{2,1,0:T(8,128)} %fusion.447, f32[5,512]{1,0:T(8,128)S(1)} %copy-done.191, pred[512,1024]{1,0:T(8,128)(4,1)S(1)} %copy-done.19, bf16[1024,5,64]{0,2,1:T(8,128)(2,1)S(1)} %bitcast.335, bf16[1024,5,64]{0,2,1:T(8,128)(2,1)} %bitcast.338, ...), kind=kOutput, calls=%fused_computation.429 | convolution fusion | flops 364875264 | bytes 23144448 | tf_op jit(solution)/shard_map/hqk,khd->qhd/dot_general | solution.py:207
  1236.4 23.4 %fusion.294 = bf16[1024,5,64]{0,2,1:T(8,128)(2,1)} fusion(bf16[512,5,64]{0,2,1:T(8,128)(2,1)S(1)} %bitcast.369, f32[5,512,1024]{2,1,0:T(8,128)} %fusion.436, f32[5,512,1024]{2,1,0:T(8,128)} %fusion.447, f32[5,512]{1,0:T(8,128)S(1)} %copy-done.191, pred[512,1024]{1,0:T(8,128)(4,1)S(1)} %copy-done.19, f32[512,5,64]{0,2,1:T(8,128)} %fusion.386), kind=kOutput, calls=%fused_computation.308 | convolution fusion | flops 365039104 | bytes 23144448 | tf_op jit(solution)/shard_map/hqk,qhd->khd/dot_general | solution.py:213
  1266.7 35.0 %reduce-scatter.49.cloned.1.call-done = bf16[1024,320]{0,1:T(8,128)(2,1)} async-done(((bf16[1024,1280]{0,1:T(8,128)(2,1)}), bf16[1024,320]{0,1:T(8,128)(2,1)}) %reduce-scatter.49.cloned.1.call-update) | async-done | bytes 655376 | tf_op jit(solution)/shard_map/reduce_scatter | solution.py:61
  1316.0 17.0 collective-permute-done.3
  1334.9 24.8 %all-gather.40.cloned.1.call-done = bf16[1024,1280]{0,1:T(8,128)(2,1)} async-done(((bf16[1024,320]{0,1:T(8,128)(2,1)}), bf16[1024,1280]{0,1:T(8,128)(2,1)}) %all-gather.40.cloned.1.call-update) | async-done | bytes 2621456 | tf_op jit(solution)/shard_map/all_gather | solution.py:53
  1359.7 13.8 convert_reduce_fusion
  1379.9 34.8 %reduce-scatter.51.cloned.1.call-done = bf16[1024,320]{0,1:T(8,128)(2,1)} async-done(((bf16[1024,1280]{0,1:T(8,128)(2,1)}), bf16[1024,320]{0,1:T(8,128)(2,1)}) %reduce-scatter.51.cloned.1.call-update) | async-done | bytes 655376 | tf_op jit(solution)/shard_map/reduce_scatter | solution.py:61
  1495.2 11.6 convolution_convert_fusion
  1566.3 24.1 %fusion.291 = bf16[1024,5,64]{0,2,1:T(8,128)(2,1)} fusion(bf16[512,5,64]{0,2,1:T(8,128)(2,1)} %bitcast.366, f32[5,512,1024]{2,1,0:T(8,128)} %fusion.434, f32[5,512,1024]{2,1,0:T(8,128)} %fusion.448, f32[5,512]{1,0:T(8,128)S(1)} %get-tuple-element.198, pred[512,1024]{1,0:T(8,128)(4,1)S(1)} %copy-done.20, f32[512,5,64]{0,2,1:T(8,128)} %fusion.383), kind=kOutput, calls=%fused_computation.307 | convolution fusion | flops 365039104 | bytes 23144448 | tf_op jit(solution)/shard_map/hqk,qhd->khd/dot_general | solution.py:213
  1590.4 21.6 fusion.404
  1643.0 51.6 %reduce-scatter.63.cloned.1.call-done = bf16[320,1280]{1,0:T(8,128)(2,1)} async-done(((bf16[1280,1280]{1,0:T(8,128)(2,1)}), bf16[320,1280]{1,0:T(8,128)(2,1)}) %reduce-scatter.63.cloned.1.call-update) | async-done | bytes 819216 | tf_op jit(solution)/shard_map/reduce_scatter | solution.py:96
  1694.6 64.9 %reduce-scatter.65.cloned.1.call-done = bf16[320,1280]{1,0:T(8,128)(2,1)} async-done(((bf16[1280,1280]{1,0:T(8,128)(2,1)}), bf16[320,1280]{1,0:T(8,128)(2,1)}) %reduce-scatter.65.cloned.1.call-update) | async-done | bytes 819216 | tf_op jit(solution)/shard_map/reduce_scatter | solution.py:96
  1762.5 61.8 %reduce-scatter.67.cloned.1.call-done = bf16[1280,320]{0,1:T(8,128)(2,1)} async-done(((bf16[1280,1280]{0,1:T(8,128)(2,1)}), bf16[1280,320]{0,1:T(8,128)(2,1)}) %reduce-scatter.67.cloned.1.call-update) | async-done | bytes 819216 | tf_op jit(solution)/shard_map/reduce_scatter | solution.py:104
  1824.3 64.7 %reduce-scatter.69.cloned.1.call-done = bf16[1280,320]{0,1:T(8,128)(2,1)} async-done(((bf16[1280,1280]{0,1:T(8,128)(2,1)}), bf16[1280,320]{0,1:T(8,128)(2,1)}) %reduce-scatter.69.cloned.1.call-update) | async-done | bytes 819216 | tf_op jit(solution)/shard_map/reduce_scatter | solution.py:104
  1889.0 64.9 %reduce-scatter.71.cloned.1.call-done = bf16[1280,320]{0,1:T(8,128)(2,1)} async-done(((bf16[1280,1280]{0,1:T(8,128)(2,1)}), bf16[1280,320]{0,1:T(8,128)(2,1)}) %reduce-scatter.71.cloned.1.call-update) | async-done | bytes 819216 | tf_op jit(solution)/shard_map/reduce_scatter | solution.py:104
  1957.2 25.9 %reduce-scatter.77.cloned.1.call-done = bf16[320,320]{1,0:T(8,128)(2,1)} async-done(((bf16[1280,320]{1,0:T(8,128)(2,1)}), bf16[320,320]{1,0:T(8,128)(2,1)}) %reduce-scatter.77.cloned.1.call-update) | async-done | bytes 204816
  1985.1 50.9 %reduce-scatter.55.cloned.1.call-done = bf16[320,960]{1,0:T(8,128)(2,1)} async-done(((bf16[1280,960]{1,0:T(8,128)(2,1)}), bf16[320,960]{1,0:T(8,128)(2,1)}) %reduce-scatter.55.cloned.1.call-update) | async-done | bytes 614416 | tf_op jit(solution)/shard_map/reduce_scatter | solution.py:93
  2036.0 54.0 %reduce-scatter.57.cloned.1.call-done = bf16[320,960]{1,0:T(8,128)(2,1)} async-done(((bf16[1280,960]{1,0:T(8,128)(2,1)}), bf16[320,960]{1,0:T(8,128)(2,1)}) %reduce-scatter.57.cloned.1.call-update) | async-done | bytes 614416 | tf_op jit(solution)/shard_map/reduce_scatter | solution.py:93
  2090.0 54.1 %reduce-scatter.59.cloned.1.call-done = bf16[320,960]{1,0:T(8,128)(2,1)} async-done(((bf16[1280,960]{1,0:T(8,128)(2,1)}), bf16[320,960]{1,0:T(8,128)(2,1)}) %reduce-scatter.59.cloned.1.call-update) | async-done | bytes 614416 | tf_op jit(solution)/shard_map/reduce_scatter | solution.py:93
  2153.1 28.4 %reduce-scatter.53.cloned.1.call-done = bf16[1024,320]{0,1:T(8,128)(2,1)} async-done(((bf16[1024,1280]{0,1:T(8,128)(2,1)}), bf16[1024,320]{0,1:T(8,128)(2,1)}) %reduce-scatter.53.cloned.1.call-update) | async-done | bytes 655376 | tf_op jit(solution)/shard_map/reduce_scatter | solution.py:61
  2193.4 19.8 all-reduce.16
  (823 shorter events, 624.6 us)
Async XLA Ops:
  7.2 113.5 %all-gather.44.cloned.1.call-start = ((), (), s32[]{:S(2)}) async-start(), calls=%async_computation.57 | async-start | bytes 4915200 | tf_op jit(solution)/shard_map/all_gather | solution.py:68
  10.1 136.9 %all-gather.20.cloned.1.call-start = ((), (), s32[]{:S(2)}) async-start(), calls=%async_computation.24 | async-start | bytes 3276800 | tf_op jit(solution)/shard_map/all_gather | solution.py:49
  20.1 1290.1 %copy-start.120 = (f32[320]{0:T(512)}, f32[320]{0:T(512)S(1)}, u32[]{:S(2)}) copy-start(f32[320]{0:T(512)S(1)} %get-tuple-element.249) | copy-start | bytes 3844
  21.3 202.2 %reduce-scatter.31.cloned.1.call-start = ((), (), s32[]{:S(2)}) async-start(), calls=%async_computation.25 | async-start | bytes 6553600 | tf_op jit(solution)/shard_map/reduce_scatter | solution.py:57
  21.4 481.7 %copy-start.177 = (f32[320]{0:T(512)}, f32[320]{0:T(512)S(1)}, u32[]{:S(2)}) copy-start(f32[320]{0:T(512)S(1)} %get-tuple-element.108) | copy-start | bytes 3844
  21.5 483.5 %copy-start.153 = (f32[5,64]{1,0:T(8,128)}, f32[5,64]{1,0:T(8,128)S(1)}, u32[]{:S(2)}) copy-start(f32[5,64]{1,0:T(8,128)S(1)} %reshape.368) | copy-start | bytes 3844
  171.9 118.8 %all-gather.46.cloned.1.call-start = ((), (), s32[]{:S(2)}) async-start(), calls=%async_computation.58 | async-start | bytes 4096000 | tf_op jit(solution)/shard_map/all_gather | solution.py:69
  172.5 144.5 %all-gather.22.cloned.1.call-start = ((), (), s32[]{:S(2)}) async-start(), calls=%async_computation.26 | async-start | bytes 3276800 | tf_op jit(solution)/shard_map/all_gather | solution.py:49
  225.1 507.1 %copy-start.5 = (f32[1024,320]{0,1:T(8,128)}, f32[1024,320]{0,1:T(8,128)S(1)}, u32[]{:S(2)}) copy-start(f32[1024,320]{0,1:T(8,128)S(1)} %get-tuple-element.165) | copy-start | bytes 3932164
  232.2 152.0 %all-gather.48.cloned.1.call-start = ((), (), s32[]{:S(2)}) async-start(), calls=%async_computation.59 | async-start | bytes 4096000 | tf_op jit(solution)/shard_map/all_gather | solution.py:73
  232.8 211.3 %reduce-scatter.33.cloned.1.call-start = ((), (), s32[]{:S(2)}) async-start(), calls=%async_computation.27 | async-start | bytes 6553600 | tf_op jit(solution)/shard_map/reduce_scatter | solution.py:57
  393.9 103.4 %all-gather.24.cloned.1.call-start = ((), (), s32[]{:S(2)}) async-start(), calls=%async_computation.28 | async-start | bytes 3276800 | tf_op jit(solution)/shard_map/all_gather | solution.py:49
  445.5 17.4 collective-permute-start
  470.6 103.9 %reduce-scatter.35.cloned.1.call-start = ((), (), s32[]{:S(2)}) async-start(), calls=%async_computation.29 | async-start | bytes 6553600 | tf_op jit(solution)/shard_map/reduce_scatter | solution.py:57
  522.9 89.7 %all-gather.26.cloned.1.call-start = ((), (), s32[]{:S(2)}) async-start(), calls=%async_computation.30 | async-start | bytes 3276800 | tf_op jit(solution)/shard_map/all_gather | solution.py:49
  585.7 54.7 %all-gather.32.cloned.1.call-start = ((), (), s32[]{:S(2)}) async-start(), calls=%async_computation.36 | async-start | bytes 3276800 | tf_op jit(solution)/shard_map/all_gather | solution.py:53
  587.9 106.5 %reduce-scatter.37.cloned.1.call-start = ((), (), s32[]{:S(2)}) async-start(), calls=%async_computation.31 | async-start | bytes 6553600 | tf_op jit(solution)/shard_map/reduce_scatter | solution.py:57
  627.1 105.1 %reduce-scatter.43.cloned.1.call-start = ((), (), s32[]{:S(2)}) async-start(), calls=%async_computation.37 | async-start | bytes 3276800 | tf_op jit(solution)/shard_map/reduce_scatter | solution.py:61
  660.8 116.0 %all-gather.28.cloned.1.call-start = ((), (), s32[]{:S(2)}) async-start(), calls=%async_computation.32 | async-start | bytes 3276800 | tf_op jit(solution)/shard_map/all_gather | solution.py:49
  697.1 38.6 %collective-permute-start.1 = (bf16[1024,320]{0,1:T(8,128)(2,1)}, bf16[1024,320]{0,1:T(8,128)(2,1)}, u32[]{:S(2)}, u32[]{:S(2)}) collective-permute-start(bf16[1024,320]{0,1:T(8,128)(2,1)} %get-tuple-element.157), channel_id=1, source_target_pairs={{0,16},{1,17},{2,18},{3,19},{4,20},{5,21},{6,22},{7,23},{8,24},{9,... | collective-permute-start | bytes 1966088 | tf_op jit(solution)/shard_map/ppermute | solution.py:17
  736.0 574.2 %copy-start.7 = (bf16[1024,320]{0,1:T(8,128)(2,1)}, bf16[1024,320]{0,1:T(8,128)(2,1)S(1)}, u32[]{:S(2)}) copy-start(bf16[1024,320]{0,1:T(8,128)(2,1)S(1)} %get-tuple-element.162) | copy-start | bytes 1966084
  749.9 54.0 %all-gather.34.cloned.1.call-start = ((), (), s32[]{:S(2)}) async-start(), calls=%async_computation.38 | async-start | bytes 3276800 | tf_op jit(solution)/shard_map/all_gather | solution.py:53
  754.9 194.2 %reduce-scatter.45.cloned.1.call-start = ((), (), s32[]{:S(2)}) async-start(), calls=%async_computation.39 | async-start | bytes 3276800 | tf_op jit(solution)/shard_map/reduce_scatter | solution.py:61
  914.2 88.7 %reduce-scatter.39.cloned.1.call-start = ((), (), s32[]{:S(2)}) async-start(), calls=%async_computation.33 | async-start | bytes 6553600 | tf_op jit(solution)/shard_map/reduce_scatter | solution.py:57
  930.4 116.5 %all-gather.30.cloned.1.call-start = ((), (), s32[]{:S(2)}) async-start(), calls=%async_computation.34 | async-start | bytes 3276800 | tf_op jit(solution)/shard_map/all_gather | solution.py:49
  1020.1 54.1 %all-gather.36.cloned.1.call-start = ((), (), s32[]{:S(2)}) async-start(), calls=%async_computation.40 | async-start | bytes 3276800 | tf_op jit(solution)/shard_map/all_gather | solution.py:53
  1024.9 18.0 collective-permute-start.2
  1044.1 85.1 %reduce-scatter.47.cloned.1.call-start = ((), (), s32[]{:S(2)}) async-start(), calls=%async_computation.41 | async-start | bytes 3276800 | tf_op jit(solution)/shard_map/reduce_scatter | solution.py:61
  1094.3 75.5 %all-gather.38.cloned.1.call-start = ((), (), s32[]{:S(2)}) async-start(), calls=%async_computation.42 | async-start | bytes 3276800 | tf_op jit(solution)/shard_map/all_gather | solution.py:53
  1143.0 158.8 %reduce-scatter.49.cloned.1.call-start = ((), (), s32[]{:S(2)}) async-start(), calls=%async_computation.43 | async-start | bytes 3276800 | tf_op jit(solution)/shard_map/reduce_scatter | solution.py:61
  1266.7 93.0 %all-gather.40.cloned.1.call-start = ((), (), s32[]{:S(2)}) async-start(), calls=%async_computation.44 | async-start | bytes 3276800 | tf_op jit(solution)/shard_map/all_gather | solution.py:53
  1314.7 18.3 collective-permute-start.3
  1334.8 79.8 %reduce-scatter.51.cloned.1.call-start = ((), (), s32[]{:S(2)}) async-start(), calls=%async_computation.45 | async-start | bytes 3276800 | tf_op jit(solution)/shard_map/reduce_scatter | solution.py:61
  1379.8 127.0 %all-gather.42.cloned.1.call-start = ((), (), s32[]{:S(2)}) async-start(), calls=%async_computation.46 | async-start | bytes 3276800 | tf_op jit(solution)/shard_map/all_gather | solution.py:53
  1429.2 206.6 %reduce-scatter.73.cloned.1.call-start = ((), (), s32[]{:S(2)}) async-start(), calls=%async_computation.60 | async-start | bytes 1228800
  1433.4 205.1 %reduce-scatter.41.cloned.1.call-start = ((), (), s32[]{:S(2)}) async-start(), calls=%async_computation.35 | async-start | bytes 6553600 | tf_op jit(solution)/shard_map/reduce_scatter | solution.py:57
  1443.5 198.1 %reduce-scatter.75.cloned.1.call-start = ((), (), s32[]{:S(2)}) async-start(), calls=%async_computation.61 | async-start | bytes 1228800
  1448.6 194.3 %reduce-scatter.61.cloned.1.call-start = ((), (), s32[]{:S(2)}) async-start(), calls=%async_computation.51 | async-start | bytes 4096000 | tf_op jit(solution)/shard_map/reduce_scatter | solution.py:96
  1456.6 238.0 %reduce-scatter.63.cloned.1.call-start = ((), (), s32[]{:S(2)}) async-start(), calls=%async_computation.52 | async-start | bytes 4096000 | tf_op jit(solution)/shard_map/reduce_scatter | solution.py:96
  1465.0 294.5 %reduce-scatter.65.cloned.1.call-start = ((), (), s32[]{:S(2)}) async-start(), calls=%async_computation.53 | async-start | bytes 4096000 | tf_op jit(solution)/shard_map/reduce_scatter | solution.py:96
  1473.0 351.4 %reduce-scatter.67.cloned.1.call-start = ((), (), s32[]{:S(2)}) async-start(), calls=%async_computation.54 | async-start | bytes 4096000 | tf_op jit(solution)/shard_map/reduce_scatter | solution.py:104
  1484.0 405.1 %reduce-scatter.69.cloned.1.call-start = ((), (), s32[]{:S(2)}) async-start(), calls=%async_computation.55 | async-start | bytes 4096000 | tf_op jit(solution)/shard_map/reduce_scatter | solution.py:104
  1495.1 458.8 %reduce-scatter.71.cloned.1.call-start = ((), (), s32[]{:S(2)}) async-start(), calls=%async_computation.56 | async-start | bytes 4096000 | tf_op jit(solution)/shard_map/reduce_scatter | solution.py:104
  1506.8 476.4 %reduce-scatter.77.cloned.1.call-start = ((), (), s32[]{:S(2)}) async-start(), calls=%async_computation.62 | async-start | bytes 1228800
  1511.1 525.0 %reduce-scatter.55.cloned.1.call-start = ((), (), s32[]{:S(2)}) async-start(), calls=%async_computation.48 | async-start | bytes 3276800 | tf_op jit(solution)/shard_map/reduce_scatter | solution.py:93
  1517.5 572.5 %reduce-scatter.57.cloned.1.call-start = ((), (), s32[]{:S(2)}) async-start(), calls=%async_computation.49 | async-start | bytes 3276800 | tf_op jit(solution)/shard_map/reduce_scatter | solution.py:93
  1531.7 612.4 %reduce-scatter.59.cloned.1.call-start = ((), (), s32[]{:S(2)}) async-start(), calls=%async_computation.50 | async-start | bytes 3276800 | tf_op jit(solution)/shard_map/reduce_scatter | solution.py:93
  1629.6 551.9 %reduce-scatter.53.cloned.1.call-start = ((), (), s32[]{:S(2)}) async-start(), calls=%async_computation.47 | async-start | bytes 3276800 | tf_op jit(solution)/shard_map/reduce_scatter | solution.py:61
  (249 other events, 6442.7 us)
Sparse Core Ops, SparseCore 0:
  10.2 110.4 all-gather.43
  122.8 24.1 all-gather.19
  172.0 51.3 reduce-scatter.30
  225.0 65.6 all-gather.45
  292.7 24.1 all-gather.21
  318.5 65.6 all-gather.47
  394.0 49.9 reduce-scatter.32
  470.7 26.5 all-gather.23
  523.0 51.3 reduce-scatter.34
  585.8 26.6 all-gather.25
  614.8 25.5 all-gather.31
  642.9 51.3 reduce-scatter.36
  697.5 34.6 reduce-scatter.42
  750.0 26.7 all-gather.27
  778.3 25.5 all-gather.33
  914.3 34.7 reduce-scatter.44
  951.5 51.3 reduce-scatter.38
  1020.2 26.6 all-gather.29
  1048.6 25.5 all-gather.35
  1094.5 34.6 reduce-scatter.46
  1143.1 26.6 all-gather.37
  1266.8 34.9 reduce-scatter.48
  1335.0 24.6 all-gather.39
  1379.9 34.6 reduce-scatter.50
  1429.3 26.6 all-gather.41
  1458.7 26.1 reduce-scatter.72
  1487.4 49.9 reduce-scatter.40
  1540.3 26.1 reduce-scatter.74
  1568.9 60.9 reduce-scatter.60
  1632.1 62.3 reduce-scatter.62
  1697.0 62.3 reduce-scatter.64
  1761.9 62.3 reduce-scatter.66
  1826.6 62.3 reduce-scatter.68
  1891.4 62.3 reduce-scatter.70
  1956.9 26.2 reduce-scatter.76
  1985.3 50.6 reduce-scatter.54
  2038.2 51.7 reduce-scatter.56
  2092.3 51.7 reduce-scatter.58
  2147.1 34.3 reduce-scatter.52
where the time goes:
time: 2230 us; the launch traced here: 2220 us
  waiting for transfers between devices  1300 us (58%)
  matrix products  557 us (25%)
  blocking collectives  160 us (7%)
  other arithmetic  108 us (5%)
  local copies, waits for them, and re-layouts  59.9 us (3%)
    reduce_scatter x6, waiting for transfers between devices, branch_sum(): lax.psum_scatter(partial_terms, 'col', scatter_dimension=1, tiled=True)  237 us
    reduce_scatter x3, waiting for transfers between devices, reduce_weights(): lax.psum_scatter(contract_grad.astype(jnp.bfloat16), 'row', scatter_dimen...  191 us
    reduce_scatter x6, waiting for transfers between devices, input_sum(): lax.psum_scatter(partial_terms.astype(jnp.bfloat16), 'col', scatter_dimen...  182 us
    reduce_scatter x3, waiting for transfers between devices, reduce_weights(): lax.psum_scatter(attend_grad.astype(jnp.bfloat16), 'row', scatter_dimensi...  159 us
    reduce_scatter x3, waiting for transfers between devices, reduce_weights(): lax.psum_scatter(expand_grad.astype(jnp.bfloat16), 'row', scatter_dimensi...  116 us
    all_gather x6, waiting for transfers between devices, gather_cols(): return lax.all_gather(values, 'col', axis=1, tiled=True)  112 us
    dot_general x6, matrix products, attention_backward(): jnp.einsum('hqk,qhd->khd', grad_scores, query_heads[row_begin:finish], pr...  99.4 us
    dot_general x6, matrix products, attention_backward(): jnp.einsum('hqk,khd->qhd', grad_scores, key_heads[:finish], preferred_ele...  95.3 us
  transfers between devices with their start and end apart: 43, of which 37 were waited for; matrix products, arithmetic and copies ran while one was open for 16% of the time, Pallas kernels for 0%

commit v1 on v0

v1 whole, which is shorter than its diff:
```python
import jax
import jax.numpy as jnp
from jax import lax
from jax.sharding import PartitionSpec as P

HEAD = 64
LENGTH = 1024
EPS = 1e-05
LOW = jnp.bfloat16
WIDE = jnp.float32


def gelu(t):
    return 0.5 * t * (1.0 + jnp.tanh(0.7978845608028654 * (t + 0.044715 * t * t * t)))


def nn(left, right):
    return jnp.dot(left, right, preferred_element_type=WIDE)


def nt(left, right):
    return lax.dot_general(left, right, (((1,), (1,)), ((), ())), preferred_element_type=WIDE)


def tn(left, right):
    return lax.dot_general(left, right, (((0,), (0,)), ((), ())), preferred_element_type=WIDE)


def gather_rows(own):
    return lax.all_gather(own, "col", axis=0, tiled=True)


def scatter_rows(partial):
    return lax.psum_scatter(
        partial.astype(LOW), "col", scatter_dimension=0, tiled=True
    ).astype(WIDE)


def swap_sections(value):
    return lax.ppermute(value, "section", [(0, 1), (1, 0)])


def normalise(values):
    center = jnp.mean(values, axis=1, keepdims=True)
    centred = values - center
    scale = lax.rsqrt(jnp.mean(centred * centred, axis=1, keepdims=True) + EPS)
    return centred * scale, scale


def norm_backward(grad, hat, scale, gain):
    scaled = grad * gain
    mean_one = jnp.mean(scaled, axis=1, keepdims=True)
    mean_two = jnp.mean(scaled * hat, axis=1, keepdims=True)
    return (
        scale * (scaled - mean_one - hat * mean_two),
        jnp.sum(grad * hat, axis=0),
        jnp.sum(grad, axis=0),
    )


def split_heads(values):
    return values.reshape(values.shape[0], values.shape[1] // HEAD, HEAD)


def block_scores(query_heads, key_heads, begin, finish):
    scores = jnp.einsum(
        "qhd,khd->hqk",
        query_heads[begin:finish],
        key_heads[:finish],
        preferred_element_type=WIDE,
    ) * HEAD ** (-0.5)
    rows = begin + lax.broadcasted_iota(jnp.int32, (finish - begin, finish), 0)
    cols = lax.broadcasted_iota(jnp.int32, (finish - begin, finish), 1)
    return jnp.where((rows >= cols)[None], scores, -1000000000.0)


def attention_forward(queries, keys, values):
    length = queries.shape[0]
    block = min(512, length)
    qh, kh, vh = split_heads(queries), split_heads(keys), split_heads(values)
    outputs, totals = [], []
    for begin in range(0, length, block):
        finish = begin + block
        scores = block_scores(qh, kh, begin, finish)
        highest = jnp.max(scores, axis=-1, keepdims=True)
        powers = jnp.exp(scores - highest)
        summed = jnp.sum(powers, axis=-1, keepdims=True)
        probs = (powers / summed).astype(LOW)
        outputs.append(
            jnp.einsum("hqk,khd->qhd", probs, vh[:finish], preferred_element_type=WIDE)
        )
        totals.append((highest + jnp.log(summed))[:, :, 0])
    return (
        jnp.concatenate(outputs, 0).astype(LOW).reshape(length, -1),
        jnp.concatenate(totals, 1),
    )


def attention_backward(queries, keys, values, totals, grad):
    length = queries.shape[0]
    block = min(512, length)
    qh, kh, vh = split_heads(queries), split_heads(keys), split_heads(values)
    gh = split_heads(grad)
    query_grads = []
    key_grad = jnp.zeros(kh.shape, WIDE)
    value_grad = jnp.zeros(vh.shape, WIDE)
    for begin in range(0, length, block):
        finish = begin + block
        scores = block_scores(qh, kh, begin, finish)
        probs = jnp.exp(scores - totals[:, begin:finish, None])
        grad_probs = jnp.einsum(
            "qhd,khd->hqk", gh[begin:finish], vh[:finish], preferred_element_type=WIDE
        )
        grad_scores = (
            probs
            * (grad_probs - jnp.sum(probs * grad_probs, axis=-1, keepdims=True))
            * HEAD ** (-0.5)
        ).astype(LOW)
        query_grads.append(
            jnp.einsum("hqk,khd->qhd", grad_scores, kh[:finish], preferred_element_type=WIDE)
        )
        padding = ((0, length - finish), (0, 0), (0, 0))
        key_grad = key_grad + jnp.pad(
            jnp.einsum(
                "hqk,qhd->khd", grad_scores, qh[begin:finish], preferred_element_type=WIDE
            ),
            padding,
        )
        value_grad = value_grad + jnp.pad(
            jnp.einsum(
                "hqk,qhd->khd", probs.astype(LOW), gh[begin:finish], preferred_element_type=WIDE
            ),
            padding,
        )
    return (
        jnp.concatenate(query_grads, 0).astype(LOW).reshape(length, -1),
        key_grad.astype(LOW).reshape(length, -1),
        value_grad.astype(LOW).reshape(length, -1),
    )


def layer_forward(x_full, x_own, small, mats):
    attend, out_t, expand, contract_t = mats
    width = out_t.shape[1]
    hat, _ = normalise(x_full.astype(WIDE))
    normed = (hat * small["gain_one"] + small["shift_one"]).astype(LOW)
    projected = nn(normed, attend)
    queries = (projected[:, :width] + small["query_bias"]).astype(LOW)
    keys = projected[:, width : 2 * width].astype(LOW)
    values = (projected[:, 2 * width :] + small["value_bias"]).astype(LOW)
    attended, totals = attention_forward(queries, keys, values)
    hidden = x_own + scatter_rows(nt(attended, out_t)) + small["out_bias"]
    hat_two, scale_two = normalise(hidden)
    second_own = (hat_two * small["gain_two"] + small["shift_two"]).astype(LOW)
    second = gather_rows(second_own)
    before = nn(second, expand) + small["expand_bias"]
    active = gelu(before).astype(LOW)
    result = hidden + scatter_rows(nt(active, contract_t)) + small["contract_bias"]
    kept = (normed, queries, keys, values, attended, totals, hat_two, scale_two, second, before, active)
    return result, kept


def layer_backward(grad_full, grad_own, x_own, kept, small, mats):
    attend, out_t, expand, contract_t = mats
    normed, queries, keys, values, attended, totals, hat_two, scale_two, second, before, active = kept
    grad_active = nn(grad_full, contract_t)
    contract_grad = tn(grad_full, active).astype(LOW)
    contract_bias_grad = jnp.sum(grad_own, axis=0)
    _, pullback = jax.vjp(gelu, before)
    grad_before = pullback(grad_active)[0].astype(LOW)
    expand_grad = tn(second, grad_before).astype(LOW)
    expand_bias_grad = jnp.sum(grad_before.astype(WIDE), axis=0)
    grad_second = scatter_rows(nt(grad_before, expand))
    through, gain_two_grad, shift_two_grad = norm_backward(
        grad_second, hat_two, scale_two, small["gain_two"]
    )
    grad_hidden = grad_own + through
    hidden_full = gather_rows(grad_hidden.astype(LOW))
    out_grad = tn(hidden_full, attended).astype(LOW)
    out_bias_grad = jnp.sum(grad_hidden, axis=0)
    grad_attended = nn(hidden_full, out_t).astype(LOW)
    gq, gk, gv = attention_backward(queries, keys, values, totals, grad_attended)
    mixed = jnp.concatenate([gq, gk, gv], 1)
    attend_grad = tn(normed, mixed).astype(LOW)
    attend_bias_grad = jnp.stack(
        [jnp.sum(gq.astype(WIDE), axis=0), jnp.sum(gv.astype(WIDE), axis=0)]
    )
    grad_first = scatter_rows(nt(mixed, attend))
    hat, scale = normalise(x_own)
    through, gain_one_grad, shift_one_grad = norm_backward(
        grad_first, hat, scale, small["gain_one"]
    )
    grad_input = grad_hidden + through
    wide_vectors = jnp.stack(
        [
            gain_one_grad,
            shift_one_grad,
            out_bias_grad,
            gain_two_grad,
            shift_two_grad,
            contract_bias_grad,
        ]
    )
    own_vectors = (attend_bias_grad, expand_bias_grad)
    return grad_input, (attend_grad, out_grad, expand_grad, contract_grad), wide_vectors, own_vectors


def on_device(
    tokens,
    cotangent,
    first_gain,
    first_shift,
    attend_weight,
    attend_bias,
    output_weight,
    output_bias,
    second_gain,
    second_shift,
    expand_weight,
    expand_bias,
    contract_weight,
    contract_bias,
):
    section = lax.axis_index("section")
    column = lax.axis_index("col")
    first_section = section == 0
    columns = lax.axis_size("col")
    width = tokens.shape[1]
    rows = LENGTH // columns
    hidden_width = expand_bias.shape[1]

    def pick(early, later):
        return jnp.where(first_section, early, later)

    def both(own):
        other = swap_sections(own)
        return pick(own, other), pick(other, own)

    packed = jnp.concatenate(
        [
            first_gain[0],
            first_shift[0],
            output_bias[0],
            second_gain[0],
            second_shift[0],
            contract_bias[0],
        ]
    )
    wide_small = lax.all_gather(packed, ("section", "col"), axis=0, tiled=False)
    wide_small = wide_small.reshape(2, columns, 6, width).astype(WIDE)
    wide_small = jnp.swapaxes(wide_small, 1, 2).reshape(2, 6, columns * width)
    own_small = both(
        jnp.concatenate([attend_bias[0, 0], attend_bias[0, 1], expand_bias[0]]).astype(WIDE)
    )
    small = []
    for layer in range(2):
        names = ("gain_one", "shift_one", "out_bias", "gain_two", "shift_two", "contract_bias")
        entry = {name: wide_small[layer, i] for i, name in enumerate(names)}
        entry["query_bias"] = own_small[layer][:width]
        entry["value_bias"] = own_small[layer][width : 2 * width]
        entry["expand_bias"] = own_small[layer][2 * width :]
        small.append(entry)

    x0_full = lax.all_gather(
        lax.dynamic_slice_in_dim(tokens, section * LENGTH, LENGTH, 0), "col", axis=1, tiled=True
    )
    gy_full = lax.all_gather(
        lax.dynamic_slice_in_dim(cotangent, section * LENGTH, LENGTH, 0), "col", axis=1, tiled=True
    )

    def fetch(block):
        own = lax.all_gather(block, "row", axis=0, tiled=True)
        return both(own)

    block_rows = attend_weight.shape[1]
    attend = fetch(attend_weight[0].reshape(block_rows, -1))
    out_t = fetch(output_weight[0].T)
    expand = fetch(expand_weight[0])
    contract_t = fetch(contract_weight[0].T)
    mats = [(attend[i], out_t[i], expand[i], contract_t[i]) for i in range(2)]

    def own_rows(full):
        return lax.dynamic_slice_in_dim(full, column * rows, rows, 0).astype(WIDE)

    def own_features(full):
        return lax.dynamic_slice_in_dim(full, column * width, width, 1)

    x0_own = own_rows(x0_full)
    y0, kept0 = layer_forward(x0_full, x0_own, small[0], mats[0])
    y0_low = y0.astype(LOW)
    x1_full = gather_rows(y0_low)
    x1_own = y0_low.astype(WIDE)
    y1, kept1 = layer_forward(x1_full, x1_own, small[1], mats[1])
    y1_full = gather_rows(y1.astype(LOW))

    gx1, mat_grads1, wide1, own1 = layer_backward(
        gy_full, own_rows(gy_full), x1_own, kept1, small[1], mats[1]
    )
    gx1_low = gx1.astype(LOW)
    gx1_full = gather_rows(gx1_low)
    gx0, mat_grads0, wide0, own0 = layer_backward(
        gx1_full, gx1_low.astype(WIDE), x0_own, kept0, small[0], mats[0]
    )
    gx0_full = gather_rows(gx0.astype(LOW))

    def to_sections(layer0, layer1):
        kept = pick(layer0, layer1)
        got = swap_sections(pick(layer1, layer0))
        return jnp.concatenate([pick(kept, got), pick(got, kept)], 0)

    layer_outputs = to_sections(own_features(x1_full), own_features(y1_full))
    input_grads = to_sections(own_features(gx0_full), own_features(gx1_full)).astype(WIDE)

    def reduce_grad(layer0, layer1):
        kept = pick(layer0, layer1)
        got = swap_sections(pick(layer1, layer0))
        total = (kept.astype(WIDE) + got.astype(WIDE)).astype(LOW)
        return lax.psum_scatter(total, "row", scatter_dimension=0, tiled=True).astype(WIDE)

    attend_part, out_part, expand_part, contract_part = [
        reduce_grad(a, b) for a, b in zip(mat_grads0, mat_grads1)
    ]

    wide_sum = lax.psum(jnp.stack([wide0, wide1]), ("section", "row", "col"))
    own_sum = lax.psum(
        jnp.stack([jnp.concatenate([a.reshape(-1), b]) for a, b in (own0, own1)]),
        ("section", "row"),
    )
    wide_mine = lax.dynamic_slice_in_dim(pick(wide_sum[0], wide_sum[1]), column * width, width, 1)
    own_mine = pick(own_sum[0], own_sum[1])
    return (
        layer_outputs[None],
        input_grads[None],
        wide_mine[0][None],
        wide_mine[1][None],
        attend_part.reshape(block_rows, 3, width)[None],
        own_mine[: 2 * width].reshape(1, 2, width),
        out_part.T[None],
        wide_mine[2][None],
        wide_mine[3][None],
        wide_mine[4][None],
        expand_part[None],
        own_mine[2 * width :][None],
        contract_part.T[None],
        wide_mine[5][None],
    )


def solution(mesh):
    return jax.shard_map(
        on_device,
        mesh=mesh,
        in_specs=(
            P("row", "col"),
            P("row", "col"),
            P("section", "col"),
            P("section", "col"),
            P("section", "row", None, "col"),
            P("section", None, "col"),
            P("section", "col", "row"),
            P("section", "col"),
            P("section", "col"),
            P("section", "col"),
            P("section", "row", "col"),
            P("section", "col"),
            P("section", "col", "row"),
            P("section", "col"),
        ),
        out_specs=(
            P("section", "row", "col"),
            P("section", "row", "col"),
            P("section", "col"),
            P("section", "col"),
            P("section", "row", None, "col"),
            P("section", None, "col"),
            P("section", "col", "row"),
            P("section", "col"),
            P("section", "col"),
            P("section", "col"),
            P("section", "row", "col"),
            P("section", "col"),
            P("section", "col", "row"),
            P("section", "col"),
        ),
        check_vma=False,
    )
```

time: 2230 us -> 1510 us (0.68)
  waiting for transfers between devices: 1300 us -> 855 us
  matrix products: 557 us -> 331 us
  other arithmetic: 108 us -> 80.2 us
    reduce_scatter x21 -> x10, waiting for transfers between devices: 886 us -> 228 us  [the longest x8 228 us: scatter_rows(): lax.psum_scatter(partial.astype(LOW), 'col', scatter_dimension=0, tiled=T...]
    ppermute x4 -> x11, waiting for transfers between devices: 47.7 us -> 284 us  [swap_sections(): return lax.ppermute(value, 'section', [(0, 1), (1, 0)])]
    dot_general x78 -> x48, matrix products: 557 us -> 331 us  [the longest x4 65.3 us: attention_backward(): jnp.einsum('hqk,qhd->khd', grad_scores, qh[begin:finish], preferred_eleme...]
    unnamed x42 -> x27, waiting for transfers between devices: 27.6 us -> 1.44 us
    psum x11 -> x2, blocking collectives: 92 us -> 77.8 us  [the longest x1 39.2 us: on_device(): lax.psum(jnp.stack([jnp.concatenate([a.reshape(-1), b]) for a, b in (own0...]
    all_gather x1 -> x2, blocking collectives: 67.9 us -> 74.2 us  [the longest x1 54.2 us: on_device(): wide_small = lax.all_gather(packed, ('section', 'col'), axis=0, tiled=False)]
    all_gather x15 -> x13, waiting for transfers between devices: 342 us -> 341 us  [the longest x3 180 us: fetch(): own = lax.all_gather(block, 'row', axis=0, tiled=True)]
  transfers between devices with their start and end apart: 43 -> 36, of which waited for: 37 -> 25; matrix products, arithmetic and copies ran while one was open for 16% -> 10% of each run, Pallas kernels for 0% -> 0%
where the time goes in v1:
time: 1510 us; the launch traced here: 1500 us
  waiting for transfers between devices  855 us (57%)
  matrix products  331 us (22%)
  blocking collectives  152 us (10%)
  other arithmetic  80.2 us (5%)
  local copies, waits for them, and re-layouts  46.6 us (3%)
  starting transfers between devices  20.9 us (1%)
  between operations  16.3 us (1%)
    ppermute x11, waiting for transfers between devices, swap_sections(): return lax.ppermute(value, 'section', [(0, 1), (1, 0)])  284 us
    reduce_scatter x8, waiting for transfers between devices, scatter_rows(): lax.psum_scatter(partial.astype(LOW), 'col', scatter_dimension=0, tiled=T...  228 us
    all_gather x3, waiting for transfers between devices, fetch(): own = lax.all_gather(block, 'row', axis=0, tiled=True)  180 us
    all_gather x8, waiting for transfers between devices, gather_rows(): return lax.all_gather(own, 'col', axis=0, tiled=True)  144 us
    dot_general x4, matrix products, attention_backward(): jnp.einsum('hqk,qhd->khd', grad_scores, qh[begin:finish], preferred_eleme...  65.3 us
    dot_general x4, matrix products, attention_backward(): jnp.einsum('hqk,khd->qhd', grad_scores, kh[:finish], preferred_element_ty...  63.7 us
    all_gather x1, blocking collectives, on_device(): wide_small = lax.all_gather(packed, ('section', 'col'), axis=0, tiled=False)  54.2 us
    dot_general x8, matrix products, nn(): return jnp.dot(left, right, preferred_element_type=WIDE)  53.8 us
  transfers between devices with their start and end apart: 36, of which 25 were waited for; matrix products, arithmetic and copies ran while one was open for 10% of the time, Pallas kernels for 0%

profile of v1, /device:TPU:0, one launch (start us, length us, event | category | flops | bytes accessed | tf_op | source)
XLA Modules:
  0.0 1501.4 jit_solution(13653723947229503250)
XLA Ops:
  14.4 53.3 %all-gather.19.cloned.1.call-done = bf16[1280,960]{1,0:T(8,128)(2,1)} async-done(((bf16[320,960]{1,0:T(8,128)(2,1)}), bf16[1280,960]{1,0:T(8,128)(2,1)}) %all-gather.19.cloned.1.call-update) | async-done | bytes 2457616 | tf_op jit(solution)/shard_map/all_gather | solution.py:272
  73.5 20.0 %all_gather.52 = bf16[1280,320]{1,0:T(8,128)(2,1)S(1)} all-gather(bf16[320,320]{1,0:T(8,128)(2,1)S(1)} %bitcast.220), channel_id=1, replica_groups=mesh['section'=2,'row'=4,'col'=4] {'row'}, dimensions={0}, use_global_device_ids=true | all-gather | bytes 1024000 | tf_op jit(solution)/shard_map/all_gather | solution.py:272
  95.1 54.2 %all-gather.2 = bf16[8,1,1920]{2,1,0:T(2,128)(2,1)S(1)} all-gather(bf16[1,1,1920]{2,1,0:T(2,128)(2,1)S(1)} %reshape.374), channel_id=2, replica_groups=mesh['section'=2,'row'=4,'col'=4] {'section','col'}, dimensions={0}, use_global_device_ids=true | all-gather | bytes 34560 | tf_op jit(solution)/shard_map/all_gather | solution.py:249
  176.2 33.2 %reduce-scatter.17.cloned.1.call-done = bf16[256,1280]{1,0:T(8,128)(2,1)} async-done(((bf16[1024,1280]{1,0:T(8,128)(2,1)}), bf16[256,1280]{1,0:T(8,128)(2,1)}) %reduce-scatter.17.cloned.1.call-update) | async-done | bytes 655376 | tf_op jit(solution)/shard_map/reduce_scatter | solution.py:34
  214.7 61.9 %all-gather.41.cloned.1.call-done = bf16[1,1280,1280]{2,1,0:T(8,128)(2,1)} async-done(((bf16[1,320,1280]{2,1,0:T(8,128)(2,1)}), bf16[1,1280,1280]{2,1,0:T(8,128)(2,1)}) %all-gather.41.cloned.1.call-update) | async-done | bytes 3276816 | tf_op jit(solution)/shard_map/all_gather | solution.py:272
  278.1 64.4 %all-gather.23.cloned.1.call-done = bf16[1280,1280]{1,0:T(8,128)(2,1)} async-done(((bf16[320,1280]{1,0:T(8,128)(2,1)}), bf16[1280,1280]{1,0:T(8,128)(2,1)}) %all-gather.23.cloned.1.call-update) | async-done | bytes 3276816 | tf_op jit(solution)/shard_map/all_gather | solution.py:272
  343.9 6.8 collective-permute-done.3
  350.8 18.0 %all-gather.21.cloned.1.call-done = bf16[1024,1280]{1,0:T(8,128)(2,1)} async-done(((bf16[256,1280]{1,0:T(8,128)(2,1)}), bf16[1024,1280]{1,0:T(8,128)(2,1)}) %all-gather.21.cloned.1.call-update) | async-done | bytes 2621456 | tf_op jit(solution)/shard_map/all_gather | solution.py:30
  375.2 44.6 %collective-permute-done.4 = bf16[1280,1280]{1,0:T(8,128)(2,1)} collective-permute-done((bf16[1280,1280]{1,0:T(8,128)(2,1)}, bf16[1280,1280]{1,0:T(8,128)(2,1)}, u32[]{:S(2)}, u32[]{:S(2)}) %collective-permute-start.4) | collective-permute-done | bytes 3276832 | tf_op jit(solution)/shard_map/ppermute | solution.py:40
  426.4 35.4 %reduce-scatter.19.cloned.1.call-done = bf16[256,1280]{1,0:T(8,128)(2,1)} async-done(((bf16[1024,1280]{1,0:T(8,128)(2,1)}), bf16[256,1280]{1,0:T(8,128)(2,1)}) %reduce-scatter.19.cloned.1.call-update) | async-done | bytes 655376 | tf_op jit(solution)/shard_map/reduce_scatter | solution.py:34
  464.2 25.6 %all-gather.25.cloned.1.call-done = bf16[1024,1280]{1,0:T(8,128)(2,1)} async-done(((bf16[256,1280]{1,0:T(8,128)(2,1)}), bf16[1024,1280]{1,0:T(8,128)(2,1)}) %all-gather.25.cloned.1.call-update) | async-done | bytes 2621456 | tf_op jit(solution)/shard_map/all_gather | solution.py:30
  516.1 33.9 %reduce-scatter.21.cloned.1.call-done = bf16[256,1280]{1,0:T(8,128)(2,1)} async-done(((bf16[1024,1280]{1,0:T(8,128)(2,1)}), bf16[256,1280]{1,0:T(8,128)(2,1)}) %reduce-scatter.21.cloned.1.call-update) | async-done | bytes 655376 | tf_op jit(solution)/shard_map/reduce_scatter | solution.py:34
  557.3 23.6 %all-gather.27.cloned.1.call-done = bf16[1024,1280]{1,0:T(8,128)(2,1)} async-done(((bf16[256,1280]{1,0:T(8,128)(2,1)}), bf16[1024,1280]{1,0:T(8,128)(2,1)}) %all-gather.27.cloned.1.call-update) | async-done | bytes 2621456 | tf_op jit(solution)/shard_map/all_gather | solution.py:30
  580.9 9.5 fusion.230
  590.4 18.3 %all-gather.31.cloned.1.call-done = bf16[1024,1280]{0,1:T(8,128)(2,1)} async-done(((bf16[1024,320]{0,1:T(8,128)(2,1)}), bf16[1024,1280]{0,1:T(8,128)(2,1)}) %all-gather.31.cloned.1.call-update) | async-done | bytes 2621456 | tf_op jit(solution)/shard_map/all_gather | solution.py:267
  608.8 12.4 convert_reduce_fusion.2
  622.6 6.9 convolution_convert_fusion.7
  629.6 9.8 convolution_convert_fusion.8
  643.9 19.6 %reduce-scatter.25.cloned.1.call-done = bf16[256,1280]{1,0:T(8,128)(2,1)} async-done(((bf16[1024,1280]{1,0:T(8,128)(2,1)}), bf16[256,1280]{1,0:T(8,128)(2,1)}) %reduce-scatter.25.cloned.1.call-update) | async-done | bytes 655376 | tf_op jit(solution)/shard_map/reduce_scatter | solution.py:34
  666.2 34.5 %reduce-scatter.23.cloned.1.call-done = bf16[256,1280]{1,0:T(8,128)(2,1)} async-done(((bf16[1024,1280]{1,0:T(8,128)(2,1)}), bf16[256,1280]{1,0:T(8,128)(2,1)}) %reduce-scatter.23.cloned.1.call-update) | async-done | bytes 655376 | tf_op jit(solution)/shard_map/reduce_scatter | solution.py:34
  706.9 25.6 %all-gather.33.cloned.1.call-done = bf16[1024,1280]{1,0:T(8,128)(2,1)} async-done(((bf16[256,1280]{1,0:T(8,128)(2,1)}), bf16[1024,1280]{1,0:T(8,128)(2,1)}) %all-gather.33.cloned.1.call-update) | async-done | bytes 2621456 | tf_op jit(solution)/shard_map/all_gather | solution.py:30
  743.8 10.3 fusion.237
  754.2 9.5 fusion.225
  763.7 6.6 fusion.319
  770.3 7.3 convert_reduce_fusion.12
  777.6 22.2 %fusion.243 = bf16[5,64,512]{2,1,0:T(8,128)(2,1)} fusion(bf16[1024,5,64]{0,2,1:T(8,128)(2,1)S(1)} %bitcast.199, f32[5,512,1024]{2,1,0:T(8,128)} %fusion.319, f32[5,512,1024]{2,1,0:T(8,128)} %copy-done.6, f32[5,512]{1,0:T(8,128)S(1)} %log_add_fusion.2, pred[512,1024]{1,0:T(8,128)(4,1)S(1)} %iota_compare_fusion), kind=kOutput, calls=%fused_computation.272 | convolution fusion | flops 364547584 | bytes 22489088 | tf_op jit(solution)/shard_map/hqk,khd->qhd/dot_general | solution.py:120
  799.8 23.4 %fusion.179 = bf16[1024,5,64]{0,2,1:T(8,128)(2,1)} fusion(bf16[512,5,64]{0,2,1:T(8,128)(2,1)S(1)} %bitcast.205, f32[5,512,1024]{2,1,0:T(8,128)} %fusion.319, f32[5,512,1024]{2,1,0:T(8,128)} %copy-done.6, f32[5,512]{1,0:T(8,128)S(1)} %log_add_fusion.2, pred[512,1024]{1,0:T(8,128)(4,1)S(1)} %iota_compare_fusion, f32[512,5,64]{0,2,1:T(8,128)} %fusion.225), kind=kOutput, calls=%fused_computation.210 | convolution fusion | flops 365039104 | bytes 23144448 | tf_op jit(solution)/shard_map/hqk,qhd->khd/dot_general | solution.py:124
  823.3 6.5 convolution_convert_fusion.6
  829.9 34.8 %reduce-scatter.27.cloned.1.call-done = bf16[256,1280]{1,0:T(8,128)(2,1)} async-done(((bf16[1024,1280]{1,0:T(8,128)(2,1)}), bf16[256,1280]{1,0:T(8,128)(2,1)}) %reduce-scatter.27.cloned.1.call-update) | async-done | bytes 655376 | tf_op jit(solution)/shard_map/reduce_scatter | solution.py:34
  869.4 25.7 %all-gather.35.cloned.1.call-done = bf16[1024,1280]{1,0:T(8,128)(2,1)} async-done(((bf16[256,1280]{1,0:T(8,128)(2,1)}), bf16[1024,1280]{1,0:T(8,128)(2,1)}) %all-gather.35.cloned.1.call-update) | async-done | bytes 2621456 | tf_op jit(solution)/shard_map/all_gather | solution.py:30
  895.0 11.9 convert_reduce_fusion.3
  913.5 36.7 %reduce-scatter.29.cloned.1.call-done = bf16[256,1280]{1,0:T(8,128)(2,1)} async-done(((bf16[1024,1280]{1,0:T(8,128)(2,1)}), bf16[256,1280]{1,0:T(8,128)(2,1)}) %reduce-scatter.29.cloned.1.call-update) | async-done | bytes 655376 | tf_op jit(solution)/shard_map/reduce_scatter | solution.py:34
  957.8 25.0 %all-gather.37.cloned.1.call-done = bf16[1024,1280]{1,0:T(8,128)(2,1)} async-done(((bf16[256,1280]{1,0:T(8,128)(2,1)}), bf16[1024,1280]{1,0:T(8,128)(2,1)}) %all-gather.37.cloned.1.call-update) | async-done | bytes 2621456 | tf_op jit(solution)/shard_map/all_gather | solution.py:30
  992.5 9.7 fusion.234
  1002.2 9.6 fusion.222
  1017.2 7.2 convert_reduce_fusion.14
  1024.4 21.5 %fusion.240 = bf16[5,64,512]{2,1,0:T(8,128)(2,1)S(1)} fusion(bf16[1024,5,64]{0,2,1:T(8,128)(2,1)S(1)} %bitcast.197, f32[5,512,1024]{2,1,0:T(8,128)} %fusion.321, f32[5,512,1024]{2,1,0:T(8,128)} %copy-done.5, f32[5,512]{1,0:T(8,128)S(1)} %copy-done.78, pred[512,1024]{1,0:T(8,128)(4,1)S(1)} %iota_compare_fusion), kind=kOutput, calls=%fused_computation.271 | convolution fusion | flops 364547584 | bytes 22489088 | tf_op jit(solution)/shard_map/hqk,khd->qhd/dot_general | solution.py:120
  1046.0 22.7 %fusion.176 = bf16[1024,5,64]{0,2,1:T(8,128)(2,1)S(1)} fusion(bf16[512,5,64]{0,2,1:T(8,128)(2,1)S(1)} %bitcast.201, f32[5,512,1024]{2,1,0:T(8,128)} %fusion.321, f32[5,512,1024]{2,1,0:T(8,128)} %copy-done.5, f32[5,512]{1,0:T(8,128)S(1)} %copy-done.78, pred[512,1024]{1,0:T(8,128)(4,1)S(1)} %iota_compare_fusion, f32[512,5,64]{0,2,1:T(8,128)} %fusion.222), kind=kOutput, calls=%fused_computation.209 | convolution fusion | flops 365039104 | bytes 23144448 | tf_op jit(solution)/shard_map/hqk,qhd->khd/dot_general | solution.py:124
  1068.8 8.0 convolution_convert_fusion.4
  1090.6 71.8 %collective-permute-done.9 = bf16[1280,1280]{1,0:T(8,128)(2,1)} collective-permute-done((bf16[1280,1280]{1,0:T(8,128)(2,1)}, bf16[1280,1280]{1,0:T(8,128)(2,1)}, u32[]{:S(2)}, u32[]{:S(2)}) %collective-permute-start.9) | collective-permute-done | bytes 3276832 | tf_op jit(solution)/shard_map/ppermute | solution.py:40
  1168.9 7.2 convolution_convert_fusion.1
  1184.0 70.8 %collective-permute-done.10 = bf16[1280,1280]{1,0:T(8,128)(2,1)S(1)} collective-permute-done((bf16[1280,1280]{1,0:T(8,128)(2,1)S(1)}, bf16[1280,1280]{1,0:T(8,128)(2,1)S(1)}, u32[]{:S(2)}, u32[]{:S(2)}) %collective-permute-start.10) | collective-permute-done | bytes 3276832 | tf_op jit(solution)/shard_map/ppermute | solution.py:40
  1264.4 17.2 %collective-permute-done.8 = bf16[1280,320]{0,1:T(8,128)(2,1)S(1)} collective-permute-done((bf16[1280,320]{0,1:T(8,128)(2,1)S(1)}, bf16[1280,320]{0,1:T(8,128)(2,1)S(1)}, u32[]{:S(2)}, u32[]{:S(2)}) %collective-permute-start.8) | collective-permute-done | bytes 819232 | tf_op jit(solution)/shard_map/ppermute | solution.py:40
  1302.1 51.1 %collective-permute-done.7 = bf16[1280,960]{0,1:T(8,128)(2,1)S(1)} collective-permute-done((bf16[1280,960]{0,1:T(8,128)(2,1)S(1)}, bf16[1280,960]{0,1:T(8,128)(2,1)S(1)}, u32[]{:S(2)}, u32[]{:S(2)}) %collective-permute-start.7) | collective-permute-done | bytes 2457632 | tf_op jit(solution)/shard_map/ppermute | solution.py:40
  1365.1 11.6 collective-permute-done.5
  1382.0 39.2 %psum.15 = f32[2,1920]{1,0:T(2,128)S(1)} all-reduce(f32[2,1920]{1,0:T(2,128)S(1)} %pad_maximum_fusion.13), channel_id=1, replica_groups=mesh['section'=2,'row'=4,'col'=4] {'section','row'}, use_global_device_ids=true, to_apply=%region_60.61 | all-reduce | flops 3840 | bytes 30720 | tf_op jit(solution)/shard_map/psum | solution.py:325
  1429.4 38.6 %psum.14 = f32[2,6,1280]{2,1,0:T(8,128)S(1)} all-reduce(f32[2,6,1280]{2,1,0:T(8,128)S(1)} %pad_maximum_fusion.12), channel_id=1, replica_groups=mesh['section'=2,'row'=4,'col'=4] {'section','row','col'}, use_global_device_ids=true, to_apply=%region_52.53 | all-reduce | flops 15360 | bytes 122880 | tf_op jit(solution)/shard_map/psum | solution.py:324
  1476.6 9.8 collective-permute-done.6
  (512 shorter events, 257.6 us)
Async XLA Ops:
  7.2 60.5 %all-gather.19.cloned.1.call-start = ((), (), s32[]{:S(2)}) async-start(), calls=%async_computation.13 | async-start | bytes 3276800 | tf_op jit(solution)/shard_map/all_gather | solution.py:272
  10.0 140.4 %all-gather.17.cloned.1.call-start = ((), (), s32[]{:S(2)}) async-start(), calls=%async_computation.12 | async-start | bytes 3276800 | tf_op jit(solution)/shard_map/all_gather | solution.py:264
  11.0 198.4 %reduce-scatter.17.cloned.1.call-start = ((), (), s32[]{:S(2)}) async-start(), calls=%async_computation.14 | async-start | bytes 3276800 | tf_op jit(solution)/shard_map/reduce_scatter | solution.py:34
  11.2 139.1 %collective-permute-start.1 = (f32[1920]{0:T(1024)S(1)}, f32[1920]{0:T(1024)S(1)}, u32[]{:S(2)}, u32[]{:S(2)}) collective-permute-start(f32[1920]{0:T(1024)S(1)} %convert_element_type.294), channel_id=1, source_target_pairs={{0,16},{16,0},{1,17},{17,1},{2,18},{18,2},{3,19},{19,3},{4,20},{20... | collective-permute-start | bytes 23048 | tf_op jit(solution)/shard_map/ppermute | solution.py:40
  14.4 80.4 %copy-start.102 = (bf16[1,320]{1,0:T(2,128)(2,1)S(1)}, bf16[1,320]{1,0:T(2,128)(2,1)}, u32[]{:S(2)}) copy-start(bf16[1,320]{1,0:T(2,128)(2,1)} %param.16) | copy-start | bytes 1924
  14.4 80.5 %copy-start.103 = (bf16[1,320]{1,0:T(2,128)(2,1)S(1)}, bf16[1,320]{1,0:T(2,128)(2,1)}, u32[]{:S(2)}) copy-start(bf16[1,320]{1,0:T(2,128)(2,1)} %param.17) | copy-start | bytes 1924
  14.4 80.5 %copy-start.104 = (bf16[1,320]{1,0:T(2,128)(2,1)S(1)}, bf16[1,320]{1,0:T(2,128)(2,1)}, u32[]{:S(2)}) copy-start(bf16[1,320]{1,0:T(2,128)(2,1)} %param.21) | copy-start | bytes 1924
  14.4 80.5 %copy-start.105 = (bf16[1,320]{1,0:T(2,128)(2,1)S(1)}, bf16[1,320]{1,0:T(2,128)(2,1)}, u32[]{:S(2)}) copy-start(bf16[1,320]{1,0:T(2,128)(2,1)} %param.22) | copy-start | bytes 1924
  14.4 80.5 %copy-start.106 = (bf16[1,320]{1,0:T(2,128)(2,1)S(1)}, bf16[1,320]{1,0:T(2,128)(2,1)}, u32[]{:S(2)}) copy-start(bf16[1,320]{1,0:T(2,128)(2,1)} %param.23) | copy-start | bytes 1924
  14.4 80.5 %copy-start.107 = (bf16[1,320]{1,0:T(2,128)(2,1)S(1)}, bf16[1,320]{1,0:T(2,128)(2,1)}, u32[]{:S(2)}) copy-start(bf16[1,320]{1,0:T(2,128)(2,1)} %param.27) | copy-start | bytes 1924
  72.1 81.7 %collective-permute-start = (bf16[1280,960]{0,1:T(8,128)(2,1)}, bf16[1280,960]{0,1:T(8,128)(2,1)}, u32[]{:S(2)}, u32[]{:S(2)}) collective-permute-start(bf16[1280,960]{0,1:T(8,128)(2,1)} %copy.90), channel_id=1, source_target_pairs={{0,16},{16,0},{1,17},{17,1},{2,18},{18,2},{3,19},{19,3},{4,20},{20... | collective-permute-start | bytes 7372808 | tf_op jit(solution)/shard_map/ppermute | solution.py:40
  94.2 76.4 %copy-start.44 = (bf16[1280,320]{0,1:T(8,128)(2,1)}, bf16[1280,320]{0,1:T(8,128)(2,1)S(1)}, u32[]{:S(2)}) copy-start(bf16[1280,320]{0,1:T(8,128)(2,1)S(1)} %copy.94) | copy-start | bytes 2457604
  94.2 76.3 %collective-permute-start.2 = (bf16[1280,320]{0,1:T(8,128)(2,1)S(1)}, bf16[1280,320]{0,1:T(8,128)(2,1)}, u32[]{:S(2)}, u32[]{:S(2)}) collective-permute-start(bf16[1280,320]{0,1:T(8,128)(2,1)S(1)} %copy.94), channel_id=1, source_target_pairs={{0,16},{16,0},{1,17},{17,1},{2,18},{18,2},{3,19},{19,3},{4,20},{20... | collective-permute-start | bytes 2457608 | tf_op jit(solution)/shard_map/ppermute | solution.py:40
  149.9 343.3 %copy-start.83 = (f32[1280]{0:T(1024)}, f32[1280]{0:T(1024)S(1)}, u32[]{:S(2)}) copy-start(f32[1280]{0:T(1024)S(1)} %get-tuple-element.92) | copy-start | bytes 15364
  173.6 103.0 %all-gather.41.cloned.1.call-start = ((), (), s32[]{:S(2)}) async-start(), calls=%async_computation.34 | async-start | bytes 4096000 | tf_op jit(solution)/shard_map/all_gather | solution.py:272
  174.2 168.3 %all-gather.23.cloned.1.call-start = ((), (), s32[]{:S(2)}) async-start(), calls=%async_computation.16 | async-start | bytes 4096000 | tf_op jit(solution)/shard_map/all_gather | solution.py:272
  174.8 194.0 %all-gather.21.cloned.1.call-start = ((), (), s32[]{:S(2)}) async-start(), calls=%async_computation.15 | async-start | bytes 3276800 | tf_op jit(solution)/shard_map/all_gather | solution.py:30
  210.8 164.4 %copy-start.72 = (f32[256]{0:T(256)}, f32[256]{0:T(256)S(1)}, u32[]{:S(2)}) copy-start(f32[256]{0:T(256)S(1)} %broadcast_multiply_fusion.13) | copy-start | bytes 3076
  212.3 162.9 %copy-start.79 = (f32[256]{0:T(256)}, f32[256]{0:T(256)S(1)}, u32[]{:S(2)}) copy-start(f32[256]{0:T(256)S(1)} %add_rsqrt_fusion.5) | copy-start | bytes 3076
  214.7 247.2 %reduce-scatter.19.cloned.1.call-start = ((), (), s32[]{:S(2)}) async-start(), calls=%async_computation.17 | async-start | bytes 3276800 | tf_op jit(solution)/shard_map/reduce_scatter | solution.py:34
  276.6 74.1 %collective-permute-start.3 = (bf16[1280,1280]{1,0:T(8,128)(2,1)}, bf16[1280,1280]{1,0:T(8,128)(2,1)}, u32[]{:S(2)}, u32[]{:S(2)}) collective-permute-start(bf16[1280,1280]{1,0:T(8,128)(2,1)} %bitcast.237), channel_id=1, source_target_pairs={{0,16},{16,0},{1,17},{17,1},{2,18},{18,2},{3,19},{19,3},{4,20},{20... | collective-permute-start | bytes 9830408 | tf_op jit(solution)/shard_map/ppermute | solution.py:40
  342.5 77.3 %collective-permute-start.4 = (bf16[1280,1280]{1,0:T(8,128)(2,1)}, bf16[1280,1280]{1,0:T(8,128)(2,1)}, u32[]{:S(2)}, u32[]{:S(2)}) collective-permute-start(bf16[1280,1280]{1,0:T(8,128)(2,1)} %all-gather.23.cloned.1.call-done), channel_id=1, source_target_pairs={{0,16},{16,0},{1,17},{17,1},{2,18},{18,2},{3,19},{19,3},{4,20},{20... | collective-permute-start | bytes 9830408 | tf_op jit(solution)/shard_map/ppermute | solution.py:40
  343.9 551.1 %copy-start.88 = (f32[1280]{0:T(1024)}, f32[1280]{0:T(1024)S(1)}, u32[]{:S(2)}) copy-start(f32[1280]{0:T(1024)S(1)} %slice.314) | copy-start | bytes 15364
  375.2 86.6 %copy-start.7 = (bf16[256,1280]{1,0:T(8,128)(2,1)S(1)}, bf16[256,1280]{1,0:T(8,128)(2,1)}, u32[]{:S(2)}) copy-start(bf16[256,1280]{1,0:T(8,128)(2,1)} %reduce-scatter.17.cloned.1.call-done) | copy-start | bytes 1966084
  426.3 63.5 %all-gather.25.cloned.1.call-start = ((), (), s32[]{:S(2)}) async-start(), calls=%async_computation.18 | async-start | bytes 3276800 | tf_op jit(solution)/shard_map/all_gather | solution.py:30
  464.1 85.9 %reduce-scatter.21.cloned.1.call-start = ((), (), s32[]{:S(2)}) async-start(), calls=%async_computation.19 | async-start | bytes 3276800 | tf_op jit(solution)/shard_map/reduce_scatter | solution.py:34
  516.1 64.8 %all-gather.27.cloned.1.call-start = ((), (), s32[]{:S(2)}) async-start(), calls=%async_computation.20 | async-start | bytes 3276800 | tf_op jit(solution)/shard_map/all_gather | solution.py:30
  555.2 53.5 %all-gather.31.cloned.1.call-start = ((), (), s32[]{:S(2)}) async-start(), calls=%async_computation.23 | async-start | bytes 3276800 | tf_op jit(solution)/shard_map/all_gather | solution.py:267
  557.3 106.2 %reduce-scatter.25.cloned.1.call-start = ((), (), s32[]{:S(2)}) async-start(), calls=%async_computation.24 | async-start | bytes 3276800 | tf_op jit(solution)/shard_map/reduce_scatter | solution.py:34
  629.6 71.1 %reduce-scatter.23.cloned.1.call-start = ((), (), s32[]{:S(2)}) async-start(), calls=%async_computation.21 | async-start | bytes 3276800 | tf_op jit(solution)/shard_map/reduce_scatter | solution.py:34
  639.5 93.0 %all-gather.33.cloned.1.call-start = ((), (), s32[]{:S(2)}) async-start(), calls=%async_computation.25 | async-start | bytes 3276800 | tf_op jit(solution)/shard_map/all_gather | solution.py:30
  706.8 157.9 %reduce-scatter.27.cloned.1.call-start = ((), (), s32[]{:S(2)}) async-start(), calls=%async_computation.26 | async-start | bytes 3276800 | tf_op jit(solution)/shard_map/reduce_scatter | solution.py:34
  829.8 65.2 %all-gather.35.cloned.1.call-start = ((), (), s32[]{:S(2)}) async-start(), calls=%async_computation.27 | async-start | bytes 3276800 | tf_op jit(solution)/shard_map/all_gather | solution.py:30
  869.3 80.9 %reduce-scatter.29.cloned.1.call-start = ((), (), s32[]{:S(2)}) async-start(), calls=%async_computation.28 | async-start | bytes 3276800 | tf_op jit(solution)/shard_map/reduce_scatter | solution.py:34
  913.5 69.3 %all-gather.37.cloned.1.call-start = ((), (), s32[]{:S(2)}) async-start(), calls=%async_computation.29 | async-start | bytes 3276800 | tf_op jit(solution)/shard_map/all_gather | solution.py:30
  957.0 333.0 %reduce-scatter.31.cloned.1.call-start = ((), (), s32[]{:S(2)}) async-start(), calls=%async_computation.30 | async-start | bytes 3276800 | tf_op jit(solution)/shard_map/reduce_scatter | solution.py:34
  1076.8 283.4 %all-gather.29.cloned.1.call-start = ((), (), s32[]{:S(2)}) async-start(), calls=%async_computation.22 | async-start | bytes 3276800 | tf_op jit(solution)/shard_map/all_gather | solution.py:30
  1089.0 73.4 %collective-permute-start.9 = (bf16[1280,1280]{1,0:T(8,128)(2,1)}, bf16[1280,1280]{1,0:T(8,128)(2,1)}, u32[]{:S(2)}, u32[]{:S(2)}) collective-permute-start(bf16[1280,1280]{1,0:T(8,128)(2,1)} %get-tuple-element.166), channel_id=1, source_target_pairs={{0,16},{16,0},{1,17},{17,1},{2,18},{18,2},{3,19},{19,3},{4,20},{20... | collective-permute-start | bytes 9830408 | tf_op jit(solution)/shard_map/ppermute | solution.py:40
  1090.5 332.0 %reduce-scatter.33.cloned.1.call-start = ((), (), s32[]{:S(2)}) async-start(), calls=%async_computation.32 | async-start | bytes 4096000 | tf_op jit(solution)/shard_map/reduce_scatter | solution.py:318
  1168.2 256.7 %reduce-scatter.35.cloned.1.call-start = ((), (), s32[]{:S(2)}) async-start(), calls=%async_computation.33 | async-start | bytes 4096000 | tf_op jit(solution)/shard_map/reduce_scatter | solution.py:318
  1182.4 72.3 %collective-permute-start.10 = (bf16[1280,1280]{1,0:T(8,128)(2,1)S(1)}, bf16[1280,1280]{1,0:T(8,128)(2,1)S(1)}, u32[]{:S(2)}, u32[]{:S(2)}) collective-permute-start(bf16[1280,1280]{1,0:T(8,128)(2,1)S(1)} %get-tuple-element.168), channel_id=1, source_target_pairs={{0,16},{16,0},{1,17},{17,1},{2,18},{18,2},{3,19},{19,3},{4,20},{20... | collective-permute-start | bytes 9830408 | tf_op jit(solution)/shard_map/ppermute | solution.py:40
  1257.8 169.5 %reduce-scatter.39.cloned.1.call-start = ((), (), s32[]{:S(2)}) async-start(), calls=%async_computation.36 | async-start | bytes 1228800
  1262.8 18.7 %collective-permute-start.8 = (bf16[1280,320]{0,1:T(8,128)(2,1)S(1)}, bf16[1280,320]{0,1:T(8,128)(2,1)S(1)}, u32[]{:S(2)}, u32[]{:S(2)}) collective-permute-start(bf16[1280,320]{0,1:T(8,128)(2,1)S(1)} %get-tuple-element.164), channel_id=1, source_target_pairs={{0,16},{16,0},{1,17},{17,1},{2,18},{18,2},{3,19},{19,3},{4,20},{20... | collective-permute-start | bytes 2457608 | tf_op jit(solution)/shard_map/ppermute | solution.py:40
  1283.2 184.8 %all-gather.39.cloned.1.call-start = ((), (), s32[]{:S(2)}) async-start(), calls=%async_computation.31 | async-start | bytes 3276800 | tf_op jit(solution)/shard_map/all_gather | solution.py:30
  1294.3 179.4 %reduce-scatter.37.cloned.1.call-start = ((), (), s32[]{:S(2)}) async-start(), calls=%async_computation.35 | async-start | bytes 3276800
  1299.8 53.4 %collective-permute-start.7 = (bf16[1280,960]{0,1:T(8,128)(2,1)S(1)}, bf16[1280,960]{0,1:T(8,128)(2,1)S(1)}, u32[]{:S(2)}, u32[]{:S(2)}) collective-permute-start(bf16[1280,960]{0,1:T(8,128)(2,1)S(1)} %get-tuple-element.154), channel_id=1, source_target_pairs={{0,16},{16,0},{1,17},{17,1},{2,18},{18,2},{3,19},{19,3},{4,20},{20... | collective-permute-start | bytes 7372808 | tf_op jit(solution)/shard_map/ppermute | solution.py:40
  1362.9 13.9 collective-permute-start.5
  1470.7 15.7 %collective-permute-start.6 = (bf16[1024,320]{0,1:T(8,128)(2,1)S(1)}, bf16[1024,320]{0,1:T(8,128)(2,1)S(1)}, u32[]{:S(2)}, u32[]{:S(2)}) collective-permute-start(bf16[1024,320]{0,1:T(8,128)(2,1)S(1)} %copy.108), channel_id=1, source_target_pairs={{0,16},{16,0},{1,17},{17,1},{2,18},{18,2},{3,19},{19,3},{4,20},{20... | collective-permute-start | bytes 1966088 | tf_op jit(solution)/shard_map/ppermute | solution.py:40
  (115 other events, 1251.9 us)
Sparse Core Ops, SparseCore 0:
  10.2 57.4 all-gather.18
  69.9 24.3 all-gather.16
  173.7 35.6 reduce-scatter.16
  210.9 65.6 all-gather.40
  278.1 64.2 all-gather.22
  344.5 24.1 all-gather.20
  426.5 35.3 reduce-scatter.18
  464.2 25.5 all-gather.24
  516.2 33.7 reduce-scatter.20
  555.3 25.5 all-gather.26
  583.2 25.5 all-gather.30
  629.7 33.7 reduce-scatter.24
  666.0 34.6 reduce-scatter.22
  706.9 25.5 all-gather.32
  829.9 34.6 reduce-scatter.26
  869.4 25.5 all-gather.34
  913.6 36.6 reduce-scatter.28
  957.1 25.5 all-gather.36
  1076.9 34.6 reduce-scatter.30
  1113.6 25.5 all-gather.28
  1168.3 62.2 reduce-scatter.32
  1257.9 62.5 reduce-scatter.34
  1323.4 26.2 reduce-scatter.38
  1351.2 24.1 all-gather.38
  1378.3 53.0 reduce-scatter.36

commit v2 on v1

v2 whole, which is shorter than its diff:
```python
import functools

import jax
import jax.numpy as jnp
from jax import lax
from jax.experimental import pallas as pl
from jax.experimental.pallas import tpu as pltpu
from jax.sharding import PartitionSpec as P

HEAD = 64
LENGTH = 1024
EPS = 1e-05
LOW = jnp.bfloat16
WIDE = jnp.float32
MESH = pl.DeviceIdType.MESH
PARTS = 2
TILE = 256
MEBI = 1024 * 1024


def nn(left, right):
    return lax.dot_general(left, right, (((1,), (0,)), ((), ())), preferred_element_type=WIDE)


def nt(left, right):
    return lax.dot_general(left, right, (((1,), (1,)), ((), ())), preferred_element_type=WIDE)


def tn(left, right):
    return lax.dot_general(left, right, (((0,), (0,)), ((), ())), preferred_element_type=WIDE)


def normalise(values):
    center = jnp.mean(values, axis=1, keepdims=True)
    centred = values - center
    scale = lax.rsqrt(jnp.mean(centred * centred, axis=1, keepdims=True) + EPS)
    return centred * scale, scale


def norm_backward(grad, hat, scale, gain):
    scaled = grad * gain
    mean_one = jnp.mean(scaled, axis=1, keepdims=True)
    mean_two = jnp.mean(scaled * hat, axis=1, keepdims=True)
    return scale * (scaled - mean_one - hat * mean_two)


class Group:
    def __init__(self, rows):
        self.me = lax.axis_index("col")
        chip, core = self.me // 2, self.me % 2
        self.sib = chip * 2 + 1 - core
        self.peer = (1 - chip) * 2 + core
        self.diag = (1 - chip) * 2 + 1 - core
        self.rows = rows
        self.part = rows // PARTS

    def greet(self):
        barrier = pltpu.get_barrier_semaphore()
        for other in (self.sib, self.peer):
            pl.semaphore_signal(barrier, inc=1, device_id={"col": other}, device_id_type=MESH)
        pl.semaphore_wait(barrier, 2)

    def slab(self, owner, j):
        return pl.ds(pl.multiple_of(owner * self.rows + j * self.part, self.part), self.part)

    def chunk(self, owner):
        return pl.ds(pl.multiple_of(owner * self.rows, self.rows), self.rows)


def push(src, dst, sems, slot, target):
    return pltpu.make_async_remote_copy(
        src_ref=src,
        dst_ref=dst,
        send_sem=sems.at[0, slot],
        recv_sem=sems.at[1, slot],
        device_id={"col": target},
        device_id_type=MESH,
    )


class Gather:
    def __init__(self, group, full, sems):
        self.group, self.full, self.sems = group, full, sems

    def start(self):
        g = self.group
        self.over, self.near, self.relayed = [], [], []
        for j in range(PARTS):
            piece = self.full.at[g.slab(g.me, j)]
            self.over.append(push(piece, piece, self.sems, j, g.peer))
            self.over[-1].start()
        for j in range(PARTS):
            piece = self.full.at[g.slab(g.me, j)]
            self.near.append(push(piece, piece, self.sems, PARTS + j, g.sib))
            self.near[-1].start()

    def sibling(self):
        for copy in self.near:
            copy.wait_recv()

    def relay(self):
        g = self.group
        for j in range(PARTS):
            self.over[j].wait_recv()
            piece = self.full.at[g.slab(g.peer, j)]
            self.relayed.append(push(piece, piece, self.sems, 2 * PARTS + j, g.sib))
            self.relayed[-1].start()

    def diagonal(self):
        for copy in self.relayed:
            copy.wait_recv()

    def done(self):
        for copy in self.over + self.near + self.relayed:
            copy.wait_send()

    def each(self, body):
        g = self.group
        self.start()
        body(g.chunk(g.me))
        self.sibling()
        body(g.chunk(g.sib))
        self.relay()
        body(g.chunk(g.peer))
        self.diagonal()
        body(g.chunk(g.diag))
        self.done()


class Scatter:
    def __init__(self, group, stage, land, total, sems):
        self.group, self.stage, self.land, self.total, self.sems = group, stage, land, total, sems

    def start(self, part):
        g, stage, land = self.group, self.stage, self.land
        self.first, self.over, self.near = [], [], []
        for j in range(PARTS):
            stage[0, j] = part(g.slab(g.diag, j)).astype(LOW)
            self.first.append(push(stage.at[0, j], land.at[0, j], self.sems, j, g.sib))
            self.first[-1].start()
        for j in range(PARTS):
            mine = part(g.slab(g.peer, j))
            self.first[j].wait_recv()
            stage[1, j] = (mine + land[0, j].astype(WIDE)).astype(LOW)
            self.over.append(push(stage.at[1, j], land.at[1, j], self.sems, PARTS + j, g.peer))
            self.over[-1].start()
        for j in range(PARTS):
            stage[2, j] = part(g.slab(g.sib, j)).astype(LOW)
            self.near.append(push(stage.at[2, j], land.at[2, j], self.sems, 2 * PARTS + j, g.sib))
            self.near[-1].start()
        for j in range(PARTS):
            self.total[j] = part(g.slab(g.me, j))

    def take(self, j):
        self.near[j].wait_recv()
        self.over[j].wait_recv()
        land = self.land
        return self.total[j] + (land[1, j].astype(WIDE) + land[2, j].astype(WIDE))

    def done(self):
        for copy in self.first + self.over + self.near:
            copy.wait_send()


def scatter_scratch(rows, width):
    part = rows // PARTS
    return [
        pltpu.VMEM((3, PARTS, part, width), LOW),
        pltpu.VMEM((3, PARTS, part, width), LOW),
        pltpu.VMEM((PARTS, part, width), WIDE),
        pltpu.SemaphoreType.DMA((2, 3 * PARTS)),
    ]


class Halves:
    def __init__(self, pair, whole, sems, slot):
        section = lax.axis_index("section")
        half = whole.shape[1] // 2
        self.copies = []
        for n, place in enumerate((section, 1 - section)):
            columns = pl.ds(pl.multiple_of(place * half, half), half)
            self.copies.append(
                pltpu.make_async_copy(pair[n], whole.at[:, columns], sems.at[slot + n])
            )

    def start(self):
        for copy in self.copies:
            copy.start()

    def wait(self):
        for copy in self.copies:
            copy.wait()


def attention_out(heads_ref, o3, lse_ref, heads):
    length = heads_ref.shape[1]
    size = min(TILE, length)

    @pl.loop(0, heads)
    def _(h):
        for i in range(length // size):
            rows = slice(i * size, (i + 1) * size)
            finish = (i + 1) * size
            queries = heads_ref[h, rows, :]
            scores = nt(heads_ref[heads + h, :finish, :], queries)
            keep = lax.broadcasted_iota(jnp.int32, (size, size), 0) <= lax.broadcasted_iota(
                jnp.int32, (size, size), 1
            )
            last = jnp.where(keep, scores[finish - size :], -1000000000.0)
            scores = last if i == 0 else jnp.concatenate([scores[: finish - size], last], 0)
            highest = jnp.max(scores, axis=0, keepdims=True)
            powers = jnp.exp(scores - highest)
            summed = jnp.sum(powers, axis=0, keepdims=True)
            mixed = tn(heads_ref[2 * heads + h, :finish, :], powers.astype(LOW))
            o3[h, rows, :] = (mixed / summed).T.astype(LOW)
            lse_ref[pl.ds(h, 1), rows] = highest + jnp.log(summed)


def attention_back(heads_ref, go3, lse_ref, dots_ref, g3, key_acc, value_acc, heads):
    length = heads_ref.shape[1]
    size = min(TILE, length)

    @pl.loop(0, heads)
    def _(h):
        for i in reversed(range(length // size)):
            rows = slice(i * size, (i + 1) * size)
            finish = (i + 1) * size
            queries = heads_ref[h, rows, :]
            keys = heads_ref[heads + h, :finish, :]
            grads = go3[h, rows, :]
            scores = nt(keys, queries) - lse_ref[pl.ds(h, 1), rows]
            keep = lax.broadcasted_iota(jnp.int32, (size, size), 0) <= lax.broadcasted_iota(
                jnp.int32, (size, size), 1
            )
            last = jnp.where(keep, scores[finish - size :], -1000000000.0)
            scores = last if i == 0 else jnp.concatenate([scores[: finish - size], last], 0)
            probs = jnp.exp(scores)
            grad_probs = nt(heads_ref[2 * heads + h, :finish, :], grads)
            grad_scores = (probs * (grad_probs - dots_ref[pl.ds(h, 1), rows])).astype(LOW)
            g3[h, rows, :] = (tn(grad_scores, keys) * HEAD ** (-0.5)).astype(LOW)
            key_part = nn(grad_scores, queries)
            value_part = nn(probs.astype(LOW), grads)
            if finish == length:
                key_acc[...] = key_part
                value_acc[...] = value_part
            else:
                key_acc[:finish, :] += key_part
                value_acc[:finish, :] += value_part
        g3[heads + h] = key_acc[...].astype(LOW)
        g3[2 * heads + h] = value_acc[...].astype(LOW)


def attend_kernel(
    gathered, heads, x_ref, mine_ref, other_ref, vec_ref, bias_ref,
    full_ref, normed_ref, heads_ref, o_ref, lse_ref, hidden_ref, second_ref,
    weight, o3, stage, land, total, scatter_sems, gather_sems, local_sems,
):
    width = o_ref.shape[1]
    group = Group(hidden_ref.shape[0])
    halves = Halves((mine_ref, other_ref), weight, local_sems, 0)
    halves.start()
    group.greet()
    if not gathered:
        full_ref[group.chunk(group.me), :] = x_ref[...]
    halves.wait()

    def project(rows):
        values = (x_ref if gathered else full_ref)[rows, :].astype(WIDE)
        hat, _ = normalise(values)
        normed = (hat * vec_ref[0:1, :] + vec_ref[1:2, :]).astype(LOW)
        normed_ref[rows, :] = normed
        mixed = nn(normed, weight[:, : 3 * width]) + bias_ref[...]
        for j in range(3 * heads):
            piece = mixed[:, j * HEAD : (j + 1) * HEAD]
            if j < heads:
                piece = piece * HEAD ** (-0.5)
            heads_ref[j, rows, :] = piece.astype(LOW)

    if gathered:
        full_ref[...] = jnp.zeros_like(full_ref)

        @pl.loop(0, LENGTH // group.rows)
        def _(n):
            project(group.chunk(n))
    else:
        Gather(group, full_ref, gather_sems).each(project)

    attention_out(heads_ref, o3, lse_ref, heads)
    for h in range(heads):
        o_ref[:, h * HEAD : (h + 1) * HEAD] = o3[h]

    scatter = Scatter(group, stage, land, total, scatter_sems)
    scatter.start(lambda rows: nt(o_ref[rows, :], weight[:, 3 * width :]))
    for j in range(PARTS):
        rows = slice(j * group.part, (j + 1) * group.part)
        residual = (x_ref if gathered else full_ref)[group.slab(group.me, j), :].astype(WIDE)
        hidden = residual + scatter.take(j) + vec_ref[2:3, :]
        hidden_ref[rows, :] = hidden
        hat, _ = normalise(hidden)
        second_ref[rows, :] = (hat * vec_ref[3:4, :] + vec_ref[4:5, :]).astype(LOW)
    scatter.done()


def expand_kernel(
    second_ref, hidden_ref, em_ref, eo_ref, cm_ref, co_ref, vec_ref, bias_ref,
    full_ref, active_ref, slope_ref, result_ref,
    expand, contract, stage, land, total, scatter_sems, gather_sems, local_sems,
):
    group = Group(hidden_ref.shape[0])
    first = Halves((em_ref, eo_ref), expand, local_sems, 0)
    then = Halves((cm_ref, co_ref), contract, local_sems, 2)
    first.start()
    then.start()
    group.greet()
    full_ref[group.chunk(group.me), :] = second_ref[...]
    first.wait()

    def widen(rows):
        t = nn(full_ref[rows, :], expand[...]) + bias_ref[...]
        square = t * t
        bent = jnp.tanh(0.7978845608028654 * t * (1.0 + 0.044715 * square))
        active_ref[rows, :] = (0.5 * t * (1.0 + bent)).astype(LOW)
        slope_ref[rows, :] = (
            0.5 * (1.0 + bent)
            + (0.5 * 0.7978845608028654) * t * (1.0 - bent * bent) * (1.0 + 3 * 0.044715 * square)
        ).astype(LOW)

    Gather(group, full_ref, gather_sems).each(widen)
    then.wait()
    scatter = Scatter(group, stage, land, total, scatter_sems)
    scatter.start(lambda rows: nt(active_ref[rows, :], contract[...]))
    for j in range(PARTS):
        rows = slice(j * group.part, (j + 1) * group.part)
        result = hidden_ref[rows, :] + scatter.take(j) + vec_ref[5:6, :]
        result_ref[rows, :] = result.astype(LOW)
    scatter.done()


def outer_halves(left_ref, right_ref, keep_ref, send_ref):
    section = lax.axis_index("section")
    half = right_ref.shape[1] // 2
    for place, out in ((section, keep_ref), (1 - section, send_ref)):
        columns = pl.ds(pl.multiple_of(place * half, half), half)

        @pl.loop(0, left_ref.shape[1] // TILE)
        def _(n):
            rows = pl.ds(pl.multiple_of(n * TILE, TILE), TILE)
            out[rows, :] = tn(left_ref[:, rows], right_ref[:, columns]).astype(LOW)


def expand_back_kernel(
    gathered, g_ref, em_ref, eo_ref, cm_ref, co_ref, active_ref, slope_ref, second_ref, hidden_ref, vec_ref,
    full_ref, ek_ref, es_ref, ck_ref, cs_ref, grad_ref, low_ref, sums_ref,
    expand, contract, before, stage, land, total, scatter_sems, gather_sems, local_sems,
):
    group = Group(hidden_ref.shape[0])
    first = Halves((cm_ref, co_ref), contract, local_sems, 0)
    then = Halves((em_ref, eo_ref), expand, local_sems, 2)
    first.start()
    then.start()
    group.greet()
    sums_ref[...] = jnp.zeros_like(sums_ref)
    if gathered:
        full_ref[...] = g_ref[...]
    else:
        full_ref[group.chunk(group.me), :] = g_ref[...]
    first.wait()

    def bend(rows):
        grad = (nn(full_ref[rows, :], contract[...]) * slope_ref[rows, :].astype(WIDE)).astype(LOW)
        before[rows, :] = grad
        sums_ref[4:5, :] += jnp.sum(grad.astype(WIDE), axis=0, keepdims=True)

    if gathered:

        @pl.loop(0, LENGTH // group.rows)
        def _(n):
            bend(group.chunk(n))
    else:
        Gather(group, full_ref, gather_sems).each(bend)
    then.wait()
    scatter = Scatter(group, stage, land, total, scatter_sems)
    scatter.start(lambda rows: nt(before[rows, :], expand[...]))
    outer_halves(full_ref, active_ref, ck_ref, cs_ref)
    outer_halves(second_ref, before, ek_ref, es_ref)
    for j in range(PARTS):
        rows = slice(j * group.part, (j + 1) * group.part)
        grad = scatter.take(j)
        hat, scale = normalise(hidden_ref[rows, :])
        own = full_ref[group.slab(group.me, j), :].astype(WIDE)
        out = own + norm_backward(grad, hat, scale, vec_ref[3:4, :])
        grad_ref[rows, :] = out
        low_ref[rows, :] = out.astype(LOW)
        for n, term in enumerate((grad * hat, grad, own, out)):
            sums_ref[n : n + 1, :] += jnp.sum(term, axis=0, keepdims=True)
    scatter.done()


def attend_back_kernel(
    heads, low_ref, grad_ref, x_ref, mine_ref, other_ref, normed_ref, heads_ref, o_ref, lse_ref, vec_ref,
    wk_ref, ws_ref, out_ref, sums_ref,
    weight, full, go3, dots, g3, key_acc, value_acc, mixed, outer,
    stage, land, total, scatter_sems, gather_sems, local_sems,
):
    width = o_ref.shape[1]
    group = Group(grad_ref.shape[0])
    section = lax.axis_index("section")
    halves = Halves((mine_ref, other_ref), weight, local_sems, 0)
    halves.start()
    group.greet()
    sums_ref[...] = jnp.zeros_like(sums_ref)
    full[group.chunk(group.me), :] = low_ref[...]
    halves.wait()
    picks = (
        lax.broadcasted_iota(jnp.int32, (8, width), 1) // HEAD
        == lax.broadcasted_iota(jnp.int32, (8, width), 0)
    ).astype(WIDE)

    def spread(rows):
        grads = nn(full[rows, :], weight[:, 3 * width :]).astype(LOW)
        for h in range(heads):
            go3[h, rows, :] = grads[:, h * HEAD : (h + 1) * HEAD]
        term = grads.astype(WIDE) * o_ref[rows, :].astype(WIDE)
        dots[:, rows] = lax.dot_general(
            picks,
            term,
            (((1,), (1,)), ((), ())),
            precision=lax.Precision.HIGHEST,
            preferred_element_type=WIDE,
        )

    Gather(group, full, gather_sems).each(spread)
    attention_back(heads_ref, go3, lse_ref, dots, g3, key_acc, value_acc, heads)
    for j in range(3 * heads):
        mixed[:, j * HEAD : (j + 1) * HEAD] = g3[j]

    scatter = Scatter(group, stage, land, total, scatter_sems)
    scatter.start(lambda rows: nt(mixed[rows, :], weight[:, : 3 * width]))

    half = weight.shape[1] // 2

    @pl.loop(0, weight.shape[0] // TILE)
    def _(n):
        rows = pl.ds(pl.multiple_of(n * TILE, TILE), TILE)
        outer[section, rows, :] = tn(normed_ref[:, rows], mixed[:, :half]).astype(LOW)
        outer[1 - section, rows, : 3 * width - half] = tn(
            normed_ref[:, rows], mixed[:, half:]
        ).astype(LOW)
        outer[1 - section, rows, 3 * width - half :] = tn(full[:, rows], o_ref[...]).astype(LOW)

    keep = pltpu.make_async_copy(outer.at[0], wk_ref, local_sems.at[2])
    send = pltpu.make_async_copy(outer.at[1], ws_ref, local_sems.at[3])
    keep.start()
    send.start()
    sums_ref[2:3, : 3 * width] = jnp.sum(mixed[...].astype(WIDE), axis=0, keepdims=True)
    for j in range(PARTS):
        rows = slice(j * group.part, (j + 1) * group.part)
        grad = scatter.take(j)
        hat, scale = normalise(x_ref[rows, :].astype(WIDE))
        out = grad_ref[rows, :] + norm_backward(grad, hat, scale, vec_ref[0:1, :])
        out_ref[rows, :] = out.astype(LOW)
        for n, term in enumerate((grad * hat, grad)):
            sums_ref[n : n + 1, :] += jnp.sum(term, axis=0, keepdims=True)
    scatter.done()
    keep.wait()
    send.wait()


VM = pl.BlockSpec(memory_space=pltpu.VMEM)
ANY = pl.BlockSpec(memory_space=pl.ANY)


def shape(dims, kind=LOW):
    return jax.ShapeDtypeStruct(dims, kind)


def launch(kernel, number, in_specs, outs, out_specs, scratch, flops):
    return pl.pallas_call(
        kernel,
        out_shape=outs,
        in_specs=in_specs,
        out_specs=out_specs,
        scratch_shapes=scratch,
        compiler_params=pltpu.CompilerParams(
            collective_id=number, has_side_effects=True, vmem_limit_bytes=56 * MEBI
        ),
        cost_estimate=pl.CostEstimate(
            flops=int(flops), bytes_accessed=30 * MEBI, transcendentals=0
        ),
    )


def attend_call(number, gathered, x, pair, vec, bias, rows, width):
    size = vec.shape[1]
    heads = width // HEAD
    outs = (
        shape((LENGTH, size) if not gathered else (16, 128)),
        shape((LENGTH, size)),
        shape((3 * heads, LENGTH, HEAD)),
        shape((LENGTH, width)),
        shape((8, LENGTH), WIDE),
        shape((rows, size), WIDE),
        shape((rows, size)),
    )
    scratch = [
        pltpu.VMEM((size, 4 * width), LOW),
        pltpu.VMEM((heads, LENGTH, HEAD), LOW),
        *scatter_scratch(rows, size),
        pltpu.SemaphoreType.DMA((2, 3 * PARTS)),
        pltpu.SemaphoreType.DMA((4,)),
    ]
    return launch(
        functools.partial(attend_kernel, gathered, heads),
        number, [VM, ANY, ANY, VM, VM], outs, (VM,) * 7, scratch, 3e10,
    )(x, *pair, vec, bias)


def expand_call(number, second, hidden, expand, contract, vec, bias):
    rows, size = hidden.shape
    wide = bias.shape[1]
    outs = (
        shape((LENGTH, size)),
        shape((LENGTH, wide)),
        shape((LENGTH, wide)),
        shape((rows, size)),
    )
    scratch = [
        pltpu.VMEM((size, wide), LOW),
        pltpu.VMEM((size, wide), LOW),
        *scatter_scratch(rows, size),
        pltpu.SemaphoreType.DMA((2, 3 * PARTS)),
        pltpu.SemaphoreType.DMA((4,)),
    ]
    return launch(
        expand_kernel, number, [VM, VM, ANY, ANY, ANY, ANY, VM, VM], outs, (VM,) * 4, scratch, 3e10
    )(second, hidden, *expand, *contract, vec, bias)


def expand_back_call(number, gathered, grad, expand, contract, active, slope, second, hidden, vec):
    rows, size = hidden.shape
    wide = active.shape[1]
    half = wide // 2
    outs = (
        shape((LENGTH, size)),
        *[shape((size, half))] * 4,
        shape((rows, size), WIDE),
        shape((rows, size)),
        shape((8, wide), WIDE),
    )
    scratch = [
        pltpu.VMEM((size, wide), LOW),
        pltpu.VMEM((size, wide), LOW),
        pltpu.VMEM((LENGTH, wide), LOW),
        *scatter_scratch(rows, size),
        pltpu.SemaphoreType.DMA((2, 3 * PARTS)),
        pltpu.SemaphoreType.DMA((4,)),
    ]
    return launch(
        functools.partial(expand_back_kernel, gathered),
        number, [VM, ANY, ANY, ANY, ANY, VM, VM, VM, VM, VM], outs, (VM,) * 8, scratch, 3e10,
    )(grad, *expand, *contract, active, slope, second, hidden, vec)


def attend_back_call(number, low, grad, x_own, pair, normed, heads_all, o, lse, vec):
    rows, size = grad.shape
    width = o.shape[1]
    heads = width // HEAD
    half = 2 * width
    outs = (shape((size, half)), shape((size, half)), shape((rows, size)), shape((8, size), WIDE))
    scratch = [
        pltpu.VMEM((size, 4 * width), LOW),
        pltpu.VMEM((LENGTH, size), LOW),
        pltpu.VMEM((heads, LENGTH, HEAD), LOW),
        pltpu.VMEM((8, LENGTH), WIDE),
        pltpu.VMEM((3 * heads, LENGTH, HEAD), LOW),
        pltpu.VMEM((LENGTH, HEAD), WIDE),
        pltpu.VMEM((LENGTH, HEAD), WIDE),
        pltpu.VMEM((LENGTH, 3 * width), LOW),
        pltpu.VMEM((2, size, half), LOW),
        *scatter_scratch(rows, size),
        pltpu.SemaphoreType.DMA((2, 3 * PARTS)),
        pltpu.SemaphoreType.DMA((4,)),
    ]
    return launch(
        functools.partial(attend_back_kernel, heads),
        number, [VM, VM, VM, ANY, ANY, VM, VM, VM, VM, VM], outs, (ANY, ANY, VM, VM), scratch, 3e10,
    )(low, grad, x_own, *pair, normed, heads_all, o, lse, vec)


def swap_sections(value):
    return lax.ppermute(value, "section", [(0, 1), (1, 0)])


def on_device(
    tokens,
    cotangent,
    first_gain,
    first_shift,
    attend_weight,
    attend_bias,
    output_weight,
    output_bias,
    second_gain,
    second_shift,
    expand_weight,
    expand_bias,
    contract_weight,
    contract_bias,
):
    section = lax.axis_index("section")
    column = lax.axis_index("col")
    first_section = section == 0
    columns = lax.axis_size("col")
    width = tokens.shape[1]
    size = width * columns
    rows = LENGTH // columns

    def pick(early, later):
        return jnp.where(first_section, early, later)

    block_rows = attend_weight.shape[1]
    units = (
        jnp.concatenate(
            [attend_weight[0].reshape(block_rows, 3 * width), output_weight[0].T], axis=1
        ),
        expand_weight[0],
        contract_weight[0].T,
    )
    mine, theirs = [], []
    for unit in units:
        half = unit.shape[1] // 2
        low, high = unit[:, :half], unit[:, half:]
        mine.append(pick(low, high))
        theirs.append(swap_sections(pick(high, low)))
    mats = []
    for layer in range(2):
        entry = []
        for own, got in zip(mine, theirs):
            block = pick(own, got) if layer == 0 else pick(got, own)
            gathered = lax.all_gather(block, "row", axis=0, tiled=True)
            entry.append((gathered, swap_sections(gathered)))
        mats.append(entry)

    packed = jnp.concatenate(
        [
            first_gain[0],
            first_shift[0],
            output_bias[0],
            second_gain[0],
            second_shift[0],
            contract_bias[0],
        ]
    )
    vectors = lax.all_gather(packed, ("section", "col"), axis=0, tiled=False)
    vectors = vectors.reshape(2, columns, 6, width).astype(WIDE)
    vectors = jnp.swapaxes(vectors, 1, 2).reshape(2, 6, size)
    vectors = jnp.pad(vectors, ((0, 0), (0, 2), (0, 0)))
    own_small = jnp.concatenate(
        [
            attend_bias[0, 0],
            jnp.zeros_like(attend_bias[0, 0]),
            attend_bias[0, 1],
            expand_bias[0],
        ]
    )[None].astype(WIDE)
    other_small = swap_sections(own_small)
    biases = (pick(own_small, other_small), pick(other_small, own_small))
    biases = [(b[:, : 3 * width], b[:, 3 * width :]) for b in biases]

    x0_full = lax.all_gather(
        lax.dynamic_slice_in_dim(tokens, section * LENGTH, LENGTH, 0), "col", axis=1, tiled=True
    )
    gy_full = lax.all_gather(
        lax.dynamic_slice_in_dim(cotangent, section * LENGTH, LENGTH, 0), "col", axis=1, tiled=True
    )

    def own_rows(full):
        return lax.dynamic_slice_in_dim(full, column * rows, rows, 0)

    def own_features(full):
        return lax.dynamic_slice_in_dim(full, column * width, width, 1)

    def gather_rows(own):
        return lax.all_gather(own, "col", axis=0, tiled=True)

    kept = []
    x = x0_full
    fulls = []
    owns = [own_rows(x0_full)]
    for layer in range(2):
        attn, expand, contract = mats[layer]
        full, normed, heads, o, lse, hidden, second_own = attend_call(
            1 + 2 * layer, layer == 0, x, attn, vectors[layer], biases[layer][0], rows, width
        )
        second, active, slope, result = expand_call(
            2 + 2 * layer, second_own, hidden, expand, contract, vectors[layer], biases[layer][1]
        )
        kept.append((normed, heads, o, lse, hidden, second, active, slope))
        fulls.append(full)
        owns.append(result)
        x = result
    x1_full = fulls[1]
    y1_full = gather_rows(owns[2])

    grad = gy_full
    unit_grads, sums, grads = [None, None], [None, None], []
    for layer in (1, 0):
        attn, expand, contract = mats[layer]
        normed, heads, o, lse, hidden, second, active, slope = kept[layer]
        grad_full, ek, es, ck, cs, grad_hidden, low, ff_sums = expand_back_call(
            9 - 2 * layer, layer == 1, grad, expand, contract, active, slope, second, hidden, vectors[layer]
        )
        wk, ws, grad, attn_sums = attend_back_call(
            10 - 2 * layer, low, grad_hidden, owns[layer], attn, normed, heads, o, lse, vectors[layer]
        )
        unit_grads[layer] = ((wk, ws), (ek, es), (ck, cs))
        sums[layer] = (ff_sums, attn_sums)
        grads.append(grad_full)
    gx1_full = grads[1]
    gx0_full = gather_rows(grad)

    def to_sections(layer0, layer1):
        stays = pick(layer0, layer1)
        got = swap_sections(pick(layer1, layer0))
        return jnp.concatenate([pick(stays, got), pick(got, stays)], 0)

    layer_outputs = to_sections(own_features(x1_full), own_features(y1_full))
    input_grads = to_sections(own_features(gx0_full), own_features(gx1_full)).astype(WIDE)

    reduced = []
    for layer in (1, 0):
        entry = []
        for keep, send in unit_grads[layer]:
            total = (keep.astype(WIDE) + swap_sections(send).astype(WIDE)).astype(LOW)
            entry.append(lax.psum_scatter(total, "row", scatter_dimension=0, tiled=True))
        reduced.append(entry)
    units = []
    for late, early in zip(*reduced):
        stays = pick(early, late)
        got = swap_sections(pick(late, early))
        units.append(jnp.concatenate([pick(stays, got), pick(got, stays)], 1).astype(WIDE))
    attn_part, expand_part, contract_part = units

    wide_sum, own_sum = [], []
    for layer in range(2):
        ff_sums, attn_sums = sums[layer]
        wide_sum.append(
            jnp.stack(
                [attn_sums[0], attn_sums[1], ff_sums[3], ff_sums[0], ff_sums[1], ff_sums[2]]
            )
        )
        own_sum.append(
            jnp.concatenate(
                [attn_sums[2, :width], attn_sums[2, 2 * width : 3 * width], ff_sums[4]]
            )
        )
    wide_sum = lax.psum(jnp.stack(wide_sum), ("section", "row", "col"))
    own_sum = lax.psum(jnp.stack(own_sum), ("section", "row"))
    wide_mine = lax.dynamic_slice_in_dim(pick(wide_sum[0], wide_sum[1]), column * width, width, 1)
    own_mine = pick(own_sum[0], own_sum[1])
    return (
        layer_outputs[None],
        input_grads[None],
        wide_mine[0][None],
        wide_mine[1][None],
        attn_part[:, : 3 * width].reshape(block_rows, 3, width)[None],
        own_mine[: 2 * width].reshape(1, 2, width),
        attn_part[:, 3 * width :].T[None],
        wide_mine[2][None],
        wide_mine[3][None],
        wide_mine[4][None],
        expand_part[None],
        own_mine[2 * width :][None],
        contract_part.T[None],
        wide_mine[5][None],
    )


def solution(mesh):
    return jax.shard_map(
        on_device,
        mesh=mesh,
        in_specs=(
            P("row", "col"),
            P("row", "col"),
            P("section", "col"),
            P("section", "col"),
            P("section", "row", None, "col"),
            P("section", None, "col"),
            P("section", "col", "row"),
            P("section", "col"),
            P("section", "col"),
            P("section", "col"),
            P("section", "row", "col"),
            P("section", "col"),
            P("section", "col", "row"),
            P("section", "col"),
        ),
        out_specs=(
            P("section", "row", "col"),
            P("section", "row", "col"),
            P("section", "col"),
            P("section", "col"),
            P("section", "row", None, "col"),
            P("section", None, "col"),
            P("section", "col", "row"),
            P("section", "col"),
            P("section", "col"),
            P("section", "col"),
            P("section", "row", "col"),
            P("section", "col"),
            P("section", "col", "row"),
            P("section", "col"),
        ),
        check_vma=False,
    )
```

time: 1510 us -> 1080 us (0.72)
  waiting for transfers between devices: 855 us -> 432 us
  Pallas kernels: 0 us -> 406 us
  matrix products: 331 us -> 0 us
  other arithmetic: 80.2 us -> 36 us
  blocking collectives: 152 us -> 120 us
  local copies, waits for them, and re-layouts: 46.6 us -> 31.2 us
    pallas_call x0 -> x8, Pallas kernels: none -> 406 us  [the longest x2 121 us: attend_back_call(): launch(functools.partial(attend_back_kernel, heads), number, [VM, VM, VM,...]
    dot_general x48 -> x0, matrix products: 331 us -> none  [the longest x4 65.3 us: attention_backward(): jnp.einsum('hqk,qhd->khd', grad_scores, qh[begin:finish], preferred_eleme...]
    reduce_scatter x10 -> x6, waiting for transfers between devices: 228 us -> 0.01 us  [on_device(): lax.psum_scatter(total, 'row', scatter_dimension=0, tiled=True)]
    all_gather x8 -> x2, waiting for transfers between devices: 144 us -> 0.02 us  [gather_rows(): return lax.all_gather(own, 'col', axis=0, tiled=True)]
    ppermute x11 -> x21, waiting for transfers between devices: 284 us -> 229 us  [swap_sections(): return lax.ppermute(value, 'section', [(0, 1), (1, 0)])]
    reduce_sum x21 -> x0, other arithmetic: 37.7 us -> none  [the longest x4 8.29 us: norm_backward(): jnp.sum(grad * hat, axis=0)]
    all_gather x2 -> x1, blocking collectives: 74.2 us -> 39.7 us  [on_device(): vectors = lax.all_gather(packed, ('section', 'col'), axis=0, tiled=False)]
    all_gather x3 -> x6, waiting for transfers between devices: 180 us -> 151 us  [on_device(): gathered = lax.all_gather(block, 'row', axis=0, tiled=True)]
  transfers between devices with their start and end apart: 36 -> 37, of which waited for: 25 -> 20; matrix products, arithmetic and copies ran while one was open for 10% -> 6% of each run, Pallas kernels for 0% -> 34%
where the time goes in v2:
time: 1080 us; the launch traced here: 1070 us
  waiting for transfers between devices  432 us (40%)
  Pallas kernels  406 us (38%)
  blocking collectives  120 us (11%)
  other arithmetic  36 us (3%)
  starting transfers between devices  31.7 us (3%)
  local copies, waits for them, and re-layouts  31.2 us (3%)
  between operations  14.9 us (1%)
    ppermute x21, waiting for transfers between devices, swap_sections(): return lax.ppermute(value, 'section', [(0, 1), (1, 0)])  229 us
    all_gather x6, waiting for transfers between devices, on_device(): gathered = lax.all_gather(block, 'row', axis=0, tiled=True)  151 us
    pallas_call x2, Pallas kernels, attend_back_call(): launch(functools.partial(attend_back_kernel, heads), number, [VM, VM, VM,...  121 us
    pallas_call x2, Pallas kernels, attend_call(): launch(functools.partial(attend_kernel, gathered, heads), number, [VM, AN...  97.8 us
    pallas_call x2, Pallas kernels, expand_call(): launch(expand_kernel, number, [VM, VM, ANY, ANY, ANY, ANY, VM, VM], outs,...  93.5 us
    pallas_call x2, Pallas kernels, expand_back_call(): launch(functools.partial(expand_back_kernel, gathered), number, [VM, ANY,...  93.3 us
    psum x1, blocking collectives, on_device(): wide_sum = lax.psum(jnp.stack(wide_sum), ('section', 'row', 'col'))  41.1 us
    all_gather x1, blocking collectives, on_device(): vectors = lax.all_gather(packed, ('section', 'col'), axis=0, tiled=False)  39.7 us
  transfers between devices with their start and end apart: 37, of which 20 were waited for; matrix products, arithmetic and copies ran while one was open for 6% of the time, Pallas kernels for 34%

profile of v2, /device:TPU:0, one launch (start us, length us, event | category | flops | bytes accessed | tf_op | source)
XLA Modules:
  0.0 1071.5 jit_solution(1733763683921762321)
XLA Ops:
  9.7 3.0 collective-permute-start
  12.7 9.5 collective-permute-done
  23.3 1.8 collective-permute-start.3
  25.1 8.9 collective-permute-done.3
  37.7 8.3 collective-permute-done.5
  46.0 2.1 broadcast_select_fusion.16
  52.2 10.8 %all-gather.15.cloned.1.call-done.mine_ref = bf16[1280,640]{1,0:T(8,128)(2,1)} async-done(((bf16[320,640]{1,0:T(8,128)(2,1)}), bf16[1280,640]{1,0:T(8,128)(2,1)}) %all-gather.15.cloned.1.call-update) | async-done | bytes 1638416 | tf_op jit(solution)/shard_map/all_gather | solution.py:640
  65.5 39.7 %all-gather.1 = bf16[8,1,1920]{2,1,0:T(2,128)(2,1)S(1)} all-gather(bf16[1,1,1920]{2,1,0:T(2,128)(2,1)S(1)} %reshape.167), channel_id=2, replica_groups=mesh['section'=2,'row'=4,'col'=4] {'section','col'}, dimensions={0}, use_global_device_ids=true | all-gather | bytes 34560 | tf_op jit(solution)/shard_map/all_gather | solution.py:654
  110.2 30.6 %all-gather.19.cloned.1.call-done.cm_ref = bf16[1280,640]{1,0:T(8,128)(2,1)} async-done(((bf16[320,640]{1,0:T(8,128)(2,1)}), bf16[1280,640]{1,0:T(8,128)(2,1)}) %all-gather.19.cloned.1.call-update) | async-done | bytes 1638416 | tf_op jit(solution)/shard_map/all_gather | solution.py:640
  142.3 37.6 %all-gather.21.cloned.1.call-done.mine_ref = bf16[1280,640]{1,0:T(8,128)(2,1)} async-done(((bf16[320,640]{1,0:T(8,128)(2,1)}), bf16[1280,640]{1,0:T(8,128)(2,1)}) %all-gather.21.cloned.1.call-update) | async-done | bytes 1638416 | tf_op jit(solution)/shard_map/all_gather | solution.py:640
  181.3 37.6 %all-gather.23.cloned.1.call-done.em_ref = bf16[1280,640]{1,0:T(8,128)(2,1)} async-done(((bf16[320,640]{1,0:T(8,128)(2,1)}), bf16[1280,640]{1,0:T(8,128)(2,1)}) %all-gather.23.cloned.1.call-update) | async-done | bytes 1638416 | tf_op jit(solution)/shard_map/all_gather | solution.py:640
  220.4 25.0 %all-gather.13.cloned.1.call-done = bf16[1024,1280]{0,1:T(8,128)(2,1)} async-done(((bf16[1024,320]{0,1:T(8,128)(2,1)}), bf16[1024,1280]{0,1:T(8,128)(2,1)}) %all-gather.13.cloned.1.call-update) | async-done | bytes 2621456 | tf_op jit(solution)/shard_map/all_gather | solution.py:670
  245.3 3.0 copy.55.x_ref
  248.3 24.7 %all-gather.29.cloned.1.call-done = bf16[1024,1280]{0,1:T(8,128)(2,1)} async-done(((bf16[1024,320]{0,1:T(8,128)(2,1)}), bf16[1024,1280]{0,1:T(8,128)(2,1)}) %all-gather.29.cloned.1.call-update) | async-done | bytes 2621456 | tf_op jit(solution)/shard_map/all_gather | solution.py:673
  273.0 4.4 copy.59.g_ref
  278.4 34.5 %all-gather.25.cloned.1.call-done.cm_ref = bf16[1280,640]{1,0:T(8,128)(2,1)} async-done(((bf16[320,640]{1,0:T(8,128)(2,1)}), bf16[1280,640]{1,0:T(8,128)(2,1)}) %all-gather.25.cloned.1.call-update) | async-done | bytes 1638416 | tf_op jit(solution)/shard_map/all_gather | solution.py:640
  314.3 42.4 %shard_map.245 = (bf16[16,128]{1,0:T(8,128)(2,1)}, bf16[1024,1280]{1,0:T(8,128)(2,1)}, bf16[15,1024,64]{2,1,0:T(8,128)(2,1)}, bf16[1024,320]{1,0:T(8,128)(2,1)},...) custom-call(bf16[1024,1280]{1,0:T(8,128)(2,1)} %copy-done.2, ...), custom_call_target="tpu_custom_call" | custom-call | flops 30000001024 | bytes 31457280 | tf_op jit(solution)/shard_map/pallas_call | solution.py:512
  356.7 46.9 %shard_map.246 = (bf16[1024,1280]{1,0:T(8,128)(2,1)}, bf16[1024,1280]{1,0:T(8,128)(2,1)}, bf16[1024,1280]{1,0:T(8,128)(2,1)}, bf16[256,1280]{1,0:T(8,128)(2,1)}) custom-call(bf16[256,1280]{1,0:T(8,128)(2,1)} %get-tuple-element.58.second_ref, f32[256,1280]{1,0:T(8,128)} %get-tuple-element.59.hidden_ref, ...), custom_call_target="tpu_custom_call" | custom-call | flops 30000001024 | bytes 31457280 | tf_op jit(solution)/shard_map/pallas_call | solution.py:534
  403.6 55.5 %shard_map.247 = (bf16[1024,1280]{1,0:T(8,128)(2,1)}, bf16[1024,1280]{1,0:T(8,128)(2,1)}, bf16[15,1024,64]{2,1,0:T(8,128)(2,1)}, bf16[1024,320]{1,0:T(8,128)(2,1...) custom-call(bf16[256,1280]{1,0:T(8,128)(2,1)} %get-tuple-element.60.x_ref, ...), custom_call_target="tpu_custom_call" | custom-call | flops 30000001024 | bytes 31457280 | tf_op jit(solution)/shard_map/pallas_call | solution.py:512
  460.2 46.6 %shard_map.248 = (bf16[1024,1280]{1,0:T(8,128)(2,1)}, bf16[1024,1280]{1,0:T(8,128)(2,1)}, bf16[1024,1280]{1,0:T(8,128)(2,1)}, bf16[256,1280]{1,0:T(8,128)(2,1)}) custom-call(bf16[256,1280]{1,0:T(8,128)(2,1)} %get-tuple-element.62.second_ref, f32[256,1280]{1,0:T(8,128)} %get-tuple-element.63.hidden_ref, ...), custom_call_target="tpu_custom_call" | custom-call | flops 30000001024 | bytes 31457280 | tf_op jit(solution)/shard_map/pallas_call | solution.py:534
  506.9 40.7 %shard_map.249 = (bf16[1024,1280]{1,0:T(8,128)(2,1)}, bf16[1280,640]{1,0:T(8,128)(2,1)}, bf16[1280,640]{1,0:T(8,128)(2,1)}, bf16[1280,640]{1,0:T(8,128)(2,1)}, b...) custom-call(bf16[1024,1280]{1,0:T(8,128)(2,1)} %copy.59.g_ref, ...), custom_call_target="tpu_custom_call" | custom-call | flops 30000001024 | bytes 31457280 | tf_op jit(solution)/shard_map/pallas_call | solution.py:558
  547.7 60.4 %shard_map.250 = (bf16[1280,640]{1,0:T(8,128)(2,1)}, bf16[1280,640]{1,0:T(8,128)(2,1)}, bf16[256,1280]{1,0:T(8,128)(2,1)}, f32[8,1280]{1,0:T(8,128)}) custom-call(bf16[256,1280]{1,0:T(8,128)(2,1)} %get-tuple-element.68.low_ref, f32[256,1280]{1,0:T(8,128)} %get-tuple-element.69.grad_ref, bf16[256,1280]{1,0:T(8,128)(2,1)} %get-tuple-element.60.x_ref, ...), custom_call_target="tpu_custom_call" | custom-call | flops 30000001024 | bytes 31457280 | tf_op jit(solution)/shard_map/pallas_call | solution.py:584
  608.1 52.6 %shard_map.251 = (bf16[1024,1280]{1,0:T(8,128)(2,1)}, bf16[1280,640]{1,0:T(8,128)(2,1)}, bf16[1280,640]{1,0:T(8,128)(2,1)}, bf16[1280,640]{1,0:T(8,128)(2,1)}, b...) custom-call(bf16[256,1280]{1,0:T(8,128)(2,1)} %get-tuple-element.74.g_ref, ...), custom_call_target="tpu_custom_call" | custom-call | flops 30000001024 | bytes 31457280 | tf_op jit(solution)/shard_map/pallas_call | solution.py:558
  660.7 61.0 %shard_map.252 = (bf16[1280,640]{1,0:T(8,128)(2,1)}, bf16[1280,640]{1,0:T(8,128)(2,1)}, bf16[256,1280]{1,0:T(8,128)(2,1)}, f32[8,1280]{1,0:T(8,128)}) custom-call(bf16[256,1280]{1,0:T(8,128)(2,1)} %get-tuple-element.78.low_ref, f32[256,1280]{1,0:T(8,128)} %get-tuple-element.79.grad_ref, bf16[256,1280]{1,0:T(8,128)(2,1)} %constant_dynamic-slice_fusion.x_ref, ...), custom_call_target="tpu_custom_call" | custom-call | flops 30000001024 | bytes 31457280 | tf_op jit(solution)/shard_map/pallas_call | solution.py:584
  721.8 1.8 collective-permute-start.13
  723.6 35.8 %collective-permute-done.13 = bf16[1280,640]{1,0:T(8,128)(2,1)S(1)} collective-permute-done((bf16[1280,640]{1,0:T(8,128)(2,1)S(1)}, bf16[1280,640]{1,0:T(8,128)(2,1)S(1)}, u32[]{:S(2)}, u32[]{:S(2)}) %collective-permute-start.13) | collective-permute-done | bytes 1638432 | tf_op jit(solution)/shard_map/ppermute | solution.py:591
  761.0 1.7 collective-permute-start.12
  762.8 34.9 %collective-permute-done.12 = bf16[1280,640]{1,0:T(8,128)(2,1)S(1)} collective-permute-done((bf16[1280,640]{1,0:T(8,128)(2,1)S(1)}, bf16[1280,640]{1,0:T(8,128)(2,1)S(1)}, u32[]{:S(2)}, u32[]{:S(2)}) %collective-permute-start.12) | collective-permute-done | bytes 1638432 | tf_op jit(solution)/shard_map/ppermute | solution.py:591
  799.4 1.7 collective-permute-start.16
  801.1 34.1 %collective-permute-done.16 = bf16[1280,640]{1,0:T(8,128)(2,1)S(1)} collective-permute-done((bf16[1280,640]{1,0:T(8,128)(2,1)S(1)}, bf16[1280,640]{1,0:T(8,128)(2,1)S(1)}, u32[]{:S(2)}, u32[]{:S(2)}) %collective-permute-start.16) | collective-permute-done | bytes 1638432 | tf_op jit(solution)/shard_map/ppermute | solution.py:591
  836.9 1.7 collective-permute-start.15
  838.6 33.3 %collective-permute-done.15 = bf16[1280,640]{1,0:T(8,128)(2,1)S(1)} collective-permute-done((bf16[1280,640]{1,0:T(8,128)(2,1)S(1)}, bf16[1280,640]{1,0:T(8,128)(2,1)S(1)}, u32[]{:S(2)}, u32[]{:S(2)}) %collective-permute-start.15) | collective-permute-done | bytes 1638432 | tf_op jit(solution)/shard_map/ppermute | solution.py:591
  875.2 32.6 %collective-permute-done.19 = bf16[1280,640]{1,0:T(8,128)(2,1)S(1)} collective-permute-done((bf16[1280,640]{1,0:T(8,128)(2,1)S(1)}, bf16[1280,640]{1,0:T(8,128)(2,1)S(1)}, u32[]{:S(2)}, u32[]{:S(2)}) %collective-permute-start.19) | collective-permute-done | bytes 1638432 | tf_op jit(solution)/shard_map/ppermute | solution.py:591
  914.3 39.2 %psum.15 = f32[2,1920]{1,0:T(2,128)S(1)} all-reduce(f32[2,1920]{1,0:T(2,128)S(1)} %pad_maximum_fusion.2), channel_id=1, replica_groups=mesh['section'=2,'row'=4,'col'=4] {'section','row'}, use_global_device_ids=true, to_apply=%region_3.4 | all-reduce | flops 3840 | bytes 30720 | tf_op jit(solution)/shard_map/psum | solution.py:758
  955.2 41.1 %psum.14 = f32[2,6,1280]{2,1,0:T(8,128)S(1)} all-reduce(f32[2,6,1280]{2,1,0:T(8,128)S(1)} %pad_maximum_fusion.1), channel_id=1, replica_groups=mesh['section'=2,'row'=4,'col'=4] {'section','row','col'}, use_global_device_ids=true, to_apply=%region_0.1 | all-reduce | flops 15360 | bytes 122880 | tf_op jit(solution)/shard_map/psum | solution.py:757
  996.3 2.4 broadcast_select_fusion.4
  999.0 2.4 collective-permute-start.10
  1002.6 2.4 broadcast_select_fusion
  1006.1 11.0 %collective-permute-done.10 = bf16[1024,320]{0,1:T(8,128)(2,1)S(1)} collective-permute-done((bf16[1024,320]{0,1:T(8,128)(2,1)S(1)}, bf16[1024,320]{0,1:T(8,128)(2,1)S(1)}, u32[]{:S(2)}, u32[]{:S(2)}) %collective-permute-start.10) | collective-permute-done | bytes 655392 | tf_op jit(solution)/shard_map/ppermute | solution.py:591
  1017.4 2.6 broadcast_select_fusion.3
  1021.7 7.1 collective-permute-done.11
  1029.2 2.6 select_bitcast_fusion.1
  1031.9 2.2 copy.66
  1036.2 1.8 broadcast_select_fusion.10
  1039.2 1.8 broadcast_select_fusion.8
  1041.9 5.9 collective-permute-done.14
  1050.9 5.7 collective-permute-done.17
  1060.2 2.1 collective-permute-done.20
  (216 shorter events, 61.5 us)
Async XLA Ops:
  7.2 42.2 %copy-start = (bf16[2048,320]{0,1:T(8,128)(2,1)S(1)}, bf16[2048,320]{0,1:T(8,128)(2,1)}, u32[]{:S(2)}) copy-start(bf16[2048,320]{0,1:T(8,128)(2,1)} %param.14) | copy-start | bytes 3932164
  7.2 55.8 %all-gather.15.cloned.1.call-start = ((), (), s32[]{:S(2)}) async-start(), calls=%async_computation.7 | async-start | bytes 2048000 | tf_op jit(solution)/shard_map/all_gather | solution.py:640
  9.7 12.5 %collective-permute-start = (bf16[320,640]{1,0:T(8,128)(2,1)S(1)}, bf16[320,640]{1,0:T(8,128)(2,1)S(1)}, u32[]{:S(2)}, u32[]{:S(2)}) collective-permute-start(bf16[320,640]{1,0:T(8,128)(2,1)S(1)} %get-tuple-element.148), channel_id=1, source_target_pairs={{0,16},{16,0},{1,17},{17,1},{2,18},{18,2},{3,19},{19,3},{4,20},{20... | collective-permute-start | bytes 1228808 | tf_op jit(solution)/shard_map/ppermute | solution.py:591
  23.1 85.7 %all-gather.17.cloned.1.call-start = ((), (), s32[]{:S(2)}) async-start(), calls=%async_computation.8 | async-start | bytes 2048000 | tf_op jit(solution)/shard_map/all_gather | solution.py:640
  23.3 10.7 %collective-permute-start.3 = (bf16[320,640]{1,0:T(8,128)(2,1)S(1)}, bf16[320,640]{1,0:T(8,128)(2,1)S(1)}, u32[]{:S(2)}, u32[]{:S(2)}) collective-permute-start(bf16[320,640]{1,0:T(8,128)(2,1)S(1)} %broadcast_select_fusion.23), channel_id=1, source_target_pairs={{0,16},{16,0},{1,17},{17,1},{2,18},{18,2},{3,19},{19,3},{4,20},{20... | collective-permute-start | bytes 1228808 | tf_op jit(solution)/shard_map/ppermute | solution.py:591
  35.0 105.8 %all-gather.19.cloned.1.call-start = ((), (), s32[]{:S(2)}) async-start(), calls=%async_computation.9 | async-start | bytes 2048000 | tf_op jit(solution)/shard_map/all_gather | solution.py:640
  36.2 9.8 collective-permute-start.5
  48.2 131.7 %all-gather.21.cloned.1.call-start = ((), (), s32[]{:S(2)}) async-start(), calls=%async_computation.10 | async-start | bytes 2048000 | tf_op jit(solution)/shard_map/all_gather | solution.py:640
  48.7 170.1 %all-gather.23.cloned.1.call-start = ((), (), s32[]{:S(2)}) async-start(), calls=%async_computation.11 | async-start | bytes 2048000 | tf_op jit(solution)/shard_map/all_gather | solution.py:640
  49.3 196.0 %all-gather.13.cloned.1.call-start = ((), (), s32[]{:S(2)}) async-start(), calls=%async_computation.6 | async-start | bytes 3276800 | tf_op jit(solution)/shard_map/all_gather | solution.py:670
  50.3 15.0 %copy-start.28 = (bf16[1,320]{1,0:T(2,128)(2,1)S(1)}, bf16[1,320]{1,0:T(2,128)(2,1)}, u32[]{:S(2)}) copy-start(bf16[1,320]{1,0:T(2,128)(2,1)} %param.23) | copy-start | bytes 1924
  50.3 15.0 %copy-start.29 = (bf16[1,320]{1,0:T(2,128)(2,1)S(1)}, bf16[1,320]{1,0:T(2,128)(2,1)}, u32[]{:S(2)}) copy-start(bf16[1,320]{1,0:T(2,128)(2,1)} %param.27) | copy-start | bytes 1924
  50.4 222.7 %all-gather.29.cloned.1.call-start = ((), (), s32[]{:S(2)}) async-start(), calls=%async_computation.14 | async-start | bytes 3276800 | tf_op jit(solution)/shard_map/all_gather | solution.py:673
  51.4 261.5 %all-gather.25.cloned.1.call-start = ((), (), s32[]{:S(2)}) async-start(), calls=%async_computation.12 | async-start | bytes 2048000 | tf_op jit(solution)/shard_map/all_gather | solution.py:640
  52.1 944.2 %all-gather.27.cloned.1.call-start = ((), (), s32[]{:S(2)}) async-start(), calls=%async_computation.13 | async-start | bytes 3276800 | tf_op jit(solution)/shard_map/all_gather | solution.py:684
  63.0 249.9 %collective-permute-start.1 = (bf16[1280,640]{1,0:T(8,128)(2,1)}, bf16[1280,640]{1,0:T(8,128)(2,1)}, u32[]{:S(2)}, u32[]{:S(2)}) collective-permute-start(bf16[1280,640]{1,0:T(8,128)(2,1)} %all-gather.15.cloned.1.call-done.mine_ref), channel_id=1, source_target_pairs={{0,16},{16,0},{1,17},{17,1},{2,18},{18,2},{3,19},{19,3},{4,20},{20... | collective-permute-start | bytes 4915208 | tf_op jit(solution)/shard_map/ppermute | solution.py:591
  64.6 41.6 %collective-permute-start.2 = (f32[1,2240]{1,0:T(1,128)S(1)}, f32[1,2240]{1,0:T(1,128)S(1)}, u32[]{:S(2)}, u32[]{:S(2)}) collective-permute-start(f32[1,2240]{1,0:T(1,128)S(1)} %convert_element_type.96), channel_id=1, source_target_pairs={{0,16},{16,0},{1,17},{17,1},{2,18},{18,2},{3,19},{19,3},{4,20},{20... | collective-permute-start | bytes 26888 | tf_op jit(solution)/shard_map/ppermute | solution.py:591
  108.8 247.9 %collective-permute-start.4 = (bf16[1280,640]{1,0:T(8,128)(2,1)}, bf16[1280,640]{1,0:T(8,128)(2,1)}, u32[]{:S(2)}, u32[]{:S(2)}) collective-permute-start(bf16[1280,640]{1,0:T(8,128)(2,1)} %all-gather.17.cloned.1.call-done.em_ref), channel_id=1, source_target_pairs={{0,16},{16,0},{1,17},{17,1},{2,18},{18,2},{3,19},{19,3},{4,20},{20... | collective-permute-start | bytes 4915208 | tf_op jit(solution)/shard_map/ppermute | solution.py:591
  140.8 215.9 %collective-permute-start.6 = (bf16[1280,640]{1,0:T(8,128)(2,1)}, bf16[1280,640]{1,0:T(8,128)(2,1)}, u32[]{:S(2)}, u32[]{:S(2)}) collective-permute-start(bf16[1280,640]{1,0:T(8,128)(2,1)} %all-gather.19.cloned.1.call-done.cm_ref), channel_id=1, source_target_pairs={{0,16},{16,0},{1,17},{17,1},{2,18},{18,2},{3,19},{19,3},{4,20},{20... | collective-permute-start | bytes 4915208 | tf_op jit(solution)/shard_map/ppermute | solution.py:591
  179.8 223.7 %collective-permute-start.7 = (bf16[1280,640]{1,0:T(8,128)(2,1)}, bf16[1280,640]{1,0:T(8,128)(2,1)}, u32[]{:S(2)}, u32[]{:S(2)}) collective-permute-start(bf16[1280,640]{1,0:T(8,128)(2,1)} %all-gather.21.cloned.1.call-done.mine_ref), channel_id=1, source_target_pairs={{0,16},{16,0},{1,17},{17,1},{2,18},{18,2},{3,19},{19,3},{4,20},{20... | collective-permute-start | bytes 4915208 | tf_op jit(solution)/shard_map/ppermute | solution.py:591
  218.9 240.2 %collective-permute-start.8 = (bf16[1280,640]{1,0:T(8,128)(2,1)}, bf16[1280,640]{1,0:T(8,128)(2,1)}, u32[]{:S(2)}, u32[]{:S(2)}) collective-permute-start(bf16[1280,640]{1,0:T(8,128)(2,1)} %all-gather.23.cloned.1.call-done.em_ref), channel_id=1, source_target_pairs={{0,16},{16,0},{1,17},{17,1},{2,18},{18,2},{3,19},{19,3},{4,20},{20... | collective-permute-start | bytes 4915208 | tf_op jit(solution)/shard_map/ppermute | solution.py:591
  248.3 29.2 %copy-start.2 = (bf16[1024,1280]{1,0:T(8,128)(2,1)}, bf16[1024,1280]{1,0:T(8,128)(2,1)S(1)}, u32[]{:S(2)}) copy-start(bf16[1024,1280]{1,0:T(8,128)(2,1)S(1)} %copy.55.x_ref) | copy-start | bytes 7864324
  312.8 146.2 %collective-permute-start.9 = (bf16[1280,640]{1,0:T(8,128)(2,1)}, bf16[1280,640]{1,0:T(8,128)(2,1)S(1)}, u32[]{:S(2)}, u32[]{:S(2)}) collective-permute-start(bf16[1280,640]{1,0:T(8,128)(2,1)} %all-gather.25.cloned.1.call-done.cm_ref), channel_id=1, source_target_pairs={{0,16},{16,0},{1,17},{17,1},{2,18},{18,2},{3,19},{19,3},{4,20},{20... | collective-permute-start | bytes 4915208 | tf_op jit(solution)/shard_map/ppermute | solution.py:591
  506.9 495.8 %all-gather.31.cloned.1.call-start = ((), (), s32[]{:S(2)}) async-start(), calls=%async_computation.15 | async-start | bytes 3276800 | tf_op jit(solution)/shard_map/all_gather | solution.py:684
  660.7 61.1 %copy-start.34 = (bf16[1280,640]{1,0:T(8,128)(2,1)S(1)}, bf16[1280,640]{1,0:T(8,128)(2,1)}, u32[]{:S(2)}) copy-start(bf16[1280,640]{1,0:T(8,128)(2,1)} %get-tuple-element.93) | copy-start | bytes 4915204
  660.7 98.7 %copy-start.10 = (bf16[1280,640]{1,0:T(8,128)(2,1)S(1)}, bf16[1280,640]{1,0:T(8,128)(2,1)}, u32[]{:S(2)}) copy-start(bf16[1280,640]{1,0:T(8,128)(2,1)} %get-tuple-element.92) | copy-start | bytes 4915204
  721.7 312.4 %reduce-scatter.9.cloned.1.call-start = ((), (), s32[]{:S(2)}) async-start(), calls=%async_computation.17 | async-start | bytes 2048000 | tf_op jit(solution)/shard_map/reduce_scatter | solution.py:735
  721.8 37.5 %collective-permute-start.13 = (bf16[1280,640]{1,0:T(8,128)(2,1)S(1)}, bf16[1280,640]{1,0:T(8,128)(2,1)S(1)}, u32[]{:S(2)}, u32[]{:S(2)}) collective-permute-start(bf16[1280,640]{1,0:T(8,128)(2,1)S(1)} %copy-done.34), channel_id=1, source_target_pairs={{0,16},{16,0},{1,17},{17,1},{2,18},{18,2},{3,19},{19,3},{4,20},{20... | collective-permute-start | bytes 4915208 | tf_op jit(solution)/shard_map/ppermute | solution.py:591
  761.0 36.7 %copy-start.11 = (bf16[1280,640]{1,0:T(8,128)(2,1)S(1)}, bf16[1280,640]{1,0:T(8,128)(2,1)}, u32[]{:S(2)}) copy-start(bf16[1280,640]{1,0:T(8,128)(2,1)} %get-tuple-element.90) | copy-start | bytes 4915204
  761.0 273.2 %reduce-scatter.7.cloned.1.call-start = ((), (), s32[]{:S(2)}) async-start(), calls=%async_computation.16 | async-start | bytes 2048000 | tf_op jit(solution)/shard_map/reduce_scatter | solution.py:735
  761.0 36.7 %collective-permute-start.12 = (bf16[1280,640]{1,0:T(8,128)(2,1)S(1)}, bf16[1280,640]{1,0:T(8,128)(2,1)S(1)}, u32[]{:S(2)}, u32[]{:S(2)}) collective-permute-start(bf16[1280,640]{1,0:T(8,128)(2,1)S(1)} %copy-done.35), channel_id=1, source_target_pairs={{0,16},{16,0},{1,17},{17,1},{2,18},{18,2},{3,19},{19,3},{4,20},{20... | collective-permute-start | bytes 4915208 | tf_op jit(solution)/shard_map/ppermute | solution.py:591
  799.3 35.9 %copy-start.8 = (bf16[1280,640]{1,0:T(8,128)(2,1)S(1)}, bf16[1280,640]{1,0:T(8,128)(2,1)}, u32[]{:S(2)}) copy-start(bf16[1280,640]{1,0:T(8,128)(2,1)} %get-tuple-element.96) | copy-start | bytes 4915204
  799.3 236.9 %reduce-scatter.13.cloned.1.call-start = ((), (), s32[]{:S(2)}) async-start(), calls=%async_computation.19 | async-start | bytes 2048000 | tf_op jit(solution)/shard_map/reduce_scatter | solution.py:735
  799.4 35.8 %collective-permute-start.16 = (bf16[1280,640]{1,0:T(8,128)(2,1)S(1)}, bf16[1280,640]{1,0:T(8,128)(2,1)S(1)}, u32[]{:S(2)}, u32[]{:S(2)}) collective-permute-start(bf16[1280,640]{1,0:T(8,128)(2,1)S(1)} %copy-done.31), channel_id=1, source_target_pairs={{0,16},{16,0},{1,17},{17,1},{2,18},{18,2},{3,19},{19,3},{4,20},{20... | collective-permute-start | bytes 4915208 | tf_op jit(solution)/shard_map/ppermute | solution.py:591
  836.8 35.1 %copy-start.9 = (bf16[1280,640]{1,0:T(8,128)(2,1)S(1)}, bf16[1280,640]{1,0:T(8,128)(2,1)}, u32[]{:S(2)}) copy-start(bf16[1280,640]{1,0:T(8,128)(2,1)} %get-tuple-element.94) | copy-start | bytes 4915204
  836.8 199.4 %reduce-scatter.11.cloned.1.call-start = ((), (), s32[]{:S(2)}) async-start(), calls=%async_computation.18 | async-start | bytes 2048000 | tf_op jit(solution)/shard_map/reduce_scatter | solution.py:735
  836.9 35.0 %collective-permute-start.15 = (bf16[1280,640]{1,0:T(8,128)(2,1)S(1)}, bf16[1280,640]{1,0:T(8,128)(2,1)S(1)}, u32[]{:S(2)}, u32[]{:S(2)}) collective-permute-start(bf16[1280,640]{1,0:T(8,128)(2,1)S(1)} %copy-done.32), channel_id=1, source_target_pairs={{0,16},{16,0},{1,17},{17,1},{2,18},{18,2},{3,19},{19,3},{4,20},{20... | collective-permute-start | bytes 4915208 | tf_op jit(solution)/shard_map/ppermute | solution.py:591
  873.5 34.2 %copy-start.7 = (bf16[1280,640]{1,0:T(8,128)(2,1)S(1)}, bf16[1280,640]{1,0:T(8,128)(2,1)}, u32[]{:S(2)}) copy-start(bf16[1280,640]{1,0:T(8,128)(2,1)} %get-tuple-element.100) | copy-start | bytes 4915204
  873.5 165.7 %reduce-scatter.17.cloned.1.call-start = ((), (), s32[]{:S(2)}) async-start(), calls=%async_computation.21 | async-start | bytes 2048000 | tf_op jit(solution)/shard_map/reduce_scatter | solution.py:735
  873.6 34.1 %collective-permute-start.19 = (bf16[1280,640]{1,0:T(8,128)(2,1)S(1)}, bf16[1280,640]{1,0:T(8,128)(2,1)S(1)}, u32[]{:S(2)}, u32[]{:S(2)}) collective-permute-start(bf16[1280,640]{1,0:T(8,128)(2,1)S(1)} %copy-done.30), channel_id=1, source_target_pairs={{0,16},{16,0},{1,17},{17,1},{2,18},{18,2},{3,19},{19,3},{4,20},{20... | collective-permute-start | bytes 4915208 | tf_op jit(solution)/shard_map/ppermute | solution.py:591
  909.4 44.2 %copy-start.6 = (bf16[1280,640]{1,0:T(8,128)(2,1)S(1)}, bf16[1280,640]{1,0:T(8,128)(2,1)}, u32[]{:S(2)}) copy-start(bf16[1280,640]{1,0:T(8,128)(2,1)} %get-tuple-element.98) | copy-start | bytes 4915204
  909.4 129.8 %reduce-scatter.15.cloned.1.call-start = ((), (), s32[]{:S(2)}) async-start(), calls=%async_computation.20 | async-start | bytes 2048000 | tf_op jit(solution)/shard_map/reduce_scatter | solution.py:735
  909.5 44.1 %collective-permute-start.18 = (bf16[1280,640]{1,0:T(8,128)(2,1)}, bf16[1280,640]{1,0:T(8,128)(2,1)S(1)}, u32[]{:S(2)}, u32[]{:S(2)}) collective-permute-start(bf16[1280,640]{1,0:T(8,128)(2,1)} %get-tuple-element.99), channel_id=1, source_target_pairs={{0,16},{16,0},{1,17},{17,1},{2,18},{18,2},{3,19},{19,3},{4,20},{20... | collective-permute-start | bytes 4915208 | tf_op jit(solution)/shard_map/ppermute | solution.py:591
  999.0 18.0 %collective-permute-start.10 = (bf16[1024,320]{0,1:T(8,128)(2,1)S(1)}, bf16[1024,320]{0,1:T(8,128)(2,1)S(1)}, u32[]{:S(2)}, u32[]{:S(2)}) collective-permute-start(bf16[1024,320]{0,1:T(8,128)(2,1)S(1)} %copy.56), channel_id=1, source_target_pairs={{0,16},{16,0},{1,17},{17,1},{2,18},{18,2},{3,19},{19,3},{4,20},{20... | collective-permute-start | bytes 1966088 | tf_op jit(solution)/shard_map/ppermute | solution.py:591
  1005.3 23.5 %collective-permute-start.11 = (bf16[1024,320]{0,1:T(8,128)(2,1)S(1)}, bf16[1024,320]{0,1:T(8,128)(2,1)S(1)}, u32[]{:S(2)}, u32[]{:S(2)}) collective-permute-start(bf16[1024,320]{0,1:T(8,128)(2,1)S(1)} %copy.61), channel_id=1, source_target_pairs={{0,16},{16,0},{1,17},{17,1},{2,18},{18,2},{3,19},{19,3},{4,20},{20... | collective-permute-start | bytes 1966088 | tf_op jit(solution)/shard_map/ppermute | solution.py:591
  1035.3 12.5 %collective-permute-start.14 = (bf16[320,640]{1,0:T(8,128)(2,1)S(1)}, bf16[320,640]{1,0:T(8,128)(2,1)S(1)}, u32[]{:S(2)}, u32[]{:S(2)}) collective-permute-start(bf16[320,640]{1,0:T(8,128)(2,1)S(1)} %broadcast_select_fusion.14), channel_id=1, source_target_pairs={{0,16},{16,0},{1,17},{17,1},{2,18},{18,2},{3,19},{19,3},{4,20},{20... | collective-permute-start | bytes 1228808 | tf_op jit(solution)/shard_map/ppermute | solution.py:591
  1038.0 18.6 %collective-permute-start.17 = (bf16[320,640]{1,0:T(8,128)(2,1)}, bf16[320,640]{1,0:T(8,128)(2,1)}, u32[]{:S(2)}, u32[]{:S(2)}) collective-permute-start(bf16[320,640]{1,0:T(8,128)(2,1)} %broadcast_select_fusion.10), channel_id=1, source_target_pairs={{0,16},{16,0},{1,17},{17,1},{2,18},{18,2},{3,19},{19,3},{4,20},{20... | collective-permute-start | bytes 1228808 | tf_op jit(solution)/shard_map/ppermute | solution.py:591
  1041.0 21.2 %collective-permute-start.20 = (bf16[320,640]{1,0:T(8,128)(2,1)}, bf16[320,640]{1,0:T(8,128)(2,1)}, u32[]{:S(2)}, u32[]{:S(2)}) collective-permute-start(bf16[320,640]{1,0:T(8,128)(2,1)} %broadcast_select_fusion.8), channel_id=1, source_target_pairs={{0,16},{16,0},{1,17},{17,1},{2,18},{18,2},{3,19},{19,3},{4,20},{20... | collective-permute-start | bytes 1228808 | tf_op jit(solution)/shard_map/ppermute | solution.py:591
  (25 other events, 180.3 us)
Sparse Core Ops, SparseCore 0:
  23.3 39.6 all-gather.14
  65.1 37.0 all-gather.16
  103.7 37.0 all-gather.18
  142.8 37.0 all-gather.20
  181.8 37.0 all-gather.22
  220.9 24.4 all-gather.12
  247.5 25.5 all-gather.28
  274.6 38.1 all-gather.24
  507.0 28.0 all-gather.26
  721.9 26.6 all-gather.30
  761.1 37.4 reduce-scatter.8
  801.4 35.4 reduce-scatter.6
  839.3 35.2 reduce-scatter.12
  876.9 35.3 reduce-scatter.10
  914.4 36.1 reduce-scatter.16
  955.3 34.9 reduce-scatter.14

commit v3 on v2

--- a/solution.py
+++ b/solution.py
@@ -54,11 +54,16 @@
         self.rows = rows
         self.part = rows // PARTS
 
-    def greet(self):
+    def greet(self, swaps, diagonal):
         barrier = pltpu.get_barrier_semaphore()
-        for other in (self.sib, self.peer):
-            pl.semaphore_signal(barrier, inc=1, device_id={"col": other}, device_id_type=MESH)
-        pl.semaphore_wait(barrier, 2)
+        others = [{"col": self.sib}, {"col": self.peer}]
+        if diagonal:
+            others.append({"col": self.diag})
+        if swaps:
+            others.append({"section": 1 - lax.axis_index("section")})
+        for other in others:
+            pl.semaphore_signal(barrier, inc=1, device_id=other, device_id_type=MESH)
+        pl.semaphore_wait(barrier, len(others))
 
     def slab(self, owner, j):
         return pl.ds(pl.multiple_of(owner * self.rows + j * self.part, self.part), self.part)
@@ -67,30 +72,36 @@
         return pl.ds(pl.multiple_of(owner * self.rows, self.rows), self.rows)
 
 
-def push(src, dst, sems, slot, target):
+def push(src, dst, sems, slot, target, axis="col"):
     return pltpu.make_async_remote_copy(
         src_ref=src,
         dst_ref=dst,
         send_sem=sems.at[0, slot],
         recv_sem=sems.at[1, slot],
-        device_id={"col": target},
+        device_id={axis: target},
         device_id_type=MESH,
     )
 
 
 class Gather:
-    def __init__(self, group, full, sems):
-        self.group, self.full, self.sems = group, full, sems
+    def __init__(self, group, full, sems, blocks=False):
+        self.group, self.full, self.sems, self.blocks = group, full, sems, blocks
+
+    def piece(self, owner, j):
+        if not self.blocks:
+            return self.full.at[self.group.slab(owner, j)]
+        part = self.full.shape[1] // PARTS
+        return self.full.at[owner, pl.ds(j * part, part)]
 
     def start(self):
         g = self.group
         self.over, self.near, self.relayed = [], [], []
         for j in range(PARTS):
-            piece = self.full.at[g.slab(g.me, j)]
+            piece = self.piece(g.me, j)
             self.over.append(push(piece, piece, self.sems, j, g.peer))
             self.over[-1].start()
         for j in range(PARTS):
-            piece = self.full.at[g.slab(g.me, j)]
+            piece = self.piece(g.me, j)
             self.near.append(push(piece, piece, self.sems, PARTS + j, g.sib))
             self.near[-1].start()
 
@@ -102,7 +113,7 @@
         g = self.group
         for j in range(PARTS):
             self.over[j].wait_recv()
-            piece = self.full.at[g.slab(g.peer, j)]
+            piece = self.piece(g.peer, j)
             self.relayed.append(push(piece, piece, self.sems, 2 * PARTS + j, g.sib))
             self.relayed[-1].start()
 
@@ -160,6 +171,28 @@
     def done(self):
         for copy in self.first + self.over + self.near:
             copy.wait_send()
+
+
+class Deliver:
+    def __init__(self, group, stage, out, sems):
+        self.group, self.stage, self.out, self.sems = group, stage, out, sems
+
+    def start(self, rows_ref):
+        g, width = self.group, self.out.shape[1]
+        for c in range(self.stage.shape[0]):
+            self.stage[c] = rows_ref[:, c * width : (c + 1) * width]
+        place = self.out.at[g.chunk(g.me)]
+        self.copies = [
+            push(self.stage.at[other], place, self.sems, n, other)
+            for n, other in enumerate((g.peer, g.diag, g.sib))
+        ]
+        for copy in self.copies:
+            copy.start()
+        self.out[g.chunk(g.me), :] = self.stage[g.me]
+
+    def done(self):
+        for copy in self.copies:
+            copy.wait()
 
 
 def scatter_scratch(rows, width):
@@ -250,16 +283,48 @@
         g3[2 * heads + h] = value_acc[...].astype(LOW)
 
 
+def start_kernel(
+    tokens_ref, cotangent_ref, small_ref, x_ref, g_ref, vectors_ref,
+    x4, g4, s4, other4, x_sems, g_sems, s_sems, local_sems,
+):
+    section = lax.axis_index("section")
+    group = Group(x_ref.shape[0] // 4)
+    length = x_ref.shape[0]
+    loads = []
+    rows = pl.ds(pl.multiple_of(section * length, length), length)
+    for n, (source, into) in enumerate(((tokens_ref.at[rows], x4), (cotangent_ref.at[rows], g4), (small_ref, s4))):
+        loads.append(pltpu.make_async_copy(source, into.at[group.me], local_sems.at[n]))
+        loads[-1].start()
+    group.greet(True, False)
+    gathers = [Gather(group, x4, x_sems, True), Gather(group, s4, s_sems, True), Gather(group, g4, g_sems, True)]
+    for gather, load in zip(gathers, (loads[0], loads[2], loads[1])):
+        load.wait()
+        gather.start()
+    for gather in gathers:
+        gather.sibling()
+        gather.relay()
+        gather.diagonal()
+    swap = push(s4, other4, s_sems, 3 * PARTS, 1 - section, "section")
+    swap.start()
+    width = x4.shape[2]
+    for c in range(x4.shape[0]):
+        x_ref[:, c * width : (c + 1) * width] = x4[c]
+        g_ref[:, c * width : (c + 1) * width] = g4[c]
+    swap.wait()
+    vectors_ref[section] = s4[...]
+    vectors_ref[1 - section] = other4[...]
+    for gather in gathers:
+        gather.done()
+
+
 def attend_kernel(
-    gathered, heads, x_ref, mine_ref, other_ref, vec_ref, bias_ref,
+    gathered, heads, group, x_ref, mine_ref, other_ref, vec_ref, bias_ref,
     full_ref, normed_ref, heads_ref, o_ref, lse_ref, hidden_ref, second_ref,
     weight, o3, stage, land, total, scatter_sems, gather_sems, local_sems,
 ):
     width = o_ref.shape[1]
-    group = Group(hidden_ref.shape[0])
     halves = Halves((mine_ref, other_ref), weight, local_sems, 0)
     halves.start()
-    group.greet()
     if not gathered:
         full_ref[group.chunk(group.me), :] = x_ref[...]
     halves.wait()
@@ -301,19 +366,15 @@
     scatter.done()
 
 
-def expand_kernel(
-    second_ref, hidden_ref, em_ref, eo_ref, cm_ref, co_ref, vec_ref, bias_ref,
-    full_ref, active_ref, slope_ref, result_ref,
-    expand, contract, stage, land, total, scatter_sems, gather_sems, local_sems,
+def widen_kernel(
+    group, second_ref, em_ref, eo_ref, bias_ref,
+    full_ref, active_ref, slope_ref,
+    expand, gather_sems, local_sems,
 ):
-    group = Group(hidden_ref.shape[0])
-    first = Halves((em_ref, eo_ref), expand, local_sems, 0)
-    then = Halves((cm_ref, co_ref), contract, local_sems, 2)
-    first.start()
-    then.start()
-    group.greet()
+    halves = Halves((em_ref, eo_ref), expand, local_sems, 0)
+    halves.start()
     full_ref[group.chunk(group.me), :] = second_ref[...]
-    first.wait()
+    halves.wait()
 
     def widen(rows):
         t = nn(full_ref[rows, :], expand[...]) + bias_ref[...]
@@ -326,14 +387,6 @@
         ).astype(LOW)
 
     Gather(group, full_ref, gather_sems).each(widen)
-    then.wait()
-    scatter = Scatter(group, stage, land, total, scatter_sems)
-    scatter.start(lambda rows: nt(active_ref[rows, :], contract[...]))
-    for j in range(PARTS):
-        rows = slice(j * group.part, (j + 1) * group.part)
-        result = hidden_ref[rows, :] + scatter.take(j) + vec_ref[5:6, :]
-        result_ref[rows, :] = result.astype(LOW)
-    scatter.done()
 
 
 def outer_halves(left_ref, right_ref, keep_ref, send_ref):
@@ -348,46 +401,79 @@
             out[rows, :] = tn(left_ref[:, rows], right_ref[:, columns]).astype(LOW)
 
 
-def expand_back_kernel(
-    gathered, g_ref, em_ref, eo_ref, cm_ref, co_ref, active_ref, slope_ref, second_ref, hidden_ref, vec_ref,
-    full_ref, ek_ref, es_ref, ck_ref, cs_ref, grad_ref, low_ref, sums_ref,
-    expand, contract, before, stage, land, total, scatter_sems, gather_sems, local_sems,
-):
-    group = Group(hidden_ref.shape[0])
-    first = Halves((cm_ref, co_ref), contract, local_sems, 0)
-    then = Halves((em_ref, eo_ref), expand, local_sems, 2)
-    first.start()
-    then.start()
-    group.greet()
+def contract_kernel(last, group, *refs):
+    active_ref, hidden_ref, cm_ref, co_ref, vec_ref, *refs = refs
+    if last:
+        g_ref, *refs = refs
+    result_ref, *refs = refs
+    if last:
+        out_ref, ck_ref, cs_ref, *refs = refs
+    contract, stage, land, total, scatter_sems, local_sems, *refs = refs
+    if last:
+        stage4, deliver_sems = refs
+    halves = Halves((cm_ref, co_ref), contract, local_sems, 0)
+    halves.start()
+    halves.wait()
+    scatter = Scatter(group, stage, land, total, scatter_sems)
+    scatter.start(lambda rows: nt(active_ref[rows, :], contract[...]))
+    if last:
+        outer_halves(g_ref, active_ref, ck_ref, cs_ref)
+    for j in range(PARTS):
+        rows = slice(j * group.part, (j + 1) * group.part)
+        result = hidden_ref[rows, :] + scatter.take(j) + vec_ref[5:6, :]
+        result_ref[rows, :] = result.astype(LOW)
+    if last:
+        deliver = Deliver(group, stage4, out_ref, deliver_sems)
+        deliver.start(result_ref)
+        deliver.done()
+    scatter.done()
+
+
+def bend_kernel(last, group, g_ref, cm_ref, co_ref, active_ref, slope_ref, *refs):
+    before, sums_ref, *refs = refs
+    if not last:
+        full_ref, ck_ref, cs_ref, *refs = refs
+    contract, gather_sems, local_sems = refs
+    halves = Halves((cm_ref, co_ref), contract, local_sems, 0)
+    halves.start()
     sums_ref[...] = jnp.zeros_like(sums_ref)
-    if gathered:
-        full_ref[...] = g_ref[...]
-    else:
+    if not last:
         full_ref[group.chunk(group.me), :] = g_ref[...]
-    first.wait()
+    halves.wait()
 
     def bend(rows):
-        grad = (nn(full_ref[rows, :], contract[...]) * slope_ref[rows, :].astype(WIDE)).astype(LOW)
+        rows_grad = (g_ref if last else full_ref)[rows, :]
+        grad = (nn(rows_grad, contract[...]) * slope_ref[rows, :].astype(WIDE)).astype(LOW)
         before[rows, :] = grad
-        sums_ref[4:5, :] += jnp.sum(grad.astype(WIDE), axis=0, keepdims=True)
-
-    if gathered:
+        sums_ref[0:1, :] += jnp.sum(grad.astype(WIDE), axis=0, keepdims=True)
+
+    if last:
 
         @pl.loop(0, LENGTH // group.rows)
         def _(n):
             bend(group.chunk(n))
     else:
         Gather(group, full_ref, gather_sems).each(bend)
-    then.wait()
+        outer_halves(full_ref, active_ref, ck_ref, cs_ref)
+
+
+def narrow_kernel(
+    group, before, g_ref, em_ref, eo_ref, second_ref, hidden_ref, vec_ref,
+    ek_ref, es_ref, grad_ref, low_ref, sums_ref,
+    expand, stage, land, total, scatter_sems, local_sems,
+):
+    halves = Halves((em_ref, eo_ref), expand, local_sems, 0)
+    halves.start()
+    sums_ref[...] = jnp.zeros_like(sums_ref)
+    halves.wait()
     scatter = Scatter(group, stage, land, total, scatter_sems)
     scatter.start(lambda rows: nt(before[rows, :], expand[...]))
-    outer_halves(full_ref, active_ref, ck_ref, cs_ref)
     outer_halves(second_ref, before, ek_ref, es_ref)
     for j in range(PARTS):
         rows = slice(j * group.part, (j + 1) * group.part)
         grad = scatter.take(j)
         hat, scale = normalise(hidden_ref[rows, :])
-        own = full_ref[group.slab(group.me, j), :].astype(WIDE)
+        own = g_ref[rows, :].astype(WIDE)
         out = own + norm_backward(grad, hat, scale, vec_ref[3:4, :])
         grad_ref[rows, :] = out
         low_ref[rows, :] = out.astype(LOW)
@@ -397,17 +483,20 @@
 
 
 def attend_back_kernel(
-    heads, low_ref, grad_ref, x_ref, mine_ref, other_ref, normed_ref, heads_ref, o_ref, lse_ref, vec_ref,
-    wk_ref, ws_ref, out_ref, sums_ref,
-    weight, full, go3, dots, g3, key_acc, value_acc, mixed, outer,
-    stage, land, total, scatter_sems, gather_sems, local_sems,
+    last, heads, group, low_ref, grad_ref, x_ref, mine_ref, other_ref, normed_ref, heads_ref, o_ref, lse_ref, vec_ref,
+    *refs,
 ):
+    wk_ref, ws_ref, out_ref, sums_ref, *refs = refs
+    if not last:
+        spread_ref, *refs = refs
+    weight, full, go3, dots, g3, key_acc, value_acc, mixed, outer, *refs = refs
+    stage, land, total, scatter_sems, gather_sems, local_sems, *refs = refs
+    if not last:
+        stage4, deliver_sems = refs
     width = o_ref.shape[1]
-    group = Group(grad_ref.shape[0])
     section = lax.axis_index("section")
     halves = Halves((mine_ref, other_ref), weight, local_sems, 0)
     halves.start()
-    group.greet()
     sums_ref[...] = jnp.zeros_like(sums_ref)
     full[group.chunk(group.me), :] = low_ref[...]
     halves.wait()
@@ -461,6 +550,10 @@
         out_ref[rows, :] = out.astype(LOW)
         for n, term in enumerate((grad * hat, grad)):
             sums_ref[n : n + 1, :] += jnp.sum(term, axis=0, keepdims=True)
+    if not last:
+        deliver = Deliver(group, stage4, spread_ref, deliver_sems)
+        deliver.start(out_ref)
+        deliver.done()
     scatter.done()
     keep.wait()
     send.wait()
@@ -468,29 +561,73 @@
 
 VM = pl.BlockSpec(memory_space=pltpu.VMEM)
 ANY = pl.BlockSpec(memory_space=pl.ANY)
+PAIRS = pltpu.SemaphoreType.DMA((2, 3 * PARTS))
+LOCAL = pltpu.SemaphoreType.DMA((4,))
 
 
 def shape(dims, kind=LOW):
     return jax.ShapeDtypeStruct(dims, kind)
 
 
-def launch(kernel, number, in_specs, outs, out_specs, scratch, flops):
-    return pl.pallas_call(
+def launch(body, number, rows, in_specs, ins, outs, out_specs, scratch, swaps=(), diagonal=False, flops=3e10):
+    def kernel(*refs):
+        n_in, n_out, n = len(in_specs), len(outs), len(swaps)
+        group = Group(rows)
+        group.greet(n, diagonal)
+        sources, lands = refs[n_in : n_in + n], refs[n_in + n + n_out : n_in + 2 * n + n_out]
+        other = 1 - lax.axis_index("section")
+        copies = [
+            push(source, land, refs[-1], i, other, "section")
+            for i, (source, land) in enumerate(zip(sources, lands))
+        ]
+        for copy in copies:
+            copy.start()
+        rest = refs[n_in + 2 * n + n_out :]
+        body(group, *refs[:n_in], *refs[n_in + n : n_in + n + n_out], *(rest[:-1] if n else rest))
+        for copy in copies:
+            copy.wait()
+
+    extra = [pltpu.SemaphoreType.DMA((2, len(swaps)))] if swaps else []
+    results = pl.pallas_call(
         kernel,
-        out_shape=outs,
-        in_specs=in_specs,
-        out_specs=out_specs,
-        scratch_shapes=scratch,
+        out_shape=(*outs, *[shape(s.shape, s.dtype) for s in swaps]),
+        in_specs=[*in_specs, *[ANY] * len(swaps)],
+        out_specs=(*out_specs, *[ANY] * len(swaps)),
+        scratch_shapes=[*scratch, *extra],
         compiler_params=pltpu.CompilerParams(
             collective_id=number, has_side_effects=True, vmem_limit_bytes=56 * MEBI
         ),
         cost_estimate=pl.CostEstimate(
             flops=int(flops), bytes_accessed=30 * MEBI, transcendentals=0
         ),
-    )
-
-
-def attend_call(number, gathered, x, pair, vec, bias, rows, width):
+    )(*ins, *swaps)
+    return results[: len(outs)], results[len(outs) :]
+
+
+def start_call(number, tokens, cotangent, small, columns):
+    width = tokens.shape[1]
+    size = width * columns
+    kinds = small.shape[0]
+    outs = (shape((LENGTH, size)), shape((LENGTH, size)), shape((2, columns, kinds, width)))
+    blocks = pltpu.VMEM((columns, LENGTH, width), LOW)
+    vectors = pltpu.VMEM((columns, kinds, width), LOW)
+    return pl.pallas_call(
+        start_kernel,
+        out_shape=outs,
+        in_specs=[ANY] * 3,
+        out_specs=(VM,) * 3,
+        scratch_shapes=[
+            blocks, blocks, vectors, vectors, PAIRS, PAIRS,
+            pltpu.SemaphoreType.DMA((2, 3 * PARTS + 1)), LOCAL,
+        ],
+        compiler_params=pltpu.CompilerParams(
+            collective_id=number, has_side_effects=True, vmem_limit_bytes=56 * MEBI
+        ),
+        cost_estimate=pl.CostEstimate(flops=int(3e10), bytes_accessed=30 * MEBI, transcendentals=0),
+    )(tokens, cotangent, small)
+
+
+def attend_call(number, gathered, x, pair, vec, bias, rows, width, swaps):
     size = vec.shape[1]
     heads = width // HEAD
     outs = (
@@ -505,68 +642,77 @@
     scratch = [
         pltpu.VMEM((size, 4 * width), LOW),
         pltpu.VMEM((heads, LENGTH, HEAD), LOW),
-        *scatter_scratch(rows, size),
-        pltpu.SemaphoreType.DMA((2, 3 * PARTS)),
-        pltpu.SemaphoreType.DMA((4,)),
+        *scatter_scratch(rows, size), PAIRS, LOCAL,
     ]
     return launch(
         functools.partial(attend_kernel, gathered, heads),
-        number, [VM, ANY, ANY, VM, VM], outs, (VM,) * 7, scratch, 3e10,
-    )(x, *pair, vec, bias)
-
-
-def expand_call(number, second, hidden, expand, contract, vec, bias):
-    rows, size = hidden.shape
+        number, rows, [VM, ANY, ANY, VM, VM], (x, *pair, vec, bias), outs, (VM,) * 7, scratch, swaps,
+    )
+
+
+def widen_call(number, second, pair, bias, swaps):
+    rows, size = second.shape
     wide = bias.shape[1]
-    outs = (
-        shape((LENGTH, size)),
-        shape((LENGTH, wide)),
-        shape((LENGTH, wide)),
-        shape((rows, size)),
-    )
-    scratch = [
-        pltpu.VMEM((size, wide), LOW),
-        pltpu.VMEM((size, wide), LOW),
-        *scatter_scratch(rows, size),
-        pltpu.SemaphoreType.DMA((2, 3 * PARTS)),
-        pltpu.SemaphoreType.DMA((4,)),
-    ]
+    outs = (shape((LENGTH, size)), shape((LENGTH, wide)), shape((LENGTH, wide)))
+    scratch = [pltpu.VMEM((size, wide), LOW), PAIRS, LOCAL]
     return launch(
-        expand_kernel, number, [VM, VM, ANY, ANY, ANY, ANY, VM, VM], outs, (VM,) * 4, scratch, 3e10
-    )(second, hidden, *expand, *contract, vec, bias)
-
-
-def expand_back_call(number, gathered, grad, expand, contract, active, slope, second, hidden, vec):
+        widen_kernel, number, rows, [VM, ANY, ANY, VM], (second, *pair, bias), outs, (VM,) * 3, scratch, swaps
+    )
+
+
+def contract_call(number, active, hidden, pair, vec, grad, swaps):
     rows, size = hidden.shape
     wide = active.shape[1]
-    half = wide // 2
+    last = grad is not None
+    outs = [shape((rows, size))]
+    scratch = [pltpu.VMEM((size, wide), LOW), *scatter_scratch(rows, size), LOCAL]
+    in_specs, ins = [VM, VM, ANY, ANY, VM], [active, hidden, *pair, vec]
+    if last:
+        in_specs, ins = in_specs + [VM], ins + [grad]
+        columns = LENGTH // rows
+        outs += [shape((LENGTH, size // columns)), *[shape((size, wide // 2))] * 2]
+        scratch += [pltpu.VMEM((columns, rows, size // columns), LOW), pltpu.SemaphoreType.DMA((2, 3))]
+    return launch(
+        functools.partial(contract_kernel, last),
+        number, rows, in_specs, ins, outs, (VM,) * len(outs), scratch, swaps, last,
+    )
+
+
+def bend_call(number, last, grad, pair, active, slope, size, rows, swaps):
+    wide = active.shape[1]
+    outs = [shape((LENGTH, wide)), shape((8, wide), WIDE)]
+    if not last:
+        outs += [shape((LENGTH, size)), *[shape((size, wide // 2))] * 2]
+    scratch = [pltpu.VMEM((size, wide), LOW), PAIRS, LOCAL]
+    return launch(
+        functools.partial(bend_kernel, last),
+        number, rows, [VM, ANY, ANY, VM, VM], (grad, *pair, active, slope), outs, (VM,) * len(outs), scratch, swaps,
+    )
+
+
+def narrow_call(number, before, grad_own, pair, second, hidden, vec, swaps):
+    rows, size = hidden.shape
+    wide = before.shape[1]
     outs = (
-        shape((LENGTH, size)),
-        *[shape((size, half))] * 4,
+        *[shape((size, wide // 2))] * 2,
         shape((rows, size), WIDE),
         shape((rows, size)),
-        shape((8, wide), WIDE),
-    )
-    scratch = [
-        pltpu.VMEM((size, wide), LOW),
-        pltpu.VMEM((size, wide), LOW),
-        pltpu.VMEM((LENGTH, wide), LOW),
-        *scatter_scratch(rows, size),
-        pltpu.SemaphoreType.DMA((2, 3 * PARTS)),
-        pltpu.SemaphoreType.DMA((4,)),
-    ]
+        shape((8, size), WIDE),
+    )
+    scratch = [pltpu.VMEM((size, wide), LOW), *scatter_scratch(rows, size), LOCAL]
     return launch(
-        functools.partial(expand_back_kernel, gathered),
-        number, [VM, ANY, ANY, ANY, ANY, VM, VM, VM, VM, VM], outs, (VM,) * 8, scratch, 3e10,
-    )(grad, *expand, *contract, active, slope, second, hidden, vec)
-
-
-def attend_back_call(number, low, grad, x_own, pair, normed, heads_all, o, lse, vec):
+        narrow_kernel,
+        number, rows, [VM, VM, ANY, ANY, VM, VM, VM], (before, grad_own, *pair, second, hidden, vec),
+        outs, (VM,) * 5, scratch, swaps,
+    )
+
+
+def attend_back_call(number, last, low, grad, x_own, pair, normed, heads_all, o, lse, vec, swaps):
     rows, size = grad.shape
     width = o.shape[1]
     heads = width // HEAD
     half = 2 * width
-    outs = (shape((size, half)), shape((size, half)), shape((rows, size)), shape((8, size), WIDE))
+    outs = [shape((size, half)), shape((size, half)), shape((rows, size)), shape((8, size), WIDE)]
     scratch = [
         pltpu.VMEM((size, 4 * width), LOW),
         pltpu.VMEM((LENGTH, size), LOW),
@@ -577,14 +723,17 @@
         pltpu.VMEM((LENGTH, HEAD), WIDE),
         pltpu.VMEM((LENGTH, 3 * width), LOW),
         pltpu.VMEM((2, size, half), LOW),
-        *scatter_scratch(rows, size),
-        pltpu.SemaphoreType.DMA((2, 3 * PARTS)),
-        pltpu.SemaphoreType.DMA((4,)),
+        *scatter_scratch(rows, size), PAIRS, LOCAL,
     ]
+    out_specs = [ANY, ANY, VM, VM]
+    if not last:
+        outs, out_specs = outs + [shape((LENGTH, width))], out_specs + [VM]
+        scratch += [pltpu.VMEM((LENGTH // rows, rows, width), LOW), pltpu.SemaphoreType.DMA((2, 3))]
     return launch(
-        functools.partial(attend_back_kernel, heads),
-        number, [VM, VM, VM, ANY, ANY, VM, VM, VM, VM, VM], outs, (ANY, ANY, VM, VM), scratch, 3e10,
-    )(low, grad, x_own, *pair, normed, heads_all, o, lse, vec)
+        functools.partial(attend_back_kernel, last, heads),
+        number, rows, [VM, VM, VM, ANY, ANY, VM, VM, VM, VM, VM],
+        (low, grad, x_own, *pair, normed, heads_all, o, lse, vec), outs, out_specs, scratch, swaps, not last,
+    )
 
 
 def swap_sections(value):
@@ -626,53 +775,39 @@
         expand_weight[0],
         contract_weight[0].T,
     )
-    mine, theirs = [], []
+    mats = [[], []]
     for unit in units:
         half = unit.shape[1] // 2
         low, high = unit[:, :half], unit[:, half:]
-        mine.append(pick(low, high))
-        theirs.append(swap_sections(pick(high, low)))
-    mats = []
-    for layer in range(2):
-        entry = []
-        for own, got in zip(mine, theirs):
-            block = pick(own, got) if layer == 0 else pick(got, own)
-            gathered = lax.all_gather(block, "row", axis=0, tiled=True)
-            entry.append((gathered, swap_sections(gathered)))
-        mats.append(entry)
-
-    packed = jnp.concatenate(
+        own = pick(low, high)
+        got = swap_sections(pick(high, low))
+        for layer, block in enumerate((pick(own, got), pick(got, own))):
+            mats[layer].append(lax.all_gather(block, "row", axis=0, tiled=True))
+
+    small = jnp.concatenate(
         [
-            first_gain[0],
-            first_shift[0],
-            output_bias[0],
-            second_gain[0],
-            second_shift[0],
-            contract_bias[0],
-        ]
-    )
-    vectors = lax.all_gather(packed, ("section", "col"), axis=0, tiled=False)
-    vectors = vectors.reshape(2, columns, 6, width).astype(WIDE)
-    vectors = jnp.swapaxes(vectors, 1, 2).reshape(2, 6, size)
-    vectors = jnp.pad(vectors, ((0, 0), (0, 2), (0, 0)))
-    own_small = jnp.concatenate(
-        [
-            attend_bias[0, 0],
-            jnp.zeros_like(attend_bias[0, 0]),
-            attend_bias[0, 1],
-            expand_bias[0],
-        ]
-    )[None].astype(WIDE)
-    other_small = swap_sections(own_small)
-    biases = (pick(own_small, other_small), pick(other_small, own_small))
-    biases = [(b[:, : 3 * width], b[:, 3 * width :]) for b in biases]
-
-    x0_full = lax.all_gather(
-        lax.dynamic_slice_in_dim(tokens, section * LENGTH, LENGTH, 0), "col", axis=1, tiled=True
-    )
-    gy_full = lax.all_gather(
-        lax.dynamic_slice_in_dim(cotangent, section * LENGTH, LENGTH, 0), "col", axis=1, tiled=True
-    )
+            first_gain,
+            first_shift,
+            output_bias,
+            second_gain,
+            second_shift,
+            contract_bias,
+            attend_bias[0],
+            expand_bias[0].reshape(-1, width),
+        ],
+        0,
+    )
+    filled = small.shape[0]
+    small = jnp.pad(small, ((0, -filled % 16), (0, 0)))
+    x0_full, gy_full, vectors = start_call(1, tokens, cotangent, small, columns)
+    vectors = vectors.astype(WIDE)
+    wide_vectors = jnp.swapaxes(vectors[:, :, :6], 1, 2).reshape(2, 6, size)
+    wide_vectors = jnp.pad(wide_vectors, ((0, 0), (0, 2), (0, 0)))
+    own_vectors = lax.dynamic_index_in_dim(vectors, column, 1, keepdims=False)
+    attend_biases = jnp.stack(
+        [own_vectors[:, 6], jnp.zeros_like(own_vectors[:, 6]), own_vectors[:, 7]], 1
+    ).reshape(2, 1, 3 * width)
+    expand_biases = own_vectors[:, 8:filled].reshape(2, 1, -1)
 
     def own_rows(full):
         return lax.dynamic_slice_in_dim(full, column * rows, rows, 0)
@@ -680,78 +815,88 @@
     def own_features(full):
         return lax.dynamic_slice_in_dim(full, column * width, width, 1)
 
-    def gather_rows(own):
-        return lax.all_gather(own, "col", axis=0, tiled=True)
-
-    kept = []
+    attn = (mats[0][0], swap_sections(mats[0][0]))
     x = x0_full
-    fulls = []
+    kept, pairs = [], []
     owns = [own_rows(x0_full)]
     for layer in range(2):
-        attn, expand, contract = mats[layer]
-        full, normed, heads, o, lse, hidden, second_own = attend_call(
-            1 + 2 * layer, layer == 0, x, attn, vectors[layer], biases[layer][0], rows, width
+        last = layer == 1
+        vec = wide_vectors[layer]
+        (full, normed, heads, o, lse, hidden, second_own), (other,) = attend_call(
+            2 + 3 * layer, not last, x, attn, vec, attend_biases[layer], rows, width, [mats[layer][1]]
         )
-        second, active, slope, result = expand_call(
-            2 + 2 * layer, second_own, hidden, expand, contract, vectors[layer], biases[layer][1]
+        expand = (mats[layer][1], other)
+        (second, active, slope), (other,) = widen_call(
+            3 + 3 * layer, second_own, expand, expand_biases[layer], [mats[layer][2]]
         )
+        contract = (mats[layer][2], other)
+        outs, others = contract_call(
+            4 + 3 * layer, active, hidden, contract, vec,
+            gy_full if last else None, [] if last else [mats[1][0]],
+        )
+        pairs.append((attn, expand, contract))
         kept.append((normed, heads, o, lse, hidden, second, active, slope))
-        fulls.append(full)
-        owns.append(result)
-        x = result
-    x1_full = fulls[1]
-    y1_full = gather_rows(owns[2])
-
-    grad = gy_full
-    unit_grads, sums, grads = [None, None], [None, None], []
-    for layer in (1, 0):
-        attn, expand, contract = mats[layer]
-        normed, heads, o, lse, hidden, second, active, slope = kept[layer]
-        grad_full, ek, es, ck, cs, grad_hidden, low, ff_sums = expand_back_call(
-            9 - 2 * layer, layer == 1, grad, expand, contract, active, slope, second, hidden, vectors[layer]
-        )
-        wk, ws, grad, attn_sums = attend_back_call(
-            10 - 2 * layer, low, grad_hidden, owns[layer], attn, normed, heads, o, lse, vectors[layer]
-        )
-        unit_grads[layer] = ((wk, ws), (ek, es), (ck, cs))
-        sums[layer] = (ff_sums, attn_sums)
-        grads.append(grad_full)
-    gx1_full = grads[1]
-    gx0_full = gather_rows(grad)
-
-    def to_sections(layer0, layer1):
-        stays = pick(layer0, layer1)
-        got = swap_sections(pick(layer1, layer0))
-        return jnp.concatenate([pick(stays, got), pick(got, stays)], 0)
-
-    layer_outputs = to_sections(own_features(x1_full), own_features(y1_full))
-    input_grads = to_sections(own_features(gx0_full), own_features(gx1_full)).astype(WIDE)
-
-    reduced = []
-    for layer in (1, 0):
-        entry = []
-        for keep, send in unit_grads[layer]:
-            total = (keep.astype(WIDE) + swap_sections(send).astype(WIDE)).astype(LOW)
-            entry.append(lax.psum_scatter(total, "row", scatter_dimension=0, tiled=True))
-        reduced.append(entry)
+        x = outs[0]
+        owns.append(x)
+        if last:
+            y1, ck1, cs1 = outs[1:]
+        else:
+            attn = (mats[1][0], others[0])
+    y0 = own_features(full)
+    layer_low, layer_high = pick(y0, y1), pick(y1, y0)
+
+    attn, expand, contract = pairs[1]
+    normed, heads, o, lse, hidden, second, active, slope = kept[1]
+    (before, bend_sums1), _ = bend_call(8, True, gy_full, contract, active, slope, size, rows, [])
+    (ek1, es1, grad_hidden, low, narrow_sums1), (ct1,) = narrow_call(
+        9, before, own_rows(gy_full), expand, second, hidden, wide_vectors[1], [cs1]
+    )
+    (wk1, ws1, gx1_own, attend_sums1), (et1, layer_got) = attend_back_call(
+        10, True, low, grad_hidden, owns[1], attn, normed, heads, o, lse, wide_vectors[1], [es1, layer_high]
+    )
+    layer_outputs = jnp.concatenate([pick(layer_low, layer_got), pick(layer_got, layer_low)], 0)
+
+    attn, expand, contract = pairs[0]
+    normed, heads, o, lse, hidden, second, active, slope = kept[0]
+    (before, bend_sums0, gx1_full, ck0, cs0), (wt1,) = bend_call(
+        11, False, gx1_own, contract, active, slope, size, rows, [ws1]
+    )
+    (ek0, es0, grad_hidden, low, narrow_sums0), (ct0,) = narrow_call(
+        12, before, gx1_own, expand, second, hidden, wide_vectors[0], [cs0]
+    )
+    (wk0, ws0, _, attend_sums0, gx0), (et0,) = attend_back_call(
+        13, False, low, grad_hidden, owns[0], attn, normed, heads, o, lse, wide_vectors[0], [es0]
+    )
+    wt0 = swap_sections(ws0)
+
+    gx1 = own_features(gx1_full)
+    gx_low, gx_got = pick(gx0, gx1), swap_sections(pick(gx1, gx0))
+    input_grads = jnp.concatenate([pick(gx_low, gx_got), pick(gx_got, gx_low)], 0).astype(WIDE)
+
+    def reduce_grad(keep, got):
+        total = (keep.astype(WIDE) + got.astype(WIDE)).astype(LOW)
+        return lax.psum_scatter(total, "row", scatter_dimension=0, tiled=True)
+
+    late = [reduce_grad(*pair) for pair in ((wk1, wt1), (ek1, et1), (ck1, ct1))]
+    early = [reduce_grad(*pair) for pair in ((wk0, wt0), (ek0, et0), (ck0, ct0))]
     units = []
-    for late, early in zip(*reduced):
-        stays = pick(early, late)
-        got = swap_sections(pick(late, early))
+    for second_layer, first_layer in zip(late, early):
+        stays = pick(first_layer, second_layer)
+        got = swap_sections(pick(second_layer, first_layer))
         units.append(jnp.concatenate([pick(stays, got), pick(got, stays)], 1).astype(WIDE))
     attn_part, expand_part, contract_part = units
 
     wide_sum, own_sum = [], []
-    for layer in range(2):
-        ff_sums, attn_sums = sums[layer]
+    for attend_sums, narrow_sums, bend_sums in (
+        (attend_sums0, narrow_sums0, bend_sums0),
+        (attend_sums1, narrow_sums1, bend_sums1),
+    ):
         wide_sum.append(
-            jnp.stack(
-                [attn_sums[0], attn_sums[1], ff_sums[3], ff_sums[0], ff_sums[1], ff_sums[2]]
-            )
+            jnp.concatenate([attend_sums[:2], narrow_sums[3:4], narrow_sums[:3]], 0)
         )
         own_sum.append(
             jnp.concatenate(
-                [attn_sums[2, :width], attn_sums[2, 2 * width : 3 * width], ff_sums[4]]
+                [attend_sums[2, :width], attend_sums[2, 2 * width : 3 * width], bend_sums[0]]
             )
         )
     wide_sum = lax.psum(jnp.stack(wide_sum), ("section", "row", "col"))

time: 1080 us -> 853 us (0.79)
  waiting for transfers between devices: 432 us -> 75 us
  Pallas kernels: 406 us -> 584 us
  blocking collectives: 120 us -> 82.6 us
  starting transfers between devices: 31.7 us -> 14.1 us
    all_gather x10 -> x6, waiting for transfers between devices: 201 us -> 0.71 us  [on_device(): mats[layer].append(lax.all_gather(block, 'row', axis=0, tiled=True))]
    pallas_call x8 -> x13, Pallas kernels: 406 us -> 584 us  [the longest x12 541 us: launch(): pl.pallas_call(kernel, out_shape=(*outs, *[shape(s.shape, s.dtype) for s...]
    ppermute x21 -> x9, waiting for transfers between devices: 229 us -> 73.6 us  [swap_sections(): return lax.ppermute(value, 'section', [(0, 1), (1, 0)])]
    all_gather x1 -> x0, blocking collectives: 39.7 us -> none  [on_device(): vectors = lax.all_gather(packed, ('section', 'col'), axis=0, tiled=False)]
    ppermute x21 -> x9, starting transfers between devices: 31 us -> 13.2 us  [swap_sections(): return lax.ppermute(value, 'section', [(0, 1), (1, 0)])]
  transfers between devices with their start and end apart: 37 -> 21, of which waited for: 20 -> 8; matrix products, arithmetic and copies ran while one was open for 6% -> 7% of each run, Pallas kernels for 34% -> 53%
where the time goes in v3:
time: 853 us; the launch traced here: 846 us
  Pallas kernels  584 us (68%)
  blocking collectives  82.6 us (10%)
  waiting for transfers between devices  75 us (9%)
  other arithmetic  41.6 us (5%)
  local copies, waits for them, and re-layouts  33.1 us (4%)
  between operations  15.1 us (2%)
  starting transfers between devices  14.1 us (2%)
    pallas_call x12, Pallas kernels, launch(): pl.pallas_call(kernel, out_shape=(*outs, *[shape(s.shape, s.dtype) for s...  541 us
    ppermute x9, waiting for transfers between devices, swap_sections(): return lax.ppermute(value, 'section', [(0, 1), (1, 0)])  73.6 us
    psum x1, blocking collectives, on_device(): wide_sum = lax.psum(jnp.stack(wide_sum), ('section', 'row', 'col'))  43.7 us
    pallas_call x1, Pallas kernels, start_call(): pl.pallas_call(start_kernel, out_shape=outs, in_specs=[ANY] * 3, out_spec...  43.1 us
    psum x1, blocking collectives, on_device(): own_sum = lax.psum(jnp.stack(own_sum), ('section', 'row'))  39 us
    convert_element_type x6, other arithmetic, reduce_grad(): total = (keep.astype(WIDE) + got.astype(WIDE)).astype(LOW)  18.1 us
  transfers between devices with their start and end apart: 21, of which 8 were waited for; matrix products, arithmetic and copies ran while one was open for 7% of the time, Pallas kernels for 53%

profile of v3, /device:TPU:0, one launch (start us, length us, event | category | flops | bytes accessed | tf_op | source)
XLA Modules:
  0.0 845.8 jit_solution(16380499700504367869)
XLA Ops:
  8.4 1.5 copy.52
  10.4 3.0 collective-permute-start
  13.4 9.5 %collective-permute-done = bf16[320,640]{1,0:T(8,128)(2,1)S(1)} collective-permute-done((bf16[320,640]{1,0:T(8,128)(2,1)S(1)}, bf16[320,640]{1,0:T(8,128)(2,1)S(1)}, u32[]{:S(2)}, u32[]{:S(2)}) %collective-permute-start) | collective-permute-done | bytes 409632 | tf_op jit(solution)/shard_map/ppermute | solution.py:740
  24.0 1.8 collective-permute-start.2
  25.8 8.9 %collective-permute-done.2 = bf16[320,640]{1,0:T(8,128)(2,1)S(1)} collective-permute-done((bf16[320,640]{1,0:T(8,128)(2,1)S(1)}, bf16[320,640]{1,0:T(8,128)(2,1)S(1)}, u32[]{:S(2)}, u32[]{:S(2)}) %collective-permute-start.2) | collective-permute-done | bytes 409632 | tf_op jit(solution)/shard_map/ppermute | solution.py:740
  35.9 1.5 collective-permute-start.3
  37.4 8.3 collective-permute-done.3
  47.5 1.5 copy.50.tokens_ref
  49.1 1.6 copy.51.cotangent_ref
  51.4 43.1 %shard_map.245 = (bf16[1024,1280]{1,0:T(8,128)(2,1)}, bf16[1024,1280]{1,0:T(8,128)(2,1)}, bf16[2,4,16,320]{3,2,1,0:T(8,128)(2,1)}) custom-call(bf16[2048,320]{1,0:T(8,128)(2,1)} %copy.50.tokens_ref, bf16[2048,320]{1,0:T(8,128)(2,1)} %copy.51.cotangent_ref, bf16[16,320]{1,0:T(8,128)(2,1)} %pad.8.small_ref), custom_call_target="tpu_custom_call" | custom-call | flops 30000001024 | bytes 31457280 | tf_op jit(solution)/shard_map/pallas_call | solution.py:614
  99.7 2.0 constant_dynamic-slice_fusion.1.refs_1_
  102.3 31.9 %collective-permute-done.1.refs_2_.refs_4_ = bf16[1280,640]{1,0:T(8,128)(2,1)S(1)} collective-permute-done((bf16[1280,640]{1,0:T(8,128)(2,1)}, bf16[1280,640]{1,0:T(8,128)(2,1)S(1)}, u32[]{:S(2)}, u32[]{:S(2)}) %collective-permute-start.1) | collective-permute-done | bytes 1638432 | tf_op jit(solution)/shard_map/ppermute | solution.py:740
  135.4 44.1 %shard_map.246 = (bf16[16,128]{1,0:T(8,128)(2,1)}, bf16[1024,1280]{1,0:T(8,128)(2,1)}, bf16[15,1024,64]{2,1,0:T(8,128)(2,1)}, bf16[1024,320]{1,0:T(8,128)(2,1)},...) custom-call(bf16[1024,1280]{1,0:T(8,128)(2,1)} %get-tuple-element.76.refs_0_, ...), custom_call_target="tpu_custom_call" | custom-call | flops 30000001024 | bytes 31457280 | tf_op jit(solution)/shard_map/pallas_call | solution.py:591
  179.5 42.0 %shard_map.247 = (bf16[1024,1280]{1,0:T(8,128)(2,1)}, bf16[1024,1280]{1,0:T(8,128)(2,1)}, bf16[1024,1280]{1,0:T(8,128)(2,1)}, bf16[1280,640]{1,0:T(8,128)(2,1)}) custom-call(bf16[256,1280]{1,0:T(8,128)(2,1)} %get-tuple-element.78.refs_0_, bf16[1280,640]{1,0:T(8,128)(2,1)} %all-gather.9.cloned.1.call-done.refs_5_.refs_1_.refs_2_, ...), custom_call_target="tpu_custom_call" | custom-call | flops 30000001024 | bytes 31457280 | tf_op jit(solution)/shard_map/pallas_call | solution.py:591
  221.6 41.1 %shard_map.248 = (bf16[256,1280]{1,0:T(8,128)(2,1)}, bf16[1280,640]{1,0:T(8,128)(2,1)}) custom-call(bf16[1024,1280]{1,0:T(8,128)(2,1)} %get-tuple-element.80.refs_0_.refs_3_, f32[256,1280]{1,0:T(8,128)} %get-tuple-element.81.refs_1_.refs_5_, bf16[1280,640]{1,0:T(8,128)(2,1)} %all-gather.11.cloned.1.call-done.refs_4_.refs_2_.refs_1_, ...), custom_call_target="tpu_custom_call" | custom-call | flops 30000001024 | bytes 31457280 | tf_op jit(solution)/shard_map/pallas_call | solution.py:591
  262.7 56.4 %shard_map.249 = (bf16[1024,1280]{1,0:T(8,128)(2,1)}, bf16[1024,1280]{1,0:T(8,128)(2,1)}, bf16[15,1024,64]{2,1,0:T(8,128)(2,1)}, bf16[1024,320]{1,0:T(8,128)(2,1...) custom-call(bf16[256,1280]{1,0:T(8,128)(2,1)} %get-tuple-element.83.refs_0_., ...), custom_call_target="tpu_custom_call" | custom-call | flops 30000001024 | bytes 31457280 | tf_op jit(solution)/shard_map/pallas_call | solution.py:591
  319.2 42.1 %shard_map.250 = (bf16[1024,1280]{1,0:T(8,128)(2,1)}, bf16[1024,1280]{1,0:T(8,128)(2,1)}, bf16[1024,1280]{1,0:T(8,128)(2,1)}, bf16[1280,640]{1,0:T(8,128)(2,1)}) custom-call(bf16[256,1280]{1,0:T(8,128)(2,1)} %get-tuple-element.86.refs_0_, bf16[1280,640]{1,0:T(8,128)(2,1)} %all-gather.15.cloned.1.call-done.refs_5_.refs_1_.refs_2_, ...), custom_call_target="tpu_custom_call" | custom-call | flops 30000001024 | bytes 31457280 | tf_op jit(solution)/shard_map/pallas_call | solution.py:591
  361.2 12.3 %shard_map.252 = (bf16[1024,1280]{1,0:T(8,128)(2,1)}, f32[8,1280]{1,0:T(8,128)}) custom-call(bf16[1024,1280]{1,0:T(8,128)(2,1)} %get-tuple-element.91.refs_5_.refs_0_, bf16[1280,640]{1,0:T(8,128)(2,1)} %all-gather.17.cloned.1.call-done.refs_4_.refs_2_.refs_1_, bf16[1280,640]{1,0:T(8,128)(2,1)} %get-tuple-element.90.refs_3_.refs_2_, ...), custom_call_target="tpu_custom_call" | custom-call | flops 30000001024 | bytes 31457280 | tf_op jit(solution)/shard_map/pallas_call | solution.py:591
  373.5 37.5 %shard_map.251 = (bf16[256,1280]{1,0:T(8,128)(2,1)}, bf16[1024,320]{1,0:T(8,128)(2,1)}, bf16[1280,640]{1,0:T(8,128)(2,1)}, bf16[1280,640]{1,0:T(8,128)(2,1)}) custom-call(bf16[1024,1280]{1,0:T(8,128)(2,1)} %get-tuple-element.88.refs_0_.refs_3_, f32[256,1280]{1,0:T(8,128)} %get-tuple-element.89.refs_1_.refs_5_, ...), custom_call_target="tpu_custom_call" | custom-call | flops 30000001024 | bytes 31457280 | tf_op jit(solution)/shard_map/pallas_call | solution.py:591
  411.1 44.7 %shard_map.253 = (bf16[1280,640]{1,0:T(8,128)(2,1)}, bf16[1280,640]{1,0:T(8,128)(2,1)}, f32[256,1280]{1,0:T(8,128)}, bf16[256,1280]{1,0:T(8,128)(2,1)}, f32[8,1280]{1,0:T(8,128)}, /*index=5*/bf16[1280,640]{1,0:T(8,128)(2,1)}) custom-call(bf16[1024,1280]{1,0:T(8,128)(2,1)} %get-tuple-element.94.refs_0_, ...), custom_call_target="tpu_custom_call" | custom-call | flops 30000001024 | bytes 31457280 | tf_op jit(solution)/shard_map/pallas_call | solution.py:591
  455.8 3.0 add_convert_fusion
  459.9 2.5 broadcast_select_fusion.4.refs_11_
  462.4 61.3 %shard_map.254 = (bf16[1280,640]{1,0:T(8,128)(2,1)}, bf16[1280,640]{1,0:T(8,128)(2,1)}, bf16[256,1280]{1,0:T(8,128)(2,1)}, f32[8,1280]{1,0:T(8,128)}, bf16[1280,...) custom-call(bf16[256,1280]{1,0:T(8,128)(2,1)} %get-tuple-element.97.refs_0_, f32[256,1280]{1,0:T(8,128)} %get-tuple-element.98.refs_1_, ...), custom_call_target="tpu_custom_call" | custom-call | flops 30000001024 | bytes 31457280 | tf_op jit(solution)/shard_map/pallas_call | solution.py:591
  523.8 44.2 %shard_map.255 = (bf16[1024,1280]{1,0:T(8,128)(2,1)}, f32[8,1280]{1,0:T(8,128)}, bf16[1024,1280]{1,0:T(8,128)(2,1)}, bf16[1280,640]{1,0:T(8,128)(2,1)}, bf16[128...) custom-call(bf16[256,1280]{1,0:T(8,128)(2,1)} %get-tuple-element.105.refs_0_.refs_1_, ...), custom_call_target="tpu_custom_call" | custom-call | flops 30000001024 | bytes 31457280 | tf_op jit(solution)/shard_map/pallas_call | solution.py:591
  568.0 43.5 %shard_map.256 = (bf16[1280,640]{1,0:T(8,128)(2,1)}, bf16[1280,640]{1,0:T(8,128)(2,1)}, f32[256,1280]{1,0:T(8,128)}, bf16[256,1280]{1,0:T(8,128)(2,1)}, f32[8,1280]{1,0:T(8,128)}, /*index=5*/bf16[1280,640]{1,0:T(8,128)(2,1)}) custom-call(bf16[1024,1280]{1,0:T(8,128)(2,1)} %get-tuple-element.108.refs_0_, ...), custom_call_target="tpu_custom_call" | custom-call | flops 30000001024 | bytes 31457280 | tf_op jit(solution)/shard_map/pallas_call | solution.py:591
  611.6 3.0 add_convert_fusion.1
  614.7 2.1 constant_dynamic-slice_fusion.refs_2_
  616.7 3.0 add_convert_fusion.2
  619.9 71.9 %shard_map.257 = (bf16[1280,640]{1,0:T(8,128)(2,1)}, bf16[1280,640]{1,0:T(8,128)(2,1)}, bf16[256,1280]{1,0:T(8,128)(2,1)}, f32[8,1280]{1,0:T(8,128)}, bf16[1024,...) custom-call(bf16[256,1280]{1,0:T(8,128)(2,1)} %get-tuple-element.111.refs_0_, f32[256,1280]{1,0:T(8,128)} %get-tuple-element.112.refs_1_, ...), custom_call_target="tpu_custom_call" | custom-call | flops 30000001024 | bytes 31457280 | tf_op jit(solution)/shard_map/pallas_call | solution.py:591
  691.8 3.0 add_convert_fusion.3
  694.8 1.4 copy-done.6
  696.2 3.0 add_convert_fusion.4
  701.1 2.0 broadcast_select_fusion.3
  703.3 1.5 copy.62
  709.7 39.0 %psum.15 = f32[2,1920]{1,0:T(2,128)S(1)} all-reduce(f32[2,1920]{1,0:T(2,128)S(1)} %pad_maximum_fusion.2), channel_id=1, replica_groups=mesh['section'=2,'row'=4,'col'=4] {'section','row'}, use_global_device_ids=true, to_apply=%region_3.4 | all-reduce | flops 3840 | bytes 30720 | tf_op jit(solution)/shard_map/psum | solution.py:903
  749.3 3.1 add_convert_fusion.5
  753.5 1.7 broadcast_select_fusion
  756.4 43.7 %psum.14 = f32[2,6,1280]{2,1,0:T(8,128)S(1)} all-reduce(f32[2,6,1280]{2,1,0:T(8,128)S(1)} %pad_maximum_fusion.1), channel_id=1, replica_groups=mesh['section'=2,'row'=4,'col'=4] {'section','row','col'}, use_global_device_ids=true, to_apply=%region_0.1 | all-reduce | flops 15360 | bytes 122880 | tf_op jit(solution)/shard_map/psum | solution.py:902
  801.1 3.0 select_bitcast_fusion.1
  804.2 1.9 broadcast_select_fusion.8
  806.1 2.3 collective-permute-start.8
  808.4 1.3 maximum_convert_fusion
  809.7 2.2 copy.63
  813.1 6.0 collective-permute-done.8
  822.6 2.0 collective-permute-start.6
  824.6 3.1 collective-permute-done.7
  829.1 5.9 collective-permute-done.6
  837.1 1.6 copy.64
  (167 shorter events, 33.6 us)
Async XLA Ops:
  7.2 88.3 %all-gather.7.cloned.1.call-start = ((), (), s32[]{:S(2)}) async-start(), calls=%async_computation.6 | async-start | bytes 2048000 | tf_op jit(solution)/shard_map/all_gather | solution.py:785
  10.4 13.5 %copy-start = (bf16[1,320,1280]{2,1,0:T(8,128)(2,1)S(1)}, bf16[1,320,1280]{2,1,0:T(8,128)(2,1)}, u32[]{:S(2)}) copy-start(bf16[1,320,1280]{2,1,0:T(8,128)(2,1)} %param.24) | copy-start | bytes 2457604
  10.4 12.5 %collective-permute-start = (bf16[320,640]{1,0:T(8,128)(2,1)S(1)}, bf16[320,640]{1,0:T(8,128)(2,1)S(1)}, u32[]{:S(2)}, u32[]{:S(2)}) collective-permute-start(bf16[320,640]{1,0:T(8,128)(2,1)S(1)} %get-tuple-element.184), channel_id=1, source_target_pairs={{0,16},{16,0},{1,17},{17,1},{2,18},{18,2},{3,19},{19,3},{4,20},{20... | collective-permute-start | bytes 1228808 | tf_op jit(solution)/shard_map/ppermute | solution.py:740
  23.9 78.4 %all-gather.9.cloned.1.call-start = ((), (), s32[]{:S(2)}) async-start(), calls=%async_computation.7 | async-start | bytes 2048000 | tf_op jit(solution)/shard_map/all_gather | solution.py:785
  23.9 11.9 %copy-start.1 = (bf16[1,1280,320]{1,2,0:T(8,128)(2,1)S(1)}, bf16[1,1280,320]{1,2,0:T(8,128)(2,1)}, u32[]{:S(2)}) copy-start(bf16[1,1280,320]{1,2,0:T(8,128)(2,1)} %param.26) | copy-start | bytes 2457604
  24.0 10.7 %collective-permute-start.2 = (bf16[320,640]{1,0:T(8,128)(2,1)S(1)}, bf16[320,640]{1,0:T(8,128)(2,1)S(1)}, u32[]{:S(2)}, u32[]{:S(2)}) collective-permute-start(bf16[320,640]{1,0:T(8,128)(2,1)S(1)} %broadcast_select_fusion.23), channel_id=1, source_target_pairs={{0,16},{16,0},{1,17},{17,1},{2,18},{18,2},{3,19},{19,3},{4,20},{20... | collective-permute-start | bytes 1228808 | tf_op jit(solution)/shard_map/ppermute | solution.py:740
  35.8 143.8 %all-gather.11.cloned.1.call-start = ((), (), s32[]{:S(2)}) async-start(), calls=%async_computation.8 | async-start | bytes 2048000 | tf_op jit(solution)/shard_map/all_gather | solution.py:785
  35.9 11.5 %copy-start.21 = (bf16[1,1280]{1,0:T(2,128)(2,1)S(1)}, bf16[1,1280]{1,0:T(2,128)(2,1)}, u32[]{:S(2)}) copy-start(bf16[1,1280]{1,0:T(2,128)(2,1)} %param.25) | copy-start | bytes 7684
  35.9 11.6 %copy-start.16 = (bf16[2048,320]{0,1:T(8,128)(2,1)S(1)}, bf16[2048,320]{0,1:T(8,128)(2,1)}, u32[]{:S(2)}) copy-start(bf16[2048,320]{0,1:T(8,128)(2,1)} %param.14) | copy-start | bytes 3932164
  35.9 9.8 %collective-permute-start.3 = (bf16[320,640]{1,0:T(8,128)(2,1)S(1)}, bf16[320,640]{1,0:T(8,128)(2,1)S(1)}, u32[]{:S(2)}, u32[]{:S(2)}) collective-permute-start(bf16[320,640]{1,0:T(8,128)(2,1)S(1)} %broadcast_select_fusion.20), channel_id=1, source_target_pairs={{0,16},{16,0},{1,17},{17,1},{2,18},{18,2},{3,19},{19,3},{4,20},{20... | collective-permute-start | bytes 1228808 | tf_op jit(solution)/shard_map/ppermute | solution.py:740
  46.7 174.9 %all-gather.13.cloned.1.call-start = ((), (), s32[]{:S(2)}) async-start(), calls=%async_computation.9 | async-start | bytes 2048000 | tf_op jit(solution)/shard_map/all_gather | solution.py:785
  46.8 2.3 copy-start.17
  47.3 215.4 %all-gather.15.cloned.1.call-start = ((), (), s32[]{:S(2)}) async-start(), calls=%async_computation.10 | async-start | bytes 2048000 | tf_op jit(solution)/shard_map/all_gather | solution.py:785
  49.0 1.6 copy-start.22
  49.0 1.6 copy-start.23
  49.0 1.6 copy-start.24
  49.0 1.6 copy-start.25
  49.0 1.6 copy-start.26
  49.1 1.6 copy-start.27
  49.1 1.6 copy-start.28
  51.4 267.8 %all-gather.17.cloned.1.call-start = ((), (), s32[]{:S(2)}) async-start(), calls=%async_computation.11 | async-start | bytes 2048000 | tf_op jit(solution)/shard_map/all_gather | solution.py:785
  95.5 38.7 %collective-permute-start.1 = (bf16[1280,640]{1,0:T(8,128)(2,1)}, bf16[1280,640]{1,0:T(8,128)(2,1)S(1)}, u32[]{:S(2)}, u32[]{:S(2)}) collective-permute-start(bf16[1280,640]{1,0:T(8,128)(2,1)} %all-gather.7.cloned.1.call-done.refs_1_.refs_3_), channel_id=1, source_target_pairs={{0,16},{16,0},{1,17},{17,1},{2,18},{18,2},{3,19},{19,3},{4,20},{20... | collective-permute-start | bytes 4915208 | tf_op jit(solution)/shard_map/ppermute | solution.py:740
  101.7 702.5 %reduce-scatter.17.cloned.1.call-start = ((), (), s32[]{:S(2)}) async-start(), calls=%async_computation.17 | async-start | bytes 2048000 | tf_op jit(solution)/shard_map/reduce_scatter | solution.py:878
  134.2 1.2 copy-start.29
  411.0 44.7 %copy-start.10 = (bf16[1280,640]{1,0:T(8,128)(2,1)S(1)}, bf16[1280,640]{1,0:T(8,128)(2,1)}, u32[]{:S(2)}) copy-start(bf16[1280,640]{1,0:T(8,128)(2,1)} %get-tuple-element.136) | copy-start | bytes 4915204
  458.8 345.4 %reduce-scatter.15.cloned.1.call-start = ((), (), s32[]{:S(2)}) async-start(), calls=%async_computation.16 | async-start | bytes 2048000 | tf_op jit(solution)/shard_map/reduce_scatter | solution.py:878
  568.0 43.6 %copy-start.9 = (bf16[1280,640]{1,0:T(8,128)(2,1)S(1)}, bf16[1280,640]{1,0:T(8,128)(2,1)}, u32[]{:S(2)}) copy-start(bf16[1280,640]{1,0:T(8,128)(2,1)} %get-tuple-element.134) | copy-start | bytes 4915204
  614.6 2.2 copy-start.7
  614.6 197.3 %reduce-scatter.13.cloned.1.call-start = ((), (), s32[]{:S(2)}) async-start(), calls=%async_computation.15 | async-start | bytes 2048000 | tf_op jit(solution)/shard_map/reduce_scatter | solution.py:878
  619.8 192.1 %reduce-scatter.11.cloned.1.call-start = ((), (), s32[]{:S(2)}) async-start(), calls=%async_computation.14 | async-start | bytes 2048000 | tf_op jit(solution)/shard_map/reduce_scatter | solution.py:878
  619.9 71.9 %copy-start.8 = (bf16[1280,640]{1,0:T(8,128)(2,1)S(1)}, bf16[1280,640]{1,0:T(8,128)(2,1)}, u32[]{:S(2)}) copy-start(bf16[1280,640]{1,0:T(8,128)(2,1)} %get-tuple-element.130) | copy-start | bytes 4915204
  694.8 1.4 copy-start.6
  694.8 126.8 %reduce-scatter.9.cloned.1.call-start = ((), (), s32[]{:S(2)}) async-start(), calls=%async_computation.13 | async-start | bytes 2048000 | tf_op jit(solution)/shard_map/reduce_scatter | solution.py:878
  699.2 1.9 copy-start.18
  699.2 122.4 %reduce-scatter.7.cloned.1.call-start = ((), (), s32[]{:S(2)}) async-start(), calls=%async_computation.12 | async-start | bytes 2048000 | tf_op jit(solution)/shard_map/reduce_scatter | solution.py:878
  700.0 49.2 %collective-permute-start.5 = (bf16[1280,640]{1,0:T(8,128)(2,1)}, bf16[1280,640]{1,0:T(8,128)(2,1)}, u32[]{:S(2)}, u32[]{:S(2)}) collective-permute-start(bf16[1280,640]{1,0:T(8,128)(2,1)} %get-tuple-element.125), channel_id=1, source_target_pairs={{0,16},{16,0},{1,17},{17,1},{2,18},{18,2},{3,19},{19,3},{4,20},{20... | collective-permute-start | bytes 4915208 | tf_op jit(solution)/shard_map/ppermute | solution.py:740
  703.3 46.0 %copy-start.5 = (bf16[1280,640]{1,0:T(8,128)(2,1)S(1)}, bf16[1280,640]{1,0:T(8,128)(2,1)}, u32[]{:S(2)}) copy-start(bf16[1280,640]{1,0:T(8,128)(2,1)} %get-tuple-element.124) | copy-start | bytes 4915204
  752.3 1.1 copy-start.4
  755.4 45.3 %collective-permute-start.4 = (bf16[1024,320]{0,1:T(8,128)(2,1)S(1)}, bf16[1024,320]{0,1:T(8,128)(2,1)S(1)}, u32[]{:S(2)}, u32[]{:S(2)}) collective-permute-start(bf16[1024,320]{0,1:T(8,128)(2,1)S(1)} %copy.58), channel_id=1, source_target_pairs={{0,16},{16,0},{1,17},{17,1},{2,18},{18,2},{3,19},{19,3},{4,20},{20... | collective-permute-start | bytes 1966088 | tf_op jit(solution)/shard_map/ppermute | solution.py:740
  804.2 4.2 copy-start.2
  806.1 13.0 %collective-permute-start.8 = (bf16[320,640]{1,0:T(8,128)(2,1)}, bf16[320,640]{1,0:T(8,128)(2,1)}, u32[]{:S(2)}, u32[]{:S(2)}) collective-permute-start(bf16[320,640]{1,0:T(8,128)(2,1)} %broadcast_select_fusion.8), channel_id=1, source_target_pairs={{0,16},{16,0},{1,17},{17,1},{2,18},{18,2},{3,19},{19,3},{4,20},{20... | collective-permute-start | bytes 1228808 | tf_op jit(solution)/shard_map/ppermute | solution.py:740
  809.7 9.3 %copy-start.11 = (bf16[320,640]{1,0:T(8,128)(2,1)S(1)}, bf16[320,640]{1,0:T(8,128)(2,1)}, u32[]{:S(2)}) copy-start(bf16[320,640]{1,0:T(8,128)(2,1)} %reduce-scatter.17.cloned.1.call-done) | copy-start | bytes 1228804
  813.0 14.7 %collective-permute-start.7 = (bf16[320,640]{1,0:T(8,128)(2,1)S(1)}, bf16[320,640]{1,0:T(8,128)(2,1)S(1)}, u32[]{:S(2)}, u32[]{:S(2)}) collective-permute-start(bf16[320,640]{1,0:T(8,128)(2,1)S(1)} %broadcast_select_fusion.10), channel_id=1, source_target_pairs={{0,16},{16,0},{1,17},{17,1},{2,18},{18,2},{3,19},{19,3},{4,20},{20... | collective-permute-start | bytes 1228808 | tf_op jit(solution)/shard_map/ppermute | solution.py:740
  820.3 7.4 copy-start.12
  820.3 7.4 copy-start.14
  822.6 12.4 %collective-permute-start.6 = (bf16[320,640]{1,0:T(8,128)(2,1)S(1)}, bf16[320,640]{1,0:T(8,128)(2,1)S(1)}, u32[]{:S(2)}, u32[]{:S(2)}) collective-permute-start(bf16[320,640]{1,0:T(8,128)(2,1)S(1)} %broadcast_select_fusion.14), channel_id=1, source_target_pairs={{0,16},{16,0},{1,17},{17,1},{2,18},{18,2},{3,19},{19,3},{4,20},{20... | collective-permute-start | bytes 1228808 | tf_op jit(solution)/shard_map/ppermute | solution.py:740
  827.8 7.2 copy-start.13
  827.9 7.2 copy-start.15
  (3 other events, 2.7 us)
Sparse Core Ops, SparseCore 0:
  24.0 39.6 all-gather.6
  65.3 37.0 all-gather.8
  104.5 37.0 all-gather.10
  143.5 37.0 all-gather.12
  182.0 37.0 all-gather.14
  221.1 37.0 all-gather.16
  458.9 36.5 reduce-scatter.16
  614.7 36.6 reduce-scatter.14
  653.8 35.3 reduce-scatter.12
  694.9 37.6 reduce-scatter.10
  735.5 35.4 reduce-scatter.8
  773.2 36.0 reduce-scatter.6

commit v4 on v3

--- a/solution.py
+++ b/solution.py
@@ -1,4 +1,5 @@
 import functools
+import math
 
 import jax
 import jax.numpy as jnp
@@ -16,6 +17,7 @@
 PARTS = 2
 TILE = 256
 MEBI = 1024 * 1024
+SPARE = 14 * MEBI
 
 
 def nn(left, right):
@@ -54,13 +56,14 @@
         self.rows = rows
         self.part = rows // PARTS
 
-    def greet(self, swaps, diagonal):
+    def greet(self, swaps, diagonal, rows=()):
         barrier = pltpu.get_barrier_semaphore()
         others = [{"col": self.sib}, {"col": self.peer}]
         if diagonal:
             others.append({"col": self.diag})
         if swaps:
             others.append({"section": 1 - lax.axis_index("section")})
+        others += [{"row": row} for row in rows]
         for other in others:
             pl.semaphore_signal(barrier, inc=1, device_id=other, device_id_type=MESH)
         pl.semaphore_wait(barrier, len(others))
@@ -145,22 +148,25 @@
     def start(self, part):
         g, stage, land = self.group, self.stage, self.land
         self.first, self.over, self.near = [], [], []
-        for j in range(PARTS):
-            stage[0, j] = part(g.slab(g.diag, j)).astype(LOW)
+        def split(owner):
+            whole = part(g.chunk(owner))
+            return [whole[j * g.part : (j + 1) * g.part] for j in range(PARTS)]
+
+        for j, mine in enumerate(split(g.diag)):
+            stage[0, j] = mine.astype(LOW)
             self.first.append(push(stage.at[0, j], land.at[0, j], self.sems, j, g.sib))
             self.first[-1].start()
-        for j in range(PARTS):
-            mine = part(g.slab(g.peer, j))
+        for j, mine in enumerate(split(g.peer)):
             self.first[j].wait_recv()
             stage[1, j] = (mine + land[0, j].astype(WIDE)).astype(LOW)
             self.over.append(push(stage.at[1, j], land.at[1, j], self.sems, PARTS + j, g.peer))
             self.over[-1].start()
-        for j in range(PARTS):
-            stage[2, j] = part(g.slab(g.sib, j)).astype(LOW)
+        for j, mine in enumerate(split(g.sib)):
+            stage[2, j] = mine.astype(LOW)
             self.near.append(push(stage.at[2, j], land.at[2, j], self.sems, 2 * PARTS + j, g.sib))
             self.near[-1].start()
-        for j in range(PARTS):
-            self.total[j] = part(g.slab(g.me, j))
+        for j, mine in enumerate(split(g.me)):
+            self.total[j] = mine
 
     def take(self, j):
         self.near[j].wait_recv()
@@ -284,7 +290,7 @@
 
 
 def start_kernel(
-    tokens_ref, cotangent_ref, small_ref, x_ref, g_ref, vectors_ref,
+    tokens_ref, cotangent_ref, small_ref, raw_ref, x_ref, g_ref, vectors_ref, got_ref,
     x4, g4, s4, other4, x_sems, g_sems, s_sems, local_sems,
 ):
     section = lax.axis_index("section")
@@ -296,6 +302,8 @@
         loads.append(pltpu.make_async_copy(source, into.at[group.me], local_sems.at[n]))
         loads[-1].start()
     group.greet(True, False)
+    blocks = push(raw_ref, got_ref, s_sems, 3 * PARTS + 1, 1 - section, "section")
+    blocks.start()
     gathers = [Gather(group, x4, x_sems, True), Gather(group, s4, s_sems, True), Gather(group, g4, g_sems, True)]
     for gather, load in zip(gathers, (loads[0], loads[2], loads[1])):
         load.wait()
@@ -311,6 +319,7 @@
         x_ref[:, c * width : (c + 1) * width] = x4[c]
         g_ref[:, c * width : (c + 1) * width] = g4[c]
     swap.wait()
+    blocks.wait()
     vectors_ref[section] = s4[...]
     vectors_ref[1 - section] = other4[...]
     for gather in gathers:
@@ -407,10 +416,8 @@
         g_ref, *refs = refs
     result_ref, *refs = refs
     if last:
-        out_ref, ck_ref, cs_ref, *refs = refs
-    contract, stage, land, total, scatter_sems, local_sems, *refs = refs
-    if last:
-        stage4, deliver_sems = refs
+        ck_ref, cs_ref, *refs = refs
+    contract, stage, land, total, scatter_sems, local_sems = refs
     halves = Halves((cm_ref, co_ref), contract, local_sems, 0)
     halves.start()
     halves.wait()
@@ -422,22 +429,25 @@
         rows = slice(j * group.part, (j + 1) * group.part)
         result = hidden_ref[rows, :] + scatter.take(j) + vec_ref[5:6, :]
         result_ref[rows, :] = result.astype(LOW)
+    scatter.done()
+
+
+def bend_kernel(last, group, g_ref, cm_ref, co_ref, slope_ref, extra_ref, *refs):
+    before, sums_ref, *refs = refs
     if last:
+        out_ref, *refs = refs
+    else:
+        full_ref, ck_ref, cs_ref, *refs = refs
+    contract, gather_sems, local_sems, *refs = refs
+    if last:
+        stage4, deliver_sems = refs
         deliver = Deliver(group, stage4, out_ref, deliver_sems)
-        deliver.start(result_ref)
-        deliver.done()
-    scatter.done()
-
-
-def bend_kernel(last, group, g_ref, cm_ref, co_ref, active_ref, slope_ref, *refs):
-    before, sums_ref, *refs = refs
-    if not last:
-        full_ref, ck_ref, cs_ref, *refs = refs
-    contract, gather_sems, local_sems = refs
     halves = Halves((cm_ref, co_ref), contract, local_sems, 0)
     halves.start()
     sums_ref[...] = jnp.zeros_like(sums_ref)
-    if not last:
+    if last:
+        deliver.start(extra_ref)
+    else:
         full_ref[group.chunk(group.me), :] = g_ref[...]
     halves.wait()
 
@@ -452,9 +462,11 @@
         @pl.loop(0, LENGTH // group.rows)
         def _(n):
             bend(group.chunk(n))
+
+        deliver.done()
     else:
         Gather(group, full_ref, gather_sems).each(bend)
-        outer_halves(full_ref, active_ref, ck_ref, cs_ref)
+        outer_halves(full_ref, extra_ref, ck_ref, cs_ref)
 
 
 def narrow_kernel(
@@ -482,22 +494,14 @@
     scatter.done()
 
 
-def attend_back_kernel(
-    last, heads, group, low_ref, grad_ref, x_ref, mine_ref, other_ref, normed_ref, heads_ref, o_ref, lse_ref, vec_ref,
-    *refs,
+def scores_back_kernel(
+    heads, group, low_ref, mine_ref, other_ref, heads_ref, o_ref, lse_ref,
+    mixed, outer_ref,
+    weight, full, go3, dots, g3, key_acc, value_acc, gather_sems, local_sems,
 ):
-    wk_ref, ws_ref, out_ref, sums_ref, *refs = refs
-    if not last:
-        spread_ref, *refs = refs
-    weight, full, go3, dots, g3, key_acc, value_acc, mixed, outer, *refs = refs
-    stage, land, total, scatter_sems, gather_sems, local_sems, *refs = refs
-    if not last:
-        stage4, deliver_sems = refs
     width = o_ref.shape[1]
-    section = lax.axis_index("section")
     halves = Halves((mine_ref, other_ref), weight, local_sems, 0)
     halves.start()
-    sums_ref[...] = jnp.zeros_like(sums_ref)
     full[group.chunk(group.me), :] = low_ref[...]
     halves.wait()
     picks = (
@@ -523,24 +527,51 @@
     for j in range(3 * heads):
         mixed[:, j * HEAD : (j + 1) * HEAD] = g3[j]
 
-    scatter = Scatter(group, stage, land, total, scatter_sems)
-    scatter.start(lambda rows: nt(mixed[rows, :], weight[:, : 3 * width]))
-
-    half = weight.shape[1] // 2
-
-    @pl.loop(0, weight.shape[0] // TILE)
+    @pl.loop(0, outer_ref.shape[0] // TILE)
     def _(n):
         rows = pl.ds(pl.multiple_of(n * TILE, TILE), TILE)
-        outer[section, rows, :] = tn(normed_ref[:, rows], mixed[:, :half]).astype(LOW)
-        outer[1 - section, rows, : 3 * width - half] = tn(
-            normed_ref[:, rows], mixed[:, half:]
-        ).astype(LOW)
-        outer[1 - section, rows, 3 * width - half :] = tn(full[:, rows], o_ref[...]).astype(LOW)
-
-    keep = pltpu.make_async_copy(outer.at[0], wk_ref, local_sems.at[2])
-    send = pltpu.make_async_copy(outer.at[1], ws_ref, local_sems.at[3])
-    keep.start()
-    send.start()
+        outer_ref[rows, :] = tn(full[:, rows], o_ref[...]).astype(LOW)
+
+
+def attend_back_kernel(
+    last, group, mixed, outer_ref, grad_ref, x_ref, mine_ref, other_ref, normed_ref, vec_ref,
+    wk_ref, ws_ref, out_ref, sums_ref, *refs,
+):
+    if not last:
+        got_ref, *refs = refs
+    weight, outer, stage, land, total, scatter_sems, local_sems, *refs = refs
+    width = outer_ref.shape[1]
+    section = lax.axis_index("section")
+    halves = Halves((mine_ref, other_ref), weight, local_sems, 0)
+    halves.start()
+    sums_ref[...] = jnp.zeros_like(sums_ref)
+
+    half = weight.shape[1] // 2
+
+    def products():
+        @pl.loop(0, weight.shape[0] // TILE)
+        def _(n):
+            rows = pl.ds(pl.multiple_of(n * TILE, TILE), TILE)
+            outer[section, rows, :] = tn(normed_ref[:, rows], mixed[:, :half]).astype(LOW)
+            outer[1 - section, rows, : 3 * width - half] = tn(
+                normed_ref[:, rows], mixed[:, half:]
+            ).astype(LOW)
+            outer[1 - section, rows, 3 * width - half :] = outer_ref[rows, :]
+
+    scatter = Scatter(group, stage, land, total, scatter_sems)
+    if not last:
+        products()
+        swap = push(outer.at[1], got_ref, refs[0], 0, 1 - section, "section")
+        swap.start()
+    halves.wait()
+    scatter.start(lambda rows: nt(mixed[rows, :], weight[:, : 3 * width]))
+    if last:
+        products()
+    copies = [pltpu.make_async_copy(outer.at[0], wk_ref, local_sems.at[2])]
+    if last:
+        copies.append(pltpu.make_async_copy(outer.at[1], ws_ref, local_sems.at[3]))
+    for copy in copies:
+        copy.start()
     sums_ref[2:3, : 3 * width] = jnp.sum(mixed[...].astype(WIDE), axis=0, keepdims=True)
     for j in range(PARTS):
         rows = slice(j * group.part, (j + 1) * group.part)
@@ -550,13 +581,89 @@
         out_ref[rows, :] = out.astype(LOW)
         for n, term in enumerate((grad * hat, grad)):
             sums_ref[n : n + 1, :] += jnp.sum(term, axis=0, keepdims=True)
+    scatter.done()
+    for copy in copies:
+        copy.wait()
     if not last:
-        deliver = Deliver(group, stage4, spread_ref, deliver_sems)
-        deliver.start(out_ref)
-        deliver.done()
-    scatter.done()
-    keep.wait()
-    send.wait()
+        swap.wait()
+
+
+def finish_kernel(
+    near_ref, far_ref, a0, n0, b0, a1, n1, b1, grads_ref, sums_ref,
+    mine, stage4, block, land_col, land_x, land_z, send, land,
+    deliver_sems, col_sems, x_sems, z_sems,
+):
+    section, row = lax.axis_index("section"), lax.axis_index("row")
+    group = Group(near_ref.shape[0])
+    length, width = far_ref.shape
+    others = [lax.rem(row + d, land_z.shape[0]) for d in range(1, land_z.shape[0])]
+    group.greet(True, True, others)
+    deliver = Deliver(group, stage4, mine, deliver_sems)
+    deliver.start(near_ref)
+
+    block[...] = jnp.zeros_like(block)
+    for layer, (attn, narrow, bend) in enumerate(((a0, n0, b0), (a1, n1, b1))):
+        wide = [attn[0:1, :], attn[1:2, :], narrow[3:4, :], narrow[0:1, :], narrow[1:2, :], narrow[2:3, :]]
+        for c in range(block.shape[0]):
+            columns = slice(c * width, (c + 1) * width)
+            for n, term in enumerate(wide):
+                block[c, layer, n : n + 1, :] = term[:, columns]
+            for n, term in enumerate((attn[2:3, :width], attn[2:3, 2 * width : 3 * width])):
+                block[c, layer, 8 + n : 9 + n, :] = term
+            for n in range(bend.shape[1] // width):
+                block[c, layer, 10 + n : 11 + n, :] = bend[0:1, n * width : (n + 1) * width]
+    copies = [
+        push(block.at[other, :, pl.ds(0, 8)], land_col.at[n], col_sems, n, other)
+        for n, other in enumerate((group.peer, group.diag, group.sib))
+    ]
+    for copy in copies:
+        copy.start()
+    for copy in copies:
+        copy.wait()
+    me = group.me
+    block[me, :, :8] = block[me, :, :8] + (land_col[0] + (land_col[1] + land_col[2]))
+    swap = push(block.at[me, 1 - section], land_x, x_sems, 0, 1 - section, "section")
+    swap.start()
+    swap.wait()
+    land_z[row] = block[me, section] + land_x[...]
+    copies = [
+        push(land_z.at[row], land_z.at[row], z_sems, n, other, "row")
+        for n, other in enumerate(others)
+    ]
+    for copy in copies:
+        copy.start()
+
+    deliver.done()
+
+    @pl.when(section == 0)
+    def _():
+        send[...] = far_ref[...]
+
+    @pl.when(section == 1)
+    def _():
+        send[...] = mine[...]
+
+    swap = push(send, land, x_sems, 1, 1 - section, "section")
+    swap.start()
+    own = pl.ds(pl.multiple_of(section * length, length), length)
+    away = pl.ds(pl.multiple_of((1 - section) * length, length), length)
+
+    @pl.when(section == 0)
+    def _():
+        grads_ref[own, :] = mine[...].astype(WIDE)
+
+    @pl.when(section == 1)
+    def _():
+        grads_ref[own, :] = far_ref[...].astype(WIDE)
+
+    for copy in copies:
+        copy.wait()
+    result = land_z[0]
+    for n in range(1, land_z.shape[0]):
+        result = result + land_z[n]
+    sums_ref[...] = result
+    swap.wait()
+    grads_ref[away, :] = land[...].astype(WIDE)
 
 
 VM = pl.BlockSpec(memory_space=pltpu.VMEM)
@@ -569,11 +676,11 @@
     return jax.ShapeDtypeStruct(dims, kind)
 
 
-def launch(body, number, rows, in_specs, ins, outs, out_specs, scratch, swaps=(), diagonal=False, flops=3e10):
+def launch(body, number, rows, in_specs, ins, outs, out_specs, scratch, swaps=(), diagonal=False, across=False, flops=3e10):
     def kernel(*refs):
         n_in, n_out, n = len(in_specs), len(outs), len(swaps)
         group = Group(rows)
-        group.greet(n, diagonal)
+        group.greet(n or across, diagonal)
         sources, lands = refs[n_in : n_in + n], refs[n_in + n + n_out : n_in + 2 * n + n_out]
         other = 1 - lax.axis_index("section")
         copies = [
@@ -588,6 +695,9 @@
             copy.wait()
 
     extra = [pltpu.SemaphoreType.DMA((2, len(swaps)))] if swaps else []
+    held = [a for a, spec in zip((*ins, *outs), (*in_specs, *out_specs)) if spec is VM]
+    held += [s for s in scratch if s.memory_space == pltpu.VMEM]
+    need = sum(math.prod(s.shape[:-1]) * (-(-s.shape[-1] // 128) * 128) * s.dtype.itemsize for s in held)
     results = pl.pallas_call(
         kernel,
         out_shape=(*outs, *[shape(s.shape, s.dtype) for s in swaps]),
@@ -595,7 +705,7 @@
         out_specs=(*out_specs, *[ANY] * len(swaps)),
         scratch_shapes=[*scratch, *extra],
         compiler_params=pltpu.CompilerParams(
-            collective_id=number, has_side_effects=True, vmem_limit_bytes=56 * MEBI
+            collective_id=number, has_side_effects=True, vmem_limit_bytes=min(need + SPARE, 58 * MEBI)
         ),
         cost_estimate=pl.CostEstimate(
             flops=int(flops), bytes_accessed=30 * MEBI, transcendentals=0
@@ -604,27 +714,27 @@
     return results[: len(outs)], results[len(outs) :]
 
 
-def start_call(number, tokens, cotangent, small, columns):
+def start_call(number, tokens, cotangent, small, raw, columns):
     width = tokens.shape[1]
     size = width * columns
     kinds = small.shape[0]
-    outs = (shape((LENGTH, size)), shape((LENGTH, size)), shape((2, columns, kinds, width)))
+    outs = (shape((LENGTH, size)), shape((LENGTH, size)), shape((2, columns, kinds, width)), shape(raw.shape))
     blocks = pltpu.VMEM((columns, LENGTH, width), LOW)
     vectors = pltpu.VMEM((columns, kinds, width), LOW)
     return pl.pallas_call(
         start_kernel,
         out_shape=outs,
-        in_specs=[ANY] * 3,
-        out_specs=(VM,) * 3,
+        in_specs=[ANY] * 4,
+        out_specs=(VM, VM, VM, ANY),
         scratch_shapes=[
             blocks, blocks, vectors, vectors, PAIRS, PAIRS,
-            pltpu.SemaphoreType.DMA((2, 3 * PARTS + 1)), LOCAL,
+            pltpu.SemaphoreType.DMA((2, 3 * PARTS + 2)), LOCAL,
         ],
         compiler_params=pltpu.CompilerParams(
             collective_id=number, has_side_effects=True, vmem_limit_bytes=56 * MEBI
         ),
         cost_estimate=pl.CostEstimate(flops=int(3e10), bytes_accessed=30 * MEBI, transcendentals=0),
-    )(tokens, cotangent, small)
+    )(tokens, cotangent, small, raw)
 
 
 def attend_call(number, gathered, x, pair, vec, bias, rows, width, swaps):
@@ -669,24 +779,27 @@
     in_specs, ins = [VM, VM, ANY, ANY, VM], [active, hidden, *pair, vec]
     if last:
         in_specs, ins = in_specs + [VM], ins + [grad]
-        columns = LENGTH // rows
-        outs += [shape((LENGTH, size // columns)), *[shape((size, wide // 2))] * 2]
-        scratch += [pltpu.VMEM((columns, rows, size // columns), LOW), pltpu.SemaphoreType.DMA((2, 3))]
+        outs += [shape((size, wide // 2))] * 2
     return launch(
         functools.partial(contract_kernel, last),
-        number, rows, in_specs, ins, outs, (VM,) * len(outs), scratch, swaps, last,
-    )
-
-
-def bend_call(number, last, grad, pair, active, slope, size, rows, swaps):
-    wide = active.shape[1]
+        number, rows, in_specs, ins, outs, (VM,) * len(outs), scratch, swaps,
+    )
+
+
+def bend_call(number, last, grad, pair, slope, extra, size, rows, swaps):
+    wide = slope.shape[1]
+    columns = LENGTH // rows
     outs = [shape((LENGTH, wide)), shape((8, wide), WIDE)]
-    if not last:
+    scratch = [pltpu.VMEM((size, wide), LOW), PAIRS, LOCAL]
+    if last:
+        outs += [shape((LENGTH, size // columns))]
+        scratch += [pltpu.VMEM((columns, rows, size // columns), LOW), pltpu.SemaphoreType.DMA((2, 3))]
+    else:
         outs += [shape((LENGTH, size)), *[shape((size, wide // 2))] * 2]
-    scratch = [pltpu.VMEM((size, wide), LOW), PAIRS, LOCAL]
     return launch(
         functools.partial(bend_kernel, last),
-        number, rows, [VM, ANY, ANY, VM, VM], (grad, *pair, active, slope), outs, (VM,) * len(outs), scratch, swaps,
+        number, rows, [VM, ANY, ANY, VM, VM], (grad, *pair, slope, extra),
+        outs, (VM,) * len(outs), scratch, swaps, last,
     )
 
 
@@ -707,12 +820,11 @@
     )
 
 
-def attend_back_call(number, last, low, grad, x_own, pair, normed, heads_all, o, lse, vec, swaps):
-    rows, size = grad.shape
+def scores_back_call(number, low, pair, heads_all, o, lse, swaps):
+    rows, size = low.shape
     width = o.shape[1]
     heads = width // HEAD
-    half = 2 * width
-    outs = [shape((size, half)), shape((size, half)), shape((rows, size)), shape((8, size), WIDE)]
+    outs = (shape((LENGTH, 3 * width)), shape((size, width)))
     scratch = [
         pltpu.VMEM((size, 4 * width), LOW),
         pltpu.VMEM((LENGTH, size), LOW),
@@ -721,19 +833,67 @@
         pltpu.VMEM((3 * heads, LENGTH, HEAD), LOW),
         pltpu.VMEM((LENGTH, HEAD), WIDE),
         pltpu.VMEM((LENGTH, HEAD), WIDE),
-        pltpu.VMEM((LENGTH, 3 * width), LOW),
+        PAIRS, LOCAL,
+    ]
+    return launch(
+        functools.partial(scores_back_kernel, heads),
+        number, rows, [VM, ANY, ANY, VM, VM, VM], (low, *pair, heads_all, o, lse),
+        outs, (VM,) * 2, scratch, swaps,
+    )
+
+
+def attend_back_call(number, last, mixed, outer, grad, x_own, pair, normed, vec, swaps):
+    rows, size = grad.shape
+    width = outer.shape[1]
+    half = 2 * width
+    outs = [shape((size, half)), shape((size, half)), shape((rows, size)), shape((8, size), WIDE)]
+    out_specs = [ANY, ANY, VM, VM]
+    scratch = [
+        pltpu.VMEM((size, 4 * width), LOW),
         pltpu.VMEM((2, size, half), LOW),
-        *scatter_scratch(rows, size), PAIRS, LOCAL,
+        *scatter_scratch(rows, size), LOCAL,
     ]
-    out_specs = [ANY, ANY, VM, VM]
     if not last:
-        outs, out_specs = outs + [shape((LENGTH, width))], out_specs + [VM]
-        scratch += [pltpu.VMEM((LENGTH // rows, rows, width), LOW), pltpu.SemaphoreType.DMA((2, 3))]
+        outs[1] = shape((16, 128))
+        outs, out_specs = outs + [shape((size, half))], out_specs + [ANY]
+        scratch += [pltpu.SemaphoreType.DMA((2, 1))]
     return launch(
-        functools.partial(attend_back_kernel, last, heads),
-        number, rows, [VM, VM, VM, ANY, ANY, VM, VM, VM, VM, VM],
-        (low, grad, x_own, *pair, normed, heads_all, o, lse, vec), outs, out_specs, scratch, swaps, not last,
-    )
+        functools.partial(attend_back_kernel, last),
+        number, rows, [VM, VM, VM, VM, ANY, ANY, VM, VM],
+        (mixed, outer, grad, x_own, *pair, normed, vec), outs, out_specs, scratch, swaps, False, True,
+    )
+
+
+def finish_call(number, near, far, sums, row_count):
+    rows, size = near.shape
+    length, width = far.shape
+    columns = length // rows
+    outs = (shape((2 * length, width), WIDE), shape((16, width), WIDE))
+    scratch = [
+        pltpu.VMEM((length, width), LOW),
+        pltpu.VMEM((columns, rows, width), LOW),
+        pltpu.VMEM((columns, 2, 16, width), WIDE),
+        pltpu.VMEM((3, 2, 8, width), WIDE),
+        pltpu.VMEM((16, width), WIDE),
+        pltpu.VMEM((row_count, 16, width), WIDE),
+        pltpu.VMEM((length, width), LOW),
+        pltpu.VMEM((length, width), LOW),
+        pltpu.SemaphoreType.DMA((2, 3)),
+        pltpu.SemaphoreType.DMA((2, 3)),
+        pltpu.SemaphoreType.DMA((2, 2)),
+        pltpu.SemaphoreType.DMA((2, row_count)),
+    ]
+    return pl.pallas_call(
+        finish_kernel,
+        out_shape=outs,
+        in_specs=[VM] * 8,
+        out_specs=(VM, VM),
+        scratch_shapes=scratch,
+        compiler_params=pltpu.CompilerParams(
+            collective_id=number, has_side_effects=True, vmem_limit_bytes=32 * MEBI
+        ),
+        cost_estimate=pl.CostEstimate(flops=int(3e10), bytes_accessed=30 * MEBI, transcendentals=0),
+    )(near, far, *sums)
 
 
 def swap_sections(value):
@@ -775,14 +935,12 @@
         expand_weight[0],
         contract_weight[0].T,
     )
-    mats = [[], []]
+    kept_blocks, sent_blocks = [], []
     for unit in units:
         half = unit.shape[1] // 2
         low, high = unit[:, :half], unit[:, half:]
-        own = pick(low, high)
-        got = swap_sections(pick(high, low))
-        for layer, block in enumerate((pick(own, got), pick(got, own))):
-            mats[layer].append(lax.all_gather(block, "row", axis=0, tiled=True))
+        kept_blocks.append(pick(low, high))
+        sent_blocks.append(pick(high, low))
 
     small = jnp.concatenate(
         [
@@ -799,7 +957,14 @@
     )
     filled = small.shape[0]
     small = jnp.pad(small, ((0, -filled % 16), (0, 0)))
-    x0_full, gy_full, vectors = start_call(1, tokens, cotangent, small, columns)
+    got_attend = swap_sections(sent_blocks[0])
+    raw = jnp.stack(sent_blocks[1:])
+    got_attend, raw = lax.optimization_barrier((got_attend, raw))
+    x0_full, gy_full, vectors, got_blocks = start_call(1, tokens, cotangent, small, raw, columns)
+    mats = [[], []]
+    for own, got in zip(kept_blocks, (got_attend, got_blocks[0], got_blocks[1])):
+        for layer, block in enumerate((pick(own, got), pick(got, own))):
+            mats[layer].append(lax.all_gather(block, "row", axis=0, tiled=True))
     vectors = vectors.astype(WIDE)
     wide_vectors = jnp.swapaxes(vectors[:, :, :6], 1, 2).reshape(2, 6, size)
     wide_vectors = jnp.pad(wide_vectors, ((0, 0), (0, 2), (0, 0)))
@@ -839,46 +1004,68 @@
         x = outs[0]
         owns.append(x)
         if last:
-            y1, ck1, cs1 = outs[1:]
+            ck1, cs1 = outs[1:]
         else:
             attn = (mats[1][0], others[0])
     y0 = own_features(full)
-    layer_low, layer_high = pick(y0, y1), pick(y1, y0)
+
+    def add(keep, got, then):
+        total = (keep.astype(WIDE) + got.astype(WIDE)).astype(LOW)
+        return lax.optimization_barrier((total, then))
+
+    def scatter(total):
+        return lax.psum_scatter(total, "row", scatter_dimension=0, tiled=True)
+
+    def tie(value, then):
+        return lax.optimization_barrier((value, then))
 
     attn, expand, contract = pairs[1]
     normed, heads, o, lse, hidden, second, active, slope = kept[1]
-    (before, bend_sums1), _ = bend_call(8, True, gy_full, contract, active, slope, size, rows, [])
+    (before, bend_sums1, y1), _ = bend_call(8, True, gy_full, contract, slope, owns[2], size, rows, [])
+    layer_low, layer_high = pick(y0, y1), pick(y1, y0)
     (ek1, es1, grad_hidden, low, narrow_sums1), (ct1,) = narrow_call(
         9, before, own_rows(gy_full), expand, second, hidden, wide_vectors[1], [cs1]
     )
-    (wk1, ws1, gx1_own, attend_sums1), (et1, layer_got) = attend_back_call(
-        10, True, low, grad_hidden, owns[1], attn, normed, heads, o, lse, wide_vectors[1], [es1, layer_high]
+    total_c1, low = add(ck1, ct1, low)
+    (mixed, outer), (et1,) = scores_back_call(10, low, attn, heads, o, lse, [es1])
+    total_e1, mixed = add(ek1, et1, mixed)
+    part_c1, mixed = tie(scatter(total_c1), mixed)
+    (wk1, ws1, gx1_own, attend_sums1), (layer_got,) = attend_back_call(
+        11, True, mixed, outer, grad_hidden, owns[1], attn, normed, wide_vectors[1], [layer_high]
     )
     layer_outputs = jnp.concatenate([pick(layer_low, layer_got), pick(layer_got, layer_low)], 0)
 
     attn, expand, contract = pairs[0]
     normed, heads, o, lse, hidden, second, active, slope = kept[0]
     (before, bend_sums0, gx1_full, ck0, cs0), (wt1,) = bend_call(
-        11, False, gx1_own, contract, active, slope, size, rows, [ws1]
-    )
+        12, False, gx1_own, contract, slope, active, size, rows, [ws1]
+    )
+    total_w1, before = add(wk1, wt1, before)
+    part_e1, before = tie(scatter(total_e1), before)
     (ek0, es0, grad_hidden, low, narrow_sums0), (ct0,) = narrow_call(
-        12, before, gx1_own, expand, second, hidden, wide_vectors[0], [cs0]
-    )
-    (wk0, ws0, _, attend_sums0, gx0), (et0,) = attend_back_call(
-        13, False, low, grad_hidden, owns[0], attn, normed, heads, o, lse, wide_vectors[0], [es0]
-    )
-    wt0 = swap_sections(ws0)
-
-    gx1 = own_features(gx1_full)
-    gx_low, gx_got = pick(gx0, gx1), swap_sections(pick(gx1, gx0))
-    input_grads = jnp.concatenate([pick(gx_low, gx_got), pick(gx_got, gx_low)], 0).astype(WIDE)
-
-    def reduce_grad(keep, got):
-        total = (keep.astype(WIDE) + got.astype(WIDE)).astype(LOW)
-        return lax.psum_scatter(total, "row", scatter_dimension=0, tiled=True)
-
-    late = [reduce_grad(*pair) for pair in ((wk1, wt1), (ek1, et1), (ck1, ct1))]
-    early = [reduce_grad(*pair) for pair in ((wk0, wt0), (ek0, et0), (ck0, ct0))]
+        13, before, gx1_own, expand, second, hidden, wide_vectors[0], [cs0]
+    )
+    total_c0, low = add(ck0, ct0, low)
+    part_w1, low = tie(scatter(total_w1), low)
+    (mixed, outer), (et0,) = scores_back_call(14, low, attn, heads, o, lse, [es0])
+    total_e0, mixed = add(ek0, et0, mixed)
+    part_c0, mixed = tie(scatter(total_c0), mixed)
+    (wk0, _, gx0_own, attend_sums0, wt0), _ = attend_back_call(
+        15, False, mixed, outer, grad_hidden, owns[0], attn, normed, wide_vectors[0], []
+    )
+    total_w0, gx0_own = add(wk0, wt0, gx0_own)
+    part_e0, gx0_own = tie(scatter(total_e0), gx0_own)
+    input_grads, small_grads = finish_call(
+        16,
+        gx0_own,
+        own_features(gx1_full),
+        (attend_sums0, narrow_sums0, bend_sums0, attend_sums1, narrow_sums1, bend_sums1),
+        lax.axis_size("row"),
+    )
+
+    late = [part_w1, part_e1, part_c1]
+    part_w0, small_grads = tie(scatter(total_w0), small_grads)
+    early = [part_w0, part_e0, part_c0]
     units = []
     for second_layer, first_layer in zip(late, early):
         stays = pick(first_layer, second_layer)
@@ -886,38 +1073,21 @@
         units.append(jnp.concatenate([pick(stays, got), pick(got, stays)], 1).astype(WIDE))
     attn_part, expand_part, contract_part = units
 
-    wide_sum, own_sum = [], []
-    for attend_sums, narrow_sums, bend_sums in (
-        (attend_sums0, narrow_sums0, bend_sums0),
-        (attend_sums1, narrow_sums1, bend_sums1),
-    ):
-        wide_sum.append(
-            jnp.concatenate([attend_sums[:2], narrow_sums[3:4], narrow_sums[:3]], 0)
-        )
-        own_sum.append(
-            jnp.concatenate(
-                [attend_sums[2, :width], attend_sums[2, 2 * width : 3 * width], bend_sums[0]]
-            )
-        )
-    wide_sum = lax.psum(jnp.stack(wide_sum), ("section", "row", "col"))
-    own_sum = lax.psum(jnp.stack(own_sum), ("section", "row"))
-    wide_mine = lax.dynamic_slice_in_dim(pick(wide_sum[0], wide_sum[1]), column * width, width, 1)
-    own_mine = pick(own_sum[0], own_sum[1])
     return (
         layer_outputs[None],
         input_grads[None],
-        wide_mine[0][None],
-        wide_mine[1][None],
+        small_grads[0:1],
+        small_grads[1:2],
         attn_part[:, : 3 * width].reshape(block_rows, 3, width)[None],
-        own_mine[: 2 * width].reshape(1, 2, width),
+        small_grads[8:10][None],
         attn_part[:, 3 * width :].T[None],
-        wide_mine[2][None],
-        wide_mine[3][None],
-        wide_mine[4][None],
+        small_grads[2:3],
+        small_grads[3:4],
+        small_grads[4:5],
         expand_part[None],
-        own_mine[2 * width :][None],
+        small_grads[10 : 10 + expand_bias.shape[1] // width].reshape(1, -1),
         contract_part.T[None],
-        wide_mine[5][None],
+        small_grads[5:6],
     )
 
 

time: 853 us -> 813 us (0.953)
  local copies, waits for them, and re-layouts: 33.1 us -> 137 us
  blocking collectives: 82.6 us -> 0 us
  waiting for transfers between devices: 75 us -> 48.5 us
  Pallas kernels: 584 us -> 564 us
  other arithmetic: 41.6 us -> 28.9 us
    unnamed x68 -> x236, local copies, waits for them, and re-layouts: 16.5 us -> 127 us
    psum x2 -> x0, blocking collectives: 82.6 us -> none  [the longest x1 43.7 us: on_device(): wide_sum = lax.psum(jnp.stack(wide_sum), ('section', 'row', 'col'))]
    ppermute x9 -> x5, waiting for transfers between devices: 73.6 us -> 14.9 us  [swap_sections(): return lax.ppermute(value, 'section', [(0, 1), (1, 0)])]
    pallas_call x12 -> x14, Pallas kernels: 541 us -> 485 us  [launch(): pl.pallas_call(kernel, out_shape=(*outs, *[shape(s.shape, s.dtype) for s...]
    pallas_call x1 -> x2, Pallas kernels: 43.1 us -> 78.8 us  [the longest x1 43.6 us: start_call(): pl.pallas_call(start_kernel, out_shape=outs, in_specs=[ANY] * 4, out_spec...]
    all_gather x6, waiting for transfers between devices: 0.71 us -> 31.6 us  [on_device(): mats[layer].append(lax.all_gather(block, 'row', axis=0, tiled=True))]
    convert_element_type x7 -> x6, other arithmetic: 19.5 us -> 9.6 us  [add(): total = (keep.astype(WIDE) + got.astype(WIDE)).astype(LOW)]
  transfers between devices with their start and end apart: 21 -> 17, of which waited for: 8 -> 4; matrix products, arithmetic and copies ran while one was open for 7% -> 6% of each run, Pallas kernels for 53% -> 57%
where the time goes in v4:
time: 813 us; the launch traced here: 802 us
  Pallas kernels  564 us (69%)
  local copies, waits for them, and re-layouts  137 us (17%)
  waiting for transfers between devices  48.5 us (6%)
  other arithmetic  28.9 us (4%)
  between operations  15.1 us (2%)
    pallas_call x14, Pallas kernels, launch(): pl.pallas_call(kernel, out_shape=(*outs, *[shape(s.shape, s.dtype) for s...  485 us
    unnamed x236, local copies, waits for them, and re-layouts  127 us
    pallas_call x1, Pallas kernels, start_call(): pl.pallas_call(start_kernel, out_shape=outs, in_specs=[ANY] * 4, out_spec...  43.6 us
    pallas_call x1, Pallas kernels, finish_call(): pl.pallas_call(finish_kernel, out_shape=outs, in_specs=[VM] * 8, out_spec...  35.2 us
    all_gather x6, waiting for transfers between devices, on_device(): mats[layer].append(lax.all_gather(block, 'row', axis=0, tiled=True))  31.6 us
  transfers between devices with their start and end apart: 17, of which 4 were waited for; matrix products, arithmetic and copies ran while one was open for 6% of the time, Pallas kernels for 57%

profile of v4, /device:TPU:0, one launch (start us, length us, event | category | flops | bytes accessed | tf_op | source)
XLA Modules:
  0.0 802.2 jit_solution(5138684229151908644)
XLA Ops:
  10.4 3.0 collective-permute-start
  15.1 2.7 copy.42.cotangent_ref
  20.3 2.6 collective-permute-done
  23.9 43.6 %shard_map.245 = (bf16[1024,1280]{1,0:T(8,128)(2,1)}, bf16[1024,1280]{1,0:T(8,128)(2,1)}, bf16[2,4,16,320]{3,2,1,0:T(8,128)(2,1)}, bf16[2,320,640]{2,1,0:T(8,128)(2,1)}) custom-call(bf16[2048,320]{1,0:T(8,128)(2,1)} %copy.41.tokens_ref, bf16[2048,320]{1,0:T(8,128)(2,1)} %copy.42.cotangent_ref, bf16[16,320]{1,0:T(8,128)(2,1)} %pad.8.small_ref, ...), custom_call_target="tpu_custom_call" | custom-call | flops 30000001024 | bytes 31457280 | tf_op jit(solution)/shard_map/pallas_call | solution.py:724
  67.5 2.4 bitcast_select_fusion.2
  73.2 2.1 constant_dynamic-slice_fusion.1.refs_3_
  76.5 31.5 %all-gather.9.cloned.1.call-done.refs_5_.refs_1_.refs_2_ = bf16[1280,640]{1,0:T(8,128)(2,1)} async-done(((bf16[320,640]{1,0:T(8,128)(2,1)}), bf16[1280,640]{1,0:T(8,128)(2,1)}) %all-gather.9.cloned.1.call-update) | async-done | bytes 1638416 | tf_op jit(solution)/shard_map/all_gather | solution.py:967
  108.1 2.8 collective-permute-done.1.refs_2_.refs_5_
  110.9 1.7 copy-done.5
  114.1 38.5 %shard_map.246 = (bf16[16,128]{1,0:T(8,128)(2,1)}, bf16[1024,1280]{1,0:T(8,128)(2,1)S(1)}, bf16[15,1024,64]{2,1,0:T(8,128)(2,1)S(1)}, bf16[1024,320]{1,0:T(8,128...) custom-call(bf16[1024,1280]{1,0:T(8,128)(2,1)S(1)} %copy-done.5, ...), custom_call_target="tpu_custom_call" | custom-call | flops 30000001024 | bytes 31457280 | tf_op jit(solution)/shard_map/pallas_call | solution.py:701
  152.6 2.0 copy-done.26
  163.5 37.5 %shard_map.247 = (bf16[1024,1280]{1,0:T(8,128)(2,1)S(1)}, bf16[1024,1280]{1,0:T(8,128)(2,1)S(1)}, bf16[1024,1280]{1,0:T(8,128)(2,1)S(1)}, bf16[1280,640]{1,0:T(8,128)(2,1)S(1)}) custom-call(bf16[256,1280]{1,0:T(8,128)(2,1)S(1)} %get-tuple-element.115.refs_0_, bf16[1280,640]{1,0:T(8,128)(2,1)S(1)} %copy-done.12, bf16[1280,640]{1,0:T(8,128)(2,1)S(1)} %copy-done.48, ...), custom_call_target="tpu_custom_call" | custom-call | flops 30000001024 | bytes 31457280 | tf_op jit(solution)/shard_map/pallas_call | solution.py:701
  208.0 1.8 copy-done.39
  212.6 37.8 %shard_map.248 = (bf16[256,1280]{1,0:T(8,128)(2,1)S(1)}, bf16[1280,640]{1,0:T(8,128)(2,1)S(1)}) custom-call(bf16[1024,1280]{1,0:T(8,128)(2,1)S(1)} %copy-done.39, f32[256,1280]{1,0:T(8,128)S(1)} %copy-done.69, bf16[1280,640]{1,0:T(8,128)(2,1)S(1)} %copy-done.15, bf16[1280,640]{1,0:T(8,128)(2,1)S(1)} %copy-done.66, ...), custom_call_target="tpu_custom_call" | custom-call | flops 30000001024 | bytes 31457280 | tf_op jit(solution)/shard_map/pallas_call | solution.py:701
  251.5 1.7 copy-done.18
  256.1 48.9 %shard_map.249 = (bf16[1024,1280]{1,0:T(8,128)(2,1)S(1)}, bf16[1024,1280]{1,0:T(8,128)(2,1)S(1)}, bf16[15,1024,64]{2,1,0:T(8,128)(2,1)S(1)}, bf16[1024,320]{1,0:...) custom-call(bf16[256,1280]{1,0:T(8,128)(2,1)S(1)} %get-tuple-element, ...), custom_call_target="tpu_custom_call" | custom-call | flops 30000001024 | bytes 31457280 | tf_op jit(solution)/shard_map/pallas_call | solution.py:701
  306.4 1.9 copy-done.28
  317.9 37.5 %shard_map.250 = (bf16[1024,1280]{1,0:T(8,128)(2,1)S(1)}, bf16[1024,1280]{1,0:T(8,128)(2,1)S(1)}, bf16[1024,1280]{1,0:T(8,128)(2,1)S(1)}, bf16[1280,640]{1,0:T(8,128)(2,1)S(1)}) custom-call(bf16[256,1280]{1,0:T(8,128)(2,1)S(1)} %copy-done.97, bf16[1280,640]{1,0:T(8,128)(2,1)S(1)} %copy-done.22, bf16[1280,640]{1,0:T(8,128)(2,1)S(1)} %copy-done.51, ...), custom_call_target="tpu_custom_call" | custom-call | flops 30000001024 | bytes 31457280 | tf_op jit(solution)/shard_map/pallas_call | solution.py:701
  355.4 20.4 %shard_map.251 = (bf16[256,1280]{1,0:T(8,128)(2,1)S(1)}, bf16[1280,640]{1,0:T(8,128)(2,1)S(1)}, bf16[1280,640]{1,0:T(8,128)(2,1)S(1)}) custom-call(bf16[1024,1280]{1,0:T(8,128)(2,1)S(1)} %get-tuple-element.128.refs_0_, f32[256,1280]{1,0:T(8,128)S(1)} %copy-done.76, bf16[1280,640]{1,0:T(8,128)(2,1)S(1)} %copy-done.25, ...), custom_call_target="tpu_custom_call" | custom-call | flops 30000001024 | bytes 31457280 | tf_op jit(solution)/shard_map/pallas_call | solution.py:701
  375.8 11.7 %shard_map.252 = (bf16[1024,1280]{1,0:T(8,128)(2,1)S(1)}, f32[8,1280]{1,0:T(8,128)S(1)}, bf16[1024,320]{1,0:T(8,128)(2,1)S(1)}) custom-call(bf16[1024,1280]{1,0:T(8,128)(2,1)S(1)} %copy-done.4, bf16[1280,640]{1,0:T(8,128)(2,1)S(1)} %copy-done.25, bf16[1280,640]{1,0:T(8,128)(2,1)S(1)} %get-tuple-element.126.refs_3_.refs_2_, ...), custom_call_target="tpu_custom_call" | custom-call | flops 30000001024 | bytes 31457280 | tf_op jit(solution)/shard_map/pallas_call | solution.py:701
  388.2 38.2 %shard_map.253 = (bf16[1280,640]{1,0:T(8,128)(2,1)S(1)}, bf16[1280,640]{1,0:T(8,128)(2,1)S(1)}, f32[256,1280]{1,0:T(8,128)S(1)}, bf16[256,1280]{1,0:T(8,128)(2,1...) custom-call(bf16[1024,1280]{1,0:T(8,128)(2,1)S(1)} %get-tuple-element.133.refs_0_, ...), custom_call_target="tpu_custom_call" | custom-call | flops 30000001024 | bytes 31457280 | tf_op jit(solution)/shard_map/pallas_call | solution.py:701
  433.6 2.1 copy-done.29
  439.7 38.0 %shard_map.254 = (bf16[1024,960]{1,0:T(8,128)(2,1)S(1)}, bf16[1280,320]{1,0:T(8,128)(2,1)S(1)}, bf16[1280,640]{1,0:T(8,128)(2,1)S(1)}) custom-call(bf16[256,1280]{1,0:T(8,128)(2,1)S(1)} %copy-done.91, bf16[1280,640]{1,0:T(8,128)(2,1)S(1)} %copy-done.19, bf16[1280,640]{1,0:T(8,128)(2,1)S(1)} %copy-done.61, bf16[15,1024,64]{2,1,0:T(8,128)(2,1)S(1)} %copy-done.29, ...), custom_call_target="tpu_custom_call" | custom-call | flops 30000001024 | bytes 31457280 | tf_op jit(solution)/shard_map/pallas_call | solution.py:701
  480.0 1.6 add_convert_fusion.4
  481.7 1.7 broadcast_select_fusion.2.refs_8_
  484.8 1.7 copy-done.35
  486.6 1.7 copy-done.44
  493.3 21.0 %shard_map.255 = (bf16[1280,640]{1,0:T(8,128)(2,1)S(1)}, bf16[1280,640]{1,0:T(8,128)(2,1)S(1)}, bf16[256,1280]{1,0:T(8,128)(2,1)S(1)}, f32[8,1280]{1,0:T(8,128)S(1)}, bf16[1024,320]{1,0:T(8,128)(2,1)S(1)}) custom-call(bf16[1024,960]{1,0:T(8,128)(2,1)S(1)} %copy-done.44, bf16[1280,320]{1,0:T(8,128)(2,1)S(1)} %copy-done.78, f32[256,1280]{1,0:T(8,128)S(1)} %copy-done.74, ...), custom_call_target="tpu_custom_call" | custom-call | flops 30000001024 | bytes 31457280 | tf_op jit(solution)/shard_map/pallas_call | solution.py:701
  514.3 2.7 broadcast_select_fusion.1
  520.2 1.7 copy-done.40
  521.9 1.7 copy-done.42
  527.6 38.0 %shard_map.256 = (bf16[1024,1280]{1,0:T(8,128)(2,1)S(1)}, f32[8,1280]{1,0:T(8,128)S(1)}, bf16[1024,1280]{1,0:T(8,128)(2,1)S(1)}, bf16[1280,640]{1,0:T(8,128)(2,1...) custom-call(bf16[256,1280]{1,0:T(8,128)(2,1)S(1)} %copy-done.86, bf16[1280,640]{1,0:T(8,128)(2,1)S(1)} %copy-done.16, ...), custom_call_target="tpu_custom_call" | custom-call | flops 30000001024 | bytes 31457280 | tf_op jit(solution)/shard_map/pallas_call | solution.py:701
  573.6 1.7 copy-done.31
  575.3 1.7 copy-done.33
  577.1 1.6 copy-done.49
  582.5 37.2 %shard_map.257 = (bf16[1280,640]{1,0:T(8,128)(2,1)S(1)}, bf16[1280,640]{1,0:T(8,128)(2,1)S(1)}, f32[256,1280]{1,0:T(8,128)S(1)}, bf16[256,1280]{1,0:T(8,128)(2,1...) custom-call(bf16[1024,1280]{1,0:T(8,128)(2,1)S(1)} %copy-done.33, bf16[256,1280]{1,0:T(8,128)(2,1)S(1)} %copy-done.87, ...), custom_call_target="tpu_custom_call" | custom-call | flops 30000001024 | bytes 31457280 | tf_op jit(solution)/shard_map/pallas_call | solution.py:701
  624.4 2.6 constant_dynamic-slice_fusion.far_ref
  627.3 2.1 copy-done.27
  633.0 38.1 %shard_map.258 = (bf16[1024,960]{1,0:T(8,128)(2,1)S(1)}, bf16[1280,320]{1,0:T(8,128)(2,1)S(1)}, bf16[1280,640]{1,0:T(8,128)(2,1)S(1)}) custom-call(bf16[256,1280]{1,0:T(8,128)(2,1)S(1)} %copy-done.89, bf16[1280,640]{1,0:T(8,128)(2,1)S(1)} %copy-done.9, bf16[1280,640]{1,0:T(8,128)(2,1)} %collective-permute-done.1.refs_2_.refs_5_, ...), custom_call_target="tpu_custom_call" | custom-call | flops 30000001024 | bytes 31457280 | tf_op jit(solution)/shard_map/pallas_call | solution.py:701
  675.3 2.0 broadcast_select_fusion.6
  678.0 1.7 copy-done.37
  683.9 42.7 %shard_map.259 = (bf16[1280,640]{1,0:T(8,128)(2,1)S(1)}, bf16[16,128]{1,0:T(8,128)(2,1)}, bf16[256,1280]{1,0:T(8,128)(2,1)S(1)}, f32[8,1280]{1,0:T(8,128)S(1)}, bf16[1280,640]{1,0:T(8,128)(2,1)S(1)}) custom-call(bf16[1024,960]{1,0:T(8,128)(2,1)S(1)} %copy-done.46, bf16[1280,320]{1,0:T(8,128)(2,1)S(1)} %copy-done.80, f32[256,1280]{1,0:T(8,128)S(1)} %copy-done.72, ...), custom_call_target="tpu_custom_call" | custom-call | flops 30000001024 | bytes 31457280 | tf_op jit(solution)/shard_map/pallas_call | solution.py:701
  727.4 1.6 add_convert_fusion
  733.4 2.3 collective-permute-start.3
  738.0 35.2 %shard_map.260 = (f32[2048,320]{1,0:T(8,128)S(1)}, f32[16,320]{1,0:T(8,128)S(1)}) custom-call(bf16[256,1280]{1,0:T(8,128)(2,1)S(1)} %copy-done.95, bf16[1024,320]{1,0:T(8,128)(2,1)S(1)} %copy-done.1, f32[8,1280]{1,0:T(8,128)S(1)} %get-tuple-element.190.a0, f32[8,1280]{1,0:T(8,128)S(1)} %get-tuple-element.191.n0, f32[8,1280]{1,0:T(8,128)S(1)} %get-tuple-element.192.b0, ...), custom_call_target="tpu_custom_call" | custom-call | flops 30000001024 | bytes 31457280 | tf_op jit(solution)/shard_map/pallas_call | solution.py:886
  773.2 2.2 copy.47
  778.6 9.5 %collective-permute-done.2 = bf16[320,640]{1,0:T(8,128)(2,1)S(1)} collective-permute-done((bf16[320,640]{1,0:T(8,128)(2,1)S(1)}, bf16[320,640]{1,0:T(8,128)(2,1)S(1)}, u32[]{:S(2)}, u32[]{:S(2)}) %collective-permute-start.2) | collective-permute-done | bytes 409632 | tf_op jit(solution)/shard_map/ppermute | solution.py:900
  791.1 1.6 copy.48
  (303 shorter events, 120.9 us)
Async XLA Ops:
  7.2 64.9 %all-gather.7.cloned.1.call-start = ((), (), s32[]{:S(2)}) async-start(), calls=%async_computation.6 | async-start | bytes 2048000 | tf_op jit(solution)/shard_map/all_gather | solution.py:967
  9.9 3.6 copy-start.109
  10.1 3.4 copy-start.107
  10.4 12.5 %collective-permute-start = (bf16[320,640]{1,0:T(8,128)(2,1)S(1)}, bf16[320,640]{1,0:T(8,128)(2,1)S(1)}, u32[]{:S(2)}, u32[]{:S(2)}) collective-permute-start(bf16[320,640]{1,0:T(8,128)(2,1)S(1)} %get-tuple-element.234), channel_id=1, source_target_pairs={{0,16},{16,0},{1,17},{17,1},{2,18},{18,2},{3,19},{19,3},{4,20},{20... | collective-permute-start | bytes 1228808 | tf_op jit(solution)/shard_map/ppermute | solution.py:900
  15.1 2.7 copy-start.110
  15.1 2.7 copy-start.111
  15.1 2.7 copy-start.112
  15.1 2.7 copy-start.113
  15.1 4.1 copy-start.100
  15.1 4.1 copy-start.101
  23.9 84.2 %all-gather.9.cloned.1.call-start = ((), (), s32[]{:S(2)}) async-start(), calls=%async_computation.7 | async-start | bytes 2048000 | tf_op jit(solution)/shard_map/all_gather | solution.py:967
  69.9 2.1 copy-start.108
  70.0 89.2 %all-gather.11.cloned.1.call-start = ((), (), s32[]{:S(2)}) async-start(), calls=%async_computation.8 | async-start | bytes 2048000 | tf_op jit(solution)/shard_map/all_gather | solution.py:967
  70.7 135.9 %all-gather.13.cloned.1.call-start = ((), (), s32[]{:S(2)}) async-start(), calls=%async_computation.9 | async-start | bytes 2048000 | tf_op jit(solution)/shard_map/all_gather | solution.py:967
  71.3 180.2 %all-gather.15.cloned.1.call-start = ((), (), s32[]{:S(2)}) async-start(), calls=%async_computation.10 | async-start | bytes 2048000 | tf_op jit(solution)/shard_map/all_gather | solution.py:967
  71.9 242.0 %all-gather.17.cloned.1.call-start = ((), (), s32[]{:S(2)}) async-start(), calls=%async_computation.11 | async-start | bytes 2048000 | tf_op jit(solution)/shard_map/all_gather | solution.py:967
  72.0 38.8 %collective-permute-start.1 = (bf16[1280,640]{1,0:T(8,128)(2,1)}, bf16[1280,640]{1,0:T(8,128)(2,1)}, u32[]{:S(2)}, u32[]{:S(2)}) collective-permute-start(bf16[1280,640]{1,0:T(8,128)(2,1)} %all-gather.7.cloned.1.call-done.refs_1_.refs_4_), channel_id=1, source_target_pairs={{0,16},{16,0},{1,17},{17,1},{2,18},{18,2},{3,19},{19,3},{4,20},{20... | collective-permute-start | bytes 4915208 | tf_op jit(solution)/shard_map/ppermute | solution.py:900
  73.1 37.8 %copy-start.8 = (bf16[1280,640]{1,0:T(8,128)(2,1)S(1)}, bf16[1280,640]{1,0:T(8,128)(2,1)}, u32[]{:S(2)}) copy-start(bf16[1280,640]{1,0:T(8,128)(2,1)} %all-gather.7.cloned.1.call-done.refs_1_.refs_4_) | copy-start | bytes 4915204
  73.2 410.2 %reduce-scatter.7.cloned.1.call-start = ((), (), s32[]{:S(2)}) async-start(), calls=%async_computation.12 | async-start | bytes 2048000 | tf_op jit(solution)/shard_map/reduce_scatter | solution.py:1017
  73.2 133.4 %copy-start.6 = (f32[8,1280]{1,0:T(8,128)}, f32[8,1280]{1,0:T(8,128)S(1)}, u32[]{:S(2)}) copy-start(f32[8,1280]{1,0:T(8,128)S(1)} %get-tuple-element.253.refs_3_.refs_4_.refs_6_.refs_7_) | copy-start | bytes 122884
  110.9 1.7 copy-start.5
  152.5 2.0 copy-start.26
  163.5 43.1 %copy-start.15 = (bf16[1280,640]{1,0:T(8,128)(2,1)S(1)}, bf16[1280,640]{1,0:T(8,128)(2,1)}, u32[]{:S(2)}) copy-start(bf16[1280,640]{1,0:T(8,128)(2,1)} %all-gather.11.cloned.1.call-done.refs_4_.refs_2_.refs_1_) | copy-start | bytes 4915204
  208.0 1.8 copy-start.39
  251.5 53.4 %copy-start.92 = (bf16[256,1280]{1,0:T(8,128)(2,1)}, bf16[256,1280]{1,0:T(8,128)(2,1)S(1)}, u32[]{:S(2)}) copy-start(bf16[256,1280]{1,0:T(8,128)(2,1)S(1)} %get-tuple-element.120.refs_0_.refs_3_) | copy-start | bytes 1966084
  256.1 57.8 %copy-start.22 = (bf16[1280,640]{1,0:T(8,128)(2,1)S(1)}, bf16[1280,640]{1,0:T(8,128)(2,1)}, u32[]{:S(2)}) copy-start(bf16[1280,640]{1,0:T(8,128)(2,1)} %all-gather.15.cloned.1.call-done.refs_5_.refs_1_.refs_2_) | copy-start | bytes 4915204
  306.4 1.9 copy-start.28
  317.8 37.5 %copy-start.4 = (bf16[1024,1280]{1,0:T(8,128)(2,1)S(1)}, bf16[1024,1280]{1,0:T(8,128)(2,1)}, u32[]{:S(2)}) copy-start(bf16[1024,1280]{1,0:T(8,128)(2,1)} %get-tuple-element.123.refs_5_.refs_0_) | copy-start | bytes 7864324
  317.8 37.5 %copy-start.25 = (bf16[1280,640]{1,0:T(8,128)(2,1)S(1)}, bf16[1280,640]{1,0:T(8,128)(2,1)}, u32[]{:S(2)}) copy-start(bf16[1280,640]{1,0:T(8,128)(2,1)} %all-gather.17.cloned.1.call-done.refs_4_.refs_2_.refs_1_) | copy-start | bytes 4915204
  317.8 37.5 %copy-start.76 = (f32[256,1280]{1,0:T(8,128)S(1)}, f32[256,1280]{1,0:T(8,128)}, u32[]{:S(2)}) copy-start(f32[256,1280]{1,0:T(8,128)} %copy-done.75) | copy-start | bytes 3932164
  375.8 12.4 %copy-start.23 = (bf16[1280,640]{1,0:T(8,128)(2,1)S(1)}, bf16[1280,640]{1,0:T(8,128)(2,1)}, u32[]{:S(2)}) copy-start(bf16[1280,640]{1,0:T(8,128)(2,1)} %all-gather.15.cloned.1.call-done.refs_5_.refs_1_.refs_2_) | copy-start | bytes 4915204
  375.8 12.3 %copy-start.52 = (bf16[1280,640]{1,0:T(8,128)(2,1)S(1)}, bf16[1280,640]{1,0:T(8,128)(2,1)}, u32[]{:S(2)}) copy-start(bf16[1280,640]{1,0:T(8,128)(2,1)} %copy-done.50) | copy-start | bytes 4915204
  431.1 140.3 %reduce-scatter.9.cloned.1.call-start = ((), (), s32[]{:S(2)}) async-start(), calls=%async_computation.13 | async-start | bytes 2048000 | tf_op jit(solution)/shard_map/reduce_scatter | solution.py:1017
  433.6 2.1 copy-start.29
  481.6 145.6 %reduce-scatter.11.cloned.1.call-start = ((), (), s32[]{:S(2)}) async-start(), calls=%async_computation.14 | async-start | bytes 2048000 | tf_op jit(solution)/shard_map/reduce_scatter | solution.py:1017
  514.3 2.7 copy-start.63
  514.3 2.7 copy-start.85
  571.4 103.6 %reduce-scatter.15.cloned.1.call-start = ((), (), s32[]{:S(2)}) async-start(), calls=%async_computation.16 | async-start | bytes 2048000 | tf_op jit(solution)/shard_map/reduce_scatter | solution.py:1017
  624.4 2.8 copy-start.9
  627.0 105.6 %reduce-scatter.13.cloned.1.call-start = ((), (), s32[]{:S(2)}) async-start(), calls=%async_computation.15 | async-start | bytes 2048000 | tf_op jit(solution)/shard_map/reduce_scatter | solution.py:1017
  627.3 2.1 copy-start.27
  675.0 3.0 copy-start.2
  675.0 3.0 copy-start.10
  675.0 100.4 %reduce-scatter.17.cloned.1.call-start = ((), (), s32[]{:S(2)}) async-start(), calls=%async_computation.17 | async-start | bytes 2048000 | tf_op jit(solution)/shard_map/reduce_scatter | solution.py:1017
  677.3 51.9 %collective-permute-start.4 = (bf16[320,640]{1,0:T(8,128)(2,1)}, bf16[320,640]{1,0:T(8,128)(2,1)}, u32[]{:S(2)}, u32[]{:S(2)}) collective-permute-start(bf16[320,640]{1,0:T(8,128)(2,1)} %broadcast_select_fusion.6), channel_id=1, source_target_pairs={{0,16},{16,0},{1,17},{17,1},{2,18},{18,2},{3,19},{19,3},{4,20},{20... | collective-permute-start | bytes 1228808 | tf_op jit(solution)/shard_map/ppermute | solution.py:900
  731.3 4.4 copy-start.99
  733.4 59.3 %collective-permute-start.3 = (bf16[320,640]{1,0:T(8,128)(2,1)}, bf16[320,640]{1,0:T(8,128)(2,1)}, u32[]{:S(2)}, u32[]{:S(2)}) collective-permute-start(bf16[320,640]{1,0:T(8,128)(2,1)} %broadcast_select_fusion.8), channel_id=1, source_target_pairs={{0,16},{16,0},{1,17},{17,1},{2,18},{18,2},{3,19},{19,3},{4,20},{20... | collective-permute-start | bytes 1228808 | tf_op jit(solution)/shard_map/ppermute | solution.py:900
  777.2 10.9 %collective-permute-start.2 = (bf16[320,640]{1,0:T(8,128)(2,1)S(1)}, bf16[320,640]{1,0:T(8,128)(2,1)S(1)}, u32[]{:S(2)}, u32[]{:S(2)}) collective-permute-start(bf16[320,640]{1,0:T(8,128)(2,1)S(1)} %broadcast_select_fusion.12), channel_id=1, source_target_pairs={{0,16},{16,0},{1,17},{17,1},{2,18},{18,2},{3,19},{19,3},{4,20},{20... | collective-permute-start | bytes 1228808 | tf_op jit(solution)/shard_map/ppermute | solution.py:900
  (83 other events, 108.2 us)
Sparse Core Ops, SparseCore 0:
  24.0 39.6 all-gather.6
  70.1 37.9 all-gather.8
  110.2 37.0 all-gather.10
  148.7 37.0 all-gather.12
  187.7 37.0 all-gather.14
  226.2 37.0 all-gather.16
  431.2 36.5 reduce-scatter.6
  481.7 36.5 reduce-scatter.8
  571.5 36.5 reduce-scatter.10
  627.1 36.5 reduce-scatter.14
  675.2 36.6 reduce-scatter.12
  729.2 38.1 reduce-scatter.16

commit v5 on v4

--- a/solution.py
+++ b/solution.py
@@ -1,5 +1,4 @@
 import functools
-import math
 
 import jax
 import jax.numpy as jnp
@@ -17,7 +16,7 @@
 PARTS = 2
 TILE = 256
 MEBI = 1024 * 1024
-SPARE = 14 * MEBI
+GRANT = 58 * MEBI
 
 
 def nn(left, right):
@@ -55,6 +54,16 @@
         self.diag = (1 - chip) * 2 + 1 - core
         self.rows = rows
         self.part = rows // PARTS
+        self.loads, self.stores, self.begun = {}, {}, set()
+
+    def need(self, *places):
+        for place in places:
+            self.loads[place].wait()
+
+    def emit(self, *places):
+        for place in places:
+            self.stores[place].start()
+            self.begun.add(place)
 
     def greet(self, swaps, diagonal, rows=()):
         barrier = pltpu.get_barrier_semaphore()
@@ -128,9 +137,11 @@
         for copy in self.over + self.near + self.relayed:
             copy.wait_send()
 
-    def each(self, body):
+    def each(self, body, first=None):
         g = self.group
         self.start()
+        if first is not None:
+            first()
         body(g.chunk(g.me))
         self.sibling()
         body(g.chunk(g.sib))
@@ -358,10 +369,12 @@
             project(group.chunk(n))
     else:
         Gather(group, full_ref, gather_sems).each(project)
+    group.emit(0, 1, 2)
 
     attention_out(heads_ref, o3, lse_ref, heads)
     for h in range(heads):
         o_ref[:, h * HEAD : (h + 1) * HEAD] = o3[h]
+    group.emit(3, 4)
 
     scatter = Scatter(group, stage, land, total, scatter_sems)
     scatter.start(lambda rows: nt(o_ref[rows, :], weight[:, 3 * width :]))
@@ -424,7 +437,10 @@
     scatter = Scatter(group, stage, land, total, scatter_sems)
     scatter.start(lambda rows: nt(active_ref[rows, :], contract[...]))
     if last:
+        group.need(5)
         outer_halves(g_ref, active_ref, ck_ref, cs_ref)
+        group.emit(1, 2)
+    group.need(1)
     for j in range(PARTS):
         rows = slice(j * group.part, (j + 1) * group.part)
         result = hidden_ref[rows, :] + scatter.take(j) + vec_ref[5:6, :]
@@ -451,6 +467,9 @@
         full_ref[group.chunk(group.me), :] = g_ref[...]
     halves.wait()
 
+    if last:
+        group.need(3)
+
     def bend(rows):
         rows_grad = (g_ref if last else full_ref)[rows, :]
         grad = (nn(rows_grad, contract[...]) * slope_ref[rows, :].astype(WIDE)).astype(LOW)
@@ -465,7 +484,9 @@
 
         deliver.done()
     else:
-        Gather(group, full_ref, gather_sems).each(bend)
+        Gather(group, full_ref, gather_sems).each(bend, lambda: group.need(3))
+        group.emit(0, 2)
+        group.need(4)
         outer_halves(full_ref, extra_ref, ck_ref, cs_ref)
 
 
@@ -480,7 +501,10 @@
     halves.wait()
     scatter = Scatter(group, stage, land, total, scatter_sems)
     scatter.start(lambda rows: nt(before[rows, :], expand[...]))
+    group.need(4)
     outer_halves(second_ref, before, ek_ref, es_ref)
+    group.emit(0, 1)
+    group.need(1, 5)
     for j in range(PARTS):
         rows = slice(j * group.part, (j + 1) * group.part)
         grad = scatter.take(j)
@@ -522,10 +546,12 @@
             preferred_element_type=WIDE,
         )
 
-    Gather(group, full, gather_sems).each(spread)
+    Gather(group, full, gather_sems).each(spread, lambda: group.need(4))
+    group.need(3, 5)
     attention_back(heads_ref, go3, lse_ref, dots, g3, key_acc, value_acc, heads)
     for j in range(3 * heads):
         mixed[:, j * HEAD : (j + 1) * HEAD] = g3[j]
+    group.emit(0)
 
     @pl.loop(0, outer_ref.shape[0] // TILE)
     def _(n):
@@ -560,18 +586,21 @@
 
     scatter = Scatter(group, stage, land, total, scatter_sems)
     if not last:
+        group.need(1, 6)
         products()
         swap = push(outer.at[1], got_ref, refs[0], 0, 1 - section, "section")
         swap.start()
     halves.wait()
     scatter.start(lambda rows: nt(mixed[rows, :], weight[:, : 3 * width]))
     if last:
+        group.need(1, 6)
         products()
     copies = [pltpu.make_async_copy(outer.at[0], wk_ref, local_sems.at[2])]
     if last:
         copies.append(pltpu.make_async_copy(outer.at[1], ws_ref, local_sems.at[3]))
     for copy in copies:
         copy.start()
+    group.need(2, 3)
     sums_ref[2:3, : 3 * width] = jnp.sum(mixed[...].astype(WIDE), axis=0, keepdims=True)
     for j in range(PARTS):
         rows = slice(j * group.part, (j + 1) * group.part)
@@ -676,42 +705,66 @@
     return jax.ShapeDtypeStruct(dims, kind)
 
 
-def launch(body, number, rows, in_specs, ins, outs, out_specs, scratch, swaps=(), diagonal=False, across=False, flops=3e10):
+def launch(
+    body, number, rows, in_specs, ins, outs, out_specs, scratch, swaps=(), diagonal=False, across=False, late=(),
+):
+    n_in, n_out, n = len(ins), len(outs), len(swaps)
+    held_in = [i for i in range(n_in) if in_specs[i] is VM]
+    held_out = [i for i in range(n_out) if out_specs[i] is VM]
+
     def kernel(*refs):
-        n_in, n_out, n = len(in_specs), len(outs), len(swaps)
+        refs = list(refs)
+        takes, sources = refs[:n_in], refs[n_in : n_in + n]
+        gives = refs[n_in + n : n_in + n + n_out]
+        lands = refs[n_in + n + n_out : n_in + 2 * n + n_out]
+        rest = refs[n_in + 2 * n + n_out :]
+        own, rest = rest[: len(scratch)], rest[len(scratch) :]
+        in_held, rest = rest[: len(held_in)], rest[len(held_in) :]
+        out_held, rest = rest[: len(held_out)], rest[len(held_out) :]
+        in_sems, out_sems, swap_sems = rest
         group = Group(rows)
+        for k, i in enumerate(held_in):
+            group.loads[i] = pltpu.make_async_copy(takes[i], in_held[k], in_sems.at[k])
+            group.loads[i].start()
+            takes[i] = in_held[k]
+        for k, i in enumerate(held_out):
+            group.stores[i] = pltpu.make_async_copy(out_held[k], gives[i], out_sems.at[k])
+            gives[i] = out_held[k]
         group.greet(n or across, diagonal)
-        sources, lands = refs[n_in : n_in + n], refs[n_in + n + n_out : n_in + 2 * n + n_out]
         other = 1 - lax.axis_index("section")
         copies = [
-            push(source, land, refs[-1], i, other, "section")
+            push(source, land, swap_sems, i, other, "section")
             for i, (source, land) in enumerate(zip(sources, lands))
         ]
         for copy in copies:
             copy.start()
-        rest = refs[n_in + 2 * n + n_out :]
-        body(group, *refs[:n_in], *refs[n_in + n : n_in + n + n_out], *(rest[:-1] if n else rest))
+        group.need(*[i for i in held_in if i not in late])
+        body(group, *takes, *gives, *own)
+        group.emit(*[i for i in held_out if i not in group.begun])
         for copy in copies:
             copy.wait()
-
-    extra = [pltpu.SemaphoreType.DMA((2, len(swaps)))] if swaps else []
-    held = [a for a, spec in zip((*ins, *outs), (*in_specs, *out_specs)) if spec is VM]
-    held += [s for s in scratch if s.memory_space == pltpu.VMEM]
-    need = sum(math.prod(s.shape[:-1]) * (-(-s.shape[-1] // 128) * 128) * s.dtype.itemsize for s in held)
+        for i in held_out:
+            group.stores[i].wait()
+
     results = pl.pallas_call(
         kernel,
         out_shape=(*outs, *[shape(s.shape, s.dtype) for s in swaps]),
-        in_specs=[*in_specs, *[ANY] * len(swaps)],
-        out_specs=(*out_specs, *[ANY] * len(swaps)),
-        scratch_shapes=[*scratch, *extra],
+        in_specs=[ANY] * (n_in + n),
+        out_specs=(ANY,) * (n_out + n),
+        scratch_shapes=[
+            *scratch,
+            *[pltpu.VMEM(ins[i].shape, ins[i].dtype) for i in held_in],
+            *[pltpu.VMEM(outs[i].shape, outs[i].dtype) for i in held_out],
+            pltpu.SemaphoreType.DMA((len(held_in),)),
+            pltpu.SemaphoreType.DMA((len(held_out),)),
+            pltpu.SemaphoreType.DMA((2, max(n, 1))),
+        ],
         compiler_params=pltpu.CompilerParams(
-            collective_id=number, has_side_effects=True, vmem_limit_bytes=min(need + SPARE, 58 * MEBI)
+            collective_id=number, has_side_effects=True, vmem_limit_bytes=GRANT
         ),
-        cost_estimate=pl.CostEstimate(
-            flops=int(flops), bytes_accessed=30 * MEBI, transcendentals=0
-        ),
+        cost_estimate=pl.CostEstimate(flops=int(3e10), bytes_accessed=30 * MEBI, transcendentals=0),
     )(*ins, *swaps)
-    return results[: len(outs)], results[len(outs) :]
+    return results[:n_out], results[n_out:]
 
 
 def start_call(number, tokens, cotangent, small, raw, columns):
@@ -731,7 +784,7 @@
             pltpu.SemaphoreType.DMA((2, 3 * PARTS + 2)), LOCAL,
         ],
         compiler_params=pltpu.CompilerParams(
-            collective_id=number, has_side_effects=True, vmem_limit_bytes=56 * MEBI
+            collective_id=number, has_side_effects=True, vmem_limit_bytes=GRANT
         ),
         cost_estimate=pl.CostEstimate(flops=int(3e10), bytes_accessed=30 * MEBI, transcendentals=0),
     )(tokens, cotangent, small, raw)
@@ -782,7 +835,7 @@
         outs += [shape((size, wide // 2))] * 2
     return launch(
         functools.partial(contract_kernel, last),
-        number, rows, in_specs, ins, outs, (VM,) * len(outs), scratch, swaps,
+        number, rows, in_specs, ins, outs, (VM,) * len(outs), scratch, swaps, late=(1, 5),
     )
 
 
@@ -799,7 +852,7 @@
     return launch(
         functools.partial(bend_kernel, last),
         number, rows, [VM, ANY, ANY, VM, VM], (grad, *pair, slope, extra),
-        outs, (VM,) * len(outs), scratch, swaps, last,
+        outs, (VM,) * len(outs), scratch, swaps, last, late=(3,) if last else (3, 4),
     )
 
 
@@ -816,7 +869,7 @@
     return launch(
         narrow_kernel,
         number, rows, [VM, VM, ANY, ANY, VM, VM, VM], (before, grad_own, *pair, second, hidden, vec),
-        outs, (VM,) * 5, scratch, swaps,
+        outs, (VM,) * 5, scratch, swaps, late=(1, 4, 5),
     )
 
 
@@ -838,7 +891,7 @@
     return launch(
         functools.partial(scores_back_kernel, heads),
         number, rows, [VM, ANY, ANY, VM, VM, VM], (low, *pair, heads_all, o, lse),
-        outs, (VM,) * 2, scratch, swaps,
+        outs, (VM,) * 2, scratch, swaps, late=(3, 4, 5),
     )
 
 
@@ -860,7 +913,7 @@
     return launch(
         functools.partial(attend_back_kernel, last),
         number, rows, [VM, VM, VM, VM, ANY, ANY, VM, VM],
-        (mixed, outer, grad, x_own, *pair, normed, vec), outs, out_specs, scratch, swaps, False, True,
+        (mixed, outer, grad, x_own, *pair, normed, vec), outs, out_specs, scratch, swaps, False, True, late=(1, 2, 3, 6),
     )
 
 
@@ -890,7 +943,7 @@
         out_specs=(VM, VM),
         scratch_shapes=scratch,
         compiler_params=pltpu.CompilerParams(
-            collective_id=number, has_side_effects=True, vmem_limit_bytes=32 * MEBI
+            collective_id=number, has_side_effects=True, vmem_limit_bytes=GRANT
         ),
         cost_estimate=pl.CostEstimate(flops=int(3e10), bytes_accessed=30 * MEBI, transcendentals=0),
     )(near, far, *sums)

time: 813 us -> 733 us (0.902)
  local copies, waits for them, and re-layouts: 137 us -> 31.5 us
  Pallas kernels: 564 us -> 593 us
    unnamed x236 -> x54, local copies, waits for them, and re-layouts: 127 us -> 17.3 us
    pallas_call x14, Pallas kernels: 485 us -> 511 us  [launch(): pl.pallas_call(kernel, out_shape=(*outs, *[shape(s.shape, s.dtype) for s...]
    convert_element_type x6, other arithmetic: 9.6 us -> 18.7 us  [add(): total = (keep.astype(WIDE) + got.astype(WIDE)).astype(LOW)]
  transfers between devices with their start and end apart: 17 -> 17, of which waited for: 4 -> 4; matrix products, arithmetic and copies ran while one was open for 6% -> 7% of each run, Pallas kernels for 57% -> 66%
where the time goes in v5:
time: 733 us; the launch traced here: 727 us
  Pallas kernels  593 us (81%)
  waiting for transfers between devices  43.5 us (6%)
  other arithmetic  33 us (5%)
  local copies, waits for them, and re-layouts  31.5 us (4%)
  between operations  15.2 us (2%)
  starting transfers between devices  10.4 us (1%)
    pallas_call x14, Pallas kernels, launch(): pl.pallas_call(kernel, out_shape=(*outs, *[shape(s.shape, s.dtype) for s...  511 us
    pallas_call x1, Pallas kernels, start_call(): pl.pallas_call(start_kernel, out_shape=outs, in_specs=[ANY] * 4, out_spec...  43.6 us
    pallas_call x1, Pallas kernels, finish_call(): pl.pallas_call(finish_kernel, out_shape=outs, in_specs=[VM] * 8, out_spec...  38.4 us
    all_gather x6, waiting for transfers between devices, on_device(): mats[layer].append(lax.all_gather(block, 'row', axis=0, tiled=True))  28 us
    convert_element_type x6, other arithmetic, add(): total = (keep.astype(WIDE) + got.astype(WIDE)).astype(LOW)  18.7 us
    unnamed x54, local copies, waits for them, and re-layouts  17.3 us
  transfers between devices with their start and end apart: 17, of which 4 were waited for; matrix products, arithmetic and copies ran while one was open for 7% of the time, Pallas kernels for 66%

profile of v5, /device:TPU:0, one launch (start us, length us, event | category | flops | bytes accessed | tf_op | source)
XLA Modules:
  0.0 726.8 jit_solution(12959870571229533755)
XLA Ops:
  7.2 1.1 copy.38
  8.4 1.5 copy.37
  10.4 3.0 collective-permute-start
  13.5 1.5 copy.41.tokens_ref
  15.1 2.7 copy.42.cotangent_ref
  20.3 2.6 collective-permute-done
  24.0 43.6 %shard_map.245 = (bf16[1024,1280]{1,0:T(8,128)(2,1)}, bf16[1024,1280]{1,0:T(8,128)(2,1)}, bf16[2,4,16,320]{3,2,1,0:T(8,128)(2,1)}, bf16[2,320,640]{2,1,0:T(8,128)(2,1)}) custom-call(bf16[2048,320]{1,0:T(8,128)(2,1)} %copy.41.tokens_ref, bf16[2048,320]{1,0:T(8,128)(2,1)} %copy.42.cotangent_ref, bf16[16,320]{1,0:T(8,128)(2,1)} %pad.8.small_ref, ...), custom_call_target="tpu_custom_call" | custom-call | flops 30000001024 | bytes 31457280 | tf_op jit(solution)/shard_map/pallas_call | solution.py:777
  67.7 2.4 bitcast_select_fusion.2
  76.4 2.0 constant_dynamic-slice_fusion.1.refs_3_
  78.4 2.0 constant_dynamic-slice_fusion.2.refs_1_
  80.3 27.9 %all-gather.9.cloned.1.call-done.refs_5_.refs_1_.refs_2_ = bf16[1280,640]{1,0:T(8,128)(2,1)} async-done(((bf16[320,640]{1,0:T(8,128)(2,1)}), bf16[1280,640]{1,0:T(8,128)(2,1)}) %all-gather.9.cloned.1.call-update) | async-done | bytes 1638416 | tf_op jit(solution)/shard_map/all_gather | solution.py:1020
  108.2 2.7 collective-permute-done.1.refs_2_.refs_5_
  111.0 1.2 copy-done.22
  112.1 39.1 %shard_map.246 = (bf16[16,128]{1,0:T(8,128)(2,1)}, bf16[1024,1280]{1,0:T(8,128)(2,1)}, bf16[15,1024,64]{2,1,0:T(8,128)(2,1)}, bf16[1024,320]{1,0:T(8,128)(2,1)},...) custom-call(bf16[1024,1280]{1,0:T(8,128)(2,1)} %get-tuple-element.111.refs_0_, ...), custom_call_target="tpu_custom_call" | custom-call | flops 30000001024 | bytes 31457280 | tf_op jit(solution)/shard_map/pallas_call | solution.py:749
  151.3 38.4 %shard_map.247 = (bf16[1024,1280]{1,0:T(8,128)(2,1)}, bf16[1024,1280]{1,0:T(8,128)(2,1)}, bf16[1024,1280]{1,0:T(8,128)(2,1)}, bf16[1280,640]{1,0:T(8,128)(2,1)}) custom-call(bf16[256,1280]{1,0:T(8,128)(2,1)} %get-tuple-element.115.refs_0_, bf16[1280,640]{1,0:T(8,128)(2,1)} %all-gather.9.cloned.1.call-done.refs_5_.refs_1_.refs_2_, ...), custom_call_target="tpu_custom_call" | custom-call | flops 30000001024 | bytes 31457280 | tf_op jit(solution)/shard_map/pallas_call | solution.py:749
  189.7 38.6 %shard_map.248 = (bf16[256,1280]{1,0:T(8,128)(2,1)}, bf16[1280,640]{1,0:T(8,128)(2,1)}) custom-call(bf16[1024,1280]{1,0:T(8,128)(2,1)} %get-tuple-element.117.refs_0_.refs_4_, f32[256,1280]{1,0:T(8,128)} %get-tuple-element.118.refs_1_.refs_5_, bf16[1280,640]{1,0:T(8,128)(2,1)} %all-gather.11.cloned.1.call-done.refs_4_.refs_2_.refs_1_, ...), custom_call_target="tpu_custom_call" | custom-call | flops 30000001024 | bytes 31457280 | tf_op jit(solution)/shard_map/pallas_call | solution.py:749
  228.3 51.7 %shard_map.249 = (bf16[1024,1280]{1,0:T(8,128)(2,1)}, bf16[1024,1280]{1,0:T(8,128)(2,1)}, bf16[15,1024,64]{2,1,0:T(8,128)(2,1)}, bf16[1024,320]{1,0:T(8,128)(2,1...) custom-call(bf16[256,1280]{1,0:T(8,128)(2,1)} %get-tuple-element.120.refs_0_, ...), custom_call_target="tpu_custom_call" | custom-call | flops 30000001024 | bytes 31457280 | tf_op jit(solution)/shard_map/pallas_call | solution.py:749
  280.0 37.9 %shard_map.250 = (bf16[1024,1280]{1,0:T(8,128)(2,1)}, bf16[1024,1280]{1,0:T(8,128)(2,1)}, bf16[1024,1280]{1,0:T(8,128)(2,1)}, bf16[1280,640]{1,0:T(8,128)(2,1)}) custom-call(bf16[256,1280]{1,0:T(8,128)(2,1)} %get-tuple-element.124.refs_0_, bf16[1280,640]{1,0:T(8,128)(2,1)} %all-gather.15.cloned.1.call-done.refs_5_.refs_1_.refs_2_, ...), custom_call_target="tpu_custom_call" | custom-call | flops 30000001024 | bytes 31457280 | tf_op jit(solution)/shard_map/pallas_call | solution.py:749
  317.9 24.3 %shard_map.251 = (bf16[256,1280]{1,0:T(8,128)(2,1)}, bf16[1280,640]{1,0:T(8,128)(2,1)}, bf16[1280,640]{1,0:T(8,128)(2,1)}) custom-call(bf16[1024,1280]{1,0:T(8,128)(2,1)} %get-tuple-element.128.refs_0_, f32[256,1280]{1,0:T(8,128)} %get-tuple-element.129.refs_1_.refs_5_, bf16[1280,640]{1,0:T(8,128)(2,1)} %all-gather.17.cloned.1.call-done.refs_4_.refs_2_.refs_1_, ...), custom_call_target="tpu_custom_call" | custom-call | flops 30000001024 | bytes 31457280 | tf_op jit(solution)/shard_map/pallas_call | solution.py:749
  342.2 14.0 %shard_map.252 = (bf16[1024,1280]{1,0:T(8,128)(2,1)}, f32[8,1280]{1,0:T(8,128)}, bf16[1024,320]{1,0:T(8,128)(2,1)}) custom-call(bf16[1024,1280]{1,0:T(8,128)(2,1)} %get-tuple-element.123.refs_5_.refs_0_, bf16[1280,640]{1,0:T(8,128)(2,1)} %all-gather.17.cloned.1.call-done.refs_4_.refs_2_.refs_1_, bf16[1280,640]{1,0:T(8,128)(2,1)} %get-tuple-element.126.refs_3_.refs_2_, ...), custom_call_target="tpu_custom_call" | custom-call | flops 30000001024 | bytes 31457280 | tf_op jit(solution)/shard_map/pallas_call | solution.py:749
  356.2 39.0 %shard_map.253 = (bf16[1280,640]{1,0:T(8,128)(2,1)}, bf16[1280,640]{1,0:T(8,128)(2,1)}, f32[256,1280]{1,0:T(8,128)}, bf16[256,1280]{1,0:T(8,128)(2,1)}, f32[8,1280]{1,0:T(8,128)}, /*index=5*/bf16[1280,640]{1,0:T(8,128)(2,1)}) custom-call(bf16[1024,1280]{1,0:T(8,128)(2,1)} %get-tuple-element.133.refs_0_, ...), custom_call_target="tpu_custom_call" | custom-call | flops 30000001024 | bytes 31457280 | tf_op jit(solution)/shard_map/pallas_call | solution.py:749
  395.3 3.0 add_convert_fusion.5
  398.8 40.5 %shard_map.254 = (bf16[1024,960]{1,0:T(8,128)(2,1)}, bf16[1280,320]{1,0:T(8,128)(2,1)}, bf16[1280,640]{1,0:T(8,128)(2,1)}) custom-call(bf16[256,1280]{1,0:T(8,128)(2,1)} %get-tuple-element.140.refs_0_, bf16[1280,640]{1,0:T(8,128)(2,1)} %all-gather.13.cloned.1.call-done.refs_5_.refs_1_.refs_4_, bf16[1280,640]{1,0:T(8,128)(2,1)} %get-tuple-element.121.refs_2_.refs_5_, ...), custom_call_target="tpu_custom_call" | custom-call | flops 30000001024 | bytes 31457280 | tf_op jit(solution)/shard_map/pallas_call | solution.py:749
  439.3 3.2 add_convert_fusion.4
  443.6 1.3 broadcast_select_fusion.2.refs_8_
  444.9 25.3 %shard_map.255 = (bf16[1280,640]{1,0:T(8,128)(2,1)}, bf16[1280,640]{1,0:T(8,128)(2,1)}, bf16[256,1280]{1,0:T(8,128)(2,1)}, f32[8,1280]{1,0:T(8,128)}, bf16[1024,320]{1,0:T(8,128)(2,1)}) custom-call(bf16[1024,960]{1,0:T(8,128)(2,1)} %get-tuple-element.148.refs_0_, bf16[1280,320]{1,0:T(8,128)(2,1)} %get-tuple-element.149.refs_1_, ...), custom_call_target="tpu_custom_call" | custom-call | flops 30000001024 | bytes 31457280 | tf_op jit(solution)/shard_map/pallas_call | solution.py:749
  470.2 1.8 broadcast_select_fusion.1
  472.2 1.5 copy.46
  473.7 38.1 %shard_map.256 = (bf16[1024,1280]{1,0:T(8,128)(2,1)}, f32[8,1280]{1,0:T(8,128)}, bf16[1024,1280]{1,0:T(8,128)(2,1)}, bf16[1280,640]{1,0:T(8,128)(2,1)}, bf16[128...) custom-call(bf16[256,1280]{1,0:T(8,128)(2,1)} %get-tuple-element.155.refs_0_.refs_1_, ...), custom_call_target="tpu_custom_call" | custom-call | flops 30000001024 | bytes 31457280 | tf_op jit(solution)/shard_map/pallas_call | solution.py:749
  511.9 3.0 add_convert_fusion.3
  515.2 38.5 %shard_map.257 = (bf16[1280,640]{1,0:T(8,128)(2,1)}, bf16[1280,640]{1,0:T(8,128)(2,1)}, f32[256,1280]{1,0:T(8,128)}, bf16[256,1280]{1,0:T(8,128)(2,1)}, f32[8,1280]{1,0:T(8,128)}, /*index=5*/bf16[1280,640]{1,0:T(8,128)(2,1)}) custom-call(bf16[1024,1280]{1,0:T(8,128)(2,1)} %get-tuple-element.161.refs_0_, ...), custom_call_target="tpu_custom_call" | custom-call | flops 30000001024 | bytes 31457280 | tf_op jit(solution)/shard_map/pallas_call | solution.py:749
  553.6 3.1 add_convert_fusion.2
  556.7 2.4 constant_dynamic-slice_fusion.far_ref
  559.5 39.2 %shard_map.258 = (bf16[1024,960]{1,0:T(8,128)(2,1)}, bf16[1280,320]{1,0:T(8,128)(2,1)}, bf16[1280,640]{1,0:T(8,128)(2,1)}) custom-call(bf16[256,1280]{1,0:T(8,128)(2,1)} %get-tuple-element.170.refs_0_, bf16[1280,640]{1,0:T(8,128)(2,1)} %all-gather.7.cloned.1.call-done.refs_1_.refs_4_, bf16[1280,640]{1,0:T(8,128)(2,1)} %copy-done.22, ...), custom_call_target="tpu_custom_call" | custom-call | flops 30000001024 | bytes 31457280 | tf_op jit(solution)/shard_map/pallas_call | solution.py:749
  598.7 3.0 add_convert_fusion.1
  602.9 1.3 collective-permute-start.4
  604.2 46.7 %shard_map.259 = (bf16[1280,640]{1,0:T(8,128)(2,1)}, bf16[16,128]{1,0:T(8,128)(2,1)}, bf16[256,1280]{1,0:T(8,128)(2,1)}, f32[8,1280]{1,0:T(8,128)}, bf16[1280,640]{1,0:T(8,128)(2,1)}) custom-call(bf16[1024,960]{1,0:T(8,128)(2,1)} %get-tuple-element.180.refs_0_, bf16[1280,320]{1,0:T(8,128)(2,1)} %get-tuple-element.181.refs_1_, ...), custom_call_target="tpu_custom_call" | custom-call | flops 30000001024 | bytes 31457280 | tf_op jit(solution)/shard_map/pallas_call | solution.py:749
  650.9 3.5 add_convert_fusion
  654.6 1.3 convert_bitcast_fusion
  656.6 2.2 collective-permute-start.3
  658.9 38.4 %shard_map.260 = (f32[2048,320]{1,0:T(8,128)}, f32[16,320]{1,0:T(8,128)}) custom-call(bf16[256,1280]{1,0:T(8,128)(2,1)} %get-tuple-element.188.near_ref, bf16[1024,320]{1,0:T(8,128)(2,1)} %constant_dynamic-slice_fusion.far_ref, f32[8,1280]{1,0:T(8,128)} %get-tuple-element.190.a0, f32[8,1280]{1,0:T(8,128)} %get-tuple-element.191.n0, ...), custom_call_target="tpu_custom_call" | custom-call | flops 30000001024 | bytes 31457280 | tf_op jit(solution)/shard_map/pallas_call | solution.py:939
  697.3 3.4 copy.47
  701.5 1.5 collective-permute-start.2
  704.2 8.2 %collective-permute-done.2 = bf16[320,640]{1,0:T(8,128)(2,1)S(1)} collective-permute-done((bf16[320,640]{1,0:T(8,128)(2,1)S(1)}, bf16[320,640]{1,0:T(8,128)(2,1)S(1)}, u32[]{:S(2)}, u32[]{:S(2)}) %collective-permute-start.2) | collective-permute-done | bytes 409632 | tf_op jit(solution)/shard_map/ppermute | solution.py:953
  712.4 1.1 broadcast_select_fusion.11
  715.4 1.6 copy.48
  717.1 1.1 select_bitcast_fusion.1
  718.2 1.3 maximum_convert_fusion.1
  (121 shorter events, 18.8 us)
Async XLA Ops:
  7.2 65.0 %all-gather.7.cloned.1.call-start = ((), (), s32[]{:S(2)}) async-start(), calls=%async_computation.6 | async-start | bytes 2048000 | tf_op jit(solution)/shard_map/all_gather | solution.py:1020
  9.9 3.6 copy-start.17
  10.1 3.4 copy-start.13
  10.4 12.5 %collective-permute-start = (bf16[320,640]{1,0:T(8,128)(2,1)S(1)}, bf16[320,640]{1,0:T(8,128)(2,1)S(1)}, u32[]{:S(2)}, u32[]{:S(2)}) collective-permute-start(bf16[320,640]{1,0:T(8,128)(2,1)S(1)} %get-tuple-element.234), channel_id=1, source_target_pairs={{0,16},{16,0},{1,17},{17,1},{2,18},{18,2},{3,19},{19,3},{4,20},{20... | collective-permute-start | bytes 1228808 | tf_op jit(solution)/shard_map/ppermute | solution.py:953
  15.1 2.7 copy-start.18
  15.1 2.7 copy-start.19
  15.1 2.7 copy-start.20
  15.1 2.7 copy-start.21
  15.1 4.1 copy-start
  15.1 4.1 copy-start.1
  24.0 84.2 %all-gather.9.cloned.1.call-start = ((), (), s32[]{:S(2)}) async-start(), calls=%async_computation.7 | async-start | bytes 2048000 | tf_op jit(solution)/shard_map/all_gather | solution.py:1020
  70.1 2.1 copy-start.15
  70.1 81.2 %all-gather.11.cloned.1.call-start = ((), (), s32[]{:S(2)}) async-start(), calls=%async_computation.8 | async-start | bytes 2048000 | tf_op jit(solution)/shard_map/all_gather | solution.py:1020
  70.9 118.8 %all-gather.13.cloned.1.call-start = ((), (), s32[]{:S(2)}) async-start(), calls=%async_computation.9 | async-start | bytes 2048000 | tf_op jit(solution)/shard_map/all_gather | solution.py:1020
  71.4 156.8 %all-gather.15.cloned.1.call-start = ((), (), s32[]{:S(2)}) async-start(), calls=%async_computation.10 | async-start | bytes 2048000 | tf_op jit(solution)/shard_map/all_gather | solution.py:1020
  72.0 208.0 %all-gather.17.cloned.1.call-start = ((), (), s32[]{:S(2)}) async-start(), calls=%async_computation.11 | async-start | bytes 2048000 | tf_op jit(solution)/shard_map/all_gather | solution.py:1020
  72.2 38.7 %collective-permute-start.1 = (bf16[1280,640]{1,0:T(8,128)(2,1)}, bf16[1280,640]{1,0:T(8,128)(2,1)S(1)}, u32[]{:S(2)}, u32[]{:S(2)}) collective-permute-start(bf16[1280,640]{1,0:T(8,128)(2,1)} %all-gather.7.cloned.1.call-done.refs_1_.refs_4_), channel_id=1, source_target_pairs={{0,16},{16,0},{1,17},{17,1},{2,18},{18,2},{3,19},{19,3},{4,20},{20... | collective-permute-start | bytes 4915208 | tf_op jit(solution)/shard_map/ppermute | solution.py:953
  75.7 369.2 %reduce-scatter.7.cloned.1.call-start = ((), (), s32[]{:S(2)}) async-start(), calls=%async_computation.12 | async-start | bytes 2048000 | tf_op jit(solution)/shard_map/reduce_scatter | solution.py:1070
  110.9 1.2 copy-start.22
  356.2 39.1 %copy-start.7 = (bf16[1280,640]{1,0:T(8,128)(2,1)S(1)}, bf16[1280,640]{1,0:T(8,128)(2,1)}, u32[]{:S(2)}) copy-start(bf16[1280,640]{1,0:T(8,128)(2,1)} %get-tuple-element.132) | copy-start | bytes 4915204
  398.3 116.5 %reduce-scatter.9.cloned.1.call-start = ((), (), s32[]{:S(2)}) async-start(), calls=%async_computation.13 | async-start | bytes 2048000 | tf_op jit(solution)/shard_map/reduce_scatter | solution.py:1070
  398.8 40.5 %copy-start.6 = (bf16[1280,640]{1,0:T(8,128)(2,1)S(1)}, bf16[1280,640]{1,0:T(8,128)(2,1)}, u32[]{:S(2)}) copy-start(bf16[1280,640]{1,0:T(8,128)(2,1)} %get-tuple-element.139) | copy-start | bytes 4915204
  439.3 3.4 copy-start.14
  442.5 1.1 copy-start.2
  442.5 117.0 %reduce-scatter.11.cloned.1.call-start = ((), (), s32[]{:S(2)}) async-start(), calls=%async_computation.14 | async-start | bytes 2048000 | tf_op jit(solution)/shard_map/reduce_scatter | solution.py:1070
  473.7 38.1 %copy-start.5 = (bf16[1280,640]{1,0:T(8,128)(2,1)S(1)}, bf16[1280,640]{1,0:T(8,128)(2,1)}, u32[]{:S(2)}) copy-start(bf16[1280,640]{1,0:T(8,128)(2,1)} %get-tuple-element.154) | copy-start | bytes 4915204
  514.9 86.8 %reduce-scatter.15.cloned.1.call-start = ((), (), s32[]{:S(2)}) async-start(), calls=%async_computation.16 | async-start | bytes 2048000 | tf_op jit(solution)/shard_map/reduce_scatter | solution.py:1070
  515.2 38.5 %copy-start.3 = (bf16[1280,640]{1,0:T(8,128)(2,1)S(1)}, bf16[1280,640]{1,0:T(8,128)(2,1)}, u32[]{:S(2)}) copy-start(bf16[1280,640]{1,0:T(8,128)(2,1)} %get-tuple-element.166) | copy-start | bytes 4915204
  559.2 96.7 %reduce-scatter.13.cloned.1.call-start = ((), (), s32[]{:S(2)}) async-start(), calls=%async_computation.15 | async-start | bytes 2048000 | tf_op jit(solution)/shard_map/reduce_scatter | solution.py:1070
  559.5 39.2 %copy-start.4 = (bf16[1280,640]{1,0:T(8,128)(2,1)S(1)}, bf16[1280,640]{1,0:T(8,128)(2,1)}, u32[]{:S(2)}) copy-start(bf16[1280,640]{1,0:T(8,128)(2,1)} %get-tuple-element.164) | copy-start | bytes 4915204
  601.7 1.0 copy-start.9
  601.7 1.1 copy-start.12
  601.8 99.0 %reduce-scatter.17.cloned.1.call-start = ((), (), s32[]{:S(2)}) async-start(), calls=%async_computation.17 | async-start | bytes 2048000 | tf_op jit(solution)/shard_map/reduce_scatter | solution.py:1070
  602.9 51.5 %collective-permute-start.4 = (bf16[320,640]{1,0:T(8,128)(2,1)S(1)}, bf16[320,640]{1,0:T(8,128)(2,1)S(1)}, u32[]{:S(2)}, u32[]{:S(2)}) collective-permute-start(bf16[320,640]{1,0:T(8,128)(2,1)S(1)} %broadcast_select_fusion.6), channel_id=1, source_target_pairs={{0,16},{16,0},{1,17},{17,1},{2,18},{18,2},{3,19},{19,3},{4,20},{20... | collective-permute-start | bytes 1228808 | tf_op jit(solution)/shard_map/ppermute | solution.py:953
  654.5 1.3 copy-start.8
  656.6 60.4 %collective-permute-start.3 = (bf16[320,640]{1,0:T(8,128)(2,1)}, bf16[320,640]{1,0:T(8,128)(2,1)}, u32[]{:S(2)}, u32[]{:S(2)}) collective-permute-start(bf16[320,640]{1,0:T(8,128)(2,1)} %broadcast_select_fusion.8), channel_id=1, source_target_pairs={{0,16},{16,0},{1,17},{17,1},{2,18},{18,2},{3,19},{19,3},{4,20},{20... | collective-permute-start | bytes 1228808 | tf_op jit(solution)/shard_map/ppermute | solution.py:953
  697.3 3.5 copy-start.16
  697.3 4.2 copy-start.10
  701.5 10.9 %collective-permute-start.2 = (bf16[320,640]{1,0:T(8,128)(2,1)S(1)}, bf16[320,640]{1,0:T(8,128)(2,1)S(1)}, u32[]{:S(2)}, u32[]{:S(2)}) collective-permute-start(bf16[320,640]{1,0:T(8,128)(2,1)S(1)} %broadcast_select_fusion.12), channel_id=1, source_target_pairs={{0,16},{16,0},{1,17},{17,1},{2,18},{18,2},{3,19},{19,3},{4,20},{20... | collective-permute-start | bytes 1228808 | tf_op jit(solution)/shard_map/ppermute | solution.py:953
  715.4 1.6 copy-start.11
Sparse Core Ops, SparseCore 0:
  24.1 39.6 all-gather.6
  70.2 37.9 all-gather.8
  110.4 37.0 all-gather.10
  148.8 37.0 all-gather.12
  188.0 37.0 all-gather.14
  227.0 37.0 all-gather.16
  398.4 36.6 reduce-scatter.6
  442.6 36.5 reduce-scatter.8
  515.0 36.8 reduce-scatter.10
  559.3 36.5 reduce-scatter.14
  601.9 36.4 reduce-scatter.12
  654.5 38.0 reduce-scatter.16

commit v6 on v5

--- a/solution.py
+++ b/solution.py
@@ -388,11 +388,20 @@
     scatter.done()
 
 
-def widen_kernel(
-    group, second_ref, em_ref, eo_ref, bias_ref,
-    full_ref, active_ref, slope_ref,
-    expand, gather_sems, local_sems,
-):
+def outer_whole(left_ref, right_ref, out_ref):
+    @pl.loop(0, left_ref.shape[1] // TILE)
+    def _(n):
+        rows = pl.ds(pl.multiple_of(n * TILE, TILE), TILE)
+        out_ref[rows, :] = tn(left_ref[:, rows], right_ref[...]).astype(LOW)
+
+
+def widen_kernel(last, group, second_ref, em_ref, eo_ref, bias_ref, *refs):
+    if last:
+        g_ref, *refs = refs
+    full_ref, active_ref, slope_ref, *refs = refs
+    if last:
+        c_ref, *refs = refs
+    expand, gather_sems, local_sems = refs
     halves = Halves((em_ref, eo_ref), expand, local_sems, 0)
     halves.start()
     full_ref[group.chunk(group.me), :] = second_ref[...]
@@ -409,6 +418,10 @@
         ).astype(LOW)
 
     Gather(group, full_ref, gather_sems).each(widen)
+    if last:
+        group.emit(0, 1, 2)
+        group.need(4)
+        outer_whole(g_ref, active_ref, c_ref)
 
 
 def outer_halves(left_ref, right_ref, keep_ref, send_ref):
@@ -423,23 +436,15 @@
             out[rows, :] = tn(left_ref[:, rows], right_ref[:, columns]).astype(LOW)
 
 
-def contract_kernel(last, group, *refs):
-    active_ref, hidden_ref, cm_ref, co_ref, vec_ref, *refs = refs
-    if last:
-        g_ref, *refs = refs
-    result_ref, *refs = refs
-    if last:
-        ck_ref, cs_ref, *refs = refs
-    contract, stage, land, total, scatter_sems, local_sems = refs
+def contract_kernel(
+    group, active_ref, hidden_ref, cm_ref, co_ref, vec_ref, result_ref,
+    contract, stage, land, total, scatter_sems, local_sems,
+):
     halves = Halves((cm_ref, co_ref), contract, local_sems, 0)
     halves.start()
     halves.wait()
     scatter = Scatter(group, stage, land, total, scatter_sems)
     scatter.start(lambda rows: nt(active_ref[rows, :], contract[...]))
-    if last:
-        group.need(5)
-        outer_halves(g_ref, active_ref, ck_ref, cs_ref)
-        group.emit(1, 2)
     group.need(1)
     for j in range(PARTS):
         rows = slice(j * group.part, (j + 1) * group.part)
@@ -491,8 +496,8 @@
 
 
 def narrow_kernel(
-    group, before, g_ref, em_ref, eo_ref, second_ref, hidden_ref, vec_ref,
-    ek_ref, es_ref, grad_ref, low_ref, sums_ref,
+    last, group, before, g_ref, em_ref, eo_ref, second_ref, hidden_ref, vec_ref,
+    grad_ref, low_ref, sums_ref, ek_ref, es_ref,
     expand, stage, land, total, scatter_sems, local_sems,
 ):
     halves = Halves((em_ref, eo_ref), expand, local_sems, 0)
@@ -502,8 +507,12 @@
     scatter = Scatter(group, stage, land, total, scatter_sems)
     scatter.start(lambda rows: nt(before[rows, :], expand[...]))
     group.need(4)
-    outer_halves(second_ref, before, ek_ref, es_ref)
-    group.emit(0, 1)
+    if last:
+        outer_whole(second_ref, before, ek_ref)
+        group.emit(3)
+    else:
+        outer_halves(second_ref, before, ek_ref, es_ref)
+        group.emit(3, 4)
     group.need(1, 5)
     for j in range(PARTS):
         rows = slice(j * group.part, (j + 1) * group.part)
@@ -561,7 +570,7 @@
 
 def attend_back_kernel(
     last, group, mixed, outer_ref, grad_ref, x_ref, mine_ref, other_ref, normed_ref, vec_ref,
-    wk_ref, ws_ref, out_ref, sums_ref, *refs,
+    wk_ref, out_ref, sums_ref, *refs,
 ):
     if not last:
         got_ref, *refs = refs
@@ -578,11 +587,15 @@
         @pl.loop(0, weight.shape[0] // TILE)
         def _(n):
             rows = pl.ds(pl.multiple_of(n * TILE, TILE), TILE)
-            outer[section, rows, :] = tn(normed_ref[:, rows], mixed[:, :half]).astype(LOW)
-            outer[1 - section, rows, : 3 * width - half] = tn(
-                normed_ref[:, rows], mixed[:, half:]
-            ).astype(LOW)
-            outer[1 - section, rows, 3 * width - half :] = outer_ref[rows, :]
+            if last:
+                outer[rows, : 3 * width] = tn(normed_ref[:, rows], mixed[...]).astype(LOW)
+                outer[rows, 3 * width :] = outer_ref[rows, :]
+            else:
+                outer[section, rows, :] = tn(normed_ref[:, rows], mixed[:, :half]).astype(LOW)
+                outer[1 - section, rows, : 3 * width - half] = tn(
+                    normed_ref[:, rows], mixed[:, half:]
+                ).astype(LOW)
+                outer[1 - section, rows, 3 * width - half :] = outer_ref[rows, :]
 
     scatter = Scatter(group, stage, land, total, scatter_sems)
     if not last:
@@ -595,11 +608,8 @@
     if last:
         group.need(1, 6)
         products()
-    copies = [pltpu.make_async_copy(outer.at[0], wk_ref, local_sems.at[2])]
-    if last:
-        copies.append(pltpu.make_async_copy(outer.at[1], ws_ref, local_sems.at[3]))
-    for copy in copies:
-        copy.start()
+    store = pltpu.make_async_copy(outer if last else outer.at[0], wk_ref, local_sems.at[2])
+    store.start()
     group.need(2, 3)
     sums_ref[2:3, : 3 * width] = jnp.sum(mixed[...].astype(WIDE), axis=0, keepdims=True)
     for j in range(PARTS):
@@ -611,22 +621,38 @@
         for n, term in enumerate((grad * hat, grad)):
             sums_ref[n : n + 1, :] += jnp.sum(term, axis=0, keepdims=True)
     scatter.done()
-    for copy in copies:
-        copy.wait()
+    store.wait()
     if not last:
         swap.wait()
 
 
 def finish_kernel(
-    near_ref, far_ref, a0, n0, b0, a1, n1, b1, grads_ref, sums_ref,
+    late_ref, early1_ref, early2_ref, near_ref, far_ref, a0, n0, b0, a1, n1, b1,
+    grads_ref, sums_ref, got_late, got_early1, got_early2,
     mine, stage4, block, land_col, land_x, land_z, send, land,
-    deliver_sems, col_sems, x_sems, z_sems,
+    deliver_sems, col_sems, x_sems, z_sems, part_sems,
 ):
     section, row = lax.axis_index("section"), lax.axis_index("row")
     group = Group(near_ref.shape[0])
     length, width = far_ref.shape
     others = [lax.rem(row + d, land_z.shape[0]) for d in range(1, land_z.shape[0])]
     group.greet(True, True, others)
+    parts = [
+        push(source, into, part_sems, n, 1 - section, "section")
+        for n, (source, into) in enumerate(
+            ((late_ref, got_late), (early1_ref, got_early1), (early2_ref, got_early2))
+        )
+    ]
+
+    @pl.when(section == 0)
+    def _():
+        parts[0].start()
+
+    @pl.when(section == 1)
+    def _():
+        parts[1].start()
+        parts[2].start()
+
     deliver = Deliver(group, stage4, mine, deliver_sems)
     deliver.start(near_ref)
 
@@ -693,6 +719,18 @@
     sums_ref[...] = result
     swap.wait()
     grads_ref[away, :] = land[...].astype(WIDE)
+
+    @pl.when(section == 0)
+    def _():
+        parts[0].wait_send()
+        parts[1].wait_recv()
+        parts[2].wait_recv()
+
+    @pl.when(section == 1)
+    def _():
+        parts[1].wait_send()
+        parts[2].wait_send()
+        parts[0].wait_recv()
 
 
 VM = pl.BlockSpec(memory_space=pltpu.VMEM)
@@ -813,29 +851,28 @@
     )
 
 
-def widen_call(number, second, pair, bias, swaps):
+def widen_call(number, second, pair, bias, grad, swaps):
     rows, size = second.shape
     wide = bias.shape[1]
-    outs = (shape((LENGTH, size)), shape((LENGTH, wide)), shape((LENGTH, wide)))
+    last = grad is not None
+    ins, in_specs = [second, *pair, bias], [VM, ANY, ANY, VM]
+    outs = [shape((LENGTH, size)), shape((LENGTH, wide)), shape((LENGTH, wide))]
+    if last:
+        ins, in_specs, outs = ins + [grad], in_specs + [VM], outs + [shape((size, wide))]
     scratch = [pltpu.VMEM((size, wide), LOW), PAIRS, LOCAL]
     return launch(
-        widen_kernel, number, rows, [VM, ANY, ANY, VM], (second, *pair, bias), outs, (VM,) * 3, scratch, swaps
-    )
-
-
-def contract_call(number, active, hidden, pair, vec, grad, swaps):
+        functools.partial(widen_kernel, last),
+        number, rows, in_specs, ins, outs, (VM,) * len(outs), scratch, swaps, late=(4,),
+    )
+
+
+def contract_call(number, active, hidden, pair, vec, swaps):
     rows, size = hidden.shape
     wide = active.shape[1]
-    last = grad is not None
-    outs = [shape((rows, size))]
     scratch = [pltpu.VMEM((size, wide), LOW), *scatter_scratch(rows, size), LOCAL]
-    in_specs, ins = [VM, VM, ANY, ANY, VM], [active, hidden, *pair, vec]
-    if last:
-        in_specs, ins = in_specs + [VM], ins + [grad]
-        outs += [shape((size, wide // 2))] * 2
     return launch(
-        functools.partial(contract_kernel, last),
-        number, rows, in_specs, ins, outs, (VM,) * len(outs), scratch, swaps, late=(1, 5),
+        contract_kernel, number, rows, [VM, VM, ANY, ANY, VM], (active, hidden, *pair, vec),
+        [shape((rows, size))], (VM,), scratch, swaps, late=(1,),
     )
 
 
@@ -856,20 +893,21 @@
     )
 
 
-def narrow_call(number, before, grad_own, pair, second, hidden, vec, swaps):
+def narrow_call(number, last, before, grad_own, pair, second, hidden, vec, swaps):
     rows, size = hidden.shape
     wide = before.shape[1]
     outs = (
-        *[shape((size, wide // 2))] * 2,
         shape((rows, size), WIDE),
         shape((rows, size)),
         shape((8, size), WIDE),
+        shape((size, wide if last else wide // 2)),
+        shape((16, 128) if last else (size, wide // 2)),
     )
     scratch = [pltpu.VMEM((size, wide), LOW), *scatter_scratch(rows, size), LOCAL]
     return launch(
-        narrow_kernel,
+        functools.partial(narrow_kernel, last),
         number, rows, [VM, VM, ANY, ANY, VM, VM, VM], (before, grad_own, *pair, second, hidden, vec),
-        outs, (VM,) * 5, scratch, swaps, late=(1, 4, 5),
+        outs, (VM, VM, VM, VM, ANY if last else VM), scratch, swaps, late=(1, 4, 5),
     )
 
 
@@ -899,15 +937,14 @@
     rows, size = grad.shape
     width = outer.shape[1]
     half = 2 * width
-    outs = [shape((size, half)), shape((size, half)), shape((rows, size)), shape((8, size), WIDE)]
-    out_specs = [ANY, ANY, VM, VM]
+    outs = [shape((size, 2 * half if last else half)), shape((rows, size)), shape((8, size), WIDE)]
+    out_specs = [ANY, VM, VM]
     scratch = [
         pltpu.VMEM((size, 4 * width), LOW),
-        pltpu.VMEM((2, size, half), LOW),
+        pltpu.VMEM((size, 2 * half) if last else (2, size, half), LOW),
         *scatter_scratch(rows, size), LOCAL,
     ]
     if not last:
-        outs[1] = shape((16, 128))
         outs, out_specs = outs + [shape((size, half))], out_specs + [ANY]
         scratch += [pltpu.SemaphoreType.DMA((2, 1))]
     return launch(
@@ -917,11 +954,15 @@
     )
 
 
-def finish_call(number, near, far, sums, row_count):
+def finish_call(number, late, early1, early2, near, far, sums, row_count):
     rows, size = near.shape
     length, width = far.shape
     columns = length // rows
-    outs = (shape((2 * length, width), WIDE), shape((16, width), WIDE))
+    outs = (
+        shape((2 * length, width), WIDE),
+        shape((16, width), WIDE),
+        *[shape(part.shape) for part in (late, early1, early2)],
+    )
     scratch = [
         pltpu.VMEM((length, width), LOW),
         pltpu.VMEM((columns, rows, width), LOW),
@@ -935,18 +976,19 @@
         pltpu.SemaphoreType.DMA((2, 3)),
         pltpu.SemaphoreType.DMA((2, 2)),
         pltpu.SemaphoreType.DMA((2, row_count)),
+        pltpu.SemaphoreType.DMA((2, 3)),
     ]
     return pl.pallas_call(
         finish_kernel,
         out_shape=outs,
-        in_specs=[VM] * 8,
-        out_specs=(VM, VM),
+        in_specs=[ANY] * 3 + [VM] * 8,
+        out_specs=(VM, VM, ANY, ANY, ANY),
         scratch_shapes=scratch,
         compiler_params=pltpu.CompilerParams(
             collective_id=number, has_side_effects=True, vmem_limit_bytes=GRANT
         ),
         cost_estimate=pl.CostEstimate(flops=int(3e10), bytes_accessed=30 * MEBI, transcendentals=0),
-    )(near, far, *sums)
+    )(late, early1, early2, near, far, *sums)
 
 
 def swap_sections(value):
@@ -1044,21 +1086,22 @@
             2 + 3 * layer, not last, x, attn, vec, attend_biases[layer], rows, width, [mats[layer][1]]
         )
         expand = (mats[layer][1], other)
-        (second, active, slope), (other,) = widen_call(
-            3 + 3 * layer, second_own, expand, expand_biases[layer], [mats[layer][2]]
+        outs, (other,) = widen_call(
+            3 + 3 * layer, second_own, expand, expand_biases[layer],
+            gy_full if last else None, [mats[layer][2]],
         )
+        second, active, slope = outs[:3]
         contract = (mats[layer][2], other)
+        if last:
+            c1 = outs[3]
         outs, others = contract_call(
-            4 + 3 * layer, active, hidden, contract, vec,
-            gy_full if last else None, [] if last else [mats[1][0]],
+            4 + 3 * layer, active, hidden, contract, vec, [] if last else [mats[1][0]]
         )
         pairs.append((attn, expand, contract))
         kept.append((normed, heads, o, lse, hidden, second, active, slope))
         x = outs[0]
         owns.append(x)
-        if last:
-            ck1, cs1 = outs[1:]
-        else:
+        if not last:
             attn = (mats[1][0], others[0])
     y0 = own_features(full)
 
@@ -1076,40 +1119,40 @@
     normed, heads, o, lse, hidden, second, active, slope = kept[1]
     (before, bend_sums1, y1), _ = bend_call(8, True, gy_full, contract, slope, owns[2], size, rows, [])
     layer_low, layer_high = pick(y0, y1), pick(y1, y0)
-    (ek1, es1, grad_hidden, low, narrow_sums1), (ct1,) = narrow_call(
-        9, before, own_rows(gy_full), expand, second, hidden, wide_vectors[1], [cs1]
-    )
-    total_c1, low = add(ck1, ct1, low)
-    (mixed, outer), (et1,) = scores_back_call(10, low, attn, heads, o, lse, [es1])
-    total_e1, mixed = add(ek1, et1, mixed)
-    part_c1, mixed = tie(scatter(total_c1), mixed)
-    (wk1, ws1, gx1_own, attend_sums1), (layer_got,) = attend_back_call(
-        11, True, mixed, outer, grad_hidden, owns[1], attn, normed, wide_vectors[1], [layer_high]
+    (grad_hidden, low, narrow_sums1, e1, _), _ = narrow_call(
+        9, True, before, own_rows(gy_full), expand, second, hidden, wide_vectors[1], []
+    )
+    (mixed, outer), (layer_got,) = scores_back_call(10, low, attn, heads, o, lse, [layer_high])
+    part_c1, mixed = tie(scatter(c1), mixed)
+    (w1, gx1_own, attend_sums1), (far_c1,) = attend_back_call(
+        11, True, mixed, outer, grad_hidden, owns[1], attn, normed, wide_vectors[1], [part_c1]
     )
     layer_outputs = jnp.concatenate([pick(layer_low, layer_got), pick(layer_got, layer_low)], 0)
 
     attn, expand, contract = pairs[0]
     normed, heads, o, lse, hidden, second, active, slope = kept[0]
-    (before, bend_sums0, gx1_full, ck0, cs0), (wt1,) = bend_call(
-        12, False, gx1_own, contract, slope, active, size, rows, [ws1]
-    )
-    total_w1, before = add(wk1, wt1, before)
-    part_e1, before = tie(scatter(total_e1), before)
-    (ek0, es0, grad_hidden, low, narrow_sums0), (ct0,) = narrow_call(
-        13, before, gx1_own, expand, second, hidden, wide_vectors[0], [cs0]
+    part_e1 = scatter(e1)
+    (before, bend_sums0, gx1_full, ck0, cs0), (far_e1,) = bend_call(
+        12, False, gx1_own, contract, slope, active, size, rows, [part_e1]
+    )
+    (grad_hidden, low, narrow_sums0, ek0, es0), (ct0,) = narrow_call(
+        13, False, before, gx1_own, expand, second, hidden, wide_vectors[0], [cs0]
     )
     total_c0, low = add(ck0, ct0, low)
-    part_w1, low = tie(scatter(total_w1), low)
     (mixed, outer), (et0,) = scores_back_call(14, low, attn, heads, o, lse, [es0])
     total_e0, mixed = add(ek0, et0, mixed)
+    part_w1, mixed = tie(scatter(w1), mixed)
     part_c0, mixed = tie(scatter(total_c0), mixed)
-    (wk0, _, gx0_own, attend_sums0, wt0), _ = attend_back_call(
+    (wk0, gx0_own, attend_sums0, wt0), _ = attend_back_call(
         15, False, mixed, outer, grad_hidden, owns[0], attn, normed, wide_vectors[0], []
     )
     total_w0, gx0_own = add(wk0, wt0, gx0_own)
-    part_e0, gx0_own = tie(scatter(total_e0), gx0_own)
-    input_grads, small_grads = finish_call(
+    part_e0 = scatter(total_e0)
+    input_grads, small_grads, far_w1, far_c0, far_e0 = finish_call(
         16,
+        part_w1,
+        part_c0,
+        part_e0,
         gx0_own,
         own_features(gx1_full),
         (attend_sums0, narrow_sums0, bend_sums0, attend_sums1, narrow_sums1, bend_sums1),
@@ -1118,12 +1161,16 @@
 
     late = [part_w1, part_e1, part_c1]
     part_w0, small_grads = tie(scatter(total_w0), small_grads)
-    early = [part_w0, part_e0, part_c0]
+    far_w0 = lax.ppermute(part_w0, "section", [(1, 0)])
+
     units = []
-    for second_layer, first_layer in zip(late, early):
-        stays = pick(first_layer, second_layer)
-        got = swap_sections(pick(second_layer, first_layer))
-        units.append(jnp.concatenate([pick(stays, got), pick(got, stays)], 1).astype(WIDE))
+    for late, far_late, early, far_early in (
+        (part_w1, far_w1, part_w0, far_w0),
+        (part_e1, far_e1, part_e0, far_e0),
+        (part_c1, far_c1, part_c0, far_c0),
+    ):
+        whole = jnp.concatenate([early, far_early], 1).astype(WIDE)
+        units.append(pick(whole, late.astype(WIDE) + far_late.astype(WIDE)))
     attn_part, expand_part, contract_part = units
 
     return (

time: 733 us -> 708 us (0.966)
  Pallas kernels: 593 us -> 579 us
  other arithmetic: 33 us -> 23.8 us
    pallas_call x14, Pallas kernels: 511 us -> 491 us  [launch(): pl.pallas_call(kernel, out_shape=(*outs, *[shape(s.shape, s.dtype) for s...]
    ppermute x0 -> x1, waiting for transfers between devices: none -> 9.34 us  [on_device(): far_w0 = lax.ppermute(part_w0, 'section', [(1, 0)])]
    convert_element_type x6 -> x3, other arithmetic: 18.7 us -> 9.54 us  [add(): total = (keep.astype(WIDE) + got.astype(WIDE)).astype(LOW)]
    ppermute x5 -> x2, waiting for transfers between devices: 13.6 us -> 4.6 us  [swap_sections(): return lax.ppermute(value, 'section', [(0, 1), (1, 0)])]
    unnamed x54 -> x44, local copies, waits for them, and re-layouts: 17.3 us -> 16.9 us
  transfers between devices with their start and end apart: 17 -> 15, of which waited for: 4 -> 4; matrix products, arithmetic and copies ran while one was open for 7% -> 6% of each run, Pallas kernels for 66% -> 77%
where the time goes in v6:
time: 708 us; the launch traced here: 702 us
  Pallas kernels  579 us (82%)
  waiting for transfers between devices  45.9 us (6%)
  local copies, waits for them, and re-layouts  31.5 us (4%)
  other arithmetic  23.8 us (3%)
  between operations  15.1 us (2%)
    pallas_call x14, Pallas kernels, launch(): pl.pallas_call(kernel, out_shape=(*outs, *[shape(s.shape, s.dtype) for s...  491 us
    pallas_call x1, Pallas kernels, finish_call(): pl.pallas_call(finish_kernel, out_shape=outs, in_specs=[ANY] * 3 + [VM] *...  44.5 us
    pallas_call x1, Pallas kernels, start_call(): pl.pallas_call(start_kernel, out_shape=outs, in_specs=[ANY] * 4, out_spec...  43.5 us
    all_gather x6, waiting for transfers between devices, on_device(): mats[layer].append(lax.all_gather(block, 'row', axis=0, tiled=True))  30 us
    unnamed x44, local copies, waits for them, and re-layouts  16.9 us
  transfers between devices with their start and end apart: 15, of which 4 were waited for; matrix products, arithmetic and copies ran while one was open for 6% of the time, Pallas kernels for 77%

profile of v6, /device:TPU:0, one launch (start us, length us, event | category | flops | bytes accessed | tf_op | source)
XLA Modules:
  0.0 701.8 jit_solution(13405869294837748271)
XLA Ops:
  7.2 1.1 copy.38
  8.4 1.5 copy.37
  10.2 1.0 broadcast_select_fusion.9
  11.2 2.9 collective-permute-start
  14.3 2.5 copy.41.tokens_ref
  16.8 2.6 copy.42.cotangent_ref
  19.5 0.8 concatenate.18
  20.9 1.0 pad_maximum_fusion.raw_ref
  21.9 1.9 collective-permute-done
  23.8 1.0 broadcast_select_fusion.4
  24.8 43.5 %shard_map.245 = (bf16[1024,1280]{1,0:T(8,128)(2,1)}, bf16[1024,1280]{1,0:T(8,128)(2,1)}, bf16[2,4,16,320]{3,2,1,0:T(8,128)(2,1)}, bf16[2,320,640]{2,1,0:T(8,128)(2,1)}) custom-call(bf16[2048,320]{1,0:T(8,128)(2,1)} %copy.41.tokens_ref, bf16[2048,320]{1,0:T(8,128)(2,1)} %copy.42.cotangent_ref, bf16[16,320]{1,0:T(8,128)(2,1)} %pad.8.small_ref, ...), custom_call_target="tpu_custom_call" | custom-call | flops 30000001024 | bytes 31457280 | tf_op jit(solution)/shard_map/pallas_call | solution.py:815
  68.4 2.4 bitcast_select_fusion.2
  70.9 0.7 all-gather.11.cloned.1.call-update
  77.1 2.0 constant_dynamic-slice_fusion.2.refs_1_
  79.1 29.8 %all-gather.9.cloned.1.call-done.refs_5_.refs_1_.refs_2_ = bf16[1280,640]{1,0:T(8,128)(2,1)} async-done(((bf16[320,640]{1,0:T(8,128)(2,1)}), bf16[1280,640]{1,0:T(8,128)(2,1)}) %all-gather.9.cloned.1.call-update) | async-done | bytes 1638416 | tf_op jit(solution)/shard_map/all_gather | solution.py:1062
  108.9 2.7 collective-permute-done.1.refs_2_.refs_5_
  111.6 1.2 copy-done.17
  112.8 39.1 %shard_map.246 = (bf16[16,128]{1,0:T(8,128)(2,1)}, bf16[1024,1280]{1,0:T(8,128)(2,1)}, bf16[15,1024,64]{2,1,0:T(8,128)(2,1)}, bf16[1024,320]{1,0:T(8,128)(2,1)},...) custom-call(bf16[1024,1280]{1,0:T(8,128)(2,1)} %get-tuple-element.99.refs_0_, ...), custom_call_target="tpu_custom_call" | custom-call | flops 30000001024 | bytes 31457280 | tf_op jit(solution)/shard_map/pallas_call | solution.py:787
  151.9 38.4 %shard_map.247 = (bf16[1024,1280]{1,0:T(8,128)(2,1)}, bf16[1024,1280]{1,0:T(8,128)(2,1)}, bf16[1024,1280]{1,0:T(8,128)(2,1)}, bf16[1280,640]{1,0:T(8,128)(2,1)}) custom-call(bf16[256,1280]{1,0:T(8,128)(2,1)} %get-tuple-element.103.refs_0_, bf16[1280,640]{1,0:T(8,128)(2,1)} %all-gather.9.cloned.1.call-done.refs_5_.refs_1_.refs_2_, ...), custom_call_target="tpu_custom_call" | custom-call | flops 30000001024 | bytes 31457280 | tf_op jit(solution)/shard_map/pallas_call | solution.py:787
  190.3 38.6 %shard_map.248 = (bf16[256,1280]{1,0:T(8,128)(2,1)}, bf16[1280,640]{1,0:T(8,128)(2,1)}) custom-call(bf16[1024,1280]{1,0:T(8,128)(2,1)} %get-tuple-element.105.refs_0_.refs_4_, f32[256,1280]{1,0:T(8,128)} %get-tuple-element.106.refs_1_.refs_5_, bf16[1280,640]{1,0:T(8,128)(2,1)} %all-gather.11.cloned.1.call-done.refs_4_.refs_2_.refs_1_, ...), custom_call_target="tpu_custom_call" | custom-call | flops 30000001024 | bytes 31457280 | tf_op jit(solution)/shard_map/pallas_call | solution.py:787
  228.9 51.7 %shard_map.249 = (bf16[1024,1280]{1,0:T(8,128)(2,1)}, bf16[1024,1280]{1,0:T(8,128)(2,1)}, bf16[15,1024,64]{2,1,0:T(8,128)(2,1)}, bf16[1024,320]{1,0:T(8,128)(2,1...) custom-call(bf16[256,1280]{1,0:T(8,128)(2,1)} %get-tuple-element.108.refs_0_, ...), custom_call_target="tpu_custom_call" | custom-call | flops 30000001024 | bytes 31457280 | tf_op jit(solution)/shard_map/pallas_call | solution.py:787
  280.7 37.9 %shard_map.250 = (bf16[1024,1280]{1,0:T(8,128)(2,1)}, bf16[1024,1280]{1,0:T(8,128)(2,1)}, bf16[1024,1280]{1,0:T(8,128)(2,1)}, bf16[1280,1280]{1,0:T(8,128)(2,1)}, bf16[1280,640]{1,0:T(8,128)(2,1)}) custom-call(bf16[256,1280]{1,0:T(8,128)(2,1)} %get-tuple-element.112.refs_0_, bf16[1280,640]{1,0:T(8,128)(2,1)} %all-gather.15.cloned.1.call-done.refs_5_.refs_1_.refs_2_, ...), custom_call_target="tpu_custom_call" | custom-call | flops 30000001024 | bytes 31457280 | tf_op jit(solution)/shard_map/pallas_call | solution.py:787
  318.9 24.0 %shard_map.251.refs_4_ = bf16[256,1280]{1,0:T(8,128)(2,1)} custom-call(bf16[1024,1280]{1,0:T(8,128)(2,1)} %get-tuple-element.116.refs_0_, f32[256,1280]{1,0:T(8,128)} %get-tuple-element.117.refs_1_.refs_5_, bf16[1280,640]{1,0:T(8,128)(2,1)} %all-gather.17.cloned.1.call-done.refs_5_.refs_2_.refs_1_, bf16[1280,640]{1,0:T(8,128)(2,1)} %get-tuple-element.114.refs_3_.refs_2_, ...), custom_call_target="tpu_custom_call" | custom-call | flops 30000001024 | bytes 31457280 | tf_op jit(solution)/shard_map/pallas_call | solution.py:787
  342.9 14.3 %shard_map.252 = (bf16[1024,1280]{1,0:T(8,128)(2,1)}, f32[8,1280]{1,0:T(8,128)}, bf16[1024,320]{1,0:T(8,128)(2,1)}) custom-call(bf16[1024,1280]{1,0:T(8,128)(2,1)} %get-tuple-element.111.refs_4_.refs_0_, bf16[1280,640]{1,0:T(8,128)(2,1)} %all-gather.17.cloned.1.call-done.refs_5_.refs_2_.refs_1_, bf16[1280,640]{1,0:T(8,128)(2,1)} %get-tuple-element.114.refs_3_.refs_2_, ...), custom_call_target="tpu_custom_call" | custom-call | flops 30000001024 | bytes 31457280 | tf_op jit(solution)/shard_map/pallas_call | solution.py:787
  357.2 26.7 %shard_map.253 = (f32[256,1280]{1,0:T(8,128)}, bf16[256,1280]{1,0:T(8,128)(2,1)}, f32[8,1280]{1,0:T(8,128)}, bf16[1280,1280]{1,0:T(8,128)(2,1)}, bf16[16,128]{1,0:T(8,128)(2,1)}) custom-call(bf16[1024,1280]{1,0:T(8,128)(2,1)} %get-tuple-element.119.refs_0_, bf16[256,1280]{1,0:T(8,128)(2,1)} %constant_dynamic-slice_fusion.2.refs_1_, ...), custom_call_target="tpu_custom_call" | custom-call | flops 30000001024 | bytes 31457280 | tf_op jit(solution)/shard_map/pallas_call | solution.py:787
  384.5 2.2 constant_dynamic-slice_fusion.1.refs_3_
  386.7 1.3 broadcast_select_fusion.2.refs_6_
  388.1 39.9 %shard_map.254 = (bf16[1024,960]{1,0:T(8,128)(2,1)}, bf16[1280,320]{1,0:T(8,128)(2,1)}, bf16[1024,320]{1,0:T(8,128)(2,1)}) custom-call(bf16[256,1280]{1,0:T(8,128)(2,1)} %get-tuple-element.121.refs_0_, bf16[1280,640]{1,0:T(8,128)(2,1)} %all-gather.13.cloned.1.call-done.refs_5_.refs_1_.refs_4_, bf16[1280,640]{1,0:T(8,128)(2,1)} %get-tuple-element.109.refs_2_.refs_5_, ...), custom_call_target="tpu_custom_call" | custom-call | flops 30000001024 | bytes 31457280 | tf_op jit(solution)/shard_map/pallas_call | solution.py:787
  428.0 26.0 %shard_map.255 = (bf16[1280,1280]{1,0:T(8,128)(2,1)}, bf16[256,1280]{1,0:T(8,128)(2,1)}, f32[8,1280]{1,0:T(8,128)}, bf16[320,1280]{1,0:T(8,128)(2,1)}) custom-call(bf16[1024,960]{1,0:T(8,128)(2,1)} %get-tuple-element.128.refs_0_, bf16[1280,320]{1,0:T(8,128)(2,1)} %get-tuple-element.129.refs_1_, f32[256,1280]{1,0:T(8,128)} %get-tuple-element.130.refs_2_, ...), custom_call_target="tpu_custom_call" | custom-call | flops 30000001024 | bytes 31457280 | tf_op jit(solution)/shard_map/pallas_call | solution.py:787
  454.0 1.8 broadcast_select_fusion.1
  456.0 1.7 copy.46
  457.7 28.9 %shard_map.256 = (bf16[1024,1280]{1,0:T(8,128)(2,1)}, f32[8,1280]{1,0:T(8,128)}, bf16[1024,1280]{1,0:T(8,128)(2,1)}, bf16[1280,640]{1,0:T(8,128)(2,1)}, bf16[128...) custom-call(bf16[256,1280]{1,0:T(8,128)(2,1)} %get-tuple-element.134.refs_0_.refs_1_, ...), custom_call_target="tpu_custom_call" | custom-call | flops 30000001024 | bytes 31457280 | tf_op jit(solution)/shard_map/pallas_call | solution.py:787
  486.7 38.8 %shard_map.257 = (f32[256,1280]{1,0:T(8,128)}, bf16[256,1280]{1,0:T(8,128)(2,1)}, f32[8,1280]{1,0:T(8,128)}, bf16[1280,640]{1,0:T(8,128)(2,1)}, bf16[1280,640]{1,0:T(8,128)(2,1)}, /*index=5*/bf16[1280,640]{1,0:T(8,128)(2,1)}) custom-call(bf16[1024,1280]{1,0:T(8,128)(2,1)} %get-tuple-element.137.refs_0_, ...), custom_call_target="tpu_custom_call" | custom-call | flops 30000001024 | bytes 31457280 | tf_op jit(solution)/shard_map/pallas_call | solution.py:787
  525.6 3.0 add_convert_fusion.2
  528.9 41.3 %shard_map.258 = (bf16[1024,960]{1,0:T(8,128)(2,1)}, bf16[1280,320]{1,0:T(8,128)(2,1)}, bf16[1280,640]{1,0:T(8,128)(2,1)}) custom-call(bf16[256,1280]{1,0:T(8,128)(2,1)} %get-tuple-element.144.refs_0_, bf16[1280,640]{1,0:T(8,128)(2,1)} %all-gather.7.cloned.1.call-done.refs_1_.refs_4_, bf16[1280,640]{1,0:T(8,128)(2,1)} %copy-done.17, ...), custom_call_target="tpu_custom_call" | custom-call | flops 30000001024 | bytes 31457280 | tf_op jit(solution)/shard_map/pallas_call | solution.py:787
  570.2 3.0 add_convert_fusion.1
  573.2 2.4 constant_dynamic-slice_fusion.far_ref
  576.0 45.5 %shard_map.259 = (bf16[1280,640]{1,0:T(8,128)(2,1)}, bf16[256,1280]{1,0:T(8,128)(2,1)}, f32[8,1280]{1,0:T(8,128)}, bf16[1280,640]{1,0:T(8,128)(2,1)}) custom-call(bf16[1024,960]{1,0:T(8,128)(2,1)} %get-tuple-element.157.refs_0_, bf16[1280,320]{1,0:T(8,128)(2,1)} %get-tuple-element.158.refs_1_, f32[256,1280]{1,0:T(8,128)} %get-tuple-element.159.refs_2_, ...), custom_call_target="tpu_custom_call" | custom-call | flops 30000001024 | bytes 31457280 | tf_op jit(solution)/shard_map/pallas_call | solution.py:787
  621.5 3.5 add_convert_fusion
  625.1 44.5 %shard_map.260 = (f32[2048,320]{1,0:T(8,128)}, f32[16,320]{1,0:T(8,128)}, bf16[320,1280]{1,0:T(8,128)(2,1)}, bf16[320,640]{1,0:T(8,128)(2,1)}, bf16[320,640]{1,0:T(8,128)(2,1)}) custom-call(bf16[320,1280]{1,0:T(8,128)(2,1)} %reduce-scatter.9.cloned.1.call-done.late_ref, bf16[320,640]{1,0:T(8,128)(2,1)} %reduce-scatter.13.cloned.1.call-done.early1_ref, ...), custom_call_target="tpu_custom_call" | custom-call | flops 30000001024 | bytes 31457280 | tf_op jit(solution)/shard_map/pallas_call | solution.py:981
  669.6 3.5 copy.47
  673.2 3.6 select_bitcast_fusion
  676.8 0.7 reshape.45
  677.5 1.3 collective-permute-start.2
  680.0 9.3 %collective-permute-done.2 = bf16[320,640]{1,0:T(8,128)(2,1)S(1)} collective-permute-done((bf16[320,640]{1,0:T(8,128)(2,1)}, bf16[320,640]{1,0:T(8,128)(2,1)S(1)}, u32[]{:S(2)}, u32[]{:S(2)}) %collective-permute-start.2) | collective-permute-done | bytes 409632 | tf_op jit(solution)/shard_map/ppermute | solution.py:1164
  689.3 1.8 add_select_fusion
  691.4 1.0 copy.49
  692.9 1.6 copy.48
  (98 shorter events, 10.4 us)
Async XLA Ops:
  7.2 65.7 %all-gather.7.cloned.1.call-start = ((), (), s32[]{:S(2)}) async-start(), calls=%async_computation.6 | async-start | bytes 2048000 | tf_op jit(solution)/shard_map/all_gather | solution.py:1062
  9.9 4.2 copy-start.1
  10.1 4.0 copy-start.12
  11.2 12.6 %collective-permute-start = (bf16[320,640]{1,0:T(8,128)(2,1)}, bf16[320,640]{1,0:T(8,128)(2,1)S(1)}, u32[]{:S(2)}, u32[]{:S(2)}) collective-permute-start(bf16[320,640]{1,0:T(8,128)(2,1)} %get-tuple-element.210), channel_id=1, source_target_pairs={{0,16},{16,0},{1,17},{17,1},{2,18},{18,2},{3,19},{19,3},{4,20},{20... | collective-permute-start | bytes 1228808 | tf_op jit(solution)/shard_map/ppermute | solution.py:995
  16.8 2.6 copy-start.13
  16.8 2.6 copy-start.14
  16.8 2.6 copy-start.15
  16.8 2.6 copy-start.16
  16.8 4.0 copy-start
  24.8 84.1 %all-gather.9.cloned.1.call-start = ((), (), s32[]{:S(2)}) async-start(), calls=%async_computation.7 | async-start | bytes 2048000 | tf_op jit(solution)/shard_map/all_gather | solution.py:1062
  70.8 2.1 copy-start.10
  70.8 81.1 %all-gather.11.cloned.1.call-start = ((), (), s32[]{:S(2)}) async-start(), calls=%async_computation.8 | async-start | bytes 2048000 | tf_op jit(solution)/shard_map/all_gather | solution.py:1062
  71.6 118.8 %all-gather.13.cloned.1.call-start = ((), (), s32[]{:S(2)}) async-start(), calls=%async_computation.9 | async-start | bytes 2048000 | tf_op jit(solution)/shard_map/all_gather | solution.py:1062
  72.1 156.8 %all-gather.15.cloned.1.call-start = ((), (), s32[]{:S(2)}) async-start(), calls=%async_computation.10 | async-start | bytes 2048000 | tf_op jit(solution)/shard_map/all_gather | solution.py:1062
  72.7 208.0 %all-gather.17.cloned.1.call-start = ((), (), s32[]{:S(2)}) async-start(), calls=%async_computation.11 | async-start | bytes 2048000 | tf_op jit(solution)/shard_map/all_gather | solution.py:1062
  72.9 38.7 %collective-permute-start.1 = (bf16[1280,640]{1,0:T(8,128)(2,1)}, bf16[1280,640]{1,0:T(8,128)(2,1)S(1)}, u32[]{:S(2)}, u32[]{:S(2)}) collective-permute-start(bf16[1280,640]{1,0:T(8,128)(2,1)} %all-gather.7.cloned.1.call-done.refs_1_.refs_4_), channel_id=1, source_target_pairs={{0,16},{16,0},{1,17},{17,1},{2,18},{18,2},{3,19},{19,3},{4,20},{20... | collective-permute-start | bytes 4915208 | tf_op jit(solution)/shard_map/ppermute | solution.py:995
  76.4 351.6 %reduce-scatter.7.cloned.1.call-start = ((), (), s32[]{:S(2)}) async-start(), calls=%async_computation.12 | async-start | bytes 4096000 | tf_op jit(solution)/shard_map/reduce_scatter | solution.py:1113
  111.6 1.2 copy-start.17
  318.7 139.1 %reduce-scatter.11.cloned.1.call-start = ((), (), s32[]{:S(2)}) async-start(), calls=%async_computation.14 | async-start | bytes 4096000 | tf_op jit(solution)/shard_map/reduce_scatter | solution.py:1113
  384.0 2.7 copy-start.2
  384.0 2.7 copy-start.5
  384.0 192.0 %reduce-scatter.9.cloned.1.call-start = ((), (), s32[]{:S(2)}) async-start(), calls=%async_computation.13 | async-start | bytes 4096000 | tf_op jit(solution)/shard_map/reduce_scatter | solution.py:1113
  454.0 122.0 %reduce-scatter.13.cloned.1.call-start = ((), (), s32[]{:S(2)}) async-start(), calls=%async_computation.15 | async-start | bytes 2048000 | tf_op jit(solution)/shard_map/reduce_scatter | solution.py:1113
  486.7 38.9 %copy-start.4 = (bf16[1280,640]{1,0:T(8,128)(2,1)S(1)}, bf16[1280,640]{1,0:T(8,128)(2,1)}, u32[]{:S(2)}) copy-start(bf16[1280,640]{1,0:T(8,128)(2,1)} %get-tuple-element.141) | copy-start | bytes 4915204
  528.6 96.5 %reduce-scatter.15.cloned.1.call-start = ((), (), s32[]{:S(2)}) async-start(), calls=%async_computation.16 | async-start | bytes 2048000 | tf_op jit(solution)/shard_map/reduce_scatter | solution.py:1113
  528.8 41.4 %copy-start.3 = (bf16[1280,640]{1,0:T(8,128)(2,1)S(1)}, bf16[1280,640]{1,0:T(8,128)(2,1)}, u32[]{:S(2)}) copy-start(bf16[1280,640]{1,0:T(8,128)(2,1)} %get-tuple-element.140) | copy-start | bytes 4915204
  575.7 101.1 %reduce-scatter.17.cloned.1.call-start = ((), (), s32[]{:S(2)}) async-start(), calls=%async_computation.17 | async-start | bytes 2048000 | tf_op jit(solution)/shard_map/reduce_scatter | solution.py:1113
  669.6 3.6 copy-start.6
  669.6 3.6 copy-start.7
  669.6 3.6 copy-start.8
  669.6 3.6 copy-start.9
  673.2 3.6 copy-start.11
  677.5 11.8 %collective-permute-start.2 = (bf16[320,640]{1,0:T(8,128)(2,1)}, bf16[320,640]{1,0:T(8,128)(2,1)S(1)}, u32[]{:S(2)}, u32[]{:S(2)}) collective-permute-start(bf16[320,640]{1,0:T(8,128)(2,1)} %reduce-scatter.17.cloned.1.call-done), channel_id=1, source_target_pairs={{16,0},{17,1},{18,2},{19,3},{20,4},{21,5},{22,6},{23,7},{24,8},{25... | collective-permute-start | bytes 1228808 | tf_op jit(solution)/shard_map/ppermute | solution.py:1164
Sparse Core Ops, SparseCore 0:
  24.9 39.6 all-gather.6
  70.9 37.9 all-gather.8
  111.1 37.0 all-gather.10
  149.5 37.0 all-gather.12
  188.6 37.0 all-gather.14
  227.7 37.0 all-gather.16
  318.8 62.5 reduce-scatter.6
  384.2 62.5 reduce-scatter.10
  454.1 62.0 reduce-scatter.8
  528.7 37.3 reduce-scatter.12
  575.8 36.6 reduce-scatter.14
  625.2 38.4 reduce-scatter.16

commit v7 on v6

--- a/solution.py
+++ b/solution.py
@@ -224,6 +224,9 @@
 
 class Halves:
     def __init__(self, pair, whole, sems, slot):
+        if pair[0].shape[1] == whole.shape[1]:
+            self.copies = [pltpu.make_async_copy(pair[0], whole, sems.at[slot])]
+            return
         section = lax.axis_index("section")
         half = whole.shape[1] // 2
         self.copies = []
@@ -301,40 +304,83 @@
 
 
 def start_kernel(
-    tokens_ref, cotangent_ref, small_ref, raw_ref, x_ref, g_ref, vectors_ref, got_ref,
-    x4, g4, s4, other4, x_sems, g_sems, s_sems, local_sems,
+    tokens_ref, cotangent_ref, small_ref, keep_ref, sent_ref, contract_ref,
+    x_ref, g_ref, vectors_ref, got_ref, got_contract_ref, mine_ref, far_ref,
+    x4, g4, s4, other4, x_sems, g_sems, s_sems, row_sems, far_sems, local_sems,
 ):
-    section = lax.axis_index("section")
+    section, row = lax.axis_index("section"), lax.axis_index("row")
+    away = 1 - section
     group = Group(x_ref.shape[0] // 4)
-    length = x_ref.shape[0]
+    length, block = x_ref.shape[0], keep_ref.shape[0]
+    count = mine_ref.shape[0] // block
+    others = [lax.rem(row + d, count) for d in range(1, count)]
     loads = []
     rows = pl.ds(pl.multiple_of(section * length, length), length)
     for n, (source, into) in enumerate(((tokens_ref.at[rows], x4), (cotangent_ref.at[rows], g4), (small_ref, s4))):
         loads.append(pltpu.make_async_copy(source, into.at[group.me], local_sems.at[n]))
         loads[-1].start()
-    group.greet(True, False)
-    blocks = push(raw_ref, got_ref, s_sems, 3 * PARTS + 1, 1 - section, "section")
-    blocks.start()
+    group.greet(True, False, others)
+
+    def place(owner):
+        return pl.ds(pl.multiple_of(owner * block, block), block)
+
+    raw = push(sent_ref, got_ref, s_sems, 3 * PARTS + 1, away, "section")
+    raw.start()
     gathers = [Gather(group, x4, x_sems, True), Gather(group, s4, s_sems, True), Gather(group, g4, g_sems, True)]
     for gather, load in zip(gathers, (loads[0], loads[2], loads[1])):
         load.wait()
         gather.start()
+    own = mine_ref.at[place(row)]
+
+    @pl.when(section == 0)
+    def _():
+        copy = pltpu.make_async_copy(keep_ref, own, local_sems.at[3])
+        copy.start()
+        copy.wait()
+
+    raw.wait_recv()
+
+    @pl.when(section == 1)
+    def _():
+        copy = pltpu.make_async_copy(got_ref, own, local_sems.at[3])
+        copy.start()
+        copy.wait()
+
+    spread = [push(own, own, row_sems, n, other, "row") for n, other in enumerate(others)]
+    for copy in spread:
+        copy.start()
+    passed = [push(own, far_ref.at[place(row)], far_sems, 0, away, "section")]
+    passed[0].start()
     for gather in gathers:
         gather.sibling()
         gather.relay()
+    swap = None
+    for d in range(1, count):
+        spread[d - 1].wait_recv()
+        piece = place(lax.rem(row + count - d, count))
+        passed.append(push(mine_ref.at[piece], far_ref.at[piece], far_sems, d, away, "section"))
+        passed[-1].start()
+    for gather in gathers:
         gather.diagonal()
-    swap = push(s4, other4, s_sems, 3 * PARTS, 1 - section, "section")
+    swap = push(s4, other4, s_sems, 3 * PARTS, away, "section")
     swap.start()
+    contract = push(contract_ref, got_contract_ref, s_sems, 3 * PARTS + 2, away, "section")
+    contract.start()
     width = x4.shape[2]
     for c in range(x4.shape[0]):
         x_ref[:, c * width : (c + 1) * width] = x4[c]
         g_ref[:, c * width : (c + 1) * width] = g4[c]
     swap.wait()
-    blocks.wait()
     vectors_ref[section] = s4[...]
-    vectors_ref[1 - section] = other4[...]
+    vectors_ref[away] = other4[...]
     for gather in gathers:
         gather.done()
+    for copy in spread:
+        copy.wait_send()
+    for copy in passed:
+        copy.wait()
+    raw.wait_send()
+    contract.wait()
 
 
 def attend_kernel(
@@ -805,27 +851,32 @@
     return results[:n_out], results[n_out:]
 
 
-def start_call(number, tokens, cotangent, small, raw, columns):
+def start_call(number, tokens, cotangent, small, keep, sent, contract, columns, row_count):
     width = tokens.shape[1]
     size = width * columns
     kinds = small.shape[0]
-    outs = (shape((LENGTH, size)), shape((LENGTH, size)), shape((2, columns, kinds, width)), shape(raw.shape))
+    half = shape((keep.shape[0] * row_count, keep.shape[1]))
+    outs = (
+        shape((LENGTH, size)), shape((LENGTH, size)), shape((2, columns, kinds, width)),
+        shape(sent.shape), shape(contract.shape), half, half,
+    )
     blocks = pltpu.VMEM((columns, LENGTH, width), LOW)
     vectors = pltpu.VMEM((columns, kinds, width), LOW)
+    many = pltpu.SemaphoreType.DMA((2, row_count))
     return pl.pallas_call(
         start_kernel,
         out_shape=outs,
-        in_specs=[ANY] * 4,
-        out_specs=(VM, VM, VM, ANY),
+        in_specs=[ANY] * 6,
+        out_specs=(VM,) * 3 + (ANY,) * 4,
         scratch_shapes=[
             blocks, blocks, vectors, vectors, PAIRS, PAIRS,
-            pltpu.SemaphoreType.DMA((2, 3 * PARTS + 2)), LOCAL,
+            pltpu.SemaphoreType.DMA((2, 3 * PARTS + 3)), many, many, LOCAL,
         ],
         compiler_params=pltpu.CompilerParams(
             collective_id=number, has_side_effects=True, vmem_limit_bytes=GRANT
         ),
         cost_estimate=pl.CostEstimate(flops=int(3e10), bytes_accessed=30 * MEBI, transcendentals=0),
-    )(tokens, cotangent, small, raw)
+    )(tokens, cotangent, small, keep, sent, contract)
 
 
 def attend_call(number, gathered, x, pair, vec, bias, rows, width, swaps):
@@ -1052,14 +1103,22 @@
     )
     filled = small.shape[0]
     small = jnp.pad(small, ((0, -filled % 16), (0, 0)))
-    got_attend = swap_sections(sent_blocks[0])
-    raw = jnp.stack(sent_blocks[1:])
-    got_attend, raw = lax.optimization_barrier((got_attend, raw))
-    x0_full, gy_full, vectors, got_blocks = start_call(1, tokens, cotangent, small, raw, columns)
-    mats = [[], []]
-    for own, got in zip(kept_blocks, (got_attend, got_blocks[0], got_blocks[1])):
-        for layer, block in enumerate((pick(own, got), pick(got, own))):
-            mats[layer].append(lax.all_gather(block, "row", axis=0, tiled=True))
+    got_expand = swap_sections(sent_blocks[1])
+    sent_attend, got_expand = lax.optimization_barrier((sent_blocks[0], got_expand))
+    x0_full, gy_full, vectors, got_attend, got_contract, mine, far = start_call(
+        1, tokens, cotangent, small, kept_blocks[0], sent_attend, units[2], columns, lax.axis_size("row")
+    )
+
+    def gather_blocks(block):
+        return lax.all_gather(block, "row", axis=0, tiled=True)
+
+    half = units[2].shape[1] // 2
+    mats = [
+        [None, gather_blocks(pick(kept_blocks[1], got_expand)), None],
+        [gather_blocks(pick(got_attend, kept_blocks[0])), gather_blocks(pick(got_expand, kept_blocks[1])), None],
+    ]
+    mats[0][2] = gather_blocks(pick(kept_blocks[2], got_contract[:, half:]))
+    mats[1][2] = gather_blocks(pick(got_contract, units[2]))
     vectors = vectors.astype(WIDE)
     wide_vectors = jnp.swapaxes(vectors[:, :, :6], 1, 2).reshape(2, 6, size)
     wide_vectors = jnp.pad(wide_vectors, ((0, 0), (0, 2), (0, 0)))
@@ -1075,7 +1134,7 @@
     def own_features(full):
         return lax.dynamic_slice_in_dim(full, column * width, width, 1)
 
-    attn = (mats[0][0], swap_sections(mats[0][0]))
+    attn = (mine, far)
     x = x0_full
     kept, pairs = [], []
     owns = [own_rows(x0_full)]
@@ -1086,12 +1145,12 @@
             2 + 3 * layer, not last, x, attn, vec, attend_biases[layer], rows, width, [mats[layer][1]]
         )
         expand = (mats[layer][1], other)
-        outs, (other,) = widen_call(
+        outs, others = widen_call(
             3 + 3 * layer, second_own, expand, expand_biases[layer],
-            gy_full if last else None, [mats[layer][2]],
+            gy_full if last else None, [] if last else [mats[0][2]],
         )
         second, active, slope = outs[:3]
-        contract = (mats[layer][2], other)
+        contract = (mats[layer][2], mats[layer][2] if last else others[0])
         if last:
             c1 = outs[3]
         outs, others = contract_call(

time: 708 us -> 733 us (1.035)
  Pallas kernels: 579 us -> 640 us
  waiting for transfers between devices: 45.9 us -> 11 us
    pallas_call x1, Pallas kernels: 43.5 us -> 107 us  [start_call(): pl.pallas_call(start_kernel, out_shape=outs, in_specs=[ANY] * 6, out_spec...]
    all_gather x6 -> x5, waiting for transfers between devices: 30 us -> 0.08 us  [gather_blocks(): return lax.all_gather(block, 'row', axis=0, tiled=True)]
    pallas_call x14, Pallas kernels: 491 us -> 482 us  [launch(): pl.pallas_call(kernel, out_shape=(*outs, *[shape(s.shape, s.dtype) for s...]
    unnamed x44 -> x56, local copies, waits for them, and re-layouts: 16.9 us -> 13.8 us
  transfers between devices with their start and end apart: 15 -> 13, of which waited for: 4 -> 2; matrix products, arithmetic and copies ran while one was open for 6% -> 6% of each run, Pallas kernels for 77% -> 88%
where the time goes in v7:
time: 733 us; the launch traced here: 726 us
  Pallas kernels  640 us (87%)
  local copies, waits for them, and re-layouts  27.6 us (4%)
  other arithmetic  27.2 us (4%)
  between operations  14.9 us (2%)
  waiting for transfers between devices  11 us (2%)
    pallas_call x14, Pallas kernels, launch(): pl.pallas_call(kernel, out_shape=(*outs, *[shape(s.shape, s.dtype) for s...  482 us
    pallas_call x1, Pallas kernels, start_call(): pl.pallas_call(start_kernel, out_shape=outs, in_specs=[ANY] * 6, out_spec...  107 us
    pallas_call x1, Pallas kernels, finish_call(): pl.pallas_call(finish_kernel, out_shape=outs, in_specs=[ANY] * 3 + [VM] *...  51 us
  transfers between devices with their start and end apart: 13, of which 2 were waited for; matrix products, arithmetic and copies ran while one was open for 6% of the time, Pallas kernels for 88%

profile of v7, /device:TPU:0, one launch (start us, length us, event | category | flops | bytes accessed | tf_op | source)
XLA Modules:
  0.0 726.3 jit_solution(5955999961162306393)
XLA Ops:
  7.2 1.2 broadcast_select_fusion.9
  8.5 3.0 collective-permute-start
  11.5 0.7 reduce
  12.3 1.2 copy.39
  14.2 1.6 copy.41.tokens_ref
  15.8 2.6 copy.42.cotangent_ref
  19.1 1.2 broadcast_select_fusion.10
  20.3 0.8 collective-permute-done
  21.1 2.0 broadcast_select_fusion.6
  23.2 107.3 %shard_map.245 = (bf16[1024,1280]{1,0:T(8,128)(2,1)}, bf16[1024,1280]{1,0:T(8,128)(2,1)}, bf16[2,4,16,320]{3,2,1,0:T(8,128)(2,1)}, bf16[320,640]{1,0:T(8,128)(2,...) custom-call(bf16[2048,320]{1,0:T(8,128)(2,1)} %copy.41.tokens_ref, ...), custom_call_target="tpu_custom_call" | custom-call | flops 30000001024 | bytes 31457280 | tf_op jit(solution)/shard_map/pallas_call | solution.py:866
  130.5 1.9 fusion
  132.5 0.8 broadcast_select_fusion.5
  134.1 0.7 squeeze.48.refs_3_
  134.8 0.7 squeeze.45.refs_3_
  135.6 0.7 squeeze.47.refs_4_
  137.7 1.0 broadcast_select_fusion
  138.7 2.0 constant_dynamic-slice_fusion.2.refs_1_
  140.7 39.5 %shard_map.246 = (bf16[16,128]{1,0:T(8,128)(2,1)}, bf16[1024,1280]{1,0:T(8,128)(2,1)}, bf16[15,1024,64]{2,1,0:T(8,128)(2,1)}, bf16[1024,320]{1,0:T(8,128)(2,1)},...) custom-call(bf16[1024,1280]{1,0:T(8,128)(2,1)} %get-tuple-element.101.refs_0_, ...), custom_call_target="tpu_custom_call" | custom-call | flops 30000001024 | bytes 31457280 | tf_op jit(solution)/shard_map/pallas_call | solution.py:833
  180.2 38.4 %shard_map.247 = (bf16[1024,1280]{1,0:T(8,128)(2,1)}, bf16[1024,1280]{1,0:T(8,128)(2,1)}, bf16[1024,1280]{1,0:T(8,128)(2,1)}, bf16[1280,640]{1,0:T(8,128)(2,1)}) custom-call(bf16[256,1280]{1,0:T(8,128)(2,1)} %get-tuple-element.106.refs_0_, bf16[1280,640]{1,0:T(8,128)(2,1)} %all-gather.6.cloned.1.call-done.refs_5_.refs_1_.refs_2_, ...), custom_call_target="tpu_custom_call" | custom-call | flops 30000001024 | bytes 31457280 | tf_op jit(solution)/shard_map/pallas_call | solution.py:833
  218.7 37.9 %shard_map.248 = (bf16[256,1280]{1,0:T(8,128)(2,1)}, bf16[1280,640]{1,0:T(8,128)(2,1)}) custom-call(bf16[1024,1280]{1,0:T(8,128)(2,1)} %get-tuple-element.109.refs_0_.refs_4_, f32[256,1280]{1,0:T(8,128)} %get-tuple-element.110.refs_1_.refs_5_, bf16[1280,640]{1,0:T(8,128)(2,1)} %all-gather.8.cloned.1.call-done.refs_4_.refs_2_.refs_1_, ...), custom_call_target="tpu_custom_call" | custom-call | flops 30000001024 | bytes 31457280 | tf_op jit(solution)/shard_map/pallas_call | solution.py:833
  256.6 51.7 %shard_map.249 = (bf16[1024,1280]{1,0:T(8,128)(2,1)}, bf16[1024,1280]{1,0:T(8,128)(2,1)}, bf16[15,1024,64]{2,1,0:T(8,128)(2,1)}, bf16[1024,320]{1,0:T(8,128)(2,1...) custom-call(bf16[256,1280]{1,0:T(8,128)(2,1)} %get-tuple-element.113.refs_0_, ...), custom_call_target="tpu_custom_call" | custom-call | flops 30000001024 | bytes 31457280 | tf_op jit(solution)/shard_map/pallas_call | solution.py:833
  308.3 28.7 %shard_map.250 = (bf16[1024,1280]{1,0:T(8,128)(2,1)}, bf16[1024,1280]{1,0:T(8,128)(2,1)}, bf16[1024,1280]{1,0:T(8,128)(2,1)}, bf16[1280,1280]{1,0:T(8,128)(2,1)}) custom-call(bf16[256,1280]{1,0:T(8,128)(2,1)} %get-tuple-element.117.refs_0_, bf16[1280,640]{1,0:T(8,128)(2,1)} %all-gather.12.cloned.1.call-done.refs_5_.refs_1_.refs_2_, ...), custom_call_target="tpu_custom_call" | custom-call | flops 30000001024 | bytes 31457280 | tf_op jit(solution)/shard_map/pallas_call | solution.py:833
  337.4 23.8 %shard_map.251.refs_4_ = bf16[256,1280]{1,0:T(8,128)(2,1)} custom-call(bf16[1024,1280]{1,0:T(8,128)(2,1)} %get-tuple-element.120.refs_0_, f32[256,1280]{1,0:T(8,128)} %get-tuple-element.121.refs_1_.refs_5_, bf16[1280,1280]{1,0:T(8,128)(2,1)} %all-gather.14.cloned.1.call-done.refs_2_.refs_3_.refs_1_, ...), custom_call_target="tpu_custom_call" | custom-call | flops 30000001024 | bytes 31457280 | tf_op jit(solution)/shard_map/pallas_call | solution.py:833
  361.1 14.5 %shard_map.252 = (bf16[1024,1280]{1,0:T(8,128)(2,1)}, f32[8,1280]{1,0:T(8,128)}, bf16[1024,320]{1,0:T(8,128)(2,1)}) custom-call(bf16[1024,1280]{1,0:T(8,128)(2,1)} %get-tuple-element.116.refs_4_.refs_0_, bf16[1280,1280]{1,0:T(8,128)(2,1)} %all-gather.14.cloned.1.call-done.refs_2_.refs_3_.refs_1_, ...), custom_call_target="tpu_custom_call" | custom-call | flops 30000001024 | bytes 31457280 | tf_op jit(solution)/shard_map/pallas_call | solution.py:833
  375.7 26.4 %shard_map.253 = (f32[256,1280]{1,0:T(8,128)}, bf16[256,1280]{1,0:T(8,128)(2,1)}, f32[8,1280]{1,0:T(8,128)}, bf16[1280,1280]{1,0:T(8,128)(2,1)}, bf16[16,128]{1,0:T(8,128)(2,1)}) custom-call(bf16[1024,1280]{1,0:T(8,128)(2,1)} %get-tuple-element.123.refs_0_, bf16[256,1280]{1,0:T(8,128)(2,1)} %constant_dynamic-slice_fusion.2.refs_1_, ...), custom_call_target="tpu_custom_call" | custom-call | flops 30000001024 | bytes 31457280 | tf_op jit(solution)/shard_map/pallas_call | solution.py:833
  402.6 2.2 constant_dynamic-slice_fusion.1.refs_3_
  404.9 1.3 broadcast_select_fusion.3.refs_6_
  406.2 40.4 %shard_map.254 = (bf16[1024,960]{1,0:T(8,128)(2,1)}, bf16[1280,320]{1,0:T(8,128)(2,1)}, bf16[1024,320]{1,0:T(8,128)(2,1)}) custom-call(bf16[256,1280]{1,0:T(8,128)(2,1)} %get-tuple-element.125.refs_0_, bf16[1280,640]{1,0:T(8,128)(2,1)} %all-gather.10.cloned.1.call-done.refs_5_.refs_1_.refs_4_, bf16[1280,640]{1,0:T(8,128)(2,1)} %get-tuple-element.114.refs_2_.refs_5_, ...), custom_call_target="tpu_custom_call" | custom-call | flops 30000001024 | bytes 31457280 | tf_op jit(solution)/shard_map/pallas_call | solution.py:833
  446.6 25.2 %shard_map.255 = (bf16[1280,1280]{1,0:T(8,128)(2,1)}, bf16[256,1280]{1,0:T(8,128)(2,1)}, f32[8,1280]{1,0:T(8,128)}, bf16[320,1280]{1,0:T(8,128)(2,1)}) custom-call(bf16[1024,960]{1,0:T(8,128)(2,1)} %get-tuple-element.132.refs_0_, bf16[1280,320]{1,0:T(8,128)(2,1)} %get-tuple-element.133.refs_1_, f32[256,1280]{1,0:T(8,128)} %get-tuple-element.134.refs_2_, ...), custom_call_target="tpu_custom_call" | custom-call | flops 30000001024 | bytes 31457280 | tf_op jit(solution)/shard_map/pallas_call | solution.py:833
  471.9 1.8 broadcast_select_fusion.2
  473.8 1.7 copy.46
  475.6 29.8 %shard_map.256 = (bf16[1024,1280]{1,0:T(8,128)(2,1)}, f32[8,1280]{1,0:T(8,128)}, bf16[1024,1280]{1,0:T(8,128)(2,1)}, bf16[1280,640]{1,0:T(8,128)(2,1)}, bf16[128...) custom-call(bf16[256,1280]{1,0:T(8,128)(2,1)} %get-tuple-element.138.refs_0_.refs_1_, ...), custom_call_target="tpu_custom_call" | custom-call | flops 30000001024 | bytes 31457280 | tf_op jit(solution)/shard_map/pallas_call | solution.py:833
  505.4 38.8 %shard_map.257 = (f32[256,1280]{1,0:T(8,128)}, bf16[256,1280]{1,0:T(8,128)(2,1)}, f32[8,1280]{1,0:T(8,128)}, bf16[1280,640]{1,0:T(8,128)(2,1)}, bf16[1280,640]{1,0:T(8,128)(2,1)}, /*index=5*/bf16[1280,640]{1,0:T(8,128)(2,1)}) custom-call(bf16[1024,1280]{1,0:T(8,128)(2,1)} %get-tuple-element.141.refs_0_, ...), custom_call_target="tpu_custom_call" | custom-call | flops 30000001024 | bytes 31457280 | tf_op jit(solution)/shard_map/pallas_call | solution.py:833
  544.2 3.0 add_convert_fusion.2
  547.5 40.4 %shard_map.258 = (bf16[1024,960]{1,0:T(8,128)(2,1)}, bf16[1280,320]{1,0:T(8,128)(2,1)}, bf16[1280,640]{1,0:T(8,128)(2,1)}) custom-call(bf16[256,1280]{1,0:T(8,128)(2,1)} %get-tuple-element.148.refs_0_, bf16[1280,640]{1,0:T(8,128)(2,1)} %get-tuple-element.102.refs_1_.refs_4_, bf16[1280,640]{1,0:T(8,128)(2,1)} %get-tuple-element.103.refs_2_.refs_5_, ...), custom_call_target="tpu_custom_call" | custom-call | flops 30000001024 | bytes 31457280 | tf_op jit(solution)/shard_map/pallas_call | solution.py:833
  587.9 3.0 add_convert_fusion.1
  591.0 2.4 constant_dynamic-slice_fusion.far_ref
  593.8 46.0 %shard_map.259 = (bf16[1280,640]{1,0:T(8,128)(2,1)}, bf16[256,1280]{1,0:T(8,128)(2,1)}, f32[8,1280]{1,0:T(8,128)}, bf16[1280,640]{1,0:T(8,128)(2,1)}) custom-call(bf16[1024,960]{1,0:T(8,128)(2,1)} %get-tuple-element.161.refs_0_, bf16[1280,320]{1,0:T(8,128)(2,1)} %get-tuple-element.162.refs_1_, f32[256,1280]{1,0:T(8,128)} %get-tuple-element.163.refs_2_, ...), custom_call_target="tpu_custom_call" | custom-call | flops 30000001024 | bytes 31457280 | tf_op jit(solution)/shard_map/pallas_call | solution.py:833
  639.8 3.5 add_convert_fusion
  643.4 51.0 %shard_map.260 = (f32[2048,320]{1,0:T(8,128)}, f32[16,320]{1,0:T(8,128)}, bf16[320,1280]{1,0:T(8,128)(2,1)}, bf16[320,640]{1,0:T(8,128)(2,1)}, bf16[320,640]{1,0:T(8,128)(2,1)}) custom-call(bf16[320,1280]{1,0:T(8,128)(2,1)} %reduce-scatter.9.cloned.1.call-done.late_ref, bf16[320,640]{1,0:T(8,128)(2,1)} %reduce-scatter.13.cloned.1.call-done.early1_ref, ...), custom_call_target="tpu_custom_call" | custom-call | flops 30000001024 | bytes 31457280 | tf_op jit(solution)/shard_map/pallas_call | solution.py:1032
  694.4 3.5 copy.47
  698.0 3.6 select_bitcast_fusion
  701.6 0.7 reshape.45
  702.3 1.3 collective-permute-start.1
  704.8 9.3 %collective-permute-done.1 = bf16[320,640]{1,0:T(8,128)(2,1)S(1)} collective-permute-done((bf16[320,640]{1,0:T(8,128)(2,1)}, bf16[320,640]{1,0:T(8,128)(2,1)S(1)}, u32[]{:S(2)}, u32[]{:S(2)}) %collective-permute-start.1) | collective-permute-done | bytes 409632 | tf_op jit(solution)/shard_map/ppermute | solution.py:1223
  714.1 1.8 add_select_fusion
  716.3 1.0 copy.49
  717.7 1.6 copy.48
  (105 shorter events, 7.7 us)
Async XLA Ops:
  7.2 6.3 copy-start.13
  7.2 133.5 %all-gather.6.cloned.1.call-start = ((), (), s32[]{:S(2)}) async-start(), calls=%async_computation.6 | async-start | bytes 2048000 | tf_op jit(solution)/shard_map/all_gather | solution.py:1113
  8.5 12.6 %collective-permute-start = (bf16[320,640]{1,0:T(8,128)(2,1)S(1)}, bf16[320,640]{1,0:T(8,128)(2,1)}, u32[]{:S(2)}, u32[]{:S(2)}) collective-permute-start(bf16[320,640]{1,0:T(8,128)(2,1)S(1)} %broadcast_select_fusion.9), channel_id=1, source_target_pairs={{0,16},{16,0},{1,17},{17,1},{2,18},{18,2},{3,19},{19,3},{4,20},{20... | collective-permute-start | bytes 1228808 | tf_op jit(solution)/shard_map/ppermute | solution.py:1046
  12.3 1.9 copy-start.7
  15.8 2.6 copy-start.17
  15.8 2.6 copy-start.18
  15.8 2.6 copy-start.19
  15.8 2.7 copy-start.20
  15.8 2.7 copy-start.21
  15.8 2.7 copy-start.22
  15.8 2.7 copy-start.23
  18.4 2.7 copy-start
  23.1 157.1 %all-gather.8.cloned.1.call-start = ((), (), s32[]{:S(2)}) async-start(), calls=%async_computation.7 | async-start | bytes 2048000 | tf_op jit(solution)/shard_map/all_gather | solution.py:1113
  23.1 107.3 %copy-start.1 = (bf16[1,1280,320]{1,2,0:T(8,128)(2,1)S(1)}, bf16[1,1280,320]{1,2,0:T(8,128)(2,1)}, u32[]{:S(2)}) copy-start(bf16[1,1280,320]{1,2,0:T(8,128)(2,1)} %param.26) | copy-start | bytes 2457604
  130.5 2.0 copy-start.6
  130.5 2.0 copy-start.14
  132.4 1.6 copy-start.15
  132.4 86.2 %all-gather.10.cloned.1.call-start = ((), (), s32[]{:S(2)}) async-start(), calls=%async_computation.8 | async-start | bytes 2048000 | tf_op jit(solution)/shard_map/all_gather | solution.py:1113
  132.5 5.2 copy-start.3
  133.3 123.2 %all-gather.12.cloned.1.call-start = ((), (), s32[]{:S(2)}) async-start(), calls=%async_computation.9 | async-start | bytes 2048000 | tf_op jit(solution)/shard_map/all_gather | solution.py:1113
  133.9 203.5 %all-gather.14.cloned.1.call-start = ((), (), s32[]{:S(2)}) async-start(), calls=%async_computation.10 | async-start | bytes 4096000 | tf_op jit(solution)/shard_map/all_gather | solution.py:1113
  138.7 307.9 %reduce-scatter.7.cloned.1.call-start = ((), (), s32[]{:S(2)}) async-start(), calls=%async_computation.11 | async-start | bytes 4096000 | tf_op jit(solution)/shard_map/reduce_scatter | solution.py:1172
  337.1 138.5 %reduce-scatter.11.cloned.1.call-start = ((), (), s32[]{:S(2)}) async-start(), calls=%async_computation.13 | async-start | bytes 4096000 | tf_op jit(solution)/shard_map/reduce_scatter | solution.py:1172
  402.1 2.7 copy-start.2
  402.1 2.7 copy-start.8
  402.2 191.6 %reduce-scatter.9.cloned.1.call-start = ((), (), s32[]{:S(2)}) async-start(), calls=%async_computation.12 | async-start | bytes 4096000 | tf_op jit(solution)/shard_map/reduce_scatter | solution.py:1172
  471.8 122.0 %reduce-scatter.13.cloned.1.call-start = ((), (), s32[]{:S(2)}) async-start(), calls=%async_computation.14 | async-start | bytes 2048000 | tf_op jit(solution)/shard_map/reduce_scatter | solution.py:1172
  505.4 38.8 %copy-start.5 = (bf16[1280,640]{1,0:T(8,128)(2,1)S(1)}, bf16[1280,640]{1,0:T(8,128)(2,1)}, u32[]{:S(2)}) copy-start(bf16[1280,640]{1,0:T(8,128)(2,1)} %get-tuple-element.145) | copy-start | bytes 4915204
  547.3 96.1 %reduce-scatter.15.cloned.1.call-start = ((), (), s32[]{:S(2)}) async-start(), calls=%async_computation.15 | async-start | bytes 2048000 | tf_op jit(solution)/shard_map/reduce_scatter | solution.py:1172
  547.5 40.4 %copy-start.4 = (bf16[1280,640]{1,0:T(8,128)(2,1)S(1)}, bf16[1280,640]{1,0:T(8,128)(2,1)}, u32[]{:S(2)}) copy-start(bf16[1280,640]{1,0:T(8,128)(2,1)} %get-tuple-element.144) | copy-start | bytes 4915204
  593.4 108.2 %reduce-scatter.17.cloned.1.call-start = ((), (), s32[]{:S(2)}) async-start(), calls=%async_computation.16 | async-start | bytes 2048000 | tf_op jit(solution)/shard_map/reduce_scatter | solution.py:1172
  694.4 3.6 copy-start.9
  694.4 3.6 copy-start.10
  694.4 3.6 copy-start.11
  694.4 3.6 copy-start.12
  698.0 3.6 copy-start.16
  702.3 11.8 %collective-permute-start.1 = (bf16[320,640]{1,0:T(8,128)(2,1)}, bf16[320,640]{1,0:T(8,128)(2,1)S(1)}, u32[]{:S(2)}, u32[]{:S(2)}) collective-permute-start(bf16[320,640]{1,0:T(8,128)(2,1)} %reduce-scatter.17.cloned.1.call-done), channel_id=1, source_target_pairs={{16,0},{17,1},{18,2},{19,3},{20,4},{21,5},{22,6},{23,7},{24,8},{25... | collective-permute-start | bytes 1228808 | tf_op jit(solution)/shard_map/ppermute | solution.py:1223
Sparse Core Ops, SparseCore 0:
  23.2 67.6 all-gather.5
  132.5 44.7 all-gather.7
  179.5 37.0 all-gather.9
  218.5 37.0 all-gather.11
  257.6 64.6 all-gather.13
  337.2 69.2 reduce-scatter.6
  408.8 62.7 reduce-scatter.10
  474.0 67.1 reduce-scatter.8
  547.4 43.4 reduce-scatter.12
  593.7 43.5 reduce-scatter.14
  643.5 45.0 reduce-scatter.16

commit v8 on v6

--- a/solution.py
+++ b/solution.py
@@ -224,6 +224,9 @@
 
 class Halves:
     def __init__(self, pair, whole, sems, slot):
+        if pair[0].shape[1] == whole.shape[1]:
+            self.copies = [pltpu.make_async_copy(pair[0], whole, sems.at[slot])]
+            return
         section = lax.axis_index("section")
         half = whole.shape[1] // 2
         self.copies = []
@@ -240,6 +243,13 @@
     def wait(self):
         for copy in self.copies:
             copy.wait()
+
+
+def add_into(keep_ref, got_ref):
+    @pl.loop(0, keep_ref.shape[0] // TILE)
+    def _(n):
+        rows = pl.ds(pl.multiple_of(n * TILE, TILE), TILE)
+        keep_ref[rows, :] = (keep_ref[rows, :].astype(WIDE) + got_ref[rows, :].astype(WIDE)).astype(LOW)
 
 
 def attention_out(heads_ref, o3, lse_ref, heads):
@@ -301,7 +311,8 @@
 
 
 def start_kernel(
-    tokens_ref, cotangent_ref, small_ref, raw_ref, x_ref, g_ref, vectors_ref, got_ref,
+    tokens_ref, cotangent_ref, small_ref, expand_ref, contract_ref,
+    x_ref, g_ref, vectors_ref, got_expand_ref, got_contract_ref,
     x4, g4, s4, other4, x_sems, g_sems, s_sems, local_sems,
 ):
     section = lax.axis_index("section")
@@ -313,8 +324,12 @@
         loads.append(pltpu.make_async_copy(source, into.at[group.me], local_sems.at[n]))
         loads[-1].start()
     group.greet(True, False)
-    blocks = push(raw_ref, got_ref, s_sems, 3 * PARTS + 1, 1 - section, "section")
-    blocks.start()
+    blocks = [
+        push(source, into, s_sems, 3 * PARTS + 1 + n, 1 - section, "section")
+        for n, (source, into) in enumerate(((expand_ref, got_expand_ref), (contract_ref, got_contract_ref)))
+    ]
+    for block in blocks:
+        block.start()
     gathers = [Gather(group, x4, x_sems, True), Gather(group, s4, s_sems, True), Gather(group, g4, g_sems, True)]
     for gather, load in zip(gathers, (loads[0], loads[2], loads[1])):
         load.wait()
@@ -330,7 +345,8 @@
         x_ref[:, c * width : (c + 1) * width] = x4[c]
         g_ref[:, c * width : (c + 1) * width] = g4[c]
     swap.wait()
-    blocks.wait()
+    for block in blocks:
+        block.wait()
     vectors_ref[section] = s4[...]
     vectors_ref[1 - section] = other4[...]
     for gather in gathers:
@@ -453,35 +469,38 @@
     scatter.done()
 
 
-def bend_kernel(last, group, g_ref, cm_ref, co_ref, slope_ref, extra_ref, *refs):
-    before, sums_ref, *refs = refs
+def expand_back_kernel(
+    last, group, g_ref, cm_ref, co_ref, em_ref, eo_ref, slope_ref, extra_ref, second_ref, hidden_ref, vec_ref, *refs
+):
+    grad_ref, low_ref, sums_ref, ek_ref, *refs = refs
     if last:
+        full_ref = g_ref
         out_ref, *refs = refs
     else:
-        full_ref, ck_ref, cs_ref, *refs = refs
-    contract, gather_sems, local_sems, *refs = refs
+        es_ref, full_ref, c_ref, *refs = refs
+    contract, expand, before, stage, land, total, scatter_sems, gather_sems, local_sems, *refs = refs
+    first = Halves((cm_ref, co_ref), contract, local_sems, 0)
+    then = Halves((em_ref, eo_ref), expand, local_sems, 2)
+    first.start()
+    then.start()
+    sums_ref[...] = jnp.zeros_like(sums_ref)
     if last:
         stage4, deliver_sems = refs
         deliver = Deliver(group, stage4, out_ref, deliver_sems)
-    halves = Halves((cm_ref, co_ref), contract, local_sems, 0)
-    halves.start()
-    sums_ref[...] = jnp.zeros_like(sums_ref)
-    if last:
+        group.need(6)
         deliver.start(extra_ref)
     else:
+        outer, got, swap_sems = refs
         full_ref[group.chunk(group.me), :] = g_ref[...]
-    halves.wait()
+    first.wait()
+
+    def bend(rows):
+        grad = (nn(full_ref[rows, :], contract[...]) * slope_ref[rows, :].astype(WIDE)).astype(LOW)
+        before[rows, :] = grad
+        sums_ref[4:5, :] += jnp.sum(grad.astype(WIDE), axis=0, keepdims=True)
 
     if last:
-        group.need(3)
-
-    def bend(rows):
-        rows_grad = (g_ref if last else full_ref)[rows, :]
-        grad = (nn(rows_grad, contract[...]) * slope_ref[rows, :].astype(WIDE)).astype(LOW)
-        before[rows, :] = grad
-        sums_ref[0:1, :] += jnp.sum(grad.astype(WIDE), axis=0, keepdims=True)
-
-    if last:
+        group.need(5)
 
         @pl.loop(0, LENGTH // group.rows)
         def _(n):
@@ -489,54 +508,46 @@
 
         deliver.done()
     else:
-        Gather(group, full_ref, gather_sems).each(bend, lambda: group.need(3))
-        group.emit(0, 2)
-        group.need(4)
-        outer_halves(full_ref, extra_ref, ck_ref, cs_ref)
-
-
-def narrow_kernel(
-    last, group, before, g_ref, em_ref, eo_ref, second_ref, hidden_ref, vec_ref,
-    grad_ref, low_ref, sums_ref, ek_ref, es_ref,
-    expand, stage, land, total, scatter_sems, local_sems,
-):
-    halves = Halves((em_ref, eo_ref), expand, local_sems, 0)
-    halves.start()
-    sums_ref[...] = jnp.zeros_like(sums_ref)
-    halves.wait()
+        Gather(group, full_ref, gather_sems).each(bend, lambda: group.need(5))
+        group.emit(5)
+    then.wait()
     scatter = Scatter(group, stage, land, total, scatter_sems)
     scatter.start(lambda rows: nt(before[rows, :], expand[...]))
-    group.need(4)
     if last:
+        group.need(7)
         outer_whole(second_ref, before, ek_ref)
         group.emit(3)
     else:
+        group.need(6)
+        outer_halves(full_ref, extra_ref, outer.at[0], outer.at[1])
+        swap = push(outer.at[1], got, swap_sems, 0, 1 - lax.axis_index("section"), "section")
+        swap.start()
+        group.need(7)
         outer_halves(second_ref, before, ek_ref, es_ref)
         group.emit(3, 4)
-    group.need(1, 5)
+    group.need(8)
     for j in range(PARTS):
         rows = slice(j * group.part, (j + 1) * group.part)
         grad = scatter.take(j)
         hat, scale = normalise(hidden_ref[rows, :])
-        own = g_ref[rows, :].astype(WIDE)
+        own = full_ref[group.slab(group.me, j), :].astype(WIDE)
         out = own + norm_backward(grad, hat, scale, vec_ref[3:4, :])
         grad_ref[rows, :] = out
         low_ref[rows, :] = out.astype(LOW)
         for n, term in enumerate((grad * hat, grad, own, out)):
             sums_ref[n : n + 1, :] += jnp.sum(term, axis=0, keepdims=True)
+    group.emit(0, 1, 2)
     scatter.done()
-
-
-def scores_back_kernel(
-    heads, group, low_ref, mine_ref, other_ref, heads_ref, o_ref, lse_ref,
-    mixed, outer_ref,
-    weight, full, go3, dots, g3, key_acc, value_acc, gather_sems, local_sems,
-):
+    if not last:
+        swap.wait()
+        add_into(outer.at[0], got)
+        store = pltpu.make_async_copy(outer.at[0], c_ref, local_sems.at[0])
+        store.start()
+        store.wait()
+
+
+def scores_back(group, heads, low_ref, weight, heads_ref, o_ref, lse_ref, full, go3, dots, g3, accs, mixed, gather_sems, needs):
     width = o_ref.shape[1]
-    halves = Halves((mine_ref, other_ref), weight, local_sems, 0)
-    halves.start()
-    full[group.chunk(group.me), :] = low_ref[...]
-    halves.wait()
     picks = (
         lax.broadcasted_iota(jnp.int32, (8, width), 1) // HEAD
         == lax.broadcasted_iota(jnp.int32, (8, width), 0)
@@ -555,62 +566,22 @@
             preferred_element_type=WIDE,
         )
 
-    Gather(group, full, gather_sems).each(spread, lambda: group.need(4))
-    group.need(3, 5)
-    attention_back(heads_ref, go3, lse_ref, dots, g3, key_acc, value_acc, heads)
+    full[group.chunk(group.me), :] = low_ref[...]
+    Gather(group, full, gather_sems).each(spread, lambda: group.need(needs[0]))
+    group.need(*needs[1:])
+    attention_back(heads_ref, go3, lse_ref, dots, g3, *accs, heads)
     for j in range(3 * heads):
         mixed[:, j * HEAD : (j + 1) * HEAD] = g3[j]
-    group.emit(0)
-
+
+
+def outer_out(full, o_ref, outer_ref):
     @pl.loop(0, outer_ref.shape[0] // TILE)
     def _(n):
         rows = pl.ds(pl.multiple_of(n * TILE, TILE), TILE)
         outer_ref[rows, :] = tn(full[:, rows], o_ref[...]).astype(LOW)
 
 
-def attend_back_kernel(
-    last, group, mixed, outer_ref, grad_ref, x_ref, mine_ref, other_ref, normed_ref, vec_ref,
-    wk_ref, out_ref, sums_ref, *refs,
-):
-    if not last:
-        got_ref, *refs = refs
-    weight, outer, stage, land, total, scatter_sems, local_sems, *refs = refs
-    width = outer_ref.shape[1]
-    section = lax.axis_index("section")
-    halves = Halves((mine_ref, other_ref), weight, local_sems, 0)
-    halves.start()
-    sums_ref[...] = jnp.zeros_like(sums_ref)
-
-    half = weight.shape[1] // 2
-
-    def products():
-        @pl.loop(0, weight.shape[0] // TILE)
-        def _(n):
-            rows = pl.ds(pl.multiple_of(n * TILE, TILE), TILE)
-            if last:
-                outer[rows, : 3 * width] = tn(normed_ref[:, rows], mixed[...]).astype(LOW)
-                outer[rows, 3 * width :] = outer_ref[rows, :]
-            else:
-                outer[section, rows, :] = tn(normed_ref[:, rows], mixed[:, :half]).astype(LOW)
-                outer[1 - section, rows, : 3 * width - half] = tn(
-                    normed_ref[:, rows], mixed[:, half:]
-                ).astype(LOW)
-                outer[1 - section, rows, 3 * width - half :] = outer_ref[rows, :]
-
-    scatter = Scatter(group, stage, land, total, scatter_sems)
-    if not last:
-        group.need(1, 6)
-        products()
-        swap = push(outer.at[1], got_ref, refs[0], 0, 1 - section, "section")
-        swap.start()
-    halves.wait()
-    scatter.start(lambda rows: nt(mixed[rows, :], weight[:, : 3 * width]))
-    if last:
-        group.need(1, 6)
-        products()
-    store = pltpu.make_async_copy(outer if last else outer.at[0], wk_ref, local_sems.at[2])
-    store.start()
-    group.need(2, 3)
+def attend_grads(group, scatter, x_ref, grad_ref, vec_ref, mixed, width, out_ref, sums_ref):
     sums_ref[2:3, : 3 * width] = jnp.sum(mixed[...].astype(WIDE), axis=0, keepdims=True)
     for j in range(PARTS):
         rows = slice(j * group.part, (j + 1) * group.part)
@@ -620,14 +591,107 @@
         out_ref[rows, :] = out.astype(LOW)
         for n, term in enumerate((grad * hat, grad)):
             sums_ref[n : n + 1, :] += jnp.sum(term, axis=0, keepdims=True)
+
+
+def late_attend_kernel(
+    heads, group, low_ref, grad_ref, x_ref, mine_ref, other_ref, normed_ref, heads_ref, o_ref, lse_ref, vec_ref,
+    out_ref, sums_ref, w_ref,
+    weight, full, go3, dots, g3, key_acc, value_acc, mixed, outer, outer_o,
+    stage, land, total, scatter_sems, gather_sems, local_sems,
+):
+    width = o_ref.shape[1]
+    halves = Halves((mine_ref, other_ref), weight, local_sems, 0)
+    halves.start()
+    sums_ref[...] = jnp.zeros_like(sums_ref)
+    halves.wait()
+    scores_back(
+        group, heads, low_ref, weight, heads_ref, o_ref, lse_ref, full, go3, dots, g3,
+        (key_acc, value_acc), mixed, gather_sems, (7, 6, 8),
+    )
+    scatter = Scatter(group, stage, land, total, scatter_sems)
+    scatter.start(lambda rows: nt(mixed[rows, :], weight[:, : 3 * width]))
+    outer_out(full, o_ref, outer_o)
+    group.need(5)
+
+    @pl.loop(0, weight.shape[0] // TILE)
+    def _(n):
+        rows = pl.ds(pl.multiple_of(n * TILE, TILE), TILE)
+        outer[rows, : 3 * width] = tn(normed_ref[:, rows], mixed[...]).astype(LOW)
+        outer[rows, 3 * width :] = outer_o[rows, :]
+
+    store = pltpu.make_async_copy(outer, w_ref, local_sems.at[2])
+    store.start()
+    group.need(1, 2)
+    attend_grads(group, scatter, x_ref, grad_ref, vec_ref, mixed, width, out_ref, sums_ref)
     scatter.done()
     store.wait()
-    if not last:
-        swap.wait()
+
+
+def scores_back_kernel(
+    heads, group, low_ref, mine_ref, other_ref, heads_ref, o_ref, lse_ref, ek_ref, es_ref,
+    mixed, outer_ref, e_ref,
+    weight, full, go3, dots, g3, key_acc, value_acc, got, gather_sems, local_sems, swap_sems,
+):
+    swap = push(es_ref, got, swap_sems, 0, 1 - lax.axis_index("section"), "section")
+    swap.start()
+    halves = Halves((mine_ref, other_ref), weight, local_sems, 0)
+    halves.start()
+    halves.wait()
+    scores_back(
+        group, heads, low_ref, weight, heads_ref, o_ref, lse_ref, full, go3, dots, g3,
+        (key_acc, value_acc), mixed, gather_sems, (4, 3, 5),
+    )
+    group.emit(0)
+    outer_out(full, o_ref, outer_ref)
+    group.emit(1)
+    group.need(6)
+    swap.wait()
+    add_into(ek_ref, got)
+    store = pltpu.make_async_copy(ek_ref, e_ref, local_sems.at[0])
+    store.start()
+    store.wait()
+
+
+def attend_back_kernel(
+    group, mixed, outer_ref, grad_ref, x_ref, mine_ref, other_ref, normed_ref, vec_ref,
+    w_ref, out_ref, sums_ref,
+    weight, outer, got, stage, land, total, scatter_sems, local_sems, swap_sems,
+):
+    width = outer_ref.shape[1]
+    section = lax.axis_index("section")
+    halves = Halves((mine_ref, other_ref), weight, local_sems, 0)
+    halves.start()
+    sums_ref[...] = jnp.zeros_like(sums_ref)
+    half = weight.shape[1] // 2
+    scatter = Scatter(group, stage, land, total, scatter_sems)
+    group.need(1, 6)
+
+    @pl.loop(0, weight.shape[0] // TILE)
+    def _(n):
+        rows = pl.ds(pl.multiple_of(n * TILE, TILE), TILE)
+        outer[section, rows, :] = tn(normed_ref[:, rows], mixed[:, :half]).astype(LOW)
+        outer[1 - section, rows, : 3 * width - half] = tn(
+            normed_ref[:, rows], mixed[:, half:]
+        ).astype(LOW)
+        outer[1 - section, rows, 3 * width - half :] = outer_ref[rows, :]
+
+    swap = push(outer.at[1], got, swap_sems, 0, 1 - section, "section")
+    swap.start()
+    halves.wait()
+    scatter.start(lambda rows: nt(mixed[rows, :], weight[:, : 3 * width]))
+    group.need(2, 3)
+    attend_grads(group, scatter, x_ref, grad_ref, vec_ref, mixed, width, out_ref, sums_ref)
+    group.emit(1, 2)
+    scatter.done()
+    swap.wait()
+    add_into(outer.at[0], got)
+    store = pltpu.make_async_copy(outer.at[0], w_ref, local_sems.at[2])
+    store.start()
+    store.wait()
 
 
 def finish_kernel(
-    late_ref, early1_ref, early2_ref, near_ref, far_ref, a0, n0, b0, a1, n1, b1,
+    late_ref, early1_ref, early2_ref, near_ref, far_ref, a0, n0, a1, n1,
     grads_ref, sums_ref, got_late, got_early1, got_early2,
     mine, stage4, block, land_col, land_x, land_z, send, land,
     deliver_sems, col_sems, x_sems, z_sems, part_sems,
@@ -657,7 +721,7 @@
     deliver.start(near_ref)
 
     block[...] = jnp.zeros_like(block)
-    for layer, (attn, narrow, bend) in enumerate(((a0, n0, b0), (a1, n1, b1))):
+    for layer, (attn, narrow) in enumerate(((a0, n0), (a1, n1))):
         wide = [attn[0:1, :], attn[1:2, :], narrow[3:4, :], narrow[0:1, :], narrow[1:2, :], narrow[2:3, :]]
         for c in range(block.shape[0]):
             columns = slice(c * width, (c + 1) * width)
@@ -665,8 +729,8 @@
                 block[c, layer, n : n + 1, :] = term[:, columns]
             for n, term in enumerate((attn[2:3, :width], attn[2:3, 2 * width : 3 * width])):
                 block[c, layer, 8 + n : 9 + n, :] = term
-            for n in range(bend.shape[1] // width):
-                block[c, layer, 10 + n : 11 + n, :] = bend[0:1, n * width : (n + 1) * width]
+            for n in range(narrow.shape[1] // width):
+                block[c, layer, 10 + n : 11 + n, :] = narrow[4:5, n * width : (n + 1) * width]
     copies = [
         push(block.at[other, :, pl.ds(0, 8)], land_col.at[n], col_sems, n, other)
         for n, other in enumerate((group.peer, group.diag, group.sib))
@@ -805,27 +869,27 @@
     return results[:n_out], results[n_out:]
 
 
-def start_call(number, tokens, cotangent, small, raw, columns):
+def start_call(number, tokens, cotangent, small, expand, contract, columns):
     width = tokens.shape[1]
     size = width * columns
     kinds = small.shape[0]
-    outs = (shape((LENGTH, size)), shape((LENGTH, size)), shape((2, columns, kinds, width)), shape(raw.shape))
+    outs = (shape((LENGTH, size)), shape((LENGTH, size)), shape((2, columns, kinds, width)), shape(expand.shape), shape(contract.shape))
     blocks = pltpu.VMEM((columns, LENGTH, width), LOW)
     vectors = pltpu.VMEM((columns, kinds, width), LOW)
     return pl.pallas_call(
         start_kernel,
         out_shape=outs,
-        in_specs=[ANY] * 4,
-        out_specs=(VM, VM, VM, ANY),
+        in_specs=[ANY] * 5,
+        out_specs=(VM, VM, VM, ANY, ANY),
         scratch_shapes=[
             blocks, blocks, vectors, vectors, PAIRS, PAIRS,
-            pltpu.SemaphoreType.DMA((2, 3 * PARTS + 2)), LOCAL,
+            pltpu.SemaphoreType.DMA((2, 3 * PARTS + 3)), LOCAL,
         ],
         compiler_params=pltpu.CompilerParams(
             collective_id=number, has_side_effects=True, vmem_limit_bytes=GRANT
         ),
         cost_estimate=pl.CostEstimate(flops=int(3e10), bytes_accessed=30 * MEBI, transcendentals=0),
-    )(tokens, cotangent, small, raw)
+    )(tokens, cotangent, small, expand, contract)
 
 
 def attend_call(number, gathered, x, pair, vec, bias, rows, width, swaps):
@@ -876,47 +940,38 @@
     )
 
 
-def bend_call(number, last, grad, pair, slope, extra, size, rows, swaps):
+def expand_back_call(number, last, grad, contract, expand, slope, extra, second, hidden, vec, swaps):
+    rows, size = hidden.shape
     wide = slope.shape[1]
     columns = LENGTH // rows
-    outs = [shape((LENGTH, wide)), shape((8, wide), WIDE)]
-    scratch = [pltpu.VMEM((size, wide), LOW), PAIRS, LOCAL]
+    outs = [shape((rows, size), WIDE), shape((rows, size)), shape((8, size), WIDE)]
+    scratch = [
+        pltpu.VMEM((size, wide), LOW),
+        pltpu.VMEM((size, wide), LOW),
+        pltpu.VMEM((LENGTH, wide), LOW),
+        *scatter_scratch(rows, size), PAIRS, LOCAL,
+    ]
     if last:
-        outs += [shape((LENGTH, size // columns))]
+        outs += [shape((size, wide)), shape((LENGTH, size // columns))]
+        out_specs = [VM] * 5
         scratch += [pltpu.VMEM((columns, rows, size // columns), LOW), pltpu.SemaphoreType.DMA((2, 3))]
     else:
-        outs += [shape((LENGTH, size)), *[shape((size, wide // 2))] * 2]
+        outs += [shape((size, wide // 2))] * 2 + [shape((LENGTH, size)), shape((size, wide // 2))]
+        out_specs = [VM] * 6 + [ANY]
+        scratch += [
+            pltpu.VMEM((2, size, wide // 2), LOW), pltpu.VMEM((size, wide // 2), LOW),
+            pltpu.SemaphoreType.DMA((2, 1)),
+        ]
     return launch(
-        functools.partial(bend_kernel, last),
-        number, rows, [VM, ANY, ANY, VM, VM], (grad, *pair, slope, extra),
-        outs, (VM,) * len(outs), scratch, swaps, last, late=(3,) if last else (3, 4),
-    )
-
-
-def narrow_call(number, last, before, grad_own, pair, second, hidden, vec, swaps):
-    rows, size = hidden.shape
-    wide = before.shape[1]
-    outs = (
-        shape((rows, size), WIDE),
-        shape((rows, size)),
-        shape((8, size), WIDE),
-        shape((size, wide if last else wide // 2)),
-        shape((16, 128) if last else (size, wide // 2)),
-    )
-    scratch = [pltpu.VMEM((size, wide), LOW), *scatter_scratch(rows, size), LOCAL]
-    return launch(
-        functools.partial(narrow_kernel, last),
-        number, rows, [VM, VM, ANY, ANY, VM, VM, VM], (before, grad_own, *pair, second, hidden, vec),
-        outs, (VM, VM, VM, VM, ANY if last else VM), scratch, swaps, late=(1, 4, 5),
-    )
-
-
-def scores_back_call(number, low, pair, heads_all, o, lse, swaps):
-    rows, size = low.shape
-    width = o.shape[1]
-    heads = width // HEAD
-    outs = (shape((LENGTH, 3 * width)), shape((size, width)))
-    scratch = [
+        functools.partial(expand_back_kernel, last),
+        number, rows, [VM, ANY, ANY, ANY, ANY, VM, VM, VM, VM, VM],
+        (grad, *contract, *expand, slope, extra, second, hidden, vec),
+        outs, out_specs, scratch, swaps, last, not last, late=(5, 6, 7, 8),
+    )
+
+
+def scores_scratch(size, width, heads):
+    return [
         pltpu.VMEM((size, 4 * width), LOW),
         pltpu.VMEM((LENGTH, size), LOW),
         pltpu.VMEM((heads, LENGTH, HEAD), LOW),
@@ -924,34 +979,63 @@
         pltpu.VMEM((3 * heads, LENGTH, HEAD), LOW),
         pltpu.VMEM((LENGTH, HEAD), WIDE),
         pltpu.VMEM((LENGTH, HEAD), WIDE),
-        PAIRS, LOCAL,
+    ]
+
+
+def late_attend_call(number, low, grad, x_own, pair, normed, heads_all, o, lse, vec, swaps):
+    rows, size = grad.shape
+    width = o.shape[1]
+    heads = width // HEAD
+    outs = (shape((rows, size)), shape((8, size), WIDE), shape((size, 4 * width)))
+    scratch = [
+        *scores_scratch(size, width, heads),
+        pltpu.VMEM((LENGTH, 3 * width), LOW),
+        pltpu.VMEM((size, 4 * width), LOW),
+        pltpu.VMEM((size, width), LOW),
+        *scatter_scratch(rows, size), PAIRS, LOCAL,
+    ]
+    return launch(
+        functools.partial(late_attend_kernel, heads),
+        number, rows, [VM, VM, VM, ANY, ANY, VM, VM, VM, VM, VM],
+        (low, grad, x_own, *pair, normed, heads_all, o, lse, vec),
+        outs, (VM, VM, ANY), scratch, swaps, late=(1, 2, 5, 6, 7, 8),
+    )
+
+
+def scores_back_call(number, low, pair, heads_all, o, lse, keep, send):
+    rows, size = low.shape
+    width = o.shape[1]
+    heads = width // HEAD
+    outs = (shape((LENGTH, 3 * width)), shape((size, width)), shape(keep.shape))
+    scratch = [
+        *scores_scratch(size, width, heads),
+        pltpu.VMEM(keep.shape, LOW),
+        PAIRS, LOCAL, pltpu.SemaphoreType.DMA((2, 1)),
     ]
     return launch(
         functools.partial(scores_back_kernel, heads),
-        number, rows, [VM, ANY, ANY, VM, VM, VM], (low, *pair, heads_all, o, lse),
-        outs, (VM,) * 2, scratch, swaps, late=(3, 4, 5),
-    )
-
-
-def attend_back_call(number, last, mixed, outer, grad, x_own, pair, normed, vec, swaps):
+        number, rows, [VM, ANY, ANY, VM, VM, VM, VM, ANY], (low, *pair, heads_all, o, lse, keep, send),
+        outs, (VM, VM, ANY), scratch, (), False, True, late=(3, 4, 5, 6),
+    )[0]
+
+
+def attend_back_call(number, mixed, outer, grad, x_own, pair, normed, vec):
     rows, size = grad.shape
     width = outer.shape[1]
     half = 2 * width
-    outs = [shape((size, 2 * half if last else half)), shape((rows, size)), shape((8, size), WIDE)]
-    out_specs = [ANY, VM, VM]
+    outs = (shape((size, half)), shape((rows, size)), shape((8, size), WIDE))
     scratch = [
         pltpu.VMEM((size, 4 * width), LOW),
-        pltpu.VMEM((size, 2 * half) if last else (2, size, half), LOW),
-        *scatter_scratch(rows, size), LOCAL,
+        pltpu.VMEM((2, size, half), LOW),
+        pltpu.VMEM((size, half), LOW),
+        *scatter_scratch(rows, size), LOCAL, pltpu.SemaphoreType.DMA((2, 1)),
     ]
-    if not last:
-        outs, out_specs = outs + [shape((size, half))], out_specs + [ANY]
-        scratch += [pltpu.SemaphoreType.DMA((2, 1))]
     return launch(
-        functools.partial(attend_back_kernel, last),
+        attend_back_kernel,
         number, rows, [VM, VM, VM, VM, ANY, ANY, VM, VM],
-        (mixed, outer, grad, x_own, *pair, normed, vec), outs, out_specs, scratch, swaps, False, True, late=(1, 2, 3, 6),
-    )
+        (mixed, outer, grad, x_own, *pair, normed, vec), outs, (ANY, VM, VM), scratch, (), False, True,
+        late=(1, 2, 3, 6),
+    )[0]
 
 
 def finish_call(number, late, early1, early2, near, far, sums, row_count):
@@ -981,7 +1065,7 @@
     return pl.pallas_call(
         finish_kernel,
         out_shape=outs,
-        in_specs=[ANY] * 3 + [VM] * 8,
+        in_specs=[ANY] * 3 + [VM] * 6,
         out_specs=(VM, VM, ANY, ANY, ANY),
         scratch_shapes=scratch,
         compiler_params=pltpu.CompilerParams(
@@ -1053,13 +1137,21 @@
     filled = small.shape[0]
     small = jnp.pad(small, ((0, -filled % 16), (0, 0)))
     got_attend = swap_sections(sent_blocks[0])
-    raw = jnp.stack(sent_blocks[1:])
-    got_attend, raw = lax.optimization_barrier((got_attend, raw))
-    x0_full, gy_full, vectors, got_blocks = start_call(1, tokens, cotangent, small, raw, columns)
+    got_attend, sent_expand = lax.optimization_barrier((got_attend, sent_blocks[1]))
+    x0_full, gy_full, vectors, got_expand, got_contract = start_call(
+        1, tokens, cotangent, small, sent_expand, units[2], columns
+    )
+
+    def gather_blocks(block):
+        return lax.all_gather(block, "row", axis=0, tiled=True)
+
+    half = units[2].shape[1] // 2
     mats = [[], []]
-    for own, got in zip(kept_blocks, (got_attend, got_blocks[0], got_blocks[1])):
+    for own, got in ((kept_blocks[0], got_attend), (kept_blocks[1], got_expand)):
         for layer, block in enumerate((pick(own, got), pick(got, own))):
-            mats[layer].append(lax.all_gather(block, "row", axis=0, tiled=True))
+            mats[layer].append(gather_blocks(block))
+    mats[0].append(gather_blocks(pick(kept_blocks[2], got_contract[:, half:])))
+    mats[1].append(gather_blocks(pick(got_contract, units[2])))
     vectors = vectors.astype(WIDE)
     wide_vectors = jnp.swapaxes(vectors[:, :, :6], 1, 2).reshape(2, 6, size)
     wide_vectors = jnp.pad(wide_vectors, ((0, 0), (0, 2), (0, 0)))
@@ -1086,12 +1178,12 @@
             2 + 3 * layer, not last, x, attn, vec, attend_biases[layer], rows, width, [mats[layer][1]]
         )
         expand = (mats[layer][1], other)
-        outs, (other,) = widen_call(
+        outs, others = widen_call(
             3 + 3 * layer, second_own, expand, expand_biases[layer],
-            gy_full if last else None, [mats[layer][2]],
+            gy_full if last else None, [] if last else [mats[0][2]],
         )
         second, active, slope = outs[:3]
-        contract = (mats[layer][2], other)
+        contract = (mats[layer][2], mats[layer][2] if last else others[0])
         if last:
             c1 = outs[3]
         outs, others = contract_call(
@@ -1105,10 +1197,6 @@
             attn = (mats[1][0], others[0])
     y0 = own_features(full)
 
-    def add(keep, got, then):
-        total = (keep.astype(WIDE) + got.astype(WIDE)).astype(LOW)
-        return lax.optimization_barrier((total, then))
-
     def scatter(total):
         return lax.psum_scatter(total, "row", scatter_dimension=0, tiled=True)
 
@@ -1117,36 +1205,28 @@
 
     attn, expand, contract = pairs[1]
     normed, heads, o, lse, hidden, second, active, slope = kept[1]
-    (before, bend_sums1, y1), _ = bend_call(8, True, gy_full, contract, slope, owns[2], size, rows, [])
+    (grad_hidden, low, expand_sums1, e1, y1), _ = expand_back_call(
+        8, True, gy_full, contract, expand, slope, owns[2], second, hidden, wide_vectors[1], []
+    )
     layer_low, layer_high = pick(y0, y1), pick(y1, y0)
-    (grad_hidden, low, narrow_sums1, e1, _), _ = narrow_call(
-        9, True, before, own_rows(gy_full), expand, second, hidden, wide_vectors[1], []
-    )
-    (mixed, outer), (layer_got,) = scores_back_call(10, low, attn, heads, o, lse, [layer_high])
-    part_c1, mixed = tie(scatter(c1), mixed)
-    (w1, gx1_own, attend_sums1), (far_c1,) = attend_back_call(
-        11, True, mixed, outer, grad_hidden, owns[1], attn, normed, wide_vectors[1], [part_c1]
+    part_c1, low = tie(scatter(c1), low)
+    (gx1_own, attend_sums1, w1), (layer_got, far_c1) = late_attend_call(
+        10, low, grad_hidden, owns[1], attn, normed, heads, o, lse, wide_vectors[1], [layer_high, part_c1]
     )
     layer_outputs = jnp.concatenate([pick(layer_low, layer_got), pick(layer_got, layer_low)], 0)
 
     attn, expand, contract = pairs[0]
     normed, heads, o, lse, hidden, second, active, slope = kept[0]
     part_e1 = scatter(e1)
-    (before, bend_sums0, gx1_full, ck0, cs0), (far_e1,) = bend_call(
-        12, False, gx1_own, contract, slope, active, size, rows, [part_e1]
-    )
-    (grad_hidden, low, narrow_sums0, ek0, es0), (ct0,) = narrow_call(
-        13, False, before, gx1_own, expand, second, hidden, wide_vectors[0], [cs0]
-    )
-    total_c0, low = add(ck0, ct0, low)
-    (mixed, outer), (et0,) = scores_back_call(14, low, attn, heads, o, lse, [es0])
-    total_e0, mixed = add(ek0, et0, mixed)
+    (grad_hidden, low, expand_sums0, ek0, es0, gx1_full, total_c0), (far_e1,) = expand_back_call(
+        12, False, gx1_own, contract, expand, slope, active, second, hidden, wide_vectors[0], [part_e1]
+    )
+    mixed, outer, total_e0 = scores_back_call(14, low, attn, heads, o, lse, ek0, es0)
     part_w1, mixed = tie(scatter(w1), mixed)
     part_c0, mixed = tie(scatter(total_c0), mixed)
-    (wk0, gx0_own, attend_sums0, wt0), _ = attend_back_call(
-        15, False, mixed, outer, grad_hidden, owns[0], attn, normed, wide_vectors[0], []
-    )
-    total_w0, gx0_own = add(wk0, wt0, gx0_own)
+    total_w0, gx0_own, attend_sums0 = attend_back_call(
+        15, mixed, outer, grad_hidden, owns[0], attn, normed, wide_vectors[0]
+    )
     part_e0 = scatter(total_e0)
     input_grads, small_grads, far_w1, far_c0, far_e0 = finish_call(
         16,
@@ -1155,11 +1235,10 @@
         part_e0,
         gx0_own,
         own_features(gx1_full),
-        (attend_sums0, narrow_sums0, bend_sums0, attend_sums1, narrow_sums1, bend_sums1),
+        (attend_sums0, expand_sums0, attend_sums1, expand_sums1),
         lax.axis_size("row"),
     )
 
-    late = [part_w1, part_e1, part_c1]
     part_w0, small_grads = tie(scatter(total_w0), small_grads)
     far_w0 = lax.ppermute(part_w0, "section", [(1, 0)])
 

time: 708 us -> 688 us (0.972)
  Pallas kernels: 579 us -> 565 us
  other arithmetic: 23.8 us -> 13.5 us
  waiting for transfers between devices: 45.9 us -> 53.5 us
    pallas_call x14 -> x11, Pallas kernels: 491 us -> 478 us  [launch(): pl.pallas_call(kernel, out_shape=(*outs, *[shape(s.shape, s.dtype) for s...]
    convert_element_type x3 -> x0, other arithmetic: 9.54 us -> none  [add(): total = (keep.astype(WIDE) + got.astype(WIDE)).astype(LOW)]
    unnamed x44 -> x62, local copies, waits for them, and re-layouts: 16.9 us -> 17.3 us
  transfers between devices with their start and end apart: 15 -> 15, of which waited for: 4 -> 6; matrix products, arithmetic and copies ran while one was open for 6% -> 4% of each run, Pallas kernels for 77% -> 83%
where the time goes in v8:
time: 688 us; the launch traced here: 682 us
  Pallas kernels  565 us (82%)
  waiting for transfers between devices  53.5 us (8%)
  local copies, waits for them, and re-layouts  29 us (4%)
  between operations  15 us (2%)
  other arithmetic  13.5 us (2%)
    pallas_call x11, Pallas kernels, launch(): pl.pallas_call(kernel, out_shape=(*outs, *[shape(s.shape, s.dtype) for s...  478 us
    pallas_call x1, Pallas kernels, start_call(): pl.pallas_call(start_kernel, out_shape=outs, in_specs=[ANY] * 5, out_spec...  43.6 us
    pallas_call x1, Pallas kernels, finish_call(): pl.pallas_call(finish_kernel, out_shape=outs, in_specs=[ANY] * 3 + [VM] *...  43.4 us
    all_gather x6, waiting for transfers between devices, gather_blocks(): return lax.all_gather(block, 'row', axis=0, tiled=True)  30.8 us
    unnamed x62, local copies, waits for them, and re-layouts  17.3 us
  transfers between devices with their start and end apart: 15, of which 6 were waited for; matrix products, arithmetic and copies ran while one was open for 4% of the time, Pallas kernels for 83%

profile of v8, /device:TPU:0, one launch (start us, length us, event | category | flops | bytes accessed | tf_op | source)
XLA Modules:
  0.0 682.0 jit_solution(11092981264449673830)
XLA Ops:
  7.2 1.1 copy.38
  8.4 1.5 copy.37
  10.4 3.0 collective-permute-start
  13.5 1.5 copy.41.tokens_ref
  15.1 2.6 copy.42.cotangent_ref
  18.5 0.8 broadcast_select_fusion.11.expand_ref
  19.3 3.6 collective-permute-done
  22.9 1.0 broadcast_select_fusion.5
  23.9 43.6 %shard_map.245 = (bf16[1024,1280]{1,0:T(8,128)(2,1)}, bf16[1024,1280]{1,0:T(8,128)(2,1)}, bf16[2,4,16,320]{3,2,1,0:T(8,128)(2,1)}, bf16[320,640]{1,0:T(8,128)(2,1)}, bf16[320,1280]{1,0:T(8,128)(2,1)}) custom-call(bf16[2048,320]{1,0:T(8,128)(2,1)} %copy.41.tokens_ref, bf16[2048,320]{1,0:T(8,128)(2,1)} %copy.42.cotangent_ref, bf16[16,320]{1,0:T(8,128)(2,1)} %pad.8.small_ref, ...), custom_call_target="tpu_custom_call" | custom-call | flops 30000001024 | bytes 31457280 | tf_op jit(solution)/shard_map/pallas_call | solution.py:879
  67.5 2.1 broadcast_select_fusion.6
  69.7 0.8 fusion
  72.5 0.7 squeeze.48.refs_3_
  73.2 0.7 squeeze.45.refs_3_
  73.9 0.7 squeeze.47.refs_4_
  74.6 0.7 squeeze.44.refs_4_
  75.4 1.0 broadcast_select_fusion
  76.4 0.6 fusion.2
  77.1 30.7 %all-gather.9.cloned.1.call-done.refs_5_.refs_1_.refs_3_ = bf16[1280,640]{1,0:T(8,128)(2,1)} async-done(((bf16[320,640]{1,0:T(8,128)(2,1)}), bf16[1280,640]{1,0:T(8,128)(2,1)}) %all-gather.9.cloned.1.call-update) | async-done | bytes 1638416 | tf_op jit(solution)/shard_map/all_gather | solution.py:1146
  107.8 3.0 collective-permute-done.1.refs_2_.refs_5_
  110.7 1.2 copy-done.26
  111.9 39.0 %shard_map.246 = (bf16[16,128]{1,0:T(8,128)(2,1)}, bf16[1024,1280]{1,0:T(8,128)(2,1)}, bf16[15,1024,64]{2,1,0:T(8,128)(2,1)}, bf16[1024,320]{1,0:T(8,128)(2,1)},...) custom-call(bf16[1024,1280]{1,0:T(8,128)(2,1)} %get-tuple-element.84.refs_0_, ...), custom_call_target="tpu_custom_call" | custom-call | flops 30000001024 | bytes 31457280 | tf_op jit(solution)/shard_map/pallas_call | solution.py:851
  150.9 38.4 %shard_map.247 = (bf16[1024,1280]{1,0:T(8,128)(2,1)}, bf16[1024,1280]{1,0:T(8,128)(2,1)}, bf16[1024,1280]{1,0:T(8,128)(2,1)}, bf16[1280,640]{1,0:T(8,128)(2,1)}) custom-call(bf16[256,1280]{1,0:T(8,128)(2,1)} %get-tuple-element.88.refs_0_, bf16[1280,640]{1,0:T(8,128)(2,1)} %all-gather.9.cloned.1.call-done.refs_5_.refs_1_.refs_3_, ...), custom_call_target="tpu_custom_call" | custom-call | flops 30000001024 | bytes 31457280 | tf_op jit(solution)/shard_map/pallas_call | solution.py:851
  189.3 38.6 %shard_map.248 = (bf16[256,1280]{1,0:T(8,128)(2,1)}, bf16[1280,640]{1,0:T(8,128)(2,1)}) custom-call(bf16[1024,1280]{1,0:T(8,128)(2,1)} %get-tuple-element.91.refs_0_.refs_6_, f32[256,1280]{1,0:T(8,128)} %get-tuple-element.92.refs_1_.refs_8_, bf16[1280,640]{1,0:T(8,128)(2,1)} %all-gather.11.cloned.1.call-done.refs_4_.refs_2_.refs_1_, ...), custom_call_target="tpu_custom_call" | custom-call | flops 30000001024 | bytes 31457280 | tf_op jit(solution)/shard_map/pallas_call | solution.py:851
  228.0 52.0 %shard_map.249 = (bf16[1024,1280]{1,0:T(8,128)(2,1)}, bf16[1024,1280]{1,0:T(8,128)(2,1)}, bf16[15,1024,64]{2,1,0:T(8,128)(2,1)}, bf16[1024,320]{1,0:T(8,128)(2,1...) custom-call(bf16[256,1280]{1,0:T(8,128)(2,1)} %get-tuple-element.94.refs_0_., ...), custom_call_target="tpu_custom_call" | custom-call | flops 30000001024 | bytes 31457280 | tf_op jit(solution)/shard_map/pallas_call | solution.py:851
  280.0 28.2 %shard_map.250 = (bf16[1024,1280]{1,0:T(8,128)(2,1)}, bf16[1024,1280]{1,0:T(8,128)(2,1)}, bf16[1024,1280]{1,0:T(8,128)(2,1)}, bf16[1280,1280]{1,0:T(8,128)(2,1)}) custom-call(bf16[256,1280]{1,0:T(8,128)(2,1)} %get-tuple-element.99.refs_0_, bf16[1280,640]{1,0:T(8,128)(2,1)} %all-gather.15.cloned.1.call-done.refs_5_.refs_1_.refs_3_, ...), custom_call_target="tpu_custom_call" | custom-call | flops 30000001024 | bytes 31457280 | tf_op jit(solution)/shard_map/pallas_call | solution.py:851
  308.6 24.3 %shard_map.251.refs_6_ = bf16[256,1280]{1,0:T(8,128)(2,1)} custom-call(bf16[1024,1280]{1,0:T(8,128)(2,1)} %get-tuple-element.101.refs_0_, f32[256,1280]{1,0:T(8,128)} %get-tuple-element.102.refs_1_.refs_8_, bf16[1280,1280]{1,0:T(8,128)(2,1)} %all-gather.17.cloned.1.call-done.refs_2_.refs_3_.refs_1_, ...), custom_call_target="tpu_custom_call" | custom-call | flops 30000001024 | bytes 31457280 | tf_op jit(solution)/shard_map/pallas_call | solution.py:851
  332.8 35.5 %shard_map.252 = (f32[256,1280]{1,0:T(8,128)}, bf16[256,1280]{1,0:T(8,128)(2,1)}, f32[8,1280]{1,0:T(8,128)}, bf16[1280,1280]{1,0:T(8,128)(2,1)}, bf16[1024,320]{1,0:T(8,128)(2,1)}) custom-call(bf16[1024,1280]{1,0:T(8,128)(2,1)} %get-tuple-element.97.refs_4_.refs_0_, bf16[1280,1280]{1,0:T(8,128)(2,1)} %all-gather.17.cloned.1.call-done.refs_2_.refs_3_.refs_1_, ...), custom_call_target="tpu_custom_call" | custom-call | flops 30000001024 | bytes 31457280 | tf_op jit(solution)/shard_map/pallas_call | solution.py:851
  368.6 0.8 copy-done.2
  369.5 1.3 broadcast_select_fusion.3.refs_10_
  371.0 58.9 %shard_map.253 = (bf16[256,1280]{1,0:T(8,128)(2,1)}, f32[8,1280]{1,0:T(8,128)}, bf16[1280,1280]{1,0:T(8,128)(2,1)}, bf16[1024,320]{1,0:T(8,128)(2,1)}, bf16[320,1280]{1,0:T(8,128)(2,1)}) custom-call(bf16[256,1280]{1,0:T(8,128)(2,1)} %get-tuple-element.107.refs_0_, f32[256,1280]{1,0:T(8,128)} %get-tuple-element.108.refs_1_, ...), custom_call_target="tpu_custom_call" | custom-call | flops 30000001024 | bytes 31457280 | tf_op jit(solution)/shard_map/pallas_call | solution.py:851
  430.3 5.4 reduce-scatter.11.cloned.1.call-done.refs_10_
  435.7 75.5 %shard_map.254 = (f32[256,1280]{1,0:T(8,128)}, bf16[256,1280]{1,0:T(8,128)(2,1)}, f32[8,1280]{1,0:T(8,128)}, bf16[1280,640]{1,0:T(8,128)(2,1)}, bf16[1280,640]{1...) custom-call(bf16[256,1280]{1,0:T(8,128)(2,1)} %get-tuple-element.116.refs_0_, ...), custom_call_target="tpu_custom_call" | custom-call | flops 30000001024 | bytes 31457280 | tf_op jit(solution)/shard_map/pallas_call | solution.py:851
  511.5 2.0 constant_dynamic-slice_fusion.1.refs_3_
  513.5 40.7 %shard_map.255 = (bf16[1024,960]{1,0:T(8,128)(2,1)}, bf16[1280,320]{1,0:T(8,128)(2,1)}, bf16[1280,640]{1,0:T(8,128)(2,1)}) custom-call(bf16[256,1280]{1,0:T(8,128)(2,1)} %get-tuple-element.120.refs_0_, bf16[1280,640]{1,0:T(8,128)(2,1)} %all-gather.7.cloned.1.call-done.refs_1_.refs_4_, bf16[1280,640]{1,0:T(8,128)(2,1)} %copy-done.26, ...), custom_call_target="tpu_custom_call" | custom-call | flops 30000001024 | bytes 31457280 | tf_op jit(solution)/shard_map/pallas_call | solution.py:851
  554.4 1.8 broadcast_select_fusion.2
  556.4 1.5 copy.46
  558.0 2.4 constant_dynamic-slice_fusion.far_ref
  560.4 46.5 %shard_map.256 = (bf16[1280,640]{1,0:T(8,128)(2,1)}, bf16[256,1280]{1,0:T(8,128)(2,1)}, f32[8,1280]{1,0:T(8,128)}) custom-call(bf16[1024,960]{1,0:T(8,128)(2,1)} %get-tuple-element.132.refs_0_, bf16[1280,320]{1,0:T(8,128)(2,1)} %get-tuple-element.133.refs_1_, f32[256,1280]{1,0:T(8,128)} %get-tuple-element.134.refs_2_, ...), custom_call_target="tpu_custom_call" | custom-call | flops 30000001024 | bytes 31457280 | tf_op jit(solution)/shard_map/pallas_call | solution.py:851
  607.0 43.4 %shard_map.257 = (f32[2048,320]{1,0:T(8,128)}, f32[16,320]{1,0:T(8,128)}, bf16[320,1280]{1,0:T(8,128)(2,1)}, bf16[320,640]{1,0:T(8,128)(2,1)}, bf16[320,640]{1,0:T(8,128)(2,1)}) custom-call(bf16[320,1280]{1,0:T(8,128)(2,1)} %reduce-scatter.9.cloned.1.call-done.late_ref, bf16[320,640]{1,0:T(8,128)(2,1)} %reduce-scatter.13.cloned.1.call-done.early1_ref, ...), custom_call_target="tpu_custom_call" | custom-call | flops 30000001024 | bytes 31457280 | tf_op jit(solution)/shard_map/pallas_call | solution.py:1065
  650.4 3.5 copy.47
  654.1 1.4 select_bitcast_fusion
  656.2 1.4 select_bitcast_fusion.1
  657.7 0.7 reshape.45
  658.4 1.3 collective-permute-start.2
  660.8 9.3 %collective-permute-done.2 = bf16[320,640]{1,0:T(8,128)(2,1)S(1)} collective-permute-done((bf16[320,640]{1,0:T(8,128)(2,1)}, bf16[320,640]{1,0:T(8,128)(2,1)S(1)}, u32[]{:S(2)}, u32[]{:S(2)}) %collective-permute-start.2) | collective-permute-done | bytes 409632 | tf_op jit(solution)/shard_map/ppermute | solution.py:1243
  670.2 1.3 add_select_fusion
  671.8 1.0 copy.49
  673.2 1.6 copy.48
  (110 shorter events, 8.3 us)
Async XLA Ops:
  7.2 64.8 %all-gather.7.cloned.1.call-start = ((), (), s32[]{:S(2)}) async-start(), calls=%async_computation.6 | async-start | bytes 2048000 | tf_op jit(solution)/shard_map/all_gather | solution.py:1146
  9.9 3.6 copy-start.18
  9.9 3.7 copy-start.4
  10.4 12.5 %collective-permute-start = (bf16[320,640]{1,0:T(8,128)(2,1)S(1)}, bf16[320,640]{1,0:T(8,128)(2,1)S(1)}, u32[]{:S(2)}, u32[]{:S(2)}) collective-permute-start(bf16[320,640]{1,0:T(8,128)(2,1)S(1)} %get-tuple-element.180), channel_id=1, source_target_pairs={{0,16},{16,0},{1,17},{17,1},{2,18},{18,2},{3,19},{19,3},{4,20},{20... | collective-permute-start | bytes 1228808 | tf_op jit(solution)/shard_map/ppermute | solution.py:1079
  15.1 2.7 copy-start.19
  15.1 2.7 copy-start.20
  15.1 2.7 copy-start.21
  15.1 2.7 copy-start.22
  15.1 2.7 copy-start.23
  15.1 2.7 copy-start.24
  15.1 2.7 copy-start.25
  15.1 3.3 copy-start
  23.9 83.9 %all-gather.9.cloned.1.call-start = ((), (), s32[]{:S(2)}) async-start(), calls=%async_computation.7 | async-start | bytes 2048000 | tf_op jit(solution)/shard_map/all_gather | solution.py:1146
  67.5 2.2 copy-start.1
  67.5 2.2 copy-start.3
  69.6 2.2 copy-start.16
  69.7 81.3 %all-gather.11.cloned.1.call-start = ((), (), s32[]{:S(2)}) async-start(), calls=%async_computation.8 | async-start | bytes 2048000 | tf_op jit(solution)/shard_map/all_gather | solution.py:1146
  70.6 118.7 %all-gather.13.cloned.1.call-start = ((), (), s32[]{:S(2)}) async-start(), calls=%async_computation.9 | async-start | bytes 2048000 | tf_op jit(solution)/shard_map/all_gather | solution.py:1146
  71.1 156.8 %all-gather.15.cloned.1.call-start = ((), (), s32[]{:S(2)}) async-start(), calls=%async_computation.10 | async-start | bytes 2048000 | tf_op jit(solution)/shard_map/all_gather | solution.py:1146
  71.7 236.8 %all-gather.17.cloned.1.call-start = ((), (), s32[]{:S(2)}) async-start(), calls=%async_computation.11 | async-start | bytes 4096000 | tf_op jit(solution)/shard_map/all_gather | solution.py:1146
  72.0 38.7 %collective-permute-start.1 = (bf16[1280,640]{1,0:T(8,128)(2,1)}, bf16[1280,640]{1,0:T(8,128)(2,1)S(1)}, u32[]{:S(2)}, u32[]{:S(2)}) collective-permute-start(bf16[1280,640]{1,0:T(8,128)(2,1)} %all-gather.7.cloned.1.call-done.refs_1_.refs_4_), channel_id=1, source_target_pairs={{0,16},{16,0},{1,17},{17,1},{2,18},{18,2},{3,19},{19,3},{4,20},{20... | collective-permute-start | bytes 4915208 | tf_op jit(solution)/shard_map/ppermute | solution.py:1079
  76.4 294.6 %reduce-scatter.7.cloned.1.call-start = ((), (), s32[]{:S(2)}) async-start(), calls=%async_computation.12 | async-start | bytes 4096000 | tf_op jit(solution)/shard_map/reduce_scatter | solution.py:1201
  110.7 1.2 copy-start.26
  308.3 127.4 %reduce-scatter.11.cloned.1.call-start = ((), (), s32[]{:S(2)}) async-start(), calls=%async_computation.14 | async-start | bytes 4096000 | tf_op jit(solution)/shard_map/reduce_scatter | solution.py:1201
  332.8 35.8 %copy-start.5 = (bf16[1024,1280]{1,0:T(8,128)(2,1)S(1)}, bf16[1024,1280]{1,0:T(8,128)(2,1)}, u32[]{:S(2)}) copy-start(bf16[1024,1280]{1,0:T(8,128)(2,1)} %get-tuple-element.96) | copy-start | bytes 7864324
  368.3 1.1 copy-start.2
  368.4 192.1 %reduce-scatter.9.cloned.1.call-start = ((), (), s32[]{:S(2)}) async-start(), calls=%async_computation.13 | async-start | bytes 4096000 | tf_op jit(solution)/shard_map/reduce_scatter | solution.py:1201
  429.9 130.6 %reduce-scatter.13.cloned.1.call-start = ((), (), s32[]{:S(2)}) async-start(), calls=%async_computation.15 | async-start | bytes 2048000 | tf_op jit(solution)/shard_map/reduce_scatter | solution.py:1201
  511.3 95.7 %reduce-scatter.15.cloned.1.call-start = ((), (), s32[]{:S(2)}) async-start(), calls=%async_computation.16 | async-start | bytes 2048000 | tf_op jit(solution)/shard_map/reduce_scatter | solution.py:1201
  554.2 103.5 %reduce-scatter.17.cloned.1.call-start = ((), (), s32[]{:S(2)}) async-start(), calls=%async_computation.17 | async-start | bytes 2048000 | tf_op jit(solution)/shard_map/reduce_scatter | solution.py:1201
  650.4 3.6 copy-start.6
  650.4 3.6 copy-start.9
  650.4 3.6 copy-start.12
  650.4 3.6 copy-start.15
  654.0 1.5 copy-start.7
  654.0 1.8 copy-start.10
  654.0 2.1 copy-start.13
  654.0 2.2 copy-start.14
  656.2 1.4 copy-start.17
  656.2 13.9 %copy-start.8 = (bf16[320,1280]{1,0:T(8,128)(2,1)S(1)}, bf16[320,1280]{1,0:T(8,128)(2,1)}, u32[]{:S(2)}) copy-start(bf16[320,1280]{1,0:T(8,128)(2,1)} %reduce-scatter.9.cloned.1.call-done.late_ref) | copy-start | bytes 2457604
  656.2 13.9 %copy-start.11 = (bf16[320,1280]{1,0:T(8,128)(2,1)S(1)}, bf16[320,1280]{1,0:T(8,128)(2,1)}, u32[]{:S(2)}) copy-start(bf16[320,1280]{1,0:T(8,128)(2,1)} %get-tuple-element.147) | copy-start | bytes 2457604
  658.4 11.8 %collective-permute-start.2 = (bf16[320,640]{1,0:T(8,128)(2,1)}, bf16[320,640]{1,0:T(8,128)(2,1)S(1)}, u32[]{:S(2)}, u32[]{:S(2)}) collective-permute-start(bf16[320,640]{1,0:T(8,128)(2,1)} %reduce-scatter.17.cloned.1.call-done), channel_id=1, source_target_pairs={{16,0},{17,1},{18,2},{19,3},{20,4},{21,5},{22,6},{23,7},{24,8},{25... | collective-permute-start | bytes 1228808 | tf_op jit(solution)/shard_map/ppermute | solution.py:1243
Sparse Core Ops, SparseCore 0:
  24.0 39.6 all-gather.6
  69.8 37.9 all-gather.8
  109.9 37.0 all-gather.10
  149.0 37.0 all-gather.12
  188.0 37.0 all-gather.14
  227.0 64.5 all-gather.16
  308.4 62.5 reduce-scatter.6
  373.3 62.4 reduce-scatter.10
  438.1 62.3 reduce-scatter.8
  511.4 34.8 reduce-scatter.12
  554.3 35.9 reduce-scatter.14
  607.1 38.1 reduce-scatter.16

commit v9 on v8

--- a/solution.py
+++ b/solution.py
@@ -243,6 +243,31 @@
     def wait(self):
         for copy in self.copies:
             copy.wait()
+
+
+class Trade:
+    def __init__(self, keep, send, got, sems):
+        self.keep, self.send, self.got, self.sems = keep, send, got, sems
+        self.tiles = keep.shape[0] // TILE
+
+    def copy(self, n):
+        rows = pl.ds(pl.multiple_of(n * TILE, TILE), TILE)
+        return push(
+            self.send.at[rows], self.got.at[rows], self.sems, n, 1 - lax.axis_index("section"), "section"
+        )
+
+    def start(self, make):
+        @pl.loop(0, self.tiles)
+        def _(n):
+            make(pl.ds(pl.multiple_of(n * TILE, TILE), TILE))
+            self.copy(n).start()
+
+    def finish(self):
+        @pl.loop(0, self.tiles)
+        def _(n):
+            self.copy(n).wait()
+
+        add_into(self.keep, self.got)
 
 
 def add_into(keep_ref, got_ref):
@@ -469,63 +494,7 @@
     scatter.done()
 
 
-def expand_back_kernel(
-    last, group, g_ref, cm_ref, co_ref, em_ref, eo_ref, slope_ref, extra_ref, second_ref, hidden_ref, vec_ref, *refs
-):
-    grad_ref, low_ref, sums_ref, ek_ref, *refs = refs
-    if last:
-        full_ref = g_ref
-        out_ref, *refs = refs
-    else:
-        es_ref, full_ref, c_ref, *refs = refs
-    contract, expand, before, stage, land, total, scatter_sems, gather_sems, local_sems, *refs = refs
-    first = Halves((cm_ref, co_ref), contract, local_sems, 0)
-    then = Halves((em_ref, eo_ref), expand, local_sems, 2)
-    first.start()
-    then.start()
-    sums_ref[...] = jnp.zeros_like(sums_ref)
-    if last:
-        stage4, deliver_sems = refs
-        deliver = Deliver(group, stage4, out_ref, deliver_sems)
-        group.need(6)
-        deliver.start(extra_ref)
-    else:
-        outer, got, swap_sems = refs
-        full_ref[group.chunk(group.me), :] = g_ref[...]
-    first.wait()
-
-    def bend(rows):
-        grad = (nn(full_ref[rows, :], contract[...]) * slope_ref[rows, :].astype(WIDE)).astype(LOW)
-        before[rows, :] = grad
-        sums_ref[4:5, :] += jnp.sum(grad.astype(WIDE), axis=0, keepdims=True)
-
-    if last:
-        group.need(5)
-
-        @pl.loop(0, LENGTH // group.rows)
-        def _(n):
-            bend(group.chunk(n))
-
-        deliver.done()
-    else:
-        Gather(group, full_ref, gather_sems).each(bend, lambda: group.need(5))
-        group.emit(5)
-    then.wait()
-    scatter = Scatter(group, stage, land, total, scatter_sems)
-    scatter.start(lambda rows: nt(before[rows, :], expand[...]))
-    if last:
-        group.need(7)
-        outer_whole(second_ref, before, ek_ref)
-        group.emit(3)
-    else:
-        group.need(6)
-        outer_halves(full_ref, extra_ref, outer.at[0], outer.at[1])
-        swap = push(outer.at[1], got, swap_sems, 0, 1 - lax.axis_index("section"), "section")
-        swap.start()
-        group.need(7)
-        outer_halves(second_ref, before, ek_ref, es_ref)
-        group.emit(3, 4)
-    group.need(8)
+def narrow_grads(group, scatter, full_ref, hidden_ref, vec_ref, grad_ref, low_ref, sums_ref):
     for j in range(PARTS):
         rows = slice(j * group.part, (j + 1) * group.part)
         grad = scatter.take(j)
@@ -536,14 +505,105 @@
         low_ref[rows, :] = out.astype(LOW)
         for n, term in enumerate((grad * hat, grad, own, out)):
             sums_ref[n : n + 1, :] += jnp.sum(term, axis=0, keepdims=True)
+
+
+def bend(rows, full_ref, contract, slope_ref, before, sums_ref):
+    grad = (nn(full_ref[rows, :], contract[...]) * slope_ref[rows, :].astype(WIDE)).astype(LOW)
+    before[rows, :] = grad
+    sums_ref[4:5, :] += jnp.sum(grad.astype(WIDE), axis=0, keepdims=True)
+
+
+def late_expand_kernel(
+    group, active_ref, hidden_ref, cm_ref, co_ref, em_ref, eo_ref, g_ref, slope_ref, second_ref, vec_ref,
+    grad_ref, low_ref, sums_ref, e_ref, out_ref,
+    contract, expand, before, result, stage4,
+    stage_a, land_a, total_a, sems_a, stage, land, total, scatter_sems, deliver_sems, local_sems,
+):
+    first = Halves((cm_ref, co_ref), contract, local_sems, 0)
+    then = Halves((em_ref, eo_ref), expand, local_sems, 2)
+    first.start()
+    then.start()
+    sums_ref[...] = jnp.zeros_like(sums_ref)
+    first.wait()
+    forward = Scatter(group, stage_a, land_a, total_a, sems_a)
+    forward.start(lambda rows: nt(active_ref[rows, :], contract[...]))
+    group.need(6, 7)
+
+    @pl.loop(0, LENGTH // group.rows)
+    def _(n):
+        bend(group.chunk(n), g_ref, contract, slope_ref, before, sums_ref)
+
+    then.wait()
+    scatter = Scatter(group, stage, land, total, scatter_sems)
+    scatter.start(lambda rows: nt(before[rows, :], expand[...]))
+    group.need(1)
+    for j in range(PARTS):
+        rows = slice(j * group.part, (j + 1) * group.part)
+        result[rows, :] = (hidden_ref[rows, :] + forward.take(j) + vec_ref[5:6, :]).astype(LOW)
+    deliver = Deliver(group, stage4, out_ref, deliver_sems)
+    deliver.start(result)
+    group.need(8)
+    outer_whole(second_ref, before, e_ref)
+    group.emit(3)
+    narrow_grads(group, scatter, g_ref, hidden_ref, vec_ref, grad_ref, low_ref, sums_ref)
+    group.emit(0, 1, 2)
+    forward.done()
+    scatter.done()
+    deliver.done()
+
+
+def expand_back_kernel(
+    group, g_ref, cm_ref, co_ref, em_ref, eo_ref, slope_ref, active_ref, second_ref, hidden_ref, vec_ref,
+    grad_ref, low_ref, sums_ref, ek_ref, es_ref, full_ref, c_ref,
+    contract, expand, before, stage, land, total, scatter_sems, gather_sems, local_sems, outer, got, trade_sems,
+):
+    section = lax.axis_index("section")
+    first = Halves((cm_ref, co_ref), contract, local_sems, 0)
+    then = Halves((em_ref, eo_ref), expand, local_sems, 2)
+    first.start()
+    then.start()
+    sums_ref[...] = jnp.zeros_like(sums_ref)
+    full_ref[group.chunk(group.me), :] = g_ref[...]
+    first.wait()
+    Gather(group, full_ref, gather_sems).each(
+        lambda rows: bend(rows, full_ref, contract, slope_ref, before, sums_ref), lambda: group.need(5)
+    )
+    group.emit(5)
+    group.need(6)
+    half = active_ref.shape[1] // 2
+
+    def columns(place):
+        return pl.ds(pl.multiple_of(place * half, half), half)
+
+    def make(n):
+        def tile(rows):
+            place = section if n == 0 else 1 - section
+            outer[n, rows, :] = tn(full_ref[:, rows], active_ref[:, columns(place)]).astype(LOW)
+
+        return tile
+
+    trade = Trade(outer.at[0], outer.at[1], got, trade_sems)
+    trade.start(make(1))
+    then.wait()
+    scatter = Scatter(group, stage, land, total, scatter_sems)
+    scatter.start(lambda rows: nt(before[rows, :], expand[...]))
+    group.need(7)
+    outer_halves(second_ref, before, ek_ref, es_ref)
+    group.emit(3, 4)
+    keep = make(0)
+
+    @pl.loop(0, outer.shape[1] // TILE)
+    def _(n):
+        keep(pl.ds(pl.multiple_of(n * TILE, TILE), TILE))
+
+    group.need(8)
+    narrow_grads(group, scatter, full_ref, hidden_ref, vec_ref, grad_ref, low_ref, sums_ref)
     group.emit(0, 1, 2)
     scatter.done()
-    if not last:
-        swap.wait()
-        add_into(outer.at[0], got)
-        store = pltpu.make_async_copy(outer.at[0], c_ref, local_sems.at[0])
-        store.start()
-        store.wait()
+    trade.finish()
+    store = pltpu.make_async_copy(outer.at[0], c_ref, local_sems.at[0])
+    store.start()
+    store.wait()
 
 
 def scores_back(group, heads, low_ref, weight, heads_ref, o_ref, lse_ref, full, go3, dots, g3, accs, mixed, gather_sems, needs):
@@ -666,34 +726,45 @@
     scatter = Scatter(group, stage, land, total, scatter_sems)
     group.need(1, 6)
 
-    @pl.loop(0, weight.shape[0] // TILE)
-    def _(n):
-        rows = pl.ds(pl.multiple_of(n * TILE, TILE), TILE)
-        outer[section, rows, :] = tn(normed_ref[:, rows], mixed[:, :half]).astype(LOW)
-        outer[1 - section, rows, : 3 * width - half] = tn(
-            normed_ref[:, rows], mixed[:, half:]
-        ).astype(LOW)
-        outer[1 - section, rows, 3 * width - half :] = outer_ref[rows, :]
-
-    swap = push(outer.at[1], got, swap_sems, 0, 1 - section, "section")
-    swap.start()
+    def make(n):
+        place = section if n == 0 else 1 - section
+
+        def tile(rows):
+            @pl.when(place == 0)
+            def _():
+                outer[n, rows, :] = tn(normed_ref[:, rows], mixed[:, :half]).astype(LOW)
+
+            @pl.when(place == 1)
+            def _():
+                outer[n, rows, : 3 * width - half] = tn(normed_ref[:, rows], mixed[:, half:]).astype(LOW)
+                outer[n, rows, 3 * width - half :] = outer_ref[rows, :]
+
+        return tile
+
+    trade = Trade(outer.at[0], outer.at[1], got, swap_sems)
+    trade.start(make(1))
     halves.wait()
     scatter.start(lambda rows: nt(mixed[rows, :], weight[:, : 3 * width]))
+    keep = make(0)
+
+    @pl.loop(0, outer.shape[1] // TILE)
+    def _(n):
+        keep(pl.ds(pl.multiple_of(n * TILE, TILE), TILE))
+
     group.need(2, 3)
     attend_grads(group, scatter, x_ref, grad_ref, vec_ref, mixed, width, out_ref, sums_ref)
     group.emit(1, 2)
     scatter.done()
-    swap.wait()
-    add_into(outer.at[0], got)
+    trade.finish()
     store = pltpu.make_async_copy(outer.at[0], w_ref, local_sems.at[2])
     store.start()
     store.wait()
 
 
 def finish_kernel(
-    late_ref, early1_ref, early2_ref, near_ref, far_ref, a0, n0, a1, n1,
-    grads_ref, sums_ref, got_late, got_early1, got_early2,
-    mine, stage4, block, land_col, land_x, land_z, send, land,
+    late1_ref, late2_ref, early1_ref, early2_ref, near_ref, far_ref, a0, n0, a1, n1,
+    grads_ref, sums_ref, got_late1, got_late2, got_early1, got_early2,
+    mine, stage4, block, land_col, land_x, land_z, land,
     deliver_sems, col_sems, x_sems, z_sems, part_sems,
 ):
     section, row = lax.axis_index("section"), lax.axis_index("row")
@@ -704,18 +775,26 @@
     parts = [
         push(source, into, part_sems, n, 1 - section, "section")
         for n, (source, into) in enumerate(
-            ((late_ref, got_late), (early1_ref, got_early1), (early2_ref, got_early2))
+            (
+                (late1_ref, got_late1), (late2_ref, got_late2),
+                (early1_ref, got_early1), (early2_ref, got_early2),
+            )
         )
     ]
+
+    swap_far = push(far_ref, land, x_sems, 1, 1 - section, "section")
+    swap_near = push(mine, land, x_sems, 1, 1 - section, "section")
 
     @pl.when(section == 0)
     def _():
         parts[0].start()
+        parts[1].start()
+        swap_far.start()
 
     @pl.when(section == 1)
     def _():
-        parts[1].start()
         parts[2].start()
+        parts[3].start()
 
     deliver = Deliver(group, stage4, mine, deliver_sems)
     deliver.start(near_ref)
@@ -754,16 +833,10 @@
 
     deliver.done()
 
-    @pl.when(section == 0)
-    def _():
-        send[...] = far_ref[...]
-
     @pl.when(section == 1)
     def _():
-        send[...] = mine[...]
-
-    swap = push(send, land, x_sems, 1, 1 - section, "section")
-    swap.start()
+        swap_near.start()
+
     own = pl.ds(pl.multiple_of(section * length, length), length)
     away = pl.ds(pl.multiple_of((1 - section) * length, length), length)
 
@@ -781,20 +854,29 @@
     for n in range(1, land_z.shape[0]):
         result = result + land_z[n]
     sums_ref[...] = result
-    swap.wait()
+    @pl.when(section == 0)
+    def _():
+        swap_far.wait()
+
+    @pl.when(section == 1)
+    def _():
+        swap_near.wait()
+
     grads_ref[away, :] = land[...].astype(WIDE)
 
     @pl.when(section == 0)
     def _():
         parts[0].wait_send()
-        parts[1].wait_recv()
+        parts[1].wait_send()
         parts[2].wait_recv()
+        parts[3].wait_recv()
 
     @pl.when(section == 1)
     def _():
-        parts[1].wait_send()
         parts[2].wait_send()
+        parts[3].wait_send()
         parts[0].wait_recv()
+        parts[1].wait_recv()
 
 
 VM = pl.BlockSpec(memory_space=pltpu.VMEM)
@@ -940,33 +1022,52 @@
     )
 
 
-def expand_back_call(number, last, grad, contract, expand, slope, extra, second, hidden, vec, swaps):
+def late_expand_call(number, active, hidden, contract, expand, grad, slope, second, vec, swaps):
     rows, size = hidden.shape
     wide = slope.shape[1]
     columns = LENGTH // rows
-    outs = [shape((rows, size), WIDE), shape((rows, size)), shape((8, size), WIDE)]
+    outs = [
+        shape((rows, size), WIDE), shape((rows, size)), shape((8, size), WIDE),
+        shape((size, wide)), shape((LENGTH, size // columns)),
+    ]
+    scratch = [
+        pltpu.VMEM((size, wide), LOW),
+        pltpu.VMEM((size, wide), LOW),
+        pltpu.VMEM((LENGTH, wide), LOW),
+        pltpu.VMEM((rows, size), LOW),
+        pltpu.VMEM((columns, rows, size // columns), LOW),
+        *scatter_scratch(rows, size), *scatter_scratch(rows, size),
+        pltpu.SemaphoreType.DMA((2, 3)), LOCAL,
+    ]
+    return launch(
+        late_expand_kernel,
+        number, rows, [VM, VM, ANY, ANY, ANY, ANY, VM, VM, VM, VM],
+        (active, hidden, *contract, *expand, grad, slope, second, vec),
+        outs, [VM] * 5, scratch, swaps, True, late=(1, 6, 7, 8),
+    )
+
+
+def expand_back_call(number, grad, contract, expand, slope, active, second, hidden, vec, swaps):
+    rows, size = hidden.shape
+    wide = slope.shape[1]
+    half = wide // 2
+    outs = [
+        shape((rows, size), WIDE), shape((rows, size)), shape((8, size), WIDE),
+        shape((size, half)), shape((size, half)), shape((LENGTH, size)), shape((size, half)),
+    ]
     scratch = [
         pltpu.VMEM((size, wide), LOW),
         pltpu.VMEM((size, wide), LOW),
         pltpu.VMEM((LENGTH, wide), LOW),
         *scatter_scratch(rows, size), PAIRS, LOCAL,
+        pltpu.VMEM((2, size, half), LOW), pltpu.VMEM((size, half), LOW),
+        pltpu.SemaphoreType.DMA((2, size // TILE)),
     ]
-    if last:
-        outs += [shape((size, wide)), shape((LENGTH, size // columns))]
-        out_specs = [VM] * 5
-        scratch += [pltpu.VMEM((columns, rows, size // columns), LOW), pltpu.SemaphoreType.DMA((2, 3))]
-    else:
-        outs += [shape((size, wide // 2))] * 2 + [shape((LENGTH, size)), shape((size, wide // 2))]
-        out_specs = [VM] * 6 + [ANY]
-        scratch += [
-            pltpu.VMEM((2, size, wide // 2), LOW), pltpu.VMEM((size, wide // 2), LOW),
-            pltpu.SemaphoreType.DMA((2, 1)),
-        ]
     return launch(
-        functools.partial(expand_back_kernel, last),
+        expand_back_kernel,
         number, rows, [VM, ANY, ANY, ANY, ANY, VM, VM, VM, VM, VM],
-        (grad, *contract, *expand, slope, extra, second, hidden, vec),
-        outs, out_specs, scratch, swaps, last, not last, late=(5, 6, 7, 8),
+        (grad, *contract, *expand, slope, active, second, hidden, vec),
+        outs, [VM] * 6 + [ANY], scratch, swaps, False, True, late=(5, 6, 7, 8),
     )
 
 
@@ -1028,7 +1129,7 @@
         pltpu.VMEM((size, 4 * width), LOW),
         pltpu.VMEM((2, size, half), LOW),
         pltpu.VMEM((size, half), LOW),
-        *scatter_scratch(rows, size), LOCAL, pltpu.SemaphoreType.DMA((2, 1)),
+        *scatter_scratch(rows, size), LOCAL, pltpu.SemaphoreType.DMA((2, size // TILE)),
     ]
     return launch(
         attend_back_kernel,
@@ -1038,14 +1139,14 @@
     )[0]
 
 
-def finish_call(number, late, early1, early2, near, far, sums, row_count):
+def finish_call(number, late, early, near, far, sums, row_count):
     rows, size = near.shape
     length, width = far.shape
     columns = length // rows
     outs = (
         shape((2 * length, width), WIDE),
         shape((16, width), WIDE),
-        *[shape(part.shape) for part in (late, early1, early2)],
+        *[shape(part.shape) for part in (*late, *early)],
     )
     scratch = [
         pltpu.VMEM((length, width), LOW),
@@ -1055,24 +1156,23 @@
         pltpu.VMEM((16, width), WIDE),
         pltpu.VMEM((row_count, 16, width), WIDE),
         pltpu.VMEM((length, width), LOW),
-        pltpu.VMEM((length, width), LOW),
         pltpu.SemaphoreType.DMA((2, 3)),
         pltpu.SemaphoreType.DMA((2, 3)),
         pltpu.SemaphoreType.DMA((2, 2)),
         pltpu.SemaphoreType.DMA((2, row_count)),
-        pltpu.SemaphoreType.DMA((2, 3)),
+        pltpu.SemaphoreType.DMA((2, 4)),
     ]
     return pl.pallas_call(
         finish_kernel,
         out_shape=outs,
-        in_specs=[ANY] * 3 + [VM] * 6,
-        out_specs=(VM, VM, ANY, ANY, ANY),
+        in_specs=[ANY] * 4 + [VM] * 6,
+        out_specs=(VM, VM) + (ANY,) * 4,
         scratch_shapes=scratch,
         compiler_params=pltpu.CompilerParams(
             collective_id=number, has_side_effects=True, vmem_limit_bytes=GRANT
         ),
         cost_estimate=pl.CostEstimate(flops=int(3e10), bytes_accessed=30 * MEBI, transcendentals=0),
-    )(late, early1, early2, near, far, *sums)
+    )(*late, *early, near, far, *sums)
 
 
 def swap_sections(value):
@@ -1186,14 +1286,11 @@
         contract = (mats[layer][2], mats[layer][2] if last else others[0])
         if last:
             c1 = outs[3]
-        outs, others = contract_call(
-            4 + 3 * layer, active, hidden, contract, vec, [] if last else [mats[1][0]]
-        )
         pairs.append((attn, expand, contract))
         kept.append((normed, heads, o, lse, hidden, second, active, slope))
-        x = outs[0]
-        owns.append(x)
         if not last:
+            (x,), others = contract_call(4, active, hidden, contract, vec, [mats[1][0]])
+            owns.append(x)
             attn = (mats[1][0], others[0])
     y0 = own_features(full)
 
@@ -1205,22 +1302,22 @@
 
     attn, expand, contract = pairs[1]
     normed, heads, o, lse, hidden, second, active, slope = kept[1]
-    (grad_hidden, low, expand_sums1, e1, y1), _ = expand_back_call(
-        8, True, gy_full, contract, expand, slope, owns[2], second, hidden, wide_vectors[1], []
+    (grad_hidden, low, expand_sums1, e1, y1), _ = late_expand_call(
+        8, active, hidden, contract, expand, gy_full, slope, second, wide_vectors[1], []
     )
     layer_low, layer_high = pick(y0, y1), pick(y1, y0)
-    part_c1, low = tie(scatter(c1), low)
-    (gx1_own, attend_sums1, w1), (layer_got, far_c1) = late_attend_call(
-        10, low, grad_hidden, owns[1], attn, normed, heads, o, lse, wide_vectors[1], [layer_high, part_c1]
+    (gx1_own, attend_sums1, w1), (layer_got,) = late_attend_call(
+        10, low, grad_hidden, owns[1], attn, normed, heads, o, lse, wide_vectors[1], [layer_high]
     )
     layer_outputs = jnp.concatenate([pick(layer_low, layer_got), pick(layer_got, layer_low)], 0)
 
     attn, expand, contract = pairs[0]
     normed, heads, o, lse, hidden, second, active, slope = kept[0]
-    part_e1 = scatter(e1)
-    (grad_hidden, low, expand_sums0, ek0, es0, gx1_full, total_c0), (far_e1,) = expand_back_call(
-        12, False, gx1_own, contract, expand, slope, active, second, hidden, wide_vectors[0], [part_e1]
-    )
+    part_c1 = scatter(c1)
+    (grad_hidden, low, expand_sums0, ek0, es0, gx1_full, total_c0), (far_c1,) = expand_back_call(
+        12, gx1_own, contract, expand, slope, active, second, hidden, wide_vectors[0], [part_c1]
+    )
+    part_e1, low = tie(scatter(e1), low)
     mixed, outer, total_e0 = scores_back_call(14, low, attn, heads, o, lse, ek0, es0)
     part_w1, mixed = tie(scatter(w1), mixed)
     part_c0, mixed = tie(scatter(total_c0), mixed)
@@ -1228,11 +1325,10 @@
         15, mixed, outer, grad_hidden, owns[0], attn, normed, wide_vectors[0]
     )
     part_e0 = scatter(total_e0)
-    input_grads, small_grads, far_w1, far_c0, far_e0 = finish_call(
+    input_grads, small_grads, far_e1, far_w1, far_c0, far_e0 = finish_call(
         16,
-        part_w1,
-        part_c0,
-        part_e0,
+        (part_e1, part_w1),
+        (part_c0, part_e0),
         gx0_own,
         own_features(gx1_full),
         (attend_sums0, expand_sums0, attend_sums1, expand_sums1),

time: 688 us -> 698 us (1.015)
  Pallas kernels: 565 us -> 574 us
    pallas_call x1, Pallas kernels: 43.4 us -> 77.5 us  [finish_call(): pl.pallas_call(finish_kernel, out_shape=outs, in_specs=[ANY] * 4 + [VM] *...]
    pallas_call x11 -> x10, Pallas kernels: 478 us -> 453 us  [launch(): pl.pallas_call(kernel, out_shape=(*outs, *[shape(s.shape, s.dtype) for s...]
  transfers between devices with their start and end apart: 15 -> 15, of which waited for: 6 -> 5; matrix products, arithmetic and copies ran while one was open for 4% -> 4% of each run, Pallas kernels for 83% -> 83%
where the time goes in v9:
time: 698 us; the launch traced here: 692 us
  Pallas kernels  574 us (82%)
  waiting for transfers between devices  53.5 us (8%)
  local copies, waits for them, and re-layouts  28.8 us (4%)
  between operations  15.2 us (2%)
  other arithmetic  13.5 us (2%)
    pallas_call x10, Pallas kernels, launch(): pl.pallas_call(kernel, out_shape=(*outs, *[shape(s.shape, s.dtype) for s...  453 us
    pallas_call x1, Pallas kernels, finish_call(): pl.pallas_call(finish_kernel, out_shape=outs, in_specs=[ANY] * 4 + [VM] *...  77.5 us
    pallas_call x1, Pallas kernels, start_call(): pl.pallas_call(start_kernel, out_shape=outs, in_specs=[ANY] * 5, out_spec...  43.6 us
    all_gather x6, waiting for transfers between devices, gather_blocks(): return lax.all_gather(block, 'row', axis=0, tiled=True)  30.8 us
    unnamed x62, local copies, waits for them, and re-layouts  17.1 us
  transfers between devices with their start and end apart: 15, of which 5 were waited for; matrix products, arithmetic and copies ran while one was open for 4% of the time, Pallas kernels for 83%

profile of v9, /device:TPU:0, one launch (start us, length us, event | category | flops | bytes accessed | tf_op | source)
XLA Modules:
  0.0 691.5 jit_solution(9207206058616104276)
XLA Ops:
  7.2 1.1 copy.38
  8.4 1.5 copy.37
  10.4 3.0 collective-permute-start
  13.5 1.5 copy.41.tokens_ref
  15.1 2.6 copy.42.cotangent_ref
  17.9 0.6 pad.8.small_ref
  18.5 0.8 broadcast_select_fusion.11.expand_ref
  19.3 3.6 collective-permute-done
  22.9 1.0 broadcast_select_fusion.5
  23.9 43.6 %shard_map.245 = (bf16[1024,1280]{1,0:T(8,128)(2,1)}, bf16[1024,1280]{1,0:T(8,128)(2,1)}, bf16[2,4,16,320]{3,2,1,0:T(8,128)(2,1)}, bf16[320,640]{1,0:T(8,128)(2,1)}, bf16[320,1280]{1,0:T(8,128)(2,1)}) custom-call(bf16[2048,320]{1,0:T(8,128)(2,1)} %copy.41.tokens_ref, bf16[2048,320]{1,0:T(8,128)(2,1)} %copy.42.cotangent_ref, bf16[16,320]{1,0:T(8,128)(2,1)} %pad.8.small_ref, ...), custom_call_target="tpu_custom_call" | custom-call | flops 30000001024 | bytes 31457280 | tf_op jit(solution)/shard_map/pallas_call | solution.py:961
  67.6 2.1 broadcast_select_fusion.6
  69.8 0.8 fusion
  72.5 0.7 squeeze.48.refs_3_
  73.2 0.7 squeeze.45.refs_3_
  74.0 0.7 squeeze.47.refs_4_
  74.7 0.7 squeeze.44.refs_4_
  75.4 1.0 broadcast_select_fusion
  76.5 0.6 fusion.2
  77.1 30.7 %all-gather.9.cloned.1.call-done.refs_5_.refs_1_.refs_3_ = bf16[1280,640]{1,0:T(8,128)(2,1)} async-done(((bf16[320,640]{1,0:T(8,128)(2,1)}), bf16[1280,640]{1,0:T(8,128)(2,1)}) %all-gather.9.cloned.1.call-update) | async-done | bytes 1638416 | tf_op jit(solution)/shard_map/all_gather | solution.py:1246
  107.8 3.0 collective-permute-done.1.refs_2_.refs_5_
  110.8 1.2 copy-done.26
  111.9 39.0 %shard_map.246 = (bf16[16,128]{1,0:T(8,128)(2,1)}, bf16[1024,1280]{1,0:T(8,128)(2,1)}, bf16[15,1024,64]{2,1,0:T(8,128)(2,1)}, bf16[1024,320]{1,0:T(8,128)(2,1)},...) custom-call(bf16[1024,1280]{1,0:T(8,128)(2,1)} %get-tuple-element.84.refs_0_, ...), custom_call_target="tpu_custom_call" | custom-call | flops 30000001024 | bytes 31457280 | tf_op jit(solution)/shard_map/pallas_call | solution.py:933
  151.0 38.4 %shard_map.247 = (bf16[1024,1280]{1,0:T(8,128)(2,1)}, bf16[1024,1280]{1,0:T(8,128)(2,1)}, bf16[1024,1280]{1,0:T(8,128)(2,1)}, bf16[1280,640]{1,0:T(8,128)(2,1)}) custom-call(bf16[256,1280]{1,0:T(8,128)(2,1)} %get-tuple-element.88.refs_0_, bf16[1280,640]{1,0:T(8,128)(2,1)} %all-gather.9.cloned.1.call-done.refs_5_.refs_1_.refs_3_, ...), custom_call_target="tpu_custom_call" | custom-call | flops 30000001024 | bytes 31457280 | tf_op jit(solution)/shard_map/pallas_call | solution.py:933
  189.4 38.6 %shard_map.248 = (bf16[256,1280]{1,0:T(8,128)(2,1)}, bf16[1280,640]{1,0:T(8,128)(2,1)}) custom-call(bf16[1024,1280]{1,0:T(8,128)(2,1)} %get-tuple-element.91.refs_0_.refs_6_, f32[256,1280]{1,0:T(8,128)} %get-tuple-element.92.refs_1_.refs_8_, bf16[1280,640]{1,0:T(8,128)(2,1)} %all-gather.11.cloned.1.call-done.refs_4_.refs_2_.refs_1_, ...), custom_call_target="tpu_custom_call" | custom-call | flops 30000001024 | bytes 31457280 | tf_op jit(solution)/shard_map/pallas_call | solution.py:933
  228.1 51.8 %shard_map.249 = (bf16[1024,1280]{1,0:T(8,128)(2,1)}, bf16[1024,1280]{1,0:T(8,128)(2,1)}, bf16[15,1024,64]{2,1,0:T(8,128)(2,1)}, bf16[1024,320]{1,0:T(8,128)(2,1...) custom-call(bf16[256,1280]{1,0:T(8,128)(2,1)} %get-tuple-element.94.refs_0_., ...), custom_call_target="tpu_custom_call" | custom-call | flops 30000001024 | bytes 31457280 | tf_op jit(solution)/shard_map/pallas_call | solution.py:933
  279.8 28.2 %shard_map.250 = (bf16[1024,1280]{1,0:T(8,128)(2,1)}, bf16[1024,1280]{1,0:T(8,128)(2,1)}, bf16[1024,1280]{1,0:T(8,128)(2,1)}, bf16[1280,1280]{1,0:T(8,128)(2,1)}) custom-call(bf16[256,1280]{1,0:T(8,128)(2,1)} %get-tuple-element.97.refs_0_, bf16[1280,640]{1,0:T(8,128)(2,1)} %all-gather.15.cloned.1.call-done.refs_5_.refs_1_.refs_4_, ...), custom_call_target="tpu_custom_call" | custom-call | flops 30000001024 | bytes 31457280 | tf_op jit(solution)/shard_map/pallas_call | solution.py:933
  308.4 48.9 %shard_map.251 = (f32[256,1280]{1,0:T(8,128)}, bf16[256,1280]{1,0:T(8,128)(2,1)}, f32[8,1280]{1,0:T(8,128)}, bf16[1280,1280]{1,0:T(8,128)(2,1)}, bf16[1024,320]{1,0:T(8,128)(2,1)}) custom-call(bf16[1024,1280]{1,0:T(8,128)(2,1)} %get-tuple-element.100.refs_0_, f32[256,1280]{1,0:T(8,128)} %get-tuple-element.101.refs_1_, ...), custom_call_target="tpu_custom_call" | custom-call | flops 30000001024 | bytes 31457280 | tf_op jit(solution)/shard_map/pallas_call | solution.py:933
  357.8 0.6 copy-done.2
  358.5 1.3 broadcast_select_fusion.3.refs_10_
  359.8 59.7 %shard_map.252 = (bf16[256,1280]{1,0:T(8,128)(2,1)}, f32[8,1280]{1,0:T(8,128)}, bf16[1280,1280]{1,0:T(8,128)(2,1)}, bf16[1024,320]{1,0:T(8,128)(2,1)}) custom-call(bf16[256,1280]{1,0:T(8,128)(2,1)} %get-tuple-element.105.refs_0_, f32[256,1280]{1,0:T(8,128)} %get-tuple-element.106.refs_1_, bf16[256,1280]{1,0:T(8,128)(2,1)} %get-tuple-element.94.refs_0_.refs_2_, ...), custom_call_target="tpu_custom_call" | custom-call | flops 30000001024 | bytes 31457280 | tf_op jit(solution)/shard_map/pallas_call | solution.py:933
  419.8 64.0 %shard_map.253 = (f32[256,1280]{1,0:T(8,128)}, bf16[256,1280]{1,0:T(8,128)(2,1)}, f32[8,1280]{1,0:T(8,128)}, bf16[1280,640]{1,0:T(8,128)(2,1)}, bf16[1280,640]{1...) custom-call(bf16[256,1280]{1,0:T(8,128)(2,1)} %get-tuple-element.113.refs_0_, ...), custom_call_target="tpu_custom_call" | custom-call | flops 30000001024 | bytes 31457280 | tf_op jit(solution)/shard_map/pallas_call | solution.py:933
  484.1 2.0 constant_dynamic-slice_fusion.1.refs_3_
  486.1 41.2 %shard_map.254 = (bf16[1024,960]{1,0:T(8,128)(2,1)}, bf16[1280,320]{1,0:T(8,128)(2,1)}, bf16[1280,640]{1,0:T(8,128)(2,1)}) custom-call(bf16[256,1280]{1,0:T(8,128)(2,1)} %get-tuple-element.120.refs_0_, bf16[1280,640]{1,0:T(8,128)(2,1)} %all-gather.7.cloned.1.call-done.refs_1_.refs_4_, bf16[1280,640]{1,0:T(8,128)(2,1)} %copy-done.26, ...), custom_call_target="tpu_custom_call" | custom-call | flops 30000001024 | bytes 31457280 | tf_op jit(solution)/shard_map/pallas_call | solution.py:933
  527.7 1.8 broadcast_select_fusion.2
  529.7 1.5 copy.46
  531.2 2.4 constant_dynamic-slice_fusion.far_ref
  533.7 5.2 reduce-scatter.13.cloned.1.call-done.early1_ref
  538.9 42.9 %shard_map.255 = (bf16[1280,640]{1,0:T(8,128)(2,1)}, bf16[256,1280]{1,0:T(8,128)(2,1)}, f32[8,1280]{1,0:T(8,128)}) custom-call(bf16[1024,960]{1,0:T(8,128)(2,1)} %get-tuple-element.132.refs_0_, bf16[1280,320]{1,0:T(8,128)(2,1)} %get-tuple-element.133.refs_1_, f32[256,1280]{1,0:T(8,128)} %get-tuple-element.134.refs_2_, ...), custom_call_target="tpu_custom_call" | custom-call | flops 30000001024 | bytes 31457280 | tf_op jit(solution)/shard_map/pallas_call | solution.py:933
  581.9 77.5 %shard_map.256 = (f32[2048,320]{1,0:T(8,128)}, f32[16,320]{1,0:T(8,128)}, bf16[320,1280]{1,0:T(8,128)(2,1)}, bf16[320,1280]{1,0:T(8,128)(2,1)}, bf16[320,640]{1,0:T(8,128)(2,1)}, /*index=5*/bf16[320,640]{1,0:T(8,128)(2,1)}) custom-call(bf16[320,1280]{1,0:T(8,128)(2,1)} %reduce-scatter.7.cloned.1.call-done.late1_ref, ...), custom_call_target="tpu_custom_call" | custom-call | flops 30000001024 | bytes 31457280 | tf_op jit(solution)/shard_map/pallas_call | solution.py:1165
  659.5 3.5 copy.47
  663.1 1.4 select_bitcast_fusion
  665.2 1.4 select_bitcast_fusion.1
  666.7 0.7 reshape.45
  667.4 1.3 collective-permute-start.2
  669.8 9.7 %collective-permute-done.2 = bf16[320,640]{1,0:T(8,128)(2,1)S(1)} collective-permute-done((bf16[320,640]{1,0:T(8,128)(2,1)}, bf16[320,640]{1,0:T(8,128)(2,1)S(1)}, u32[]{:S(2)}, u32[]{:S(2)}) %collective-permute-start.2) | collective-permute-done | bytes 409632 | tf_op jit(solution)/shard_map/ppermute | solution.py:1339
  679.5 1.3 add_select_fusion
  681.2 1.0 copy.49
  682.6 1.6 copy.48
  (109 shorter events, 7.6 us)
Async XLA Ops:
  7.2 64.8 %all-gather.7.cloned.1.call-start = ((), (), s32[]{:S(2)}) async-start(), calls=%async_computation.6 | async-start | bytes 2048000 | tf_op jit(solution)/shard_map/all_gather | solution.py:1246
  9.9 3.6 copy-start.18
  9.9 3.7 copy-start.4
  10.4 12.5 %collective-permute-start = (bf16[320,640]{1,0:T(8,128)(2,1)S(1)}, bf16[320,640]{1,0:T(8,128)(2,1)S(1)}, u32[]{:S(2)}, u32[]{:S(2)}) collective-permute-start(bf16[320,640]{1,0:T(8,128)(2,1)S(1)} %get-tuple-element.180), channel_id=1, source_target_pairs={{0,16},{16,0},{1,17},{17,1},{2,18},{18,2},{3,19},{19,3},{4,20},{20... | collective-permute-start | bytes 1228808 | tf_op jit(solution)/shard_map/ppermute | solution.py:1179
  15.1 2.7 copy-start.19
  15.1 2.7 copy-start.20
  15.1 2.7 copy-start.21
  15.1 2.7 copy-start.22
  15.1 2.7 copy-start.23
  15.1 2.7 copy-start.24
  15.1 2.7 copy-start.25
  15.1 3.3 copy-start
  23.9 83.9 %all-gather.9.cloned.1.call-start = ((), (), s32[]{:S(2)}) async-start(), calls=%async_computation.7 | async-start | bytes 2048000 | tf_op jit(solution)/shard_map/all_gather | solution.py:1246
  67.5 2.2 copy-start.1
  67.6 2.2 copy-start.3
  69.7 2.2 copy-start.16
  69.7 81.3 %all-gather.11.cloned.1.call-start = ((), (), s32[]{:S(2)}) async-start(), calls=%async_computation.8 | async-start | bytes 2048000 | tf_op jit(solution)/shard_map/all_gather | solution.py:1246
  70.6 118.8 %all-gather.13.cloned.1.call-start = ((), (), s32[]{:S(2)}) async-start(), calls=%async_computation.9 | async-start | bytes 2048000 | tf_op jit(solution)/shard_map/all_gather | solution.py:1246
  71.2 156.9 %all-gather.15.cloned.1.call-start = ((), (), s32[]{:S(2)}) async-start(), calls=%async_computation.10 | async-start | bytes 2048000 | tf_op jit(solution)/shard_map/all_gather | solution.py:1246
  71.8 236.6 %all-gather.17.cloned.1.call-start = ((), (), s32[]{:S(2)}) async-start(), calls=%async_computation.11 | async-start | bytes 4096000 | tf_op jit(solution)/shard_map/all_gather | solution.py:1246
  72.0 38.7 %collective-permute-start.1 = (bf16[1280,640]{1,0:T(8,128)(2,1)}, bf16[1280,640]{1,0:T(8,128)(2,1)S(1)}, u32[]{:S(2)}, u32[]{:S(2)}) collective-permute-start(bf16[1280,640]{1,0:T(8,128)(2,1)} %all-gather.7.cloned.1.call-done.refs_1_.refs_4_), channel_id=1, source_target_pairs={{0,16},{16,0},{1,17},{17,1},{2,18},{18,2},{3,19},{19,3},{4,20},{20... | collective-permute-start | bytes 4915208 | tf_op jit(solution)/shard_map/ppermute | solution.py:1179
  76.4 343.4 %reduce-scatter.9.cloned.1.call-start = ((), (), s32[]{:S(2)}) async-start(), calls=%async_computation.13 | async-start | bytes 4096000 | tf_op jit(solution)/shard_map/reduce_scatter | solution.py:1298
  110.8 1.2 copy-start.26
  308.1 178.0 %reduce-scatter.7.cloned.1.call-start = ((), (), s32[]{:S(2)}) async-start(), calls=%async_computation.12 | async-start | bytes 4096000 | tf_op jit(solution)/shard_map/reduce_scatter | solution.py:1298
  308.4 49.4 %copy-start.5 = (bf16[1024,1280]{1,0:T(8,128)(2,1)S(1)}, bf16[1024,1280]{1,0:T(8,128)(2,1)}, u32[]{:S(2)}) copy-start(bf16[1024,1280]{1,0:T(8,128)(2,1)} %get-tuple-element.96) | copy-start | bytes 7864324
  357.3 1.1 copy-start.2
  357.4 176.3 %reduce-scatter.11.cloned.1.call-start = ((), (), s32[]{:S(2)}) async-start(), calls=%async_computation.14 | async-start | bytes 4096000 | tf_op jit(solution)/shard_map/reduce_scatter | solution.py:1298
  419.6 119.3 %reduce-scatter.13.cloned.1.call-start = ((), (), s32[]{:S(2)}) async-start(), calls=%async_computation.15 | async-start | bytes 2048000 | tf_op jit(solution)/shard_map/reduce_scatter | solution.py:1298
  483.8 98.0 %reduce-scatter.15.cloned.1.call-start = ((), (), s32[]{:S(2)}) async-start(), calls=%async_computation.16 | async-start | bytes 2048000 | tf_op jit(solution)/shard_map/reduce_scatter | solution.py:1298
  527.4 139.3 %reduce-scatter.17.cloned.1.call-start = ((), (), s32[]{:S(2)}) async-start(), calls=%async_computation.17 | async-start | bytes 2048000 | tf_op jit(solution)/shard_map/reduce_scatter | solution.py:1298
  659.4 3.6 copy-start.6
  659.4 3.6 copy-start.9
  659.4 3.6 copy-start.12
  659.4 3.6 copy-start.15
  663.0 1.5 copy-start.7
  663.0 1.8 copy-start.11
  663.0 2.1 copy-start.13
  663.1 2.2 copy-start.14
  665.2 1.4 copy-start.17
  665.2 14.3 %copy-start.8 = (bf16[320,1280]{1,0:T(8,128)(2,1)S(1)}, bf16[320,1280]{1,0:T(8,128)(2,1)}, u32[]{:S(2)}) copy-start(bf16[320,1280]{1,0:T(8,128)(2,1)} %reduce-scatter.11.cloned.1.call-done.late2_ref) | copy-start | bytes 2457604
  665.2 14.3 %copy-start.10 = (bf16[320,1280]{1,0:T(8,128)(2,1)S(1)}, bf16[320,1280]{1,0:T(8,128)(2,1)}, u32[]{:S(2)}) copy-start(bf16[320,1280]{1,0:T(8,128)(2,1)} %get-tuple-element.147) | copy-start | bytes 2457604
  667.4 12.2 %collective-permute-start.2 = (bf16[320,640]{1,0:T(8,128)(2,1)}, bf16[320,640]{1,0:T(8,128)(2,1)S(1)}, u32[]{:S(2)}, u32[]{:S(2)}) collective-permute-start(bf16[320,640]{1,0:T(8,128)(2,1)} %reduce-scatter.17.cloned.1.call-done), channel_id=1, source_target_pairs={{16,0},{17,1},{18,2},{19,3},{20,4},{21,5},{22,6},{23,7},{24,8},{25... | collective-permute-start | bytes 1228808 | tf_op jit(solution)/shard_map/ppermute | solution.py:1339
Sparse Core Ops, SparseCore 0:
  24.0 39.6 all-gather.6
  69.8 37.9 all-gather.8
  109.9 37.0 all-gather.10
  149.0 37.0 all-gather.12
  188.0 37.0 all-gather.14
  227.1 64.5 all-gather.16
  308.2 62.5 reduce-scatter.8
  373.1 62.3 reduce-scatter.6
  437.8 62.3 reduce-scatter.10
  502.4 36.4 reduce-scatter.12
  541.3 35.3 reduce-scatter.14
  582.0 34.5 reduce-scatter.16

commit v10 on v9

--- a/solution.py
+++ b/solution.py
@@ -761,43 +761,57 @@
     store.wait()
 
 
+class OneWay:
+    def __init__(self, up, down, sems):
+        self.section = lax.axis_index("section")
+        both = [*up, *down]
+        copies = [
+            push(source, into, sems, n, 1 - self.section, "section")
+            for n, (source, into) in enumerate(both)
+        ]
+        self.up, self.down = copies[: len(up)], copies[len(up) :]
+
+    def each(self, first, second):
+        @pl.when(self.section == 0)
+        def _():
+            first(self.up)
+            second(self.down)
+
+        @pl.when(self.section == 1)
+        def _():
+            first(self.down)
+            second(self.up)
+
+    def start(self):
+        self.each(lambda copies: [copy.start() for copy in copies], lambda copies: None)
+
+    def wait(self):
+        self.each(
+            lambda copies: [copy.wait_send() for copy in copies],
+            lambda copies: [copy.wait_recv() for copy in copies],
+        )
+
+
 def finish_kernel(
-    late1_ref, late2_ref, early1_ref, early2_ref, near_ref, far_ref, a0, n0, a1, n1,
-    grads_ref, sums_ref, got_late1, got_late2, got_early1, got_early2,
+    late_ref, early1_ref, early2_ref, near_ref, far_ref, a0, n0, a1, n1,
+    grads_ref, sums_ref, got_late, got_early1, got_early2,
     mine, stage4, block, land_col, land_x, land_z, land,
     deliver_sems, col_sems, x_sems, z_sems, part_sems,
 ):
     section, row = lax.axis_index("section"), lax.axis_index("row")
+    away = 1 - section
     group = Group(near_ref.shape[0])
     length, width = far_ref.shape
     others = [lax.rem(row + d, land_z.shape[0]) for d in range(1, land_z.shape[0])]
     group.greet(True, True, others)
-    parts = [
-        push(source, into, part_sems, n, 1 - section, "section")
-        for n, (source, into) in enumerate(
-            (
-                (late1_ref, got_late1), (late2_ref, got_late2),
-                (early1_ref, got_early1), (early2_ref, got_early2),
-            )
-        )
-    ]
-
-    swap_far = push(far_ref, land, x_sems, 1, 1 - section, "section")
-    swap_near = push(mine, land, x_sems, 1, 1 - section, "section")
-
-    @pl.when(section == 0)
-    def _():
-        parts[0].start()
-        parts[1].start()
-        swap_far.start()
-
-    @pl.when(section == 1)
-    def _():
-        parts[2].start()
-        parts[3].start()
-
+    gradient_up = OneWay([(far_ref, land)], [], x_sems.at[:, pl.ds(1, 1)])
+    gradient_down = OneWay([], [(mine, land)], x_sems.at[:, pl.ds(2, 1)])
+    parts = OneWay(
+        [(late_ref, got_late)], [(early1_ref, got_early1), (early2_ref, got_early2)], part_sems
+    )
     deliver = Deliver(group, stage4, mine, deliver_sems)
     deliver.start(near_ref)
+    gradient_up.start()
 
     block[...] = jnp.zeros_like(block)
     for layer, (attn, narrow) in enumerate(((a0, n0), (a1, n1))):
@@ -820,8 +834,21 @@
         copy.wait()
     me = group.me
     block[me, :, :8] = block[me, :, :8] + (land_col[0] + (land_col[1] + land_col[2]))
-    swap = push(block.at[me, 1 - section], land_x, x_sems, 0, 1 - section, "section")
+    swap = push(block.at[me, away], land_x, x_sems, 0, away, "section")
     swap.start()
+    deliver.done()
+    gradient_down.start()
+    parts.start()
+    own = pl.ds(pl.multiple_of(section * length, length), length)
+
+    @pl.when(section == 0)
+    def _():
+        grads_ref[own, :] = mine[...].astype(WIDE)
+
+    @pl.when(section == 1)
+    def _():
+        grads_ref[own, :] = far_ref[...].astype(WIDE)
+
     swap.wait()
     land_z[row] = block[me, section] + land_x[...]
     copies = [
@@ -830,53 +857,26 @@
     ]
     for copy in copies:
         copy.start()
-
-    deliver.done()
-
-    @pl.when(section == 1)
-    def _():
-        swap_near.start()
-
-    own = pl.ds(pl.multiple_of(section * length, length), length)
-    away = pl.ds(pl.multiple_of((1 - section) * length, length), length)
-
-    @pl.when(section == 0)
-    def _():
-        grads_ref[own, :] = mine[...].astype(WIDE)
-
-    @pl.when(section == 1)
-    def _():
-        grads_ref[own, :] = far_ref[...].astype(WIDE)
-
     for copy in copies:
         copy.wait()
     result = land_z[0]
     for n in range(1, land_z.shape[0]):
         result = result + land_z[n]
     sums_ref[...] = result
-    @pl.when(section == 0)
-    def _():
-        swap_far.wait()
-
-    @pl.when(section == 1)
-    def _():
-        swap_near.wait()
-
-    grads_ref[away, :] = land[...].astype(WIDE)
-
-    @pl.when(section == 0)
-    def _():
-        parts[0].wait_send()
-        parts[1].wait_send()
-        parts[2].wait_recv()
-        parts[3].wait_recv()
-
-    @pl.when(section == 1)
-    def _():
-        parts[2].wait_send()
-        parts[3].wait_send()
-        parts[0].wait_recv()
-        parts[1].wait_recv()
+    gradient_up.wait()
+    gradient_down.wait()
+    grads_ref[pl.ds(pl.multiple_of(away * length, length), length), :] = land[...].astype(WIDE)
+    parts.wait()
+
+
+def last_kernel(up_ref, down_ref, got_up, got_down, sems):
+    barrier = pltpu.get_barrier_semaphore()
+    other = 1 - lax.axis_index("section")
+    pl.semaphore_signal(barrier, inc=1, device_id={"section": other}, device_id_type=MESH)
+    pl.semaphore_wait(barrier, 1)
+    parts = OneWay([(up_ref, got_up)], [(down_ref, got_down)], sems)
+    parts.start()
+    parts.wait()
 
 
 VM = pl.BlockSpec(memory_space=pltpu.VMEM)
@@ -1158,21 +1158,32 @@
         pltpu.VMEM((length, width), LOW),
         pltpu.SemaphoreType.DMA((2, 3)),
         pltpu.SemaphoreType.DMA((2, 3)),
-        pltpu.SemaphoreType.DMA((2, 2)),
+        pltpu.SemaphoreType.DMA((2, 3)),
         pltpu.SemaphoreType.DMA((2, row_count)),
-        pltpu.SemaphoreType.DMA((2, 4)),
+        pltpu.SemaphoreType.DMA((2, 3)),
     ]
     return pl.pallas_call(
         finish_kernel,
         out_shape=outs,
-        in_specs=[ANY] * 4 + [VM] * 6,
-        out_specs=(VM, VM) + (ANY,) * 4,
+        in_specs=[ANY] * 3 + [VM] * 6,
+        out_specs=(VM, VM) + (ANY,) * 3,
         scratch_shapes=scratch,
         compiler_params=pltpu.CompilerParams(
             collective_id=number, has_side_effects=True, vmem_limit_bytes=GRANT
         ),
         cost_estimate=pl.CostEstimate(flops=int(3e10), bytes_accessed=30 * MEBI, transcendentals=0),
     )(*late, *early, near, far, *sums)
+
+
+def last_call(number, up, down):
+    return pl.pallas_call(
+        last_kernel,
+        out_shape=(shape(up.shape), shape(down.shape)),
+        in_specs=[ANY] * 2,
+        out_specs=(ANY,) * 2,
+        scratch_shapes=[pltpu.SemaphoreType.DMA((2, 2))],
+        compiler_params=pltpu.CompilerParams(collective_id=number, has_side_effects=True),
+    )(up, down)
 
 
 def swap_sections(value):
@@ -1325,9 +1336,9 @@
         15, mixed, outer, grad_hidden, owns[0], attn, normed, wide_vectors[0]
     )
     part_e0 = scatter(total_e0)
-    input_grads, small_grads, far_e1, far_w1, far_c0, far_e0 = finish_call(
+    input_grads, small_grads, far_e1, far_c0, far_e0 = finish_call(
         16,
-        (part_e1, part_w1),
+        (part_e1,),
         (part_c0, part_e0),
         gx0_own,
         own_features(gx1_full),
@@ -1336,7 +1347,7 @@
     )
 
     part_w0, small_grads = tie(scatter(total_w0), small_grads)
-    far_w0 = lax.ppermute(part_w0, "section", [(1, 0)])
+    far_w1, far_w0 = last_call(17, part_w1, part_w0)
 
     units = []
     for late, far_late, early, far_early in (

time: 698 us -> 680 us (0.974)
  waiting for transfers between devices: 53.5 us -> 43.8 us
  Pallas kernels: 574 us -> 567 us
    ppermute x1 -> x0, waiting for transfers between devices: 9.7 us -> none  [on_device(): far_w0 = lax.ppermute(part_w0, 'section', [(1, 0)])]
    pallas_call x1 -> x2, Pallas kernels: 77.5 us -> 70.8 us  [the longest x1 52.5 us: finish_call(): pl.pallas_call(finish_kernel, out_shape=outs, in_specs=[ANY] * 3 + [VM] *...]
    unnamed x62 -> x60, local copies, waits for them, and re-layouts: 17.1 us -> 17.1 us
  transfers between devices with their start and end apart: 15 -> 14, of which waited for: 5 -> 4; matrix products, arithmetic and copies ran while one was open for 4% -> 4% of each run, Pallas kernels for 83% -> 81%
where the time goes in v10:
time: 680 us; the launch traced here: 674 us
  Pallas kernels  567 us (83%)
  waiting for transfers between devices  43.8 us (6%)
  local copies, waits for them, and re-layouts  28.8 us (4%)
  between operations  15.2 us (2%)
  other arithmetic  13.9 us (2%)
    pallas_call x10, Pallas kernels, launch(): pl.pallas_call(kernel, out_shape=(*outs, *[shape(s.shape, s.dtype) for s...  453 us
    pallas_call x1, Pallas kernels, finish_call(): pl.pallas_call(finish_kernel, out_shape=outs, in_specs=[ANY] * 3 + [VM] *...  52.5 us
    pallas_call x1, Pallas kernels, start_call(): pl.pallas_call(start_kernel, out_shape=outs, in_specs=[ANY] * 5, out_spec...  43.6 us
    all_gather x6, waiting for transfers between devices, gather_blocks(): return lax.all_gather(block, 'row', axis=0, tiled=True)  30.8 us
    pallas_call x1, Pallas kernels, last_call(): pl.pallas_call(last_kernel, out_shape=(shape(up.shape), shape(down.shape)...  18.2 us
    unnamed x60, local copies, waits for them, and re-layouts  17.1 us
  transfers between devices with their start and end apart: 14, of which 4 were waited for; matrix products, arithmetic and copies ran while one was open for 4% of the time, Pallas kernels for 81%

profile of v10, /device:TPU:0, one launch (start us, length us, event | category | flops | bytes accessed | tf_op | source)
XLA Modules:
  0.0 674.1 jit_solution(13436460202167353909)
XLA Ops:
  7.2 1.1 copy.38
  8.4 1.5 copy.37
  10.4 3.0 collective-permute-start
  13.5 1.5 copy.41.tokens_ref
  15.1 2.6 copy.42.cotangent_ref
  17.9 0.6 pad.8.small_ref
  18.5 0.8 broadcast_select_fusion.11.expand_ref
  19.3 3.6 collective-permute-done
  22.9 1.0 broadcast_select_fusion.5
  23.9 43.6 %shard_map.245 = (bf16[1024,1280]{1,0:T(8,128)(2,1)}, bf16[1024,1280]{1,0:T(8,128)(2,1)}, bf16[2,4,16,320]{3,2,1,0:T(8,128)(2,1)}, bf16[320,640]{1,0:T(8,128)(2,1)}, bf16[320,1280]{1,0:T(8,128)(2,1)}) custom-call(bf16[2048,320]{1,0:T(8,128)(2,1)} %copy.41.tokens_ref, bf16[2048,320]{1,0:T(8,128)(2,1)} %copy.42.cotangent_ref, bf16[16,320]{1,0:T(8,128)(2,1)} %pad.8.small_ref, ...), custom_call_target="tpu_custom_call" | custom-call | flops 30000001024 | bytes 31457280 | tf_op jit(solution)/shard_map/pallas_call | solution.py:961
  67.6 2.1 broadcast_select_fusion.6
  69.8 0.8 fusion
  72.5 0.7 squeeze.48.refs_3_
  73.2 0.7 squeeze.45.refs_3_
  74.0 0.7 squeeze.47.refs_4_
  74.7 0.7 squeeze.44.refs_4_
  75.4 1.0 broadcast_select_fusion
  76.5 0.6 fusion.2
  77.1 30.7 %all-gather.9.cloned.1.call-done.refs_5_.refs_1_.refs_3_ = bf16[1280,640]{1,0:T(8,128)(2,1)} async-done(((bf16[320,640]{1,0:T(8,128)(2,1)}), bf16[1280,640]{1,0:T(8,128)(2,1)}) %all-gather.9.cloned.1.call-update) | async-done | bytes 1638416 | tf_op jit(solution)/shard_map/all_gather | solution.py:1257
  107.8 3.0 collective-permute-done.1.refs_2_.refs_5_
  110.8 1.2 copy-done.25
  111.9 39.0 %shard_map.246 = (bf16[16,128]{1,0:T(8,128)(2,1)}, bf16[1024,1280]{1,0:T(8,128)(2,1)}, bf16[15,1024,64]{2,1,0:T(8,128)(2,1)}, bf16[1024,320]{1,0:T(8,128)(2,1)},...) custom-call(bf16[1024,1280]{1,0:T(8,128)(2,1)} %get-tuple-element.85.refs_0_, ...), custom_call_target="tpu_custom_call" | custom-call | flops 30000001024 | bytes 31457280 | tf_op jit(solution)/shard_map/pallas_call | solution.py:933
  151.0 38.4 %shard_map.247 = (bf16[1024,1280]{1,0:T(8,128)(2,1)}, bf16[1024,1280]{1,0:T(8,128)(2,1)}, bf16[1024,1280]{1,0:T(8,128)(2,1)}, bf16[1280,640]{1,0:T(8,128)(2,1)}) custom-call(bf16[256,1280]{1,0:T(8,128)(2,1)} %get-tuple-element.89.refs_0_, bf16[1280,640]{1,0:T(8,128)(2,1)} %all-gather.9.cloned.1.call-done.refs_5_.refs_1_.refs_3_, ...), custom_call_target="tpu_custom_call" | custom-call | flops 30000001024 | bytes 31457280 | tf_op jit(solution)/shard_map/pallas_call | solution.py:933
  189.4 38.6 %shard_map.248 = (bf16[256,1280]{1,0:T(8,128)(2,1)}, bf16[1280,640]{1,0:T(8,128)(2,1)}) custom-call(bf16[1024,1280]{1,0:T(8,128)(2,1)} %get-tuple-element.92.refs_0_.refs_6_, f32[256,1280]{1,0:T(8,128)} %get-tuple-element.93.refs_1_.refs_8_, bf16[1280,640]{1,0:T(8,128)(2,1)} %all-gather.11.cloned.1.call-done.refs_4_.refs_2_.refs_1_, ...), custom_call_target="tpu_custom_call" | custom-call | flops 30000001024 | bytes 31457280 | tf_op jit(solution)/shard_map/pallas_call | solution.py:933
  228.1 51.7 %shard_map.249 = (bf16[1024,1280]{1,0:T(8,128)(2,1)}, bf16[1024,1280]{1,0:T(8,128)(2,1)}, bf16[15,1024,64]{2,1,0:T(8,128)(2,1)}, bf16[1024,320]{1,0:T(8,128)(2,1...) custom-call(bf16[256,1280]{1,0:T(8,128)(2,1)} %get-tuple-element.95.refs_0_., ...), custom_call_target="tpu_custom_call" | custom-call | flops 30000001024 | bytes 31457280 | tf_op jit(solution)/shard_map/pallas_call | solution.py:933
  279.8 28.2 %shard_map.250 = (bf16[1024,1280]{1,0:T(8,128)(2,1)}, bf16[1024,1280]{1,0:T(8,128)(2,1)}, bf16[1024,1280]{1,0:T(8,128)(2,1)}, bf16[1280,1280]{1,0:T(8,128)(2,1)}) custom-call(bf16[256,1280]{1,0:T(8,128)(2,1)} %get-tuple-element.98.refs_0_, bf16[1280,640]{1,0:T(8,128)(2,1)} %all-gather.15.cloned.1.call-done.refs_5_.refs_1_.refs_4_, ...), custom_call_target="tpu_custom_call" | custom-call | flops 30000001024 | bytes 31457280 | tf_op jit(solution)/shard_map/pallas_call | solution.py:933
  308.4 48.9 %shard_map.251 = (f32[256,1280]{1,0:T(8,128)}, bf16[256,1280]{1,0:T(8,128)(2,1)}, f32[8,1280]{1,0:T(8,128)}, bf16[1280,1280]{1,0:T(8,128)(2,1)}, bf16[1024,320]{1,0:T(8,128)(2,1)}) custom-call(bf16[1024,1280]{1,0:T(8,128)(2,1)} %get-tuple-element.101.refs_0_, f32[256,1280]{1,0:T(8,128)} %get-tuple-element.102.refs_1_, ...), custom_call_target="tpu_custom_call" | custom-call | flops 30000001024 | bytes 31457280 | tf_op jit(solution)/shard_map/pallas_call | solution.py:933
  357.8 0.6 copy-done.3
  358.4 1.3 broadcast_select_fusion.3.refs_10_
  359.8 59.7 %shard_map.252 = (bf16[256,1280]{1,0:T(8,128)(2,1)}, f32[8,1280]{1,0:T(8,128)}, bf16[1280,1280]{1,0:T(8,128)(2,1)}, bf16[1024,320]{1,0:T(8,128)(2,1)}) custom-call(bf16[256,1280]{1,0:T(8,128)(2,1)} %get-tuple-element.106.refs_0_, f32[256,1280]{1,0:T(8,128)} %get-tuple-element.107.refs_1_, bf16[256,1280]{1,0:T(8,128)(2,1)} %get-tuple-element.95.refs_0_.refs_2_, ...), custom_call_target="tpu_custom_call" | custom-call | flops 30000001024 | bytes 31457280 | tf_op jit(solution)/shard_map/pallas_call | solution.py:933
  419.7 64.0 %shard_map.253 = (f32[256,1280]{1,0:T(8,128)}, bf16[256,1280]{1,0:T(8,128)(2,1)}, f32[8,1280]{1,0:T(8,128)}, bf16[1280,640]{1,0:T(8,128)(2,1)}, bf16[1280,640]{1...) custom-call(bf16[256,1280]{1,0:T(8,128)(2,1)} %get-tuple-element.114.refs_0_, ...), custom_call_target="tpu_custom_call" | custom-call | flops 30000001024 | bytes 31457280 | tf_op jit(solution)/shard_map/pallas_call | solution.py:933
  484.1 2.0 constant_dynamic-slice_fusion.1.refs_3_
  486.0 41.2 %shard_map.254 = (bf16[1024,960]{1,0:T(8,128)(2,1)}, bf16[1280,320]{1,0:T(8,128)(2,1)}, bf16[1280,640]{1,0:T(8,128)(2,1)}) custom-call(bf16[256,1280]{1,0:T(8,128)(2,1)} %get-tuple-element.122.refs_0_, bf16[1280,640]{1,0:T(8,128)(2,1)} %all-gather.7.cloned.1.call-done.refs_1_.refs_4_, bf16[1280,640]{1,0:T(8,128)(2,1)} %copy-done.25, ...), custom_call_target="tpu_custom_call" | custom-call | flops 30000001024 | bytes 31457280 | tf_op jit(solution)/shard_map/pallas_call | solution.py:933
  527.6 1.8 broadcast_select_fusion.2
  529.6 1.5 copy.46
  531.2 2.4 constant_dynamic-slice_fusion.far_ref
  533.6 5.2 reduce-scatter.11.cloned.1.call-done.early1_ref
  538.8 42.9 %shard_map.255 = (bf16[1280,640]{1,0:T(8,128)(2,1)}, bf16[256,1280]{1,0:T(8,128)(2,1)}, f32[8,1280]{1,0:T(8,128)}) custom-call(bf16[1024,960]{1,0:T(8,128)(2,1)} %get-tuple-element.132.refs_0_, bf16[1280,320]{1,0:T(8,128)(2,1)} %get-tuple-element.133.refs_1_, f32[256,1280]{1,0:T(8,128)} %get-tuple-element.134.refs_2_, ...), custom_call_target="tpu_custom_call" | custom-call | flops 30000001024 | bytes 31457280 | tf_op jit(solution)/shard_map/pallas_call | solution.py:933
  581.8 52.5 %shard_map.256 = (f32[2048,320]{1,0:T(8,128)}, f32[16,320]{1,0:T(8,128)}, bf16[320,1280]{1,0:T(8,128)(2,1)}, bf16[320,640]{1,0:T(8,128)(2,1)}, bf16[320,640]{1,0:T(8,128)(2,1)}) custom-call(bf16[320,1280]{1,0:T(8,128)(2,1)} %reduce-scatter.7.cloned.1.call-done.late_ref, bf16[320,640]{1,0:T(8,128)(2,1)} %reduce-scatter.11.cloned.1.call-done.early1_ref, ...), custom_call_target="tpu_custom_call" | custom-call | flops 30000001024 | bytes 31457280 | tf_op jit(solution)/shard_map/pallas_call | solution.py:1165
  634.4 3.5 copy.47
  638.0 1.4 select_bitcast_fusion
  640.2 1.4 select_bitcast_fusion.1
  642.2 0.6 fusion.5
  642.8 18.2 %shard_map.257 = (bf16[320,1280]{1,0:T(8,128)(2,1)}, bf16[320,640]{1,0:T(8,128)(2,1)}) custom-call(bf16[320,1280]{1,0:T(8,128)(2,1)} %reduce-scatter.13.cloned.1.call-done.up_ref, bf16[320,640]{1,0:T(8,128)(2,1)} %reduce-scatter.17.cloned.1.call-done.down_ref), custom_call_target="tpu_custom_call" | custom-call | tf_op jit(solution)/shard_map/pallas_call | solution.py:1179
  661.0 1.6 add_select_fusion
  663.0 0.7 reshape.45
  663.7 1.0 copy.49
  665.2 1.6 copy.48
  (106 shorter events, 7.0 us)
Async XLA Ops:
  7.2 64.8 %all-gather.7.cloned.1.call-start = ((), (), s32[]{:S(2)}) async-start(), calls=%async_computation.6 | async-start | bytes 2048000 | tf_op jit(solution)/shard_map/all_gather | solution.py:1257
  9.9 3.6 copy-start.17
  9.9 3.7 copy-start.5
  10.4 12.5 %collective-permute-start = (bf16[320,640]{1,0:T(8,128)(2,1)S(1)}, bf16[320,640]{1,0:T(8,128)(2,1)S(1)}, u32[]{:S(2)}, u32[]{:S(2)}) collective-permute-start(bf16[320,640]{1,0:T(8,128)(2,1)S(1)} %get-tuple-element.182), channel_id=1, source_target_pairs={{0,16},{16,0},{1,17},{17,1},{2,18},{18,2},{3,19},{19,3},{4,20},{20... | collective-permute-start | bytes 1228808 | tf_op jit(solution)/shard_map/ppermute | solution.py:1190
  15.1 2.7 copy-start.18
  15.1 2.7 copy-start.19
  15.1 2.7 copy-start.20
  15.1 2.7 copy-start.21
  15.1 2.7 copy-start.22
  15.1 2.7 copy-start.23
  15.1 2.7 copy-start.24
  15.1 3.3 copy-start
  23.9 83.9 %all-gather.9.cloned.1.call-start = ((), (), s32[]{:S(2)}) async-start(), calls=%async_computation.7 | async-start | bytes 2048000 | tf_op jit(solution)/shard_map/all_gather | solution.py:1257
  67.5 2.2 copy-start.1
  67.6 2.2 copy-start.4
  69.7 2.2 copy-start.15
  69.7 81.3 %all-gather.11.cloned.1.call-start = ((), (), s32[]{:S(2)}) async-start(), calls=%async_computation.8 | async-start | bytes 2048000 | tf_op jit(solution)/shard_map/all_gather | solution.py:1257
  70.6 118.8 %all-gather.13.cloned.1.call-start = ((), (), s32[]{:S(2)}) async-start(), calls=%async_computation.9 | async-start | bytes 2048000 | tf_op jit(solution)/shard_map/all_gather | solution.py:1257
  71.2 156.9 %all-gather.15.cloned.1.call-start = ((), (), s32[]{:S(2)}) async-start(), calls=%async_computation.10 | async-start | bytes 2048000 | tf_op jit(solution)/shard_map/all_gather | solution.py:1257
  71.8 236.6 %all-gather.17.cloned.1.call-start = ((), (), s32[]{:S(2)}) async-start(), calls=%async_computation.11 | async-start | bytes 4096000 | tf_op jit(solution)/shard_map/all_gather | solution.py:1257
  72.0 38.7 %collective-permute-start.1 = (bf16[1280,640]{1,0:T(8,128)(2,1)}, bf16[1280,640]{1,0:T(8,128)(2,1)S(1)}, u32[]{:S(2)}, u32[]{:S(2)}) collective-permute-start(bf16[1280,640]{1,0:T(8,128)(2,1)} %all-gather.7.cloned.1.call-done.refs_1_.refs_4_), channel_id=1, source_target_pairs={{0,16},{16,0},{1,17},{17,1},{2,18},{18,2},{3,19},{19,3},{4,20},{20... | collective-permute-start | bytes 4915208 | tf_op jit(solution)/shard_map/ppermute | solution.py:1190
  76.4 343.3 %reduce-scatter.9.cloned.1.call-start = ((), (), s32[]{:S(2)}) async-start(), calls=%async_computation.13 | async-start | bytes 4096000 | tf_op jit(solution)/shard_map/reduce_scatter | solution.py:1309
  110.8 1.2 copy-start.25
  308.1 178.0 %reduce-scatter.7.cloned.1.call-start = ((), (), s32[]{:S(2)}) async-start(), calls=%async_computation.12 | async-start | bytes 4096000 | tf_op jit(solution)/shard_map/reduce_scatter | solution.py:1309
  308.4 49.4 %copy-start.6 = (bf16[1024,1280]{1,0:T(8,128)(2,1)S(1)}, bf16[1024,1280]{1,0:T(8,128)(2,1)}, u32[]{:S(2)}) copy-start(bf16[1024,1280]{1,0:T(8,128)(2,1)} %get-tuple-element.97) | copy-start | bytes 7864324
  357.3 1.1 copy-start.3
  357.3 176.3 %reduce-scatter.13.cloned.1.call-start = ((), (), s32[]{:S(2)}) async-start(), calls=%async_computation.15 | async-start | bytes 4096000 | tf_op jit(solution)/shard_map/reduce_scatter | solution.py:1309
  419.5 119.3 %reduce-scatter.11.cloned.1.call-start = ((), (), s32[]{:S(2)}) async-start(), calls=%async_computation.14 | async-start | bytes 2048000 | tf_op jit(solution)/shard_map/reduce_scatter | solution.py:1309
  483.8 98.0 %reduce-scatter.15.cloned.1.call-start = ((), (), s32[]{:S(2)}) async-start(), calls=%async_computation.16 | async-start | bytes 2048000 | tf_op jit(solution)/shard_map/reduce_scatter | solution.py:1309
  527.3 114.3 %reduce-scatter.17.cloned.1.call-start = ((), (), s32[]{:S(2)}) async-start(), calls=%async_computation.17 | async-start | bytes 2048000 | tf_op jit(solution)/shard_map/reduce_scatter | solution.py:1309
  634.4 3.6 copy-start.7
  634.4 3.6 copy-start.9
  634.4 3.6 copy-start.11
  634.4 3.6 copy-start.14
  638.0 1.5 copy-start.8
  638.0 1.8 copy-start.10
  638.0 2.1 copy-start.12
  638.0 2.2 copy-start.13
  640.2 1.4 copy-start.16
  641.6 19.4 %copy-start.2 = (bf16[320,1280]{1,0:T(8,128)(2,1)S(1)}, bf16[320,1280]{1,0:T(8,128)(2,1)}, u32[]{:S(2)}) copy-start(bf16[320,1280]{1,0:T(8,128)(2,1)} %reduce-scatter.13.cloned.1.call-done.up_ref) | copy-start | bytes 2457604
Sparse Core Ops, SparseCore 0:
  24.0 39.6 all-gather.6
  69.8 37.9 all-gather.8
  109.9 37.0 all-gather.10
  149.0 37.0 all-gather.12
  188.0 37.0 all-gather.14
  227.1 64.5 all-gather.16
  308.2 62.4 reduce-scatter.8
  373.0 62.3 reduce-scatter.6
  437.8 62.3 reduce-scatter.12
  502.4 36.4 reduce-scatter.10
  541.3 35.3 reduce-scatter.14
  581.9 36.1 reduce-scatter.16

commit v11 on v10

--- a/solution.py
+++ b/solution.py
@@ -142,13 +142,13 @@
         self.start()
         if first is not None:
             first()
-        body(g.chunk(g.me))
+        body(g.me)
         self.sibling()
-        body(g.chunk(g.sib))
+        body(g.sib)
         self.relay()
-        body(g.chunk(g.peer))
+        body(g.peer)
         self.diagonal()
-        body(g.chunk(g.diag))
+        body(g.diag)
         self.done()
 
 
@@ -160,7 +160,7 @@
         g, stage, land = self.group, self.stage, self.land
         self.first, self.over, self.near = [], [], []
         def split(owner):
-            whole = part(g.chunk(owner))
+            whole = part(owner)
             return [whole[j * g.part : (j + 1) * g.part] for j in range(PARTS)]
 
         for j, mine in enumerate(split(g.diag)):
@@ -212,6 +212,37 @@
             copy.wait()
 
 
+class OneWay:
+    def __init__(self, up, down, sems):
+        self.section = lax.axis_index("section")
+        both = [*up, *down]
+        copies = [
+            push(source, into, sems, n, 1 - self.section, "section")
+            for n, (source, into) in enumerate(both)
+        ]
+        self.up, self.down = copies[: len(up)], copies[len(up) :]
+
+    def each(self, first, second):
+        @pl.when(self.section == 0)
+        def _():
+            first(self.up)
+            second(self.down)
+
+        @pl.when(self.section == 1)
+        def _():
+            first(self.down)
+            second(self.up)
+
+    def start(self):
+        self.each(lambda copies: [copy.start() for copy in copies], lambda copies: None)
+
+    def wait(self):
+        self.each(
+            lambda copies: [copy.wait_send() for copy in copies],
+            lambda copies: [copy.wait_recv() for copy in copies],
+        )
+
+
 def scatter_scratch(rows, width):
     part = rows // PARTS
     return [
@@ -277,62 +308,50 @@
         keep_ref[rows, :] = (keep_ref[rows, :].astype(WIDE) + got_ref[rows, :].astype(WIDE)).astype(LOW)
 
 
-def attention_out(heads_ref, o3, lse_ref, heads):
-    length = heads_ref.shape[1]
-    size = min(TILE, length)
-
-    @pl.loop(0, heads)
-    def _(h):
-        for i in range(length // size):
-            rows = slice(i * size, (i + 1) * size)
-            finish = (i + 1) * size
-            queries = heads_ref[h, rows, :]
-            scores = nt(heads_ref[heads + h, :finish, :], queries)
-            keep = lax.broadcasted_iota(jnp.int32, (size, size), 0) <= lax.broadcasted_iota(
-                jnp.int32, (size, size), 1
-            )
-            last = jnp.where(keep, scores[finish - size :], -1000000000.0)
-            scores = last if i == 0 else jnp.concatenate([scores[: finish - size], last], 0)
-            highest = jnp.max(scores, axis=0, keepdims=True)
-            powers = jnp.exp(scores - highest)
-            summed = jnp.sum(powers, axis=0, keepdims=True)
-            mixed = tn(heads_ref[2 * heads + h, :finish, :], powers.astype(LOW))
-            o3[h, rows, :] = (mixed / summed).T.astype(LOW)
-            lse_ref[pl.ds(h, 1), rows] = highest + jnp.log(summed)
-
-
-def attention_back(heads_ref, go3, lse_ref, dots_ref, g3, key_acc, value_acc, heads):
-    length = heads_ref.shape[1]
-    size = min(TILE, length)
-
-    @pl.loop(0, heads)
-    def _(h):
-        for i in reversed(range(length // size)):
-            rows = slice(i * size, (i + 1) * size)
-            finish = (i + 1) * size
-            queries = heads_ref[h, rows, :]
-            keys = heads_ref[heads + h, :finish, :]
-            grads = go3[h, rows, :]
-            scores = nt(keys, queries) - lse_ref[pl.ds(h, 1), rows]
-            keep = lax.broadcasted_iota(jnp.int32, (size, size), 0) <= lax.broadcasted_iota(
-                jnp.int32, (size, size), 1
-            )
-            last = jnp.where(keep, scores[finish - size :], -1000000000.0)
-            scores = last if i == 0 else jnp.concatenate([scores[: finish - size], last], 0)
-            probs = jnp.exp(scores)
-            grad_probs = nt(heads_ref[2 * heads + h, :finish, :], grads)
-            grad_scores = (probs * (grad_probs - dots_ref[pl.ds(h, 1), rows])).astype(LOW)
-            g3[h, rows, :] = (tn(grad_scores, keys) * HEAD ** (-0.5)).astype(LOW)
-            key_part = nn(grad_scores, queries)
-            value_part = nn(probs.astype(LOW), grads)
-            if finish == length:
-                key_acc[...] = key_part
-                value_acc[...] = value_part
-            else:
-                key_acc[:finish, :] += key_part
-                value_acc[:finish, :] += value_part
-        g3[heads + h] = key_acc[...].astype(LOW)
-        g3[2 * heads + h] = value_acc[...].astype(LOW)
+def causal_scores(scores):
+    size = scores.shape[1]
+    keep = lax.broadcasted_iota(jnp.int32, (size, size), 0) <= lax.broadcasted_iota(
+        jnp.int32, (size, size), 1
+    )
+    begin = scores.shape[0] - size
+    last = jnp.where(keep, scores[begin:], -1000000000.0)
+    return last if begin == 0 else jnp.concatenate([scores[:begin], last], 0)
+
+
+def attention_out(owner, size, heads_ref, o3, lse_ref, heads):
+    for i in range(heads_ref.shape[1] // size):
+        rows, finish = slice(i * size, (i + 1) * size), (i + 1) * size
+
+        @pl.when(owner == i)
+        def _():
+            @pl.loop(0, heads)
+            def _(h):
+                scores = causal_scores(nt(heads_ref[heads + h, :finish, :], heads_ref[h, rows, :]))
+                highest = jnp.max(scores, axis=0, keepdims=True)
+                powers = jnp.exp(scores - highest)
+                summed = jnp.sum(powers, axis=0, keepdims=True)
+                mixed = tn(heads_ref[2 * heads + h, :finish, :], powers.astype(LOW))
+                o3[h, rows, :] = (mixed / summed).T.astype(LOW)
+                lse_ref[pl.ds(h, 1), rows] = highest + jnp.log(summed)
+
+
+def attention_back(owner, size, heads_ref, go3, lse_ref, dots_ref, g3, key_acc, value_acc, heads):
+    for i in range(heads_ref.shape[1] // size):
+        rows, finish = slice(i * size, (i + 1) * size), (i + 1) * size
+
+        @pl.when(owner == i)
+        def _():
+            @pl.loop(0, heads)
+            def _(h):
+                queries = heads_ref[h, rows, :]
+                keys = heads_ref[heads + h, :finish, :]
+                grads = go3[h, rows, :]
+                probs = jnp.exp(causal_scores(nt(keys, queries) - lse_ref[pl.ds(h, 1), rows]))
+                grad_probs = nt(heads_ref[2 * heads + h, :finish, :], grads)
+                grad_scores = (probs * (grad_probs - dots_ref[pl.ds(h, 1), rows])).astype(LOW)
+                g3[h, rows, :] = (tn(grad_scores, keys) * HEAD ** (-0.5)).astype(LOW)
+                key_acc[h, :finish, :] += nn(grad_scores, queries)
+                value_acc[h, :finish, :] += nn(probs.astype(LOW), grads)
 
 
 def start_kernel(
@@ -390,7 +409,8 @@
         full_ref[group.chunk(group.me), :] = x_ref[...]
     halves.wait()
 
-    def project(rows):
+    def project(owner):
+        rows = group.chunk(owner)
         values = (x_ref if gathered else full_ref)[rows, :].astype(WIDE)
         hat, _ = normalise(values)
         normed = (hat * vec_ref[0:1, :] + vec_ref[1:2, :]).astype(LOW)
@@ -407,18 +427,22 @@
 
         @pl.loop(0, LENGTH // group.rows)
         def _(n):
-            project(group.chunk(n))
+            project(n)
     else:
         Gather(group, full_ref, gather_sems).each(project)
     group.emit(0, 1, 2)
-
-    attention_out(heads_ref, o3, lse_ref, heads)
-    for h in range(heads):
-        o_ref[:, h * HEAD : (h + 1) * HEAD] = o3[h]
+    lse_ref[...] = jnp.zeros_like(lse_ref)
+
+    def attend(owner):
+        rows = group.chunk(owner)
+        attention_out(owner, group.rows, heads_ref, o3, lse_ref, heads)
+        for h in range(heads):
+            o_ref[rows, h * HEAD : (h + 1) * HEAD] = o3[h, rows, :]
+        return nt(o_ref[rows, :], weight[:, 3 * width :])
+
+    scatter = Scatter(group, stage, land, total, scatter_sems)
+    scatter.start(attend)
     group.emit(3, 4)
-
-    scatter = Scatter(group, stage, land, total, scatter_sems)
-    scatter.start(lambda rows: nt(o_ref[rows, :], weight[:, 3 * width :]))
     for j in range(PARTS):
         rows = slice(j * group.part, (j + 1) * group.part)
         residual = (x_ref if gathered else full_ref)[group.slab(group.me, j), :].astype(WIDE)
@@ -448,7 +472,8 @@
     full_ref[group.chunk(group.me), :] = second_ref[...]
     halves.wait()
 
-    def widen(rows):
+    def widen(owner):
+        rows = group.chunk(owner)
         t = nn(full_ref[rows, :], expand[...]) + bias_ref[...]
         square = t * t
         bent = jnp.tanh(0.7978845608028654 * t * (1.0 + 0.044715 * square))
@@ -485,7 +510,7 @@
     halves.start()
     halves.wait()
     scatter = Scatter(group, stage, land, total, scatter_sems)
-    scatter.start(lambda rows: nt(active_ref[rows, :], contract[...]))
+    scatter.start(lambda owner: nt(active_ref[group.chunk(owner), :], contract[...]))
     group.need(1)
     for j in range(PARTS):
         rows = slice(j * group.part, (j + 1) * group.part)
@@ -515,9 +540,9 @@
 
 def late_expand_kernel(
     group, active_ref, hidden_ref, cm_ref, co_ref, em_ref, eo_ref, g_ref, slope_ref, second_ref, vec_ref,
-    grad_ref, low_ref, sums_ref, e_ref, out_ref,
-    contract, expand, before, result, stage4,
-    stage_a, land_a, total_a, sems_a, stage, land, total, scatter_sems, deliver_sems, local_sems,
+    grad_ref, low_ref, sums_ref, e_ref, result,
+    contract, expand, before,
+    stage_a, land_a, total_a, sems_a, stage, land, total, scatter_sems, local_sems,
 ):
     first = Halves((cm_ref, co_ref), contract, local_sems, 0)
     then = Halves((em_ref, eo_ref), expand, local_sems, 2)
@@ -526,7 +551,7 @@
     sums_ref[...] = jnp.zeros_like(sums_ref)
     first.wait()
     forward = Scatter(group, stage_a, land_a, total_a, sems_a)
-    forward.start(lambda rows: nt(active_ref[rows, :], contract[...]))
+    forward.start(lambda owner: nt(active_ref[group.chunk(owner), :], contract[...]))
     group.need(6, 7)
 
     @pl.loop(0, LENGTH // group.rows)
@@ -535,13 +560,12 @@
 
     then.wait()
     scatter = Scatter(group, stage, land, total, scatter_sems)
-    scatter.start(lambda rows: nt(before[rows, :], expand[...]))
+    scatter.start(lambda owner: nt(before[group.chunk(owner), :], expand[...]))
     group.need(1)
     for j in range(PARTS):
         rows = slice(j * group.part, (j + 1) * group.part)
         result[rows, :] = (hidden_ref[rows, :] + forward.take(j) + vec_ref[5:6, :]).astype(LOW)
-    deliver = Deliver(group, stage4, out_ref, deliver_sems)
-    deliver.start(result)
+    group.emit(4)
     group.need(8)
     outer_whole(second_ref, before, e_ref)
     group.emit(3)
@@ -549,7 +573,6 @@
     group.emit(0, 1, 2)
     forward.done()
     scatter.done()
-    deliver.done()
 
 
 def expand_back_kernel(
@@ -566,7 +589,8 @@
     full_ref[group.chunk(group.me), :] = g_ref[...]
     first.wait()
     Gather(group, full_ref, gather_sems).each(
-        lambda rows: bend(rows, full_ref, contract, slope_ref, before, sums_ref), lambda: group.need(5)
+        lambda owner: bend(group.chunk(owner), full_ref, contract, slope_ref, before, sums_ref),
+        lambda: group.need(5),
     )
     group.emit(5)
     group.need(6)
@@ -586,7 +610,7 @@
     trade.start(make(1))
     then.wait()
     scatter = Scatter(group, stage, land, total, scatter_sems)
-    scatter.start(lambda rows: nt(before[rows, :], expand[...]))
+    scatter.start(lambda owner: nt(before[group.chunk(owner), :], expand[...]))
     group.need(7)
     outer_halves(second_ref, before, ek_ref, es_ref)
     group.emit(3, 4)
@@ -606,14 +630,17 @@
     store.wait()
 
 
-def scores_back(group, heads, low_ref, weight, heads_ref, o_ref, lse_ref, full, go3, dots, g3, accs, mixed, gather_sems, needs):
+def scores_back(group, heads, low_ref, weight, heads_ref, o_ref, lse_ref, full, go3, dots, g3, accs, mixed, gather_sems, first):
     width = o_ref.shape[1]
     picks = (
         lax.broadcasted_iota(jnp.int32, (8, width), 1) // HEAD
         == lax.broadcasted_iota(jnp.int32, (8, width), 0)
     ).astype(WIDE)
-
-    def spread(rows):
+    for acc in accs:
+        acc[...] = jnp.zeros_like(acc)
+
+    def spread(owner):
+        rows = group.chunk(owner)
         grads = nn(full[rows, :], weight[:, 3 * width :]).astype(LOW)
         for h in range(heads):
             go3[h, rows, :] = grads[:, h * HEAD : (h + 1) * HEAD]
@@ -625,13 +652,13 @@
             precision=lax.Precision.HIGHEST,
             preferred_element_type=WIDE,
         )
+        attention_back(owner, group.rows, heads_ref, go3, lse_ref, dots, g3, *accs, heads)
 
     full[group.chunk(group.me), :] = low_ref[...]
-    Gather(group, full, gather_sems).each(spread, lambda: group.need(needs[0]))
-    group.need(*needs[1:])
-    attention_back(heads_ref, go3, lse_ref, dots, g3, *accs, heads)
+    Gather(group, full, gather_sems).each(spread, first)
     for j in range(3 * heads):
-        mixed[:, j * HEAD : (j + 1) * HEAD] = g3[j]
+        source = g3[j] if j < heads else accs[j // heads - 1][j % heads].astype(LOW)
+        mixed[:, j * HEAD : (j + 1) * HEAD] = source
 
 
 def outer_out(full, o_ref, outer_ref):
@@ -655,21 +682,33 @@
 
 def late_attend_kernel(
     heads, group, low_ref, grad_ref, x_ref, mine_ref, other_ref, normed_ref, heads_ref, o_ref, lse_ref, vec_ref,
-    out_ref, sums_ref, w_ref,
-    weight, full, go3, dots, g3, key_acc, value_acc, mixed, outer, outer_o,
-    stage, land, total, scatter_sems, gather_sems, local_sems,
+    result_ref, y_ref,
+    out_ref, sums_ref, results_ref, w_ref,
+    weight, full, go3, dots, g3, key_acc, value_acc, mixed, outer, outer_o, late, y_land, stage4,
+    stage, land, total, scatter_sems, gather_sems, deliver_sems, y_sems, local_sems,
 ):
     width = o_ref.shape[1]
+    section = lax.axis_index("section")
     halves = Halves((mine_ref, other_ref), weight, local_sems, 0)
     halves.start()
     sums_ref[...] = jnp.zeros_like(sums_ref)
     halves.wait()
+    deliver = Deliver(group, stage4, late, deliver_sems)
+
+    def first():
+        group.need(6, 7, 8, 10)
+        deliver.start(result_ref)
+
     scores_back(
         group, heads, low_ref, weight, heads_ref, o_ref, lse_ref, full, go3, dots, g3,
-        (key_acc, value_acc), mixed, gather_sems, (7, 6, 8),
-    )
+        (key_acc, value_acc), mixed, gather_sems, first,
+    )
+    deliver.done()
+    group.need(11)
+    results = OneWay([(late, y_land)], [(y_ref, y_land)], y_sems)
+    results.start()
     scatter = Scatter(group, stage, land, total, scatter_sems)
-    scatter.start(lambda rows: nt(mixed[rows, :], weight[:, : 3 * width]))
+    scatter.start(lambda owner: nt(mixed[group.chunk(owner), :], weight[:, : 3 * width]))
     outer_out(full, o_ref, outer_o)
     group.need(5)
 
@@ -681,8 +720,21 @@
 
     store = pltpu.make_async_copy(outer, w_ref, local_sems.at[2])
     store.start()
+    length = y_ref.shape[0]
+    own = pl.ds(pl.multiple_of(section * length, length), length)
+
+    @pl.when(section == 0)
+    def _():
+        results_ref[own, :] = y_ref[...]
+
+    @pl.when(section == 1)
+    def _():
+        results_ref[own, :] = late[...]
+
     group.need(1, 2)
     attend_grads(group, scatter, x_ref, grad_ref, vec_ref, mixed, width, out_ref, sums_ref)
+    results.wait()
+    results_ref[pl.ds(pl.multiple_of((1 - section) * length, length), length), :] = y_land[...]
     scatter.done()
     store.wait()
 
@@ -699,7 +751,7 @@
     halves.wait()
     scores_back(
         group, heads, low_ref, weight, heads_ref, o_ref, lse_ref, full, go3, dots, g3,
-        (key_acc, value_acc), mixed, gather_sems, (4, 3, 5),
+        (key_acc, value_acc), mixed, gather_sems, lambda: group.need(3, 4, 5),
     )
     group.emit(0)
     outer_out(full, o_ref, outer_ref)
@@ -744,7 +796,7 @@
     trade = Trade(outer.at[0], outer.at[1], got, swap_sems)
     trade.start(make(1))
     halves.wait()
-    scatter.start(lambda rows: nt(mixed[rows, :], weight[:, : 3 * width]))
+    scatter.start(lambda owner: nt(mixed[group.chunk(owner), :], weight[:, : 3 * width]))
     keep = make(0)
 
     @pl.loop(0, outer.shape[1] // TILE)
@@ -761,40 +813,9 @@
     store.wait()
 
 
-class OneWay:
-    def __init__(self, up, down, sems):
-        self.section = lax.axis_index("section")
-        both = [*up, *down]
-        copies = [
-            push(source, into, sems, n, 1 - self.section, "section")
-            for n, (source, into) in enumerate(both)
-        ]
-        self.up, self.down = copies[: len(up)], copies[len(up) :]
-
-    def each(self, first, second):
-        @pl.when(self.section == 0)
-        def _():
-            first(self.up)
-            second(self.down)
-
-        @pl.when(self.section == 1)
-        def _():
-            first(self.down)
-            second(self.up)
-
-    def start(self):
-        self.each(lambda copies: [copy.start() for copy in copies], lambda copies: None)
-
-    def wait(self):
-        self.each(
-            lambda copies: [copy.wait_send() for copy in copies],
-            lambda copies: [copy.wait_recv() for copy in copies],
-        )
-
-
 def finish_kernel(
-    late_ref, early1_ref, early2_ref, near_ref, far_ref, a0, n0, a1, n1,
-    grads_ref, sums_ref, got_late, got_early1, got_early2,
+    late_ref, early_ref, near_ref, far_ref, a0, n0, a1, n1,
+    grads_ref, sums_ref, got_late, got_early,
     mine, stage4, block, land_col, land_x, land_z, land,
     deliver_sems, col_sems, x_sems, z_sems, part_sems,
 ):
@@ -806,12 +827,11 @@
     group.greet(True, True, others)
     gradient_up = OneWay([(far_ref, land)], [], x_sems.at[:, pl.ds(1, 1)])
     gradient_down = OneWay([], [(mine, land)], x_sems.at[:, pl.ds(2, 1)])
-    parts = OneWay(
-        [(late_ref, got_late)], [(early1_ref, got_early1), (early2_ref, got_early2)], part_sems
-    )
+    parts = OneWay([(late_ref, got_late)], [(early_ref, got_early)], part_sems)
     deliver = Deliver(group, stage4, mine, deliver_sems)
     deliver.start(near_ref)
     gradient_up.start()
+    parts.start()
 
     block[...] = jnp.zeros_like(block)
     for layer, (attn, narrow) in enumerate(((a0, n0), (a1, n1))):
@@ -838,7 +858,6 @@
     swap.start()
     deliver.done()
     gradient_down.start()
-    parts.start()
     own = pl.ds(pl.multiple_of(section * length, length), length)
 
     @pl.when(section == 0)
@@ -869,12 +888,12 @@
     parts.wait()
 
 
-def last_kernel(up_ref, down_ref, got_up, got_down, sems):
+def last_kernel(up_ref, down1_ref, down2_ref, got_up, got_down1, got_down2, sems):
     barrier = pltpu.get_barrier_semaphore()
     other = 1 - lax.axis_index("section")
     pl.semaphore_signal(barrier, inc=1, device_id={"section": other}, device_id_type=MESH)
     pl.semaphore_wait(barrier, 1)
-    parts = OneWay([(up_ref, got_up)], [(down_ref, got_down)], sems)
+    parts = OneWay([(up_ref, got_up)], [(down1_ref, got_down1), (down2_ref, got_down2)], sems)
     parts.start()
     parts.wait()
 
@@ -1025,25 +1044,21 @@
 def late_expand_call(number, active, hidden, contract, expand, grad, slope, second, vec, swaps):
     rows, size = hidden.shape
     wide = slope.shape[1]
-    columns = LENGTH // rows
     outs = [
         shape((rows, size), WIDE), shape((rows, size)), shape((8, size), WIDE),
-        shape((size, wide)), shape((LENGTH, size // columns)),
+        shape((size, wide)), shape((rows, size)),
     ]
     scratch = [
         pltpu.VMEM((size, wide), LOW),
         pltpu.VMEM((size, wide), LOW),
         pltpu.VMEM((LENGTH, wide), LOW),
-        pltpu.VMEM((rows, size), LOW),
-        pltpu.VMEM((columns, rows, size // columns), LOW),
-        *scatter_scratch(rows, size), *scatter_scratch(rows, size),
-        pltpu.SemaphoreType.DMA((2, 3)), LOCAL,
+        *scatter_scratch(rows, size), *scatter_scratch(rows, size), LOCAL,
     ]
     return launch(
         late_expand_kernel,
         number, rows, [VM, VM, ANY, ANY, ANY, ANY, VM, VM, VM, VM],
         (active, hidden, *contract, *expand, grad, slope, second, vec),
-        outs, [VM] * 5, scratch, swaps, True, late=(1, 6, 7, 8),
+        outs, [VM] * 5, scratch, swaps, late=(1, 6, 7, 8),
     )
 
 
@@ -1077,29 +1092,33 @@
         pltpu.VMEM((LENGTH, size), LOW),
         pltpu.VMEM((heads, LENGTH, HEAD), LOW),
         pltpu.VMEM((8, LENGTH), WIDE),
-        pltpu.VMEM((3 * heads, LENGTH, HEAD), LOW),
-        pltpu.VMEM((LENGTH, HEAD), WIDE),
-        pltpu.VMEM((LENGTH, HEAD), WIDE),
+        pltpu.VMEM((heads, LENGTH, HEAD), LOW),
+        pltpu.VMEM((heads, LENGTH, HEAD), WIDE),
+        pltpu.VMEM((heads, LENGTH, HEAD), WIDE),
     ]
 
 
-def late_attend_call(number, low, grad, x_own, pair, normed, heads_all, o, lse, vec, swaps):
+def late_attend_call(number, low, grad, x_own, pair, normed, heads_all, o, lse, vec, result, y, swaps):
     rows, size = grad.shape
     width = o.shape[1]
     heads = width // HEAD
-    outs = (shape((rows, size)), shape((8, size), WIDE), shape((size, 4 * width)))
+    outs = (shape((rows, size)), shape((8, size), WIDE), shape((2 * LENGTH, width)), shape((size, 4 * width)))
     scratch = [
         *scores_scratch(size, width, heads),
         pltpu.VMEM((LENGTH, 3 * width), LOW),
         pltpu.VMEM((size, 4 * width), LOW),
         pltpu.VMEM((size, width), LOW),
-        *scatter_scratch(rows, size), PAIRS, LOCAL,
+        pltpu.VMEM((LENGTH, width), LOW),
+        pltpu.VMEM((LENGTH, width), LOW),
+        pltpu.VMEM((LENGTH // rows, rows, width), LOW),
+        *scatter_scratch(rows, size), PAIRS,
+        pltpu.SemaphoreType.DMA((2, 3)), pltpu.SemaphoreType.DMA((2, 2)), LOCAL,
     ]
     return launch(
         functools.partial(late_attend_kernel, heads),
-        number, rows, [VM, VM, VM, ANY, ANY, VM, VM, VM, VM, VM],
-        (low, grad, x_own, *pair, normed, heads_all, o, lse, vec),
-        outs, (VM, VM, ANY), scratch, swaps, late=(1, 2, 5, 6, 7, 8),
+        number, rows, [VM, VM, VM, ANY, ANY, VM, VM, VM, VM, VM, VM, VM],
+        (low, grad, x_own, *pair, normed, heads_all, o, lse, vec, result, y),
+        outs, (VM, VM, VM, ANY), scratch, swaps, True, True, late=(1, 2, 5, 6, 7, 8, 10, 11),
     )
 
 
@@ -1160,13 +1179,13 @@
         pltpu.SemaphoreType.DMA((2, 3)),
         pltpu.SemaphoreType.DMA((2, 3)),
         pltpu.SemaphoreType.DMA((2, row_count)),
-        pltpu.SemaphoreType.DMA((2, 3)),
+        pltpu.SemaphoreType.DMA((2, 2)),
     ]
     return pl.pallas_call(
         finish_kernel,
         out_shape=outs,
-        in_specs=[ANY] * 3 + [VM] * 6,
-        out_specs=(VM, VM) + (ANY,) * 3,
+        in_specs=[ANY] * 2 + [VM] * 6,
+        out_specs=(VM, VM) + (ANY,) * 2,
         scratch_shapes=scratch,
         compiler_params=pltpu.CompilerParams(
             collective_id=number, has_side_effects=True, vmem_limit_bytes=GRANT
@@ -1175,15 +1194,15 @@
     )(*late, *early, near, far, *sums)
 
 
-def last_call(number, up, down):
+def last_call(number, *parts):
     return pl.pallas_call(
         last_kernel,
-        out_shape=(shape(up.shape), shape(down.shape)),
-        in_specs=[ANY] * 2,
-        out_specs=(ANY,) * 2,
-        scratch_shapes=[pltpu.SemaphoreType.DMA((2, 2))],
+        out_shape=[shape(part.shape) for part in parts],
+        in_specs=[ANY] * 3,
+        out_specs=[ANY] * 3,
+        scratch_shapes=[pltpu.SemaphoreType.DMA((2, 3))],
         compiler_params=pltpu.CompilerParams(collective_id=number, has_side_effects=True),
-    )(up, down)
+    )(*parts)
 
 
 def swap_sections(value):
@@ -1313,14 +1332,12 @@
 
     attn, expand, contract = pairs[1]
     normed, heads, o, lse, hidden, second, active, slope = kept[1]
-    (grad_hidden, low, expand_sums1, e1, y1), _ = late_expand_call(
+    (grad_hidden, low, expand_sums1, e1, result), _ = late_expand_call(
         8, active, hidden, contract, expand, gy_full, slope, second, wide_vectors[1], []
     )
-    layer_low, layer_high = pick(y0, y1), pick(y1, y0)
-    (gx1_own, attend_sums1, w1), (layer_got,) = late_attend_call(
-        10, low, grad_hidden, owns[1], attn, normed, heads, o, lse, wide_vectors[1], [layer_high]
-    )
-    layer_outputs = jnp.concatenate([pick(layer_low, layer_got), pick(layer_got, layer_low)], 0)
+    (gx1_own, attend_sums1, layer_outputs, w1), _ = late_attend_call(
+        10, low, grad_hidden, owns[1], attn, normed, heads, o, lse, wide_vectors[1], result, y0, []
+    )
 
     attn, expand, contract = pairs[0]
     normed, heads, o, lse, hidden, second, active, slope = kept[0]
@@ -1335,11 +1352,11 @@
     total_w0, gx0_own, attend_sums0 = attend_back_call(
         15, mixed, outer, grad_hidden, owns[0], attn, normed, wide_vectors[0]
     )
-    part_e0 = scatter(total_e0)
-    input_grads, small_grads, far_e1, far_c0, far_e0 = finish_call(
+    part_e0, gx0_own = tie(scatter(total_e0), gx0_own)
+    input_grads, small_grads, far_e1, far_c0 = finish_call(
         16,
         (part_e1,),
-        (part_c0, part_e0),
+        (part_c0,),
         gx0_own,
         own_features(gx1_full),
         (attend_sums0, expand_sums0, attend_sums1, expand_sums1),
@@ -1347,7 +1364,7 @@
     )
 
     part_w0, small_grads = tie(scatter(total_w0), small_grads)
-    far_w1, far_w0 = last_call(17, part_w1, part_w0)
+    far_w1, far_e0, far_w0 = last_call(17, part_w1, part_e0, part_w0)
 
     units = []
     for late, far_late, early, far_early in (

time: 680 us -> 673 us (0.990)
  Pallas kernels: 567 us -> 545 us
  waiting for transfers between devices: 43.8 us -> 57.3 us
    pallas_call x10, Pallas kernels: 453 us -> 437 us  [launch(): pl.pallas_call(kernel, out_shape=(*outs, *[shape(s.shape, s.dtype) for s...]
    reduce_scatter x6, waiting for transfers between devices: 5.28 us -> 18.8 us  [scatter(): return lax.psum_scatter(total, 'row', scatter_dimension=0, tiled=True)]
    unnamed x60 -> x58, local copies, waits for them, and re-layouts: 17.1 us -> 15.8 us
  transfers between devices with their start and end apart: 14 -> 14, of which waited for: 4 -> 4; matrix products, arithmetic and copies ran while one was open for 4% -> 4% of each run, Pallas kernels for 81% -> 79%
where the time goes in v11:
time: 673 us; the launch traced here: 663 us
  Pallas kernels  545 us (81%)
  waiting for transfers between devices  57.3 us (9%)
  local copies, waits for them, and re-layouts  30 us (4%)
  between operations  14.9 us (2%)
  other arithmetic  11.6 us (2%)
    pallas_call x10, Pallas kernels, launch(): pl.pallas_call(kernel, out_shape=(*outs, *[shape(s.shape, s.dtype) for s...  437 us
    pallas_call x1, Pallas kernels, finish_call(): pl.pallas_call(finish_kernel, out_shape=outs, in_specs=[ANY] * 2 + [VM] *...  44.5 us
    pallas_call x1, Pallas kernels, start_call(): pl.pallas_call(start_kernel, out_shape=outs, in_specs=[ANY] * 5, out_spec...  43.6 us
    all_gather x6, waiting for transfers between devices, gather_blocks(): return lax.all_gather(block, 'row', axis=0, tiled=True)  30.8 us
    pallas_call x1, Pallas kernels, last_call(): pl.pallas_call(last_kernel, out_shape=[shape(part.shape) for part in part...  19.7 us
    reduce_scatter x6, waiting for transfers between devices, scatter(): return lax.psum_scatter(total, 'row', scatter_dimension=0, tiled=True)  18.8 us
    unnamed x58, local copies, waits for them, and re-layouts  15.8 us
  transfers between devices with their start and end apart: 14, of which 4 were waited for; matrix products, arithmetic and copies ran while one was open for 4% of the time, Pallas kernels for 79%

profile of v11, /device:TPU:0, one launch (start us, length us, event | category | flops | bytes accessed | tf_op | source)
XLA Modules:
  0.0 662.7 jit_solution(5562928510493545816)
XLA Ops:
  7.2 1.1 copy.38
  8.4 1.5 copy.37
  10.4 3.0 collective-permute-start
  13.5 1.5 copy.41.tokens_ref
  15.1 2.6 copy.42.cotangent_ref
  17.9 0.6 pad.8.small_ref
  18.5 0.8 broadcast_select_fusion.7.expand_ref
  19.3 3.6 collective-permute-done
  22.9 1.0 broadcast_select_fusion.1
  23.9 43.6 %shard_map.245 = (bf16[1024,1280]{1,0:T(8,128)(2,1)}, bf16[1024,1280]{1,0:T(8,128)(2,1)}, bf16[2,4,16,320]{3,2,1,0:T(8,128)(2,1)}, bf16[320,640]{1,0:T(8,128)(2,1)}, bf16[320,1280]{1,0:T(8,128)(2,1)}) custom-call(bf16[2048,320]{1,0:T(8,128)(2,1)} %copy.41.tokens_ref, bf16[2048,320]{1,0:T(8,128)(2,1)} %copy.42.cotangent_ref, bf16[16,320]{1,0:T(8,128)(2,1)} %pad.8.small_ref, ...), custom_call_target="tpu_custom_call" | custom-call | flops 30000001024 | bytes 31457280 | tf_op jit(solution)/shard_map/pallas_call | solution.py:980
  67.6 2.1 broadcast_select_fusion.2
  69.8 0.8 fusion
  71.2 0.5 all-gather.15.cloned.1.call-update
  72.5 0.7 squeeze.48.refs_3_
  73.2 0.7 squeeze.45.refs_3_
  74.0 0.7 squeeze.47.refs_4_
  74.7 0.7 squeeze.44.refs_4_
  75.4 1.0 broadcast_select_fusion
  76.5 0.6 fusion.2
  77.1 30.7 %all-gather.9.cloned.1.call-done.refs_5_.refs_1_.refs_3_ = bf16[1280,640]{1,0:T(8,128)(2,1)} async-done(((bf16[320,640]{1,0:T(8,128)(2,1)}), bf16[1280,640]{1,0:T(8,128)(2,1)}) %all-gather.9.cloned.1.call-update) | async-done | bytes 1638416 | tf_op jit(solution)/shard_map/all_gather | solution.py:1276
  107.8 3.0 collective-permute-done.1.refs_2_.refs_5_
  110.8 1.2 copy-done.24
  111.9 38.3 %shard_map.246 = (bf16[16,128]{1,0:T(8,128)(2,1)}, bf16[1024,1280]{1,0:T(8,128)(2,1)}, bf16[15,1024,64]{2,1,0:T(8,128)(2,1)}, bf16[1024,320]{1,0:T(8,128)(2,1)},...) custom-call(bf16[1024,1280]{1,0:T(8,128)(2,1)} %get-tuple-element.87.refs_0_, ...), custom_call_target="tpu_custom_call" | custom-call | flops 30000001024 | bytes 31457280 | tf_op jit(solution)/shard_map/pallas_call | solution.py:952
  150.2 37.9 %shard_map.247 = (bf16[1024,1280]{1,0:T(8,128)(2,1)}, bf16[1024,1280]{1,0:T(8,128)(2,1)}, bf16[1024,1280]{1,0:T(8,128)(2,1)}, bf16[1280,640]{1,0:T(8,128)(2,1)}) custom-call(bf16[256,1280]{1,0:T(8,128)(2,1)} %get-tuple-element.91.refs_0_, bf16[1280,640]{1,0:T(8,128)(2,1)} %all-gather.9.cloned.1.call-done.refs_5_.refs_1_.refs_3_, ...), custom_call_target="tpu_custom_call" | custom-call | flops 30000001024 | bytes 31457280 | tf_op jit(solution)/shard_map/pallas_call | solution.py:952
  188.2 38.2 %shard_map.248 = (bf16[256,1280]{1,0:T(8,128)(2,1)}, bf16[1280,640]{1,0:T(8,128)(2,1)}) custom-call(bf16[1024,1280]{1,0:T(8,128)(2,1)} %get-tuple-element.94.refs_0_.refs_6_, f32[256,1280]{1,0:T(8,128)} %get-tuple-element.95.refs_1_.refs_8_, bf16[1280,640]{1,0:T(8,128)(2,1)} %all-gather.11.cloned.1.call-done.refs_4_.refs_2_.refs_1_, ...), custom_call_target="tpu_custom_call" | custom-call | flops 30000001024 | bytes 31457280 | tf_op jit(solution)/shard_map/pallas_call | solution.py:952
  226.4 46.3 %shard_map.249 = (bf16[1024,1280]{1,0:T(8,128)(2,1)}, bf16[1024,1280]{1,0:T(8,128)(2,1)}, bf16[15,1024,64]{2,1,0:T(8,128)(2,1)}, bf16[1024,320]{1,0:T(8,128)(2,1...) custom-call(bf16[256,1280]{1,0:T(8,128)(2,1)} %get-tuple-element.97.refs_0_., ...), custom_call_target="tpu_custom_call" | custom-call | flops 30000001024 | bytes 31457280 | tf_op jit(solution)/shard_map/pallas_call | solution.py:952
  272.7 30.5 %shard_map.250 = (bf16[1024,1280]{1,0:T(8,128)(2,1)}, bf16[1024,1280]{1,0:T(8,128)(2,1)}, bf16[1024,1280]{1,0:T(8,128)(2,1)}, bf16[1280,1280]{1,0:T(8,128)(2,1)}) custom-call(bf16[256,1280]{1,0:T(8,128)(2,1)} %get-tuple-element.99.refs_0_, bf16[1280,640]{1,0:T(8,128)(2,1)} %all-gather.15.cloned.1.call-done.refs_5_.refs_1_.refs_4_, ...), custom_call_target="tpu_custom_call" | custom-call | flops 30000001024 | bytes 31457280 | tf_op jit(solution)/shard_map/pallas_call | solution.py:952
  303.5 40.9 %shard_map.251 = (f32[256,1280]{1,0:T(8,128)}, bf16[256,1280]{1,0:T(8,128)(2,1)}, f32[8,1280]{1,0:T(8,128)}, bf16[1280,1280]{1,0:T(8,128)(2,1)}, bf16[256,1280]{1,0:T(8,128)(2,1)}) custom-call(bf16[1024,1280]{1,0:T(8,128)(2,1)} %get-tuple-element.102.refs_0_, f32[256,1280]{1,0:T(8,128)} %get-tuple-element.103.refs_1_, ...), custom_call_target="tpu_custom_call" | custom-call | flops 30000001024 | bytes 31457280 | tf_op jit(solution)/shard_map/pallas_call | solution.py:952
  344.5 2.4 constant_dynamic-slice_fusion.2.refs_11_
  347.0 55.7 %shard_map.252 = (bf16[256,1280]{1,0:T(8,128)(2,1)}, f32[8,1280]{1,0:T(8,128)}, bf16[2048,320]{1,0:T(8,128)(2,1)}, bf16[1280,1280]{1,0:T(8,128)(2,1)}) custom-call(bf16[256,1280]{1,0:T(8,128)(2,1)} %get-tuple-element.106.refs_0_, f32[256,1280]{1,0:T(8,128)} %get-tuple-element.107.refs_1_, bf16[256,1280]{1,0:T(8,128)(2,1)} %get-tuple-element.97.refs_0_.refs_2_, ...), custom_call_target="tpu_custom_call" | custom-call | flops 30000001024 | bytes 31457280 | tf_op jit(solution)/shard_map/pallas_call | solution.py:952
  402.9 66.2 %shard_map.253 = (f32[256,1280]{1,0:T(8,128)}, bf16[256,1280]{1,0:T(8,128)(2,1)}, f32[8,1280]{1,0:T(8,128)}, bf16[1280,640]{1,0:T(8,128)(2,1)}, bf16[1280,640]{1...) custom-call(bf16[256,1280]{1,0:T(8,128)(2,1)} %get-tuple-element.116.refs_0_, ...), custom_call_target="tpu_custom_call" | custom-call | flops 30000001024 | bytes 31457280 | tf_op jit(solution)/shard_map/pallas_call | solution.py:952
  469.3 39.9 %shard_map.254 = (bf16[1024,960]{1,0:T(8,128)(2,1)}, bf16[1280,320]{1,0:T(8,128)(2,1)}, bf16[1280,640]{1,0:T(8,128)(2,1)}) custom-call(bf16[256,1280]{1,0:T(8,128)(2,1)} %get-tuple-element.124.refs_0_, bf16[1280,640]{1,0:T(8,128)(2,1)} %all-gather.7.cloned.1.call-done.refs_1_.refs_4_, bf16[1280,640]{1,0:T(8,128)(2,1)} %copy-done.24, ...), custom_call_target="tpu_custom_call" | custom-call | flops 30000001024 | bytes 31457280 | tf_op jit(solution)/shard_map/pallas_call | solution.py:952
  509.2 2.1 constant_dynamic-slice_fusion.1.refs_3_
  511.3 1.5 copy.46
  512.9 2.4 constant_dynamic-slice_fusion.far_ref
  515.3 18.7 %reduce-scatter.11.cloned.1.call-done.early_ref = bf16[320,640]{1,0:T(8,128)(2,1)} async-done(((bf16[1280,640]{1,0:T(8,128)(2,1)}), bf16[320,640]{1,0:T(8,128)(2,1)}) %reduce-scatter.11.cloned.1.call-update) | async-done | bytes 409616 | tf_op jit(solution)/shard_map/reduce_scatter | solution.py:1328
  534.0 42.9 %shard_map.255 = (bf16[1280,640]{1,0:T(8,128)(2,1)}, bf16[256,1280]{1,0:T(8,128)(2,1)}, f32[8,1280]{1,0:T(8,128)}) custom-call(bf16[1024,960]{1,0:T(8,128)(2,1)} %get-tuple-element.134.refs_0_, bf16[1280,320]{1,0:T(8,128)(2,1)} %get-tuple-element.135.refs_1_, f32[256,1280]{1,0:T(8,128)} %get-tuple-element.136.refs_2_, ...), custom_call_target="tpu_custom_call" | custom-call | flops 30000001024 | bytes 31457280 | tf_op jit(solution)/shard_map/pallas_call | solution.py:952
  577.0 44.5 %shard_map.256 = (f32[2048,320]{1,0:T(8,128)}, f32[16,320]{1,0:T(8,128)}, bf16[320,1280]{1,0:T(8,128)(2,1)}, bf16[320,640]{1,0:T(8,128)(2,1)}) custom-call(bf16[320,1280]{1,0:T(8,128)(2,1)} %reduce-scatter.7.cloned.1.call-done.late_ref, bf16[320,640]{1,0:T(8,128)(2,1)} %reduce-scatter.11.cloned.1.call-done.early_ref, ...), custom_call_target="tpu_custom_call" | custom-call | flops 30000001024 | bytes 31457280 | tf_op jit(solution)/shard_map/pallas_call | solution.py:1184
  621.5 3.5 copy.47
  625.1 1.4 select_bitcast_fusion
  626.5 0.6 slice_bitcast_fusion.2
  627.1 0.6 fusion.5
  627.7 19.7 %shard_map.257 = (bf16[320,1280]{1,0:T(8,128)(2,1)}, bf16[320,640]{1,0:T(8,128)(2,1)}, bf16[320,640]{1,0:T(8,128)(2,1)}) custom-call(bf16[320,1280]{1,0:T(8,128)(2,1)} %reduce-scatter.13.cloned.1.call-done.up_ref, bf16[320,640]{1,0:T(8,128)(2,1)} %reduce-scatter.15.cloned.1.call-done.down1_ref, bf16[320,640]{1,0:T(8,128)(2,1)} %reduce-scatter.17.cloned.1.call-done.down2_ref), custom_call_target="tpu_custom_call" | custom-call | tf_op jit(solution)/shard_map/pallas_call | solution.py:1198
  647.4 1.5 add_select_fusion
  649.3 0.7 reshape.45
  650.0 1.0 copy.49
  651.4 1.6 copy.48
  653.1 2.6 select_bitcast_fusion.1
  (102 shorter events, 4.2 us)
Async XLA Ops:
  7.2 64.8 %all-gather.7.cloned.1.call-start = ((), (), s32[]{:S(2)}) async-start(), calls=%async_computation.6 | async-start | bytes 2048000 | tf_op jit(solution)/shard_map/all_gather | solution.py:1276
  9.9 3.6 copy-start.16
  9.9 3.7 copy-start.7
  10.4 12.5 %collective-permute-start = (bf16[320,640]{1,0:T(8,128)(2,1)S(1)}, bf16[320,640]{1,0:T(8,128)(2,1)S(1)}, u32[]{:S(2)}, u32[]{:S(2)}) collective-permute-start(bf16[320,640]{1,0:T(8,128)(2,1)S(1)} %get-tuple-element.186), channel_id=1, source_target_pairs={{0,16},{16,0},{1,17},{17,1},{2,18},{18,2},{3,19},{19,3},{4,20},{20... | collective-permute-start | bytes 1228808 | tf_op jit(solution)/shard_map/ppermute | solution.py:1209
  15.1 2.7 copy-start.17
  15.1 2.7 copy-start.18
  15.1 2.7 copy-start.19
  15.1 2.7 copy-start.20
  15.1 2.7 copy-start.21
  15.1 2.7 copy-start.22
  15.1 2.7 copy-start.23
  15.1 3.3 copy-start
  23.9 83.9 %all-gather.9.cloned.1.call-start = ((), (), s32[]{:S(2)}) async-start(), calls=%async_computation.7 | async-start | bytes 2048000 | tf_op jit(solution)/shard_map/all_gather | solution.py:1276
  67.5 2.2 copy-start.1
  67.6 2.2 copy-start.3
  69.7 2.2 copy-start.14
  69.7 80.5 %all-gather.11.cloned.1.call-start = ((), (), s32[]{:S(2)}) async-start(), calls=%async_computation.8 | async-start | bytes 2048000 | tf_op jit(solution)/shard_map/all_gather | solution.py:1276
  70.6 117.6 %all-gather.13.cloned.1.call-start = ((), (), s32[]{:S(2)}) async-start(), calls=%async_computation.9 | async-start | bytes 2048000 | tf_op jit(solution)/shard_map/all_gather | solution.py:1276
  71.2 155.2 %all-gather.15.cloned.1.call-start = ((), (), s32[]{:S(2)}) async-start(), calls=%async_computation.10 | async-start | bytes 2048000 | tf_op jit(solution)/shard_map/all_gather | solution.py:1276
  71.8 231.8 %all-gather.17.cloned.1.call-start = ((), (), s32[]{:S(2)}) async-start(), calls=%async_computation.11 | async-start | bytes 4096000 | tf_op jit(solution)/shard_map/all_gather | solution.py:1276
  72.0 38.7 %collective-permute-start.1 = (bf16[1280,640]{1,0:T(8,128)(2,1)}, bf16[1280,640]{1,0:T(8,128)(2,1)S(1)}, u32[]{:S(2)}, u32[]{:S(2)}) collective-permute-start(bf16[1280,640]{1,0:T(8,128)(2,1)} %all-gather.7.cloned.1.call-done.refs_1_.refs_4_), channel_id=1, source_target_pairs={{0,16},{16,0},{1,17},{17,1},{2,18},{18,2},{3,19},{19,3},{4,20},{20... | collective-permute-start | bytes 4915208 | tf_op jit(solution)/shard_map/ppermute | solution.py:1209
  76.4 326.5 %reduce-scatter.9.cloned.1.call-start = ((), (), s32[]{:S(2)}) async-start(), calls=%async_computation.13 | async-start | bytes 4096000 | tf_op jit(solution)/shard_map/reduce_scatter | solution.py:1328
  110.8 1.2 copy-start.24
  303.2 166.0 %reduce-scatter.7.cloned.1.call-start = ((), (), s32[]{:S(2)}) async-start(), calls=%async_computation.12 | async-start | bytes 4096000 | tf_op jit(solution)/shard_map/reduce_scatter | solution.py:1328
  344.5 170.8 %reduce-scatter.13.cloned.1.call-start = ((), (), s32[]{:S(2)}) async-start(), calls=%async_computation.15 | async-start | bytes 4096000 | tf_op jit(solution)/shard_map/reduce_scatter | solution.py:1328
  402.7 131.3 %reduce-scatter.11.cloned.1.call-start = ((), (), s32[]{:S(2)}) async-start(), calls=%async_computation.14 | async-start | bytes 2048000 | tf_op jit(solution)/shard_map/reduce_scatter | solution.py:1328
  469.2 107.8 %reduce-scatter.15.cloned.1.call-start = ((), (), s32[]{:S(2)}) async-start(), calls=%async_computation.16 | async-start | bytes 2048000 | tf_op jit(solution)/shard_map/reduce_scatter | solution.py:1328
  509.2 2.2 copy-start.6
  509.2 117.3 %reduce-scatter.17.cloned.1.call-start = ((), (), s32[]{:S(2)}) async-start(), calls=%async_computation.17 | async-start | bytes 2048000 | tf_op jit(solution)/shard_map/reduce_scatter | solution.py:1328
  621.5 3.6 copy-start.9
  621.5 3.6 copy-start.10
  621.5 3.6 copy-start.11
  621.5 3.6 copy-start.13
  625.1 1.5 copy-start.15
  626.5 20.9 %copy-start.2 = (bf16[320,1280]{1,0:T(8,128)(2,1)S(1)}, bf16[320,1280]{1,0:T(8,128)(2,1)}, u32[]{:S(2)}) copy-start(bf16[320,1280]{1,0:T(8,128)(2,1)} %reduce-scatter.13.cloned.1.call-done.up_ref) | copy-start | bytes 2457604
  626.5 20.9 %copy-start.5 = (bf16[320,640]{1,0:T(8,128)(2,1)S(1)}, bf16[320,640]{1,0:T(8,128)(2,1)}, u32[]{:S(2)}) copy-start(bf16[320,640]{1,0:T(8,128)(2,1)} %reduce-scatter.17.cloned.1.call-done.down2_ref) | copy-start | bytes 1228804
  651.4 1.7 copy-start.4
  651.4 1.7 copy-start.8
  651.4 1.6 copy-start.12
Sparse Core Ops, SparseCore 0:
  24.0 39.6 all-gather.6
  69.8 37.9 all-gather.8
  109.9 37.0 all-gather.10
  149.0 37.0 all-gather.12
  188.0 37.0 all-gather.14
  227.1 64.5 all-gather.16
  303.4 62.4 reduce-scatter.8
  368.2 62.3 reduce-scatter.6
  433.0 62.3 reduce-scatter.12
  497.5 36.4 reduce-scatter.10
  536.4 35.3 reduce-scatter.14
  577.1 34.6 reduce-scatter.16

commit v12 on v11

--- a/solution.py
+++ b/solution.py
@@ -29,6 +29,14 @@
 
 def tn(left, right):
     return lax.dot_general(left, right, (((0,), (0,)), ((), ())), preferred_element_type=WIDE)
+
+
+def turned(values):
+    width = values.shape[1]
+    unit = (
+        lax.broadcasted_iota(jnp.int32, (width, width), 0) == lax.broadcasted_iota(jnp.int32, (width, width), 1)
+    ).astype(LOW)
+    return nt(unit, values)
 
 
 def normalise(values):
@@ -725,16 +733,17 @@
 
     @pl.when(section == 0)
     def _():
-        results_ref[own, :] = y_ref[...]
+        results_ref[:, own] = turned(y_ref[...]).astype(LOW)
 
     @pl.when(section == 1)
     def _():
-        results_ref[own, :] = late[...]
+        results_ref[:, own] = turned(late[...]).astype(LOW)
 
     group.need(1, 2)
     attend_grads(group, scatter, x_ref, grad_ref, vec_ref, mixed, width, out_ref, sums_ref)
     results.wait()
-    results_ref[pl.ds(pl.multiple_of((1 - section) * length, length), length), :] = y_land[...]
+    away = pl.ds(pl.multiple_of((1 - section) * length, length), length)
+    results_ref[:, away] = turned(y_land[...]).astype(LOW)
     scatter.done()
     store.wait()
 
@@ -814,8 +823,8 @@
 
 
 def finish_kernel(
-    late_ref, early_ref, near_ref, far_ref, a0, n0, a1, n1,
-    grads_ref, sums_ref, got_late, got_early,
+    early_ref, near_ref, far_ref, a0, n0, a1, n1,
+    grads_ref, sums_ref, got_early,
     mine, stage4, block, land_col, land_x, land_z, land,
     deliver_sems, col_sems, x_sems, z_sems, part_sems,
 ):
@@ -827,7 +836,7 @@
     group.greet(True, True, others)
     gradient_up = OneWay([(far_ref, land)], [], x_sems.at[:, pl.ds(1, 1)])
     gradient_down = OneWay([], [(mine, land)], x_sems.at[:, pl.ds(2, 1)])
-    parts = OneWay([(late_ref, got_late)], [(early_ref, got_early)], part_sems)
+    parts = OneWay([], [(early_ref, got_early)], part_sems)
     deliver = Deliver(group, stage4, mine, deliver_sems)
     deliver.start(near_ref)
     gradient_up.start()
@@ -862,11 +871,11 @@
 
     @pl.when(section == 0)
     def _():
-        grads_ref[own, :] = mine[...].astype(WIDE)
+        grads_ref[:, own] = turned(mine[...])
 
     @pl.when(section == 1)
     def _():
-        grads_ref[own, :] = far_ref[...].astype(WIDE)
+        grads_ref[:, own] = turned(far_ref[...])
 
     swap.wait()
     land_z[row] = block[me, section] + land_x[...]
@@ -884,18 +893,74 @@
     sums_ref[...] = result
     gradient_up.wait()
     gradient_down.wait()
-    grads_ref[pl.ds(pl.multiple_of(away * length, length), length), :] = land[...].astype(WIDE)
+    grads_ref[:, pl.ds(pl.multiple_of(away * length, length), length)] = turned(land[...])
     parts.wait()
 
 
-def last_kernel(up_ref, down1_ref, down2_ref, got_up, got_down1, got_down2, sems):
+def greet_section():
     barrier = pltpu.get_barrier_semaphore()
     other = 1 - lax.axis_index("section")
     pl.semaphore_signal(barrier, inc=1, device_id={"section": other}, device_id_type=MESH)
     pl.semaphore_wait(barrier, 1)
-    parts = OneWay([(up_ref, got_up)], [(down1_ref, got_down1), (down2_ref, got_down2)], sems)
+
+
+def up_kernel(up_ref, got_ref, sems):
+    greet_section()
+    part = OneWay([(up_ref, got_ref)], [], sems)
+    part.start()
+    part.wait()
+
+
+def last_kernel(
+    late1_ref, early1_ref, late2_ref, early2_ref, far2_ref, attend_ref, output_ref, expand_ref,
+    own1, far1, own2, far2, sems, local_sems,
+):
+    section = lax.axis_index("section")
+    half = early1_ref.shape[1]
+    width = output_ref.shape[1]
+    greet_section()
+    parts = OneWay(
+        [(late1_ref, far1)],
+        [(early1_ref, own1.at[:, pl.ds(half, half)]), (early2_ref, own2.at[:, pl.ds(half, half)])],
+        sems,
+    )
     parts.start()
+
+    def load(pairs):
+        copies = [
+            pltpu.make_async_copy(source, into, local_sems.at[n]) for n, (source, into) in enumerate(pairs)
+        ]
+        for copy in copies:
+            copy.start()
+        for copy in copies:
+            copy.wait()
+
+    @pl.when(section == 0)
+    def _():
+        load(((early1_ref, own1.at[:, pl.ds(0, half)]), (early2_ref, own2.at[:, pl.ds(0, half)])))
+
+    @pl.when(section == 1)
+    def _():
+        load(((late1_ref, own1), (late2_ref, own2), (far2_ref, far2)))
+
     parts.wait()
+
+    def give(first, second):
+        for j in range(3):
+            attend_ref[j] = first[:, j * width : (j + 1) * width]
+        output_ref[...] = first[:, 3 * width :]
+        expand_ref[...] = second
+
+    @pl.when(section == 0)
+    def _():
+        give(own1[...].astype(WIDE), own2[...].astype(WIDE))
+
+    @pl.when(section == 1)
+    def _():
+        give(
+            own1[...].astype(WIDE) + far1[...].astype(WIDE),
+            own2[...].astype(WIDE) + far2[...].astype(WIDE),
+        )
 
 
 VM = pl.BlockSpec(memory_space=pltpu.VMEM)
@@ -1102,7 +1167,7 @@
     rows, size = grad.shape
     width = o.shape[1]
     heads = width // HEAD
-    outs = (shape((rows, size)), shape((8, size), WIDE), shape((2 * LENGTH, width)), shape((size, 4 * width)))
+    outs = (shape((rows, size)), shape((8, size), WIDE), shape((width, 2 * LENGTH)), shape((size, 4 * width)))
     scratch = [
         *scores_scratch(size, width, heads),
         pltpu.VMEM((LENGTH, 3 * width), LOW),
@@ -1158,14 +1223,14 @@
     )[0]
 
 
-def finish_call(number, late, early, near, far, sums, row_count):
+def finish_call(number, early, near, far, sums, row_count):
     rows, size = near.shape
     length, width = far.shape
     columns = length // rows
     outs = (
-        shape((2 * length, width), WIDE),
+        shape((width, 2 * length), WIDE),
         shape((16, width), WIDE),
-        *[shape(part.shape) for part in (*late, *early)],
+        shape(early.shape),
     )
     scratch = [
         pltpu.VMEM((length, width), LOW),
@@ -1184,24 +1249,40 @@
     return pl.pallas_call(
         finish_kernel,
         out_shape=outs,
-        in_specs=[ANY] * 2 + [VM] * 6,
-        out_specs=(VM, VM) + (ANY,) * 2,
+        in_specs=[ANY] + [VM] * 6,
+        out_specs=(VM, VM, ANY),
         scratch_shapes=scratch,
         compiler_params=pltpu.CompilerParams(
             collective_id=number, has_side_effects=True, vmem_limit_bytes=GRANT
         ),
         cost_estimate=pl.CostEstimate(flops=int(3e10), bytes_accessed=30 * MEBI, transcendentals=0),
-    )(*late, *early, near, far, *sums)
-
-
-def last_call(number, *parts):
+    )(early, near, far, *sums)
+
+
+def up_call(number, part):
+    return pl.pallas_call(
+        up_kernel,
+        out_shape=shape(part.shape),
+        in_specs=[ANY],
+        out_specs=ANY,
+        scratch_shapes=[pltpu.SemaphoreType.DMA((2, 1))],
+        compiler_params=pltpu.CompilerParams(collective_id=number, has_side_effects=True),
+        cost_estimate=pl.CostEstimate(flops=int(1e10), bytes_accessed=10 * MEBI, transcendentals=0),
+    )(part)
+
+
+def last_call(number, width, *parts):
+    rows, size = parts[0].shape
     return pl.pallas_call(
         last_kernel,
-        out_shape=[shape(part.shape) for part in parts],
-        in_specs=[ANY] * 3,
-        out_specs=[ANY] * 3,
-        scratch_shapes=[pltpu.SemaphoreType.DMA((2, 3))],
-        compiler_params=pltpu.CompilerParams(collective_id=number, has_side_effects=True),
+        out_shape=(shape((3, rows, width), WIDE), shape((rows, width), WIDE), shape((rows, size), WIDE)),
+        in_specs=[ANY] * 5,
+        out_specs=(VM,) * 3,
+        scratch_shapes=[pltpu.VMEM((rows, size), LOW)] * 4
+        + [pltpu.SemaphoreType.DMA((2, 3)), pltpu.SemaphoreType.DMA((3,))],
+        compiler_params=pltpu.CompilerParams(
+            collective_id=number, has_side_effects=True, vmem_limit_bytes=32 * MEBI
+        ),
     )(*parts)
 
 
@@ -1348,15 +1429,16 @@
     part_e1, low = tie(scatter(e1), low)
     mixed, outer, total_e0 = scores_back_call(14, low, attn, heads, o, lse, ek0, es0)
     part_w1, mixed = tie(scatter(w1), mixed)
+    part_e1, mixed = tie(part_e1, mixed)
+    far_e1, mixed = tie(up_call(18, part_e1), mixed)
     part_c0, mixed = tie(scatter(total_c0), mixed)
     total_w0, gx0_own, attend_sums0 = attend_back_call(
         15, mixed, outer, grad_hidden, owns[0], attn, normed, wide_vectors[0]
     )
     part_e0, gx0_own = tie(scatter(total_e0), gx0_own)
-    input_grads, small_grads, far_e1, far_c0 = finish_call(
+    input_grads, small_grads, far_c0 = finish_call(
         16,
-        (part_e1,),
-        (part_c0,),
+        part_c0,
         gx0_own,
         own_features(gx1_full),
         (attend_sums0, expand_sums0, attend_sums1, expand_sums1),
@@ -1364,26 +1446,20 @@
     )
 
     part_w0, small_grads = tie(scatter(total_w0), small_grads)
-    far_w1, far_e0, far_w0 = last_call(17, part_w1, part_e0, part_w0)
-
-    units = []
-    for late, far_late, early, far_early in (
-        (part_w1, far_w1, part_w0, far_w0),
-        (part_e1, far_e1, part_e0, far_e0),
-        (part_c1, far_c1, part_c0, far_c0),
-    ):
-        whole = jnp.concatenate([early, far_early], 1).astype(WIDE)
-        units.append(pick(whole, late.astype(WIDE) + far_late.astype(WIDE)))
-    attn_part, expand_part, contract_part = units
-
+    attend_part, output_part, expand_part = last_call(
+        17, width, part_w1, part_w0, part_e1, part_e0, far_e1
+    )
+    contract_part = pick(
+        jnp.concatenate([part_c0, far_c0], 1).astype(WIDE), part_c1.astype(WIDE) + far_c1.astype(WIDE)
+    )
     return (
-        layer_outputs[None],
-        input_grads[None],
+        layer_outputs.T[None],
+        input_grads.T[None],
         small_grads[0:1],
         small_grads[1:2],
-        attn_part[:, : 3 * width].reshape(block_rows, 3, width)[None],
+        jnp.swapaxes(attend_part, 0, 1)[None],
         small_grads[8:10][None],
-        attn_part[:, 3 * width :].T[None],
+        output_part.T[None],
         small_grads[2:3],
         small_grads[3:4],
         small_grads[4:5],

time: 673 us -> 669 us (level)
  waiting for transfers between devices: 57.3 us -> 40.2 us
  Pallas kernels: 545 us -> 555 us
    reduce_scatter x6, waiting for transfers between devices: 18.8 us -> 1.44 us  [scatter(): return lax.psum_scatter(total, 'row', scatter_dimension=0, tiled=True)]
    pallas_call x2 -> x3, Pallas kernels: 64.1 us -> 74.7 us  [the longest x1 35.4 us: finish_call(): pl.pallas_call(finish_kernel, out_shape=outs, in_specs=[ANY] + [VM] * 6,...]
    unnamed x58 -> x59, local copies, waits for them, and re-layouts: 15.8 us -> 21.7 us
  transfers between devices with their start and end apart: 14 -> 14, of which waited for: 4 -> 4; matrix products, arithmetic and copies ran while one was open for 4% -> 3% of each run, Pallas kernels for 79% -> 81%
where the time goes in v12:
time: 669 us; the launch traced here: 659 us
  Pallas kernels  555 us (83%)
  waiting for transfers between devices  40.2 us (6%)
  local copies, waits for them, and re-layouts  35 us (5%)
  between operations  14.9 us (2%)
  other arithmetic  9.29 us (1%)
    pallas_call x10, Pallas kernels, launch(): pl.pallas_call(kernel, out_shape=(*outs, *[shape(s.shape, s.dtype) for s...  437 us
    pallas_call x1, Pallas kernels, start_call(): pl.pallas_call(start_kernel, out_shape=outs, in_specs=[ANY] * 5, out_spec...  43.6 us
    pallas_call x1, Pallas kernels, finish_call(): pl.pallas_call(finish_kernel, out_shape=outs, in_specs=[ANY] + [VM] * 6,...  35.4 us
    all_gather x6, waiting for transfers between devices, gather_blocks(): return lax.all_gather(block, 'row', axis=0, tiled=True)  30.8 us
    unnamed x59, local copies, waits for them, and re-layouts  21.7 us
    pallas_call x1, Pallas kernels, last_call(): pl.pallas_call(last_kernel, out_shape=(shape((3, rows, width), WIDE), sha...  20.5 us
    pallas_call x1, Pallas kernels, up_call(): pl.pallas_call(up_kernel, out_shape=shape(part.shape), in_specs=[ANY], ou...  18.8 us
  transfers between devices with their start and end apart: 14, of which 4 were waited for; matrix products, arithmetic and copies ran while one was open for 3% of the time, Pallas kernels for 81%

profile of v12, /device:TPU:0, one launch (start us, length us, event | category | flops | bytes accessed | tf_op | source)
XLA Modules:
  0.0 659.1 jit_solution(3030713054612279075)
XLA Ops:
  7.2 1.1 copy.35
  8.4 1.5 copy.34
  10.2 1.0 broadcast_select_fusion.8
  11.2 2.9 collective-permute-start
  14.2 1.5 copy.38.tokens_ref
  15.8 2.6 copy.39.cotangent_ref
  19.2 0.8 broadcast_select_fusion.7.expand_ref
  20.0 3.8 collective-permute-done
  23.8 1.0 broadcast_select_fusion.1
  24.8 43.6 %shard_map.245 = (bf16[1024,1280]{1,0:T(8,128)(2,1)}, bf16[1024,1280]{1,0:T(8,128)(2,1)}, bf16[2,4,16,320]{3,2,1,0:T(8,128)(2,1)}, bf16[320,640]{1,0:T(8,128)(2,1)}, bf16[320,1280]{1,0:T(8,128)(2,1)}) custom-call(bf16[2048,320]{1,0:T(8,128)(2,1)} %copy.38.tokens_ref, bf16[2048,320]{1,0:T(8,128)(2,1)} %copy.39.cotangent_ref, bf16[16,320]{1,0:T(8,128)(2,1)} %pad.8.small_ref, ...), custom_call_target="tpu_custom_call" | custom-call | flops 30000001024 | bytes 31457280 | tf_op jit(solution)/shard_map/pallas_call | solution.py:1045
  68.5 2.1 broadcast_select_fusion.2
  70.7 0.8 fusion
  73.4 0.7 squeeze.48.refs_3_
  74.1 0.7 squeeze.45.refs_3_
  74.9 0.7 squeeze.47.refs_4_
  76.3 1.0 broadcast_select_fusion
  78.0 30.7 %all-gather.9.cloned.1.call-done.refs_5_.refs_1_.refs_3_ = bf16[1280,640]{1,0:T(8,128)(2,1)} async-done(((bf16[320,640]{1,0:T(8,128)(2,1)}), bf16[1280,640]{1,0:T(8,128)(2,1)}) %all-gather.9.cloned.1.call-update) | async-done | bytes 1638416 | tf_op jit(solution)/shard_map/all_gather | solution.py:1357
  108.7 3.0 collective-permute-done.1.refs_2_.refs_5_
  111.7 1.2 copy-done.24
  112.8 38.3 %shard_map.246 = (bf16[16,128]{1,0:T(8,128)(2,1)}, bf16[1024,1280]{1,0:T(8,128)(2,1)}, bf16[15,1024,64]{2,1,0:T(8,128)(2,1)}, bf16[1024,320]{1,0:T(8,128)(2,1)},...) custom-call(bf16[1024,1280]{1,0:T(8,128)(2,1)} %get-tuple-element.90.refs_0_, ...), custom_call_target="tpu_custom_call" | custom-call | flops 30000001024 | bytes 31457280 | tf_op jit(solution)/shard_map/pallas_call | solution.py:1017
  151.1 37.9 %shard_map.247 = (bf16[1024,1280]{1,0:T(8,128)(2,1)}, bf16[1024,1280]{1,0:T(8,128)(2,1)}, bf16[1024,1280]{1,0:T(8,128)(2,1)}, bf16[1280,640]{1,0:T(8,128)(2,1)}) custom-call(bf16[256,1280]{1,0:T(8,128)(2,1)} %get-tuple-element.94.refs_0_, bf16[1280,640]{1,0:T(8,128)(2,1)} %all-gather.9.cloned.1.call-done.refs_5_.refs_1_.refs_3_, ...), custom_call_target="tpu_custom_call" | custom-call | flops 30000001024 | bytes 31457280 | tf_op jit(solution)/shard_map/pallas_call | solution.py:1017
  189.1 38.2 %shard_map.248 = (bf16[256,1280]{1,0:T(8,128)(2,1)}, bf16[1280,640]{1,0:T(8,128)(2,1)}) custom-call(bf16[1024,1280]{1,0:T(8,128)(2,1)} %get-tuple-element.97.refs_0_.refs_6_, f32[256,1280]{1,0:T(8,128)} %get-tuple-element.98.refs_1_.refs_8_, bf16[1280,640]{1,0:T(8,128)(2,1)} %all-gather.11.cloned.1.call-done.refs_4_.refs_2_.refs_1_, ...), custom_call_target="tpu_custom_call" | custom-call | flops 30000001024 | bytes 31457280 | tf_op jit(solution)/shard_map/pallas_call | solution.py:1017
  227.3 46.3 %shard_map.249 = (bf16[1024,1280]{1,0:T(8,128)(2,1)}, bf16[1024,1280]{1,0:T(8,128)(2,1)}, bf16[15,1024,64]{2,1,0:T(8,128)(2,1)}, bf16[1024,320]{1,0:T(8,128)(2,1...) custom-call(bf16[256,1280]{1,0:T(8,128)(2,1)} %get-tuple-element.100.refs_0_, ...), custom_call_target="tpu_custom_call" | custom-call | flops 30000001024 | bytes 31457280 | tf_op jit(solution)/shard_map/pallas_call | solution.py:1017
  273.6 30.5 %shard_map.250 = (bf16[1024,1280]{1,0:T(8,128)(2,1)}, bf16[1024,1280]{1,0:T(8,128)(2,1)}, bf16[1024,1280]{1,0:T(8,128)(2,1)}, bf16[1280,1280]{1,0:T(8,128)(2,1)}) custom-call(bf16[256,1280]{1,0:T(8,128)(2,1)} %get-tuple-element.102.refs_0_, bf16[1280,640]{1,0:T(8,128)(2,1)} %all-gather.15.cloned.1.call-done.refs_5_.refs_1_.refs_4_, ...), custom_call_target="tpu_custom_call" | custom-call | flops 30000001024 | bytes 31457280 | tf_op jit(solution)/shard_map/pallas_call | solution.py:1017
  304.4 40.9 %shard_map.251 = (f32[256,1280]{1,0:T(8,128)}, bf16[256,1280]{1,0:T(8,128)(2,1)}, f32[8,1280]{1,0:T(8,128)}, bf16[1280,1280]{1,0:T(8,128)(2,1)}, bf16[256,1280]{1,0:T(8,128)(2,1)}) custom-call(bf16[1024,1280]{1,0:T(8,128)(2,1)} %get-tuple-element.105.refs_0_, f32[256,1280]{1,0:T(8,128)} %get-tuple-element.106.refs_1_, ...), custom_call_target="tpu_custom_call" | custom-call | flops 30000001024 | bytes 31457280 | tf_op jit(solution)/shard_map/pallas_call | solution.py:1017
  345.4 2.4 constant_dynamic-slice_fusion.2.refs_11_
  347.9 56.0 %shard_map.252 = (bf16[256,1280]{1,0:T(8,128)(2,1)}, f32[8,1280]{1,0:T(8,128)}, bf16[320,2048]{1,0:T(8,128)(2,1)}, bf16[1280,1280]{1,0:T(8,128)(2,1)}) custom-call(bf16[256,1280]{1,0:T(8,128)(2,1)} %get-tuple-element.109.refs_0_, f32[256,1280]{1,0:T(8,128)} %get-tuple-element.110.refs_1_, bf16[256,1280]{1,0:T(8,128)(2,1)} %get-tuple-element.100.refs_0_.refs_2_, ...), custom_call_target="tpu_custom_call" | custom-call | flops 30000001024 | bytes 31457280 | tf_op jit(solution)/shard_map/pallas_call | solution.py:1017
  404.2 66.2 %shard_map.253 = (f32[256,1280]{1,0:T(8,128)}, bf16[256,1280]{1,0:T(8,128)(2,1)}, f32[8,1280]{1,0:T(8,128)}, bf16[1280,640]{1,0:T(8,128)(2,1)}, bf16[1280,640]{1...) custom-call(bf16[256,1280]{1,0:T(8,128)(2,1)} %get-tuple-element.118.refs_0_, ...), custom_call_target="tpu_custom_call" | custom-call | flops 30000001024 | bytes 31457280 | tf_op jit(solution)/shard_map/pallas_call | solution.py:1017
  470.5 2.0 constant_dynamic-slice_fusion.1.refs_3_
  472.5 2.4 constant_dynamic-slice_fusion.far_ref
  474.9 39.9 %shard_map.254 = (bf16[1024,960]{1,0:T(8,128)(2,1)}, bf16[1280,320]{1,0:T(8,128)(2,1)}, bf16[1280,640]{1,0:T(8,128)(2,1)}) custom-call(bf16[256,1280]{1,0:T(8,128)(2,1)} %get-tuple-element.127.refs_0_, bf16[1280,640]{1,0:T(8,128)(2,1)} %all-gather.7.cloned.1.call-done.refs_1_.refs_4_, bf16[1280,640]{1,0:T(8,128)(2,1)} %copy-done.24, ...), custom_call_target="tpu_custom_call" | custom-call | flops 30000001024 | bytes 31457280 | tf_op jit(solution)/shard_map/pallas_call | solution.py:1017
  514.9 18.8 %shard_map.255.far2_ref = bf16[320,1280]{1,0:T(8,128)(2,1)} custom-call(bf16[320,1280]{1,0:T(8,128)(2,1)} %reduce-scatter.11.cloned.1.call-done.up_ref.late2_ref), custom_call_target="tpu_custom_call" | custom-call | flops 10000000000 | bytes 10485760 | tf_op jit(solution)/shard_map/pallas_call | solution.py:1263
  533.7 1.4 reduce-scatter.9.cloned.1.call-done.early_ref
  535.1 42.9 %shard_map.256 = (bf16[1280,640]{1,0:T(8,128)(2,1)}, bf16[256,1280]{1,0:T(8,128)(2,1)}, f32[8,1280]{1,0:T(8,128)}) custom-call(bf16[1024,960]{1,0:T(8,128)(2,1)} %get-tuple-element.140.refs_0_, bf16[1280,320]{1,0:T(8,128)(2,1)} %get-tuple-element.141.refs_1_, f32[256,1280]{1,0:T(8,128)} %get-tuple-element.142.refs_2_, ...), custom_call_target="tpu_custom_call" | custom-call | flops 30000001024 | bytes 31457280 | tf_op jit(solution)/shard_map/pallas_call | solution.py:1017
  578.1 35.4 %shard_map.257 = (f32[320,2048]{1,0:T(8,128)}, f32[16,320]{1,0:T(8,128)}, bf16[320,640]{1,0:T(8,128)(2,1)}) custom-call(bf16[320,640]{1,0:T(8,128)(2,1)} %reduce-scatter.9.cloned.1.call-done.early_ref, bf16[256,1280]{1,0:T(8,128)(2,1)} %get-tuple-element.145.near_ref, bf16[1024,320]{1,0:T(8,128)(2,1)} %constant_dynamic-slice_fusion.far_ref, ...), custom_call_target="tpu_custom_call" | custom-call | flops 30000001024 | bytes 31457280 | tf_op jit(solution)/shard_map/pallas_call | solution.py:1249
  613.5 2.5 select_bitcast_fusion
  617.2 0.7 reshape.45
  617.9 1.1 copy-done
  619.0 1.1 copy-done.1
  620.2 1.1 copy-done.2
  621.3 1.0 copy-done.5
  622.3 20.5 %shard_map.258 = (f32[3,320,320]{2,1,0:T(8,128)S(1)}, f32[320,320]{1,0:T(8,128)S(1)}, f32[320,1280]{1,0:T(8,128)S(1)}) custom-call(bf16[320,1280]{1,0:T(8,128)(2,1)S(1)} %copy-done.1, bf16[320,640]{1,0:T(8,128)(2,1)S(1)} %copy-done.5, bf16[320,1280]{1,0:T(8,128)(2,1)S(1)} %copy-done, bf16[320,640]{1,0:T(8,128)(2,1)S(1)} %copy-done.4, ...), custom_call_target="tpu_custom_call" | custom-call | tf_op jit(solution)/shard_map/pallas_call | solution.py:1276
  642.9 0.8 copy-done.3
  643.6 2.0 copy.42
  645.6 2.7 copy.49
  648.3 1.5 copy.50
  649.8 1.1 copy.51
  650.9 1.2 copy.52
  (99 shorter events, 6.8 us)
Async XLA Ops:
  7.2 65.7 %all-gather.7.cloned.1.call-start = ((), (), s32[]{:S(2)}) async-start(), calls=%async_computation.6 | async-start | bytes 2048000 | tf_op jit(solution)/shard_map/all_gather | solution.py:1357
  9.8 4.3 copy-start.16
  9.9 4.4 copy-start.10
  11.2 12.6 %collective-permute-start = (bf16[320,640]{1,0:T(8,128)(2,1)}, bf16[320,640]{1,0:T(8,128)(2,1)S(1)}, u32[]{:S(2)}, u32[]{:S(2)}) collective-permute-start(bf16[320,640]{1,0:T(8,128)(2,1)} %get-tuple-element.192), channel_id=1, source_target_pairs={{0,16},{16,0},{1,17},{17,1},{2,18},{18,2},{3,19},{19,3},{4,20},{20... | collective-permute-start | bytes 1228808 | tf_op jit(solution)/shard_map/ppermute | solution.py:1290
  15.8 2.7 copy-start.17
  15.8 2.7 copy-start.18
  15.8 2.7 copy-start.19
  15.8 2.7 copy-start.20
  15.8 2.7 copy-start.21
  15.8 2.7 copy-start.22
  15.8 2.7 copy-start.23
  15.8 3.3 copy-start.6
  24.8 83.9 %all-gather.9.cloned.1.call-start = ((), (), s32[]{:S(2)}) async-start(), calls=%async_computation.7 | async-start | bytes 2048000 | tf_op jit(solution)/shard_map/all_gather | solution.py:1357
  68.4 2.2 copy-start.7
  68.5 2.2 copy-start.9
  70.6 2.2 copy-start.14
  70.6 80.5 %all-gather.11.cloned.1.call-start = ((), (), s32[]{:S(2)}) async-start(), calls=%async_computation.8 | async-start | bytes 2048000 | tf_op jit(solution)/shard_map/all_gather | solution.py:1357
  71.5 117.6 %all-gather.13.cloned.1.call-start = ((), (), s32[]{:S(2)}) async-start(), calls=%async_computation.9 | async-start | bytes 2048000 | tf_op jit(solution)/shard_map/all_gather | solution.py:1357
  72.1 155.2 %all-gather.15.cloned.1.call-start = ((), (), s32[]{:S(2)}) async-start(), calls=%async_computation.10 | async-start | bytes 2048000 | tf_op jit(solution)/shard_map/all_gather | solution.py:1357
  72.7 231.8 %all-gather.17.cloned.1.call-start = ((), (), s32[]{:S(2)}) async-start(), calls=%async_computation.11 | async-start | bytes 4096000 | tf_op jit(solution)/shard_map/all_gather | solution.py:1357
  72.9 38.7 %collective-permute-start.1 = (bf16[1280,640]{1,0:T(8,128)(2,1)}, bf16[1280,640]{1,0:T(8,128)(2,1)S(1)}, u32[]{:S(2)}, u32[]{:S(2)}) collective-permute-start(bf16[1280,640]{1,0:T(8,128)(2,1)} %all-gather.7.cloned.1.call-done.refs_1_.refs_4_), channel_id=1, source_target_pairs={{0,16},{16,0},{1,17},{17,1},{2,18},{18,2},{3,19},{19,3},{4,20},{20... | collective-permute-start | bytes 4915208 | tf_op jit(solution)/shard_map/ppermute | solution.py:1290
  77.3 326.8 %reduce-scatter.7.cloned.1.call-start = ((), (), s32[]{:S(2)}) async-start(), calls=%async_computation.12 | async-start | bytes 4096000 | tf_op jit(solution)/shard_map/reduce_scatter | solution.py:1409
  111.7 1.2 copy-start.24
  304.1 170.8 %reduce-scatter.11.cloned.1.call-start = ((), (), s32[]{:S(2)}) async-start(), calls=%async_computation.14 | async-start | bytes 4096000 | tf_op jit(solution)/shard_map/reduce_scatter | solution.py:1409
  345.4 169.5 %reduce-scatter.13.cloned.1.call-start = ((), (), s32[]{:S(2)}) async-start(), calls=%async_computation.15 | async-start | bytes 4096000 | tf_op jit(solution)/shard_map/reduce_scatter | solution.py:1409
  403.9 131.2 %reduce-scatter.9.cloned.1.call-start = ((), (), s32[]{:S(2)}) async-start(), calls=%async_computation.13 | async-start | bytes 2048000 | tf_op jit(solution)/shard_map/reduce_scatter | solution.py:1409
  470.4 107.6 %reduce-scatter.15.cloned.1.call-start = ((), (), s32[]{:S(2)}) async-start(), calls=%async_computation.16 | async-start | bytes 2048000 | tf_op jit(solution)/shard_map/reduce_scatter | solution.py:1409
  514.9 101.1 %reduce-scatter.17.cloned.1.call-start = ((), (), s32[]{:S(2)}) async-start(), calls=%async_computation.17 | async-start | bytes 2048000 | tf_op jit(solution)/shard_map/reduce_scatter | solution.py:1409
  578.0 35.4 %copy-start.11 = (bf16[320,1280]{1,0:T(8,128)(2,1)S(1)}, bf16[320,1280]{1,0:T(8,128)(2,1)}, u32[]{:S(2)}) copy-start(bf16[320,1280]{1,0:T(8,128)(2,1)} %reduce-scatter.7.cloned.1.call-done.refs_10_) | copy-start | bytes 2457604
  578.1 35.4 %copy-start.12 = (bf16[320,1280]{1,0:T(8,128)(2,1)S(1)}, bf16[320,1280]{1,0:T(8,128)(2,1)}, u32[]{:S(2)}) copy-start(bf16[320,1280]{1,0:T(8,128)(2,1)} %get-tuple-element.163) | copy-start | bytes 2457604
  578.1 35.4 %copy-start.13 = (bf16[320,640]{1,0:T(8,128)(2,1)S(1)}, bf16[320,640]{1,0:T(8,128)(2,1)}, u32[]{:S(2)}) copy-start(bf16[320,640]{1,0:T(8,128)(2,1)} %reduce-scatter.9.cloned.1.call-done.early_ref) | copy-start | bytes 1228804
  613.5 2.5 copy-start.15
  613.5 4.4 copy-start.4
  617.9 1.1 copy-start
  619.0 1.1 copy-start.1
  620.2 1.1 copy-start.2
  621.3 1.0 copy-start.5
  642.8 0.8 copy-start.3
  645.6 2.7 copy-start.8
Sparse Core Ops, SparseCore 0:
  24.9 39.6 all-gather.6
  70.7 37.9 all-gather.8
  110.8 37.0 all-gather.10
  149.9 37.0 all-gather.12
  188.9 37.0 all-gather.14
  228.0 64.5 all-gather.16
  304.3 62.5 reduce-scatter.6
  369.1 62.3 reduce-scatter.10
  433.9 62.4 reduce-scatter.12
  498.5 36.5 reduce-scatter.8
  537.5 35.3 reduce-scatter.14
  578.1 36.2 reduce-scatter.16

commit v13 on v12

--- a/solution.py
+++ b/solution.py
@@ -406,21 +406,20 @@
 
 
 def attend_kernel(
-    gathered, heads, group, x_ref, mine_ref, other_ref, vec_ref, bias_ref,
-    full_ref, normed_ref, heads_ref, o_ref, lse_ref, hidden_ref, second_ref,
-    weight, o3, stage, land, total, scatter_sems, gather_sems, local_sems,
+    heads, group, x_ref, mine_ref, other_ref, vec_ref, bias_ref,
+    normed_ref, heads_ref, o_ref, lse_ref, hidden_ref, second_ref,
+    weight, o3, stage, land, total, scatter_sems, local_sems,
 ):
     width = o_ref.shape[1]
     halves = Halves((mine_ref, other_ref), weight, local_sems, 0)
     halves.start()
-    if not gathered:
-        full_ref[group.chunk(group.me), :] = x_ref[...]
+    lse_ref[...] = jnp.zeros_like(lse_ref)
     halves.wait()
 
-    def project(owner):
+    @pl.loop(0, LENGTH // group.rows)
+    def _(owner):
         rows = group.chunk(owner)
-        values = (x_ref if gathered else full_ref)[rows, :].astype(WIDE)
-        hat, _ = normalise(values)
+        hat, _ = normalise(x_ref[rows, :].astype(WIDE))
         normed = (hat * vec_ref[0:1, :] + vec_ref[1:2, :]).astype(LOW)
         normed_ref[rows, :] = normed
         mixed = nn(normed, weight[:, : 3 * width]) + bias_ref[...]
@@ -430,16 +429,7 @@
                 piece = piece * HEAD ** (-0.5)
             heads_ref[j, rows, :] = piece.astype(LOW)
 
-    if gathered:
-        full_ref[...] = jnp.zeros_like(full_ref)
-
-        @pl.loop(0, LENGTH // group.rows)
-        def _(n):
-            project(n)
-    else:
-        Gather(group, full_ref, gather_sems).each(project)
-    group.emit(0, 1, 2)
-    lse_ref[...] = jnp.zeros_like(lse_ref)
+    group.emit(0, 1)
 
     def attend(owner):
         rows = group.chunk(owner)
@@ -450,10 +440,10 @@
 
     scatter = Scatter(group, stage, land, total, scatter_sems)
     scatter.start(attend)
-    group.emit(3, 4)
+    group.emit(2, 3)
     for j in range(PARTS):
         rows = slice(j * group.part, (j + 1) * group.part)
-        residual = (x_ref if gathered else full_ref)[group.slab(group.me, j), :].astype(WIDE)
+        residual = x_ref[group.slab(group.me, j), :].astype(WIDE)
         hidden = residual + scatter.take(j) + vec_ref[2:3, :]
         hidden_ref[rows, :] = hidden
         hat, _ = normalise(hidden)
@@ -511,8 +501,8 @@
 
 
 def contract_kernel(
-    group, active_ref, hidden_ref, cm_ref, co_ref, vec_ref, result_ref,
-    contract, stage, land, total, scatter_sems, local_sems,
+    group, active_ref, hidden_ref, cm_ref, co_ref, vec_ref, result_ref, full_ref,
+    contract, stage, land, total, scatter_sems, gather_sems, local_sems,
 ):
     halves = Halves((cm_ref, co_ref), contract, local_sems, 0)
     halves.start()
@@ -522,8 +512,10 @@
     group.need(1)
     for j in range(PARTS):
         rows = slice(j * group.part, (j + 1) * group.part)
-        result = hidden_ref[rows, :] + scatter.take(j) + vec_ref[5:6, :]
-        result_ref[rows, :] = result.astype(LOW)
+        result = (hidden_ref[rows, :] + scatter.take(j) + vec_ref[5:6, :]).astype(LOW)
+        result_ref[rows, :] = result
+        full_ref[group.slab(group.me, j), :] = result
+    Gather(group, full_ref, gather_sems).each(lambda owner: None)
     scatter.done()
 
 
@@ -728,22 +720,18 @@
 
     store = pltpu.make_async_copy(outer, w_ref, local_sems.at[2])
     store.start()
-    length = y_ref.shape[0]
-    own = pl.ds(pl.multiple_of(section * length, length), length)
-
     @pl.when(section == 0)
     def _():
-        results_ref[:, own] = turned(y_ref[...]).astype(LOW)
+        results_ref[section] = turned(y_ref[...]).astype(LOW)
 
     @pl.when(section == 1)
     def _():
-        results_ref[:, own] = turned(late[...]).astype(LOW)
+        results_ref[section] = turned(late[...]).astype(LOW)
 
     group.need(1, 2)
     attend_grads(group, scatter, x_ref, grad_ref, vec_ref, mixed, width, out_ref, sums_ref)
     results.wait()
-    away = pl.ds(pl.multiple_of((1 - section) * length, length), length)
-    results_ref[:, away] = turned(y_land[...]).astype(LOW)
+    results_ref[1 - section] = turned(y_land[...]).astype(LOW)
     scatter.done()
     store.wait()
 
@@ -823,8 +811,8 @@
 
 
 def finish_kernel(
-    early_ref, near_ref, far_ref, a0, n0, a1, n1,
-    grads_ref, sums_ref, got_early,
+    late_ref, early1_ref, early2_ref, near_ref, far_ref, a0, n0, a1, n1,
+    grads_ref, sums_ref, got_late, got_early1, got_early2,
     mine, stage4, block, land_col, land_x, land_z, land,
     deliver_sems, col_sems, x_sems, z_sems, part_sems,
 ):
@@ -836,7 +824,9 @@
     group.greet(True, True, others)
     gradient_up = OneWay([(far_ref, land)], [], x_sems.at[:, pl.ds(1, 1)])
     gradient_down = OneWay([], [(mine, land)], x_sems.at[:, pl.ds(2, 1)])
-    parts = OneWay([], [(early_ref, got_early)], part_sems)
+    parts = OneWay(
+        [(late_ref, got_late)], [(early1_ref, got_early1), (early2_ref, got_early2)], part_sems
+    )
     deliver = Deliver(group, stage4, mine, deliver_sems)
     deliver.start(near_ref)
     gradient_up.start()
@@ -867,15 +857,14 @@
     swap.start()
     deliver.done()
     gradient_down.start()
-    own = pl.ds(pl.multiple_of(section * length, length), length)
 
     @pl.when(section == 0)
     def _():
-        grads_ref[:, own] = turned(mine[...])
+        grads_ref[section] = turned(mine[...]).astype(LOW)
 
     @pl.when(section == 1)
     def _():
-        grads_ref[:, own] = turned(far_ref[...])
+        grads_ref[section] = turned(far_ref[...]).astype(LOW)
 
     swap.wait()
     land_z[row] = block[me, section] + land_x[...]
@@ -893,7 +882,7 @@
     sums_ref[...] = result
     gradient_up.wait()
     gradient_down.wait()
-    grads_ref[:, pl.ds(pl.multiple_of(away * length, length), length)] = turned(land[...])
+    grads_ref[away] = turned(land[...]).astype(LOW)
     parts.wait()
 
 
@@ -904,31 +893,28 @@
     pl.semaphore_wait(barrier, 1)
 
 
-def up_kernel(up_ref, got_ref, sems):
+def cross_kernel(up, part_ref, got_ref, sems):
     greet_section()
-    part = OneWay([(up_ref, got_ref)], [], sems)
+    pair = [(part_ref, got_ref)]
+    part = OneWay(pair, [], sems) if up else OneWay([], pair, sems)
     part.start()
     part.wait()
 
 
-def last_kernel(
-    late1_ref, early1_ref, late2_ref, early2_ref, far2_ref, attend_ref, output_ref, expand_ref,
-    own1, far1, own2, far2, sems, local_sems,
-):
+def write_kernel(*refs):
+    (late, far_late, early, far_early), (attend_ref, output_ref, expand_ref, contract_ref) = (
+        [refs[n : n + 3] for n in (0, 3, 6, 9)],
+        refs[12:16],
+    )
+    own, far, sems = refs[16:]
+    half = early[0].shape[1]
+    width = output_ref.shape[1]
     section = lax.axis_index("section")
-    half = early1_ref.shape[1]
-    width = output_ref.shape[1]
-    greet_section()
-    parts = OneWay(
-        [(late1_ref, far1)],
-        [(early1_ref, own1.at[:, pl.ds(half, half)]), (early2_ref, own2.at[:, pl.ds(half, half)])],
-        sems,
-    )
-    parts.start()
-
-    def load(pairs):
+
+    def load(firsts, seconds):
         copies = [
-            pltpu.make_async_copy(source, into, local_sems.at[n]) for n, (source, into) in enumerate(pairs)
+            pltpu.make_async_copy(source, into, sems.at[n])
+            for n, (source, into) in enumerate((*firsts, *seconds))
         ]
         for copy in copies:
             copy.start()
@@ -937,30 +923,22 @@
 
     @pl.when(section == 0)
     def _():
-        load(((early1_ref, own1.at[:, pl.ds(0, half)]), (early2_ref, own2.at[:, pl.ds(0, half)])))
+        load(
+            [(early[n], own.at[n, :, pl.ds(0, half)]) for n in range(3)],
+            [(far_early[n], own.at[n, :, pl.ds(half, half)]) for n in range(3)],
+        )
+        far[...] = jnp.zeros_like(far)
 
     @pl.when(section == 1)
     def _():
-        load(((late1_ref, own1), (late2_ref, own2), (far2_ref, far2)))
-
-    parts.wait()
-
-    def give(first, second):
-        for j in range(3):
-            attend_ref[j] = first[:, j * width : (j + 1) * width]
-        output_ref[...] = first[:, 3 * width :]
-        expand_ref[...] = second
-
-    @pl.when(section == 0)
-    def _():
-        give(own1[...].astype(WIDE), own2[...].astype(WIDE))
-
-    @pl.when(section == 1)
-    def _():
-        give(
-            own1[...].astype(WIDE) + far1[...].astype(WIDE),
-            own2[...].astype(WIDE) + far2[...].astype(WIDE),
-        )
+        load([(late[n], own.at[n]) for n in range(3)], [(far_late[n], far.at[n]) for n in range(3)])
+
+    first = own[0].astype(WIDE) + far[0].astype(WIDE)
+    for j in range(3):
+        attend_ref[j] = first[:, j * width : (j + 1) * width]
+    output_ref[...] = first[:, 3 * width :]
+    expand_ref[...] = own[1].astype(WIDE) + far[1].astype(WIDE)
+    contract_ref[...] = own[2].astype(WIDE) + far[2].astype(WIDE)
 
 
 VM = pl.BlockSpec(memory_space=pltpu.VMEM)
@@ -1058,11 +1036,10 @@
     )(tokens, cotangent, small, expand, contract)
 
 
-def attend_call(number, gathered, x, pair, vec, bias, rows, width, swaps):
+def attend_call(number, x, pair, vec, bias, rows, width, swaps):
     size = vec.shape[1]
     heads = width // HEAD
     outs = (
-        shape((LENGTH, size) if not gathered else (16, 128)),
         shape((LENGTH, size)),
         shape((3 * heads, LENGTH, HEAD)),
         shape((LENGTH, width)),
@@ -1073,11 +1050,11 @@
     scratch = [
         pltpu.VMEM((size, 4 * width), LOW),
         pltpu.VMEM((heads, LENGTH, HEAD), LOW),
-        *scatter_scratch(rows, size), PAIRS, LOCAL,
+        *scatter_scratch(rows, size), LOCAL,
     ]
     return launch(
-        functools.partial(attend_kernel, gathered, heads),
-        number, rows, [VM, ANY, ANY, VM, VM], (x, *pair, vec, bias), outs, (VM,) * 7, scratch, swaps,
+        functools.partial(attend_kernel, heads),
+        number, rows, [VM, ANY, ANY, VM, VM], (x, *pair, vec, bias), outs, (VM,) * 6, scratch, swaps,
     )
 
 
@@ -1099,10 +1076,10 @@
 def contract_call(number, active, hidden, pair, vec, swaps):
     rows, size = hidden.shape
     wide = active.shape[1]
-    scratch = [pltpu.VMEM((size, wide), LOW), *scatter_scratch(rows, size), LOCAL]
+    scratch = [pltpu.VMEM((size, wide), LOW), *scatter_scratch(rows, size), PAIRS, LOCAL]
     return launch(
         contract_kernel, number, rows, [VM, VM, ANY, ANY, VM], (active, hidden, *pair, vec),
-        [shape((rows, size))], (VM,), scratch, swaps, late=(1,),
+        [shape((rows, size)), shape((LENGTH, size))], (VM, VM), scratch, swaps, late=(1,),
     )
 
 
@@ -1167,7 +1144,7 @@
     rows, size = grad.shape
     width = o.shape[1]
     heads = width // HEAD
-    outs = (shape((rows, size)), shape((8, size), WIDE), shape((width, 2 * LENGTH)), shape((size, 4 * width)))
+    outs = (shape((rows, size)), shape((8, size), WIDE), shape((2, width, LENGTH)), shape((size, 4 * width)))
     scratch = [
         *scores_scratch(size, width, heads),
         pltpu.VMEM((LENGTH, 3 * width), LOW),
@@ -1223,14 +1200,14 @@
     )[0]
 
 
-def finish_call(number, early, near, far, sums, row_count):
+def finish_call(number, parts, near, far, sums, row_count):
     rows, size = near.shape
     length, width = far.shape
     columns = length // rows
     outs = (
-        shape((width, 2 * length), WIDE),
+        shape((2, width, length)),
         shape((16, width), WIDE),
-        shape(early.shape),
+        *[shape(part.shape) for part in parts],
     )
     scratch = [
         pltpu.VMEM((length, width), LOW),
@@ -1244,46 +1221,47 @@
         pltpu.SemaphoreType.DMA((2, 3)),
         pltpu.SemaphoreType.DMA((2, 3)),
         pltpu.SemaphoreType.DMA((2, row_count)),
-        pltpu.SemaphoreType.DMA((2, 2)),
+        pltpu.SemaphoreType.DMA((2, 3)),
     ]
     return pl.pallas_call(
         finish_kernel,
         out_shape=outs,
-        in_specs=[ANY] + [VM] * 6,
-        out_specs=(VM, VM, ANY),
+        in_specs=[ANY] * 3 + [VM] * 6,
+        out_specs=(VM, VM) + (ANY,) * 3,
         scratch_shapes=scratch,
         compiler_params=pltpu.CompilerParams(
             collective_id=number, has_side_effects=True, vmem_limit_bytes=GRANT
         ),
         cost_estimate=pl.CostEstimate(flops=int(3e10), bytes_accessed=30 * MEBI, transcendentals=0),
-    )(early, near, far, *sums)
-
-
-def up_call(number, part):
+    )(*parts, near, far, *sums)
+
+
+def cross_call(number, up, part):
     return pl.pallas_call(
-        up_kernel,
+        functools.partial(cross_kernel, up),
         out_shape=shape(part.shape),
         in_specs=[ANY],
         out_specs=ANY,
         scratch_shapes=[pltpu.SemaphoreType.DMA((2, 1))],
-        compiler_params=pltpu.CompilerParams(collective_id=number, has_side_effects=True),
+        compiler_params=pltpu.CompilerParams(
+            collective_id=number, has_side_effects=True, vmem_limit_bytes=GRANT
+        ),
         cost_estimate=pl.CostEstimate(flops=int(1e10), bytes_accessed=10 * MEBI, transcendentals=0),
     )(part)
 
 
-def last_call(number, width, *parts):
-    rows, size = parts[0].shape
+def write_call(width, late, far_late, early, far_early):
+    rows, size = late[0].shape
     return pl.pallas_call(
-        last_kernel,
-        out_shape=(shape((3, rows, width), WIDE), shape((rows, width), WIDE), shape((rows, size), WIDE)),
-        in_specs=[ANY] * 5,
-        out_specs=(VM,) * 3,
-        scratch_shapes=[pltpu.VMEM((rows, size), LOW)] * 4
-        + [pltpu.SemaphoreType.DMA((2, 3)), pltpu.SemaphoreType.DMA((3,))],
-        compiler_params=pltpu.CompilerParams(
-            collective_id=number, has_side_effects=True, vmem_limit_bytes=32 * MEBI
+        write_kernel,
+        out_shape=(
+            shape((3, rows, width), WIDE), shape((rows, width), WIDE), shape((rows, size), WIDE), shape((rows, size), WIDE)
         ),
-    )(*parts)
+        in_specs=[ANY] * 12,
+        out_specs=(VM,) * 4,
+        scratch_shapes=[pltpu.VMEM((3, rows, size), LOW)] * 2 + [pltpu.SemaphoreType.DMA((6,))],
+        compiler_params=pltpu.CompilerParams(vmem_limit_bytes=GRANT),
+    )(*late, *far_late, *early, *far_early)
 
 
 def swap_sections(value):
@@ -1385,8 +1363,8 @@
     for layer in range(2):
         last = layer == 1
         vec = wide_vectors[layer]
-        (full, normed, heads, o, lse, hidden, second_own), (other,) = attend_call(
-            2 + 3 * layer, not last, x, attn, vec, attend_biases[layer], rows, width, [mats[layer][1]]
+        (normed, heads, o, lse, hidden, second_own), (other,) = attend_call(
+            2 + 3 * layer, x, attn, vec, attend_biases[layer], rows, width, [mats[layer][1]]
         )
         expand = (mats[layer][1], other)
         outs, others = widen_call(
@@ -1400,10 +1378,10 @@
         pairs.append((attn, expand, contract))
         kept.append((normed, heads, o, lse, hidden, second, active, slope))
         if not last:
-            (x,), others = contract_call(4, active, hidden, contract, vec, [mats[1][0]])
-            owns.append(x)
+            (own, x), others = contract_call(4, active, hidden, contract, vec, [mats[1][0]])
+            owns.append(own)
             attn = (mats[1][0], others[0])
-    y0 = own_features(full)
+    y0 = own_features(x)
 
     def scatter(total):
         return lax.psum_scatter(total, "row", scatter_dimension=0, tiled=True)
@@ -1430,15 +1408,15 @@
     mixed, outer, total_e0 = scores_back_call(14, low, attn, heads, o, lse, ek0, es0)
     part_w1, mixed = tie(scatter(w1), mixed)
     part_e1, mixed = tie(part_e1, mixed)
-    far_e1, mixed = tie(up_call(18, part_e1), mixed)
+    far_e1, mixed = tie(cross_call(18, True, part_e1), mixed)
     part_c0, mixed = tie(scatter(total_c0), mixed)
     total_w0, gx0_own, attend_sums0 = attend_back_call(
         15, mixed, outer, grad_hidden, owns[0], attn, normed, wide_vectors[0]
     )
     part_e0, gx0_own = tie(scatter(total_e0), gx0_own)
-    input_grads, small_grads, far_c0 = finish_call(
+    input_grads, small_grads, far_w1, far_c0, far_e0 = finish_call(
         16,
-        part_c0,
+        (part_w1, part_c0, part_e0),
         gx0_own,
         own_features(gx1_full),
         (attend_sums0, expand_sums0, attend_sums1, expand_sums1),
@@ -1446,15 +1424,17 @@
     )
 
     part_w0, small_grads = tie(scatter(total_w0), small_grads)
-    attend_part, output_part, expand_part = last_call(
-        17, width, part_w1, part_w0, part_e1, part_e0, far_e1
-    )
-    contract_part = pick(
-        jnp.concatenate([part_c0, far_c0], 1).astype(WIDE), part_c1.astype(WIDE) + far_c1.astype(WIDE)
+    far_w0 = cross_call(17, False, part_w0)
+    attend_part, output_part, expand_part, contract_part = write_call(
+        width,
+        (part_w1, part_e1, part_c1),
+        (far_w1, far_e1, far_c1),
+        (part_w0, part_e0, part_c0),
+        (far_w0, far_e0, far_c0),
     )
     return (
-        layer_outputs.T[None],
-        input_grads.T[None],
+        jnp.concatenate([layer_outputs[0], layer_outputs[1]], 1).T[None],
+        jnp.concatenate([input_grads[0], input_grads[1]], 1).astype(WIDE).T[None],
         small_grads[0:1],
         small_grads[1:2],
         jnp.swapaxes(attend_part, 0, 1)[None],

time: 669 us -> 657 us (0.982)
  local copies, waits for them, and re-layouts: 35 us -> 26.1 us
    unnamed x59 -> x37, local copies, waits for them, and re-layouts: 21.7 us -> 11.3 us
    pallas_call x3 -> x4, Pallas kernels: 74.7 us -> 79.3 us  [the longest x1 45 us: finish_call(): pl.pallas_call(finish_kernel, out_shape=outs, in_specs=[ANY] * 3 + [VM] *...]
  transfers between devices with their start and end apart: 14 -> 14, of which waited for: 4 -> 3; matrix products, arithmetic and copies ran while one was open for 3% -> 4% of each run, Pallas kernels for 81% -> 83%
where the time goes in v13:
time: 657 us; the launch traced here: 648 us
  Pallas kernels  554 us (84%)
  waiting for transfers between devices  38.9 us (6%)
  local copies, waits for them, and re-layouts  26.1 us (4%)
  between operations  14.8 us (2%)
  other arithmetic  9.76 us (1%)
    pallas_call x10, Pallas kernels, launch(): pl.pallas_call(kernel, out_shape=(*outs, *[shape(s.shape, s.dtype) for s...  431 us
    pallas_call x1, Pallas kernels, finish_call(): pl.pallas_call(finish_kernel, out_shape=outs, in_specs=[ANY] * 3 + [VM] *...  45 us
    pallas_call x1, Pallas kernels, start_call(): pl.pallas_call(start_kernel, out_shape=outs, in_specs=[ANY] * 5, out_spec...  43.6 us
    all_gather x6, waiting for transfers between devices, gather_blocks(): return lax.all_gather(block, 'row', axis=0, tiled=True)  30.8 us
    pallas_call x2, Pallas kernels, cross_call(): pl.pallas_call(functools.partial(cross_kernel, up), out_shape=shape(part....  29.8 us
  transfers between devices with their start and end apart: 14, of which 3 were waited for; matrix products, arithmetic and copies ran while one was open for 4% of the time, Pallas kernels for 83%

profile of v13, /device:TPU:0, one launch (start us, length us, event | category | flops | bytes accessed | tf_op | source)
XLA Modules:
  0.0 647.5 jit_solution(9068365581587550069)
XLA Ops:
  7.2 1.1 copy.35
  8.4 1.5 copy.34
  10.2 1.0 broadcast_select_fusion.8
  11.2 2.9 collective-permute-start
  14.2 1.5 copy.38.tokens_ref
  15.8 2.6 copy.39.cotangent_ref
  18.6 0.6 pad.8.small_ref
  19.2 0.8 broadcast_select_fusion.7.expand_ref
  20.0 3.8 collective-permute-done
  23.8 1.0 broadcast_select_fusion.1
  24.8 43.6 %shard_map.245 = (bf16[1024,1280]{1,0:T(8,128)(2,1)}, bf16[1024,1280]{1,0:T(8,128)(2,1)}, bf16[2,4,16,320]{3,2,1,0:T(8,128)(2,1)}, bf16[320,640]{1,0:T(8,128)(2,1)}, bf16[320,1280]{1,0:T(8,128)(2,1)}) custom-call(bf16[2048,320]{1,0:T(8,128)(2,1)} %copy.38.tokens_ref, bf16[2048,320]{1,0:T(8,128)(2,1)} %copy.39.cotangent_ref, bf16[16,320]{1,0:T(8,128)(2,1)} %pad.8.small_ref, ...), custom_call_target="tpu_custom_call" | custom-call | flops 30000001024 | bytes 31457280 | tf_op jit(solution)/shard_map/pallas_call | solution.py:1023
  68.5 2.1 broadcast_select_fusion.2
  70.7 0.8 fusion
  72.1 0.5 all-gather.15.cloned.1.call-update
  73.4 0.7 squeeze.60.refs_3_
  74.1 0.7 squeeze.57.refs_3_
  74.9 0.7 squeeze.59.refs_4_
  75.5 0.7 squeeze.56.refs_4_
  76.3 1.0 broadcast_select_fusion
  77.4 0.6 fusion.2
  78.0 30.7 %all-gather.9.cloned.1.call-done.refs_5_.refs_1_.refs_3_ = bf16[1280,640]{1,0:T(8,128)(2,1)} async-done(((bf16[320,640]{1,0:T(8,128)(2,1)}), bf16[1280,640]{1,0:T(8,128)(2,1)}) %all-gather.9.cloned.1.call-update) | async-done | bytes 1638416 | tf_op jit(solution)/shard_map/all_gather | solution.py:1335
  108.7 3.0 collective-permute-done.1.refs_2_.refs_5_
  111.7 1.2 copy-done.15
  112.8 38.2 %shard_map.246 = (bf16[1024,1280]{1,0:T(8,128)(2,1)}, bf16[15,1024,64]{2,1,0:T(8,128)(2,1)}, bf16[1024,320]{1,0:T(8,128)(2,1)}, f32[8,1024]{1,0:T(8,128)}, f32[2...) custom-call(bf16[1024,1280]{1,0:T(8,128)(2,1)} %get-tuple-element.93.refs_0_, ...), custom_call_target="tpu_custom_call" | custom-call | flops 30000001024 | bytes 31457280 | tf_op jit(solution)/shard_map/pallas_call | solution.py:995
  151.0 37.9 %shard_map.247 = (bf16[1024,1280]{1,0:T(8,128)(2,1)}, bf16[1024,1280]{1,0:T(8,128)(2,1)}, bf16[1024,1280]{1,0:T(8,128)(2,1)}, bf16[1280,640]{1,0:T(8,128)(2,1)}) custom-call(bf16[256,1280]{1,0:T(8,128)(2,1)} %get-tuple-element.97.refs_0_, bf16[1280,640]{1,0:T(8,128)(2,1)} %all-gather.9.cloned.1.call-done.refs_5_.refs_1_.refs_3_, ...), custom_call_target="tpu_custom_call" | custom-call | flops 30000001024 | bytes 31457280 | tf_op jit(solution)/shard_map/pallas_call | solution.py:995
  189.0 41.9 %shard_map.248 = (bf16[256,1280]{1,0:T(8,128)(2,1)}, bf16[1024,1280]{1,0:T(8,128)(2,1)}, bf16[1280,640]{1,0:T(8,128)(2,1)}) custom-call(bf16[1024,1280]{1,0:T(8,128)(2,1)} %get-tuple-element.100.refs_0_.refs_6_, f32[256,1280]{1,0:T(8,128)} %get-tuple-element.101.refs_1_.refs_8_, bf16[1280,640]{1,0:T(8,128)(2,1)} %all-gather.11.cloned.1.call-done.refs_4_.refs_2_.refs_1_, ...), custom_call_target="tpu_custom_call" | custom-call | flops 30000001024 | bytes 31457280 | tf_op jit(solution)/shard_map/pallas_call | solution.py:995
  230.9 38.7 %shard_map.249 = (bf16[1024,1280]{1,0:T(8,128)(2,1)}, bf16[15,1024,64]{2,1,0:T(8,128)(2,1)}, bf16[1024,320]{1,0:T(8,128)(2,1)}, f32[8,1024]{1,0:T(8,128)}, f32[2...) custom-call(bf16[1024,1280]{1,0:T(8,128)(2,1)} %get-tuple-element.103.refs_0_, ...), custom_call_target="tpu_custom_call" | custom-call | flops 30000001024 | bytes 31457280 | tf_op jit(solution)/shard_map/pallas_call | solution.py:995
  269.7 28.6 %shard_map.250 = (bf16[1024,1280]{1,0:T(8,128)(2,1)}, bf16[1024,1280]{1,0:T(8,128)(2,1)}, bf16[1024,1280]{1,0:T(8,128)(2,1)}, bf16[1280,1280]{1,0:T(8,128)(2,1)}) custom-call(bf16[256,1280]{1,0:T(8,128)(2,1)} %get-tuple-element.105.refs_0_, bf16[1280,640]{1,0:T(8,128)(2,1)} %all-gather.15.cloned.1.call-done.refs_5_.refs_1_.refs_4_, ...), custom_call_target="tpu_custom_call" | custom-call | flops 30000001024 | bytes 31457280 | tf_op jit(solution)/shard_map/pallas_call | solution.py:995
  298.5 41.3 %shard_map.251 = (f32[256,1280]{1,0:T(8,128)}, bf16[256,1280]{1,0:T(8,128)(2,1)}, f32[8,1280]{1,0:T(8,128)}, bf16[1280,1280]{1,0:T(8,128)(2,1)}, bf16[256,1280]{1,0:T(8,128)(2,1)}) custom-call(bf16[1024,1280]{1,0:T(8,128)(2,1)} %get-tuple-element.108.refs_0_, f32[256,1280]{1,0:T(8,128)} %get-tuple-element.109.refs_1_, ...), custom_call_target="tpu_custom_call" | custom-call | flops 30000001024 | bytes 31457280 | tf_op jit(solution)/shard_map/pallas_call | solution.py:995
  339.9 2.5 constant_dynamic-slice_fusion.2.refs_11_
  342.4 54.9 %shard_map.252 = (bf16[256,1280]{1,0:T(8,128)(2,1)}, f32[8,1280]{1,0:T(8,128)}, bf16[2,320,1024]{2,1,0:T(8,128)(2,1)}, bf16[1280,1280]{1,0:T(8,128)(2,1)}) custom-call(bf16[256,1280]{1,0:T(8,128)(2,1)} %get-tuple-element.112.refs_0_, f32[256,1280]{1,0:T(8,128)} %get-tuple-element.113.refs_1_, bf16[256,1280]{1,0:T(8,128)(2,1)} %get-tuple-element.114.refs_2_, ...), custom_call_target="tpu_custom_call" | custom-call | flops 30000001024 | bytes 31457280 | tf_op jit(solution)/shard_map/pallas_call | solution.py:995
  397.6 2.0 constant_dynamic-slice_fusion.1.refs_3_
  399.6 66.2 %shard_map.253 = (f32[256,1280]{1,0:T(8,128)}, bf16[256,1280]{1,0:T(8,128)(2,1)}, f32[8,1280]{1,0:T(8,128)}, bf16[1280,640]{1,0:T(8,128)(2,1)}, bf16[1280,640]{1...) custom-call(bf16[256,1280]{1,0:T(8,128)(2,1)} %get-tuple-element.123.refs_0_, ...), custom_call_target="tpu_custom_call" | custom-call | flops 30000001024 | bytes 31457280 | tf_op jit(solution)/shard_map/pallas_call | solution.py:995
  465.9 1.2 copy-done.4
  467.3 1.2 maximum_bitcast_fusion
  468.4 2.4 constant_dynamic-slice_fusion.far_ref
  470.9 40.3 %shard_map.254 = (bf16[1024,960]{1,0:T(8,128)(2,1)}, bf16[1280,320]{1,0:T(8,128)(2,1)}, bf16[1280,640]{1,0:T(8,128)(2,1)}) custom-call(bf16[256,1280]{1,0:T(8,128)(2,1)} %get-tuple-element.128.refs_0_, bf16[1280,640]{1,0:T(8,128)(2,1)} %all-gather.7.cloned.1.call-done.refs_1_.refs_4_, bf16[1280,640]{1,0:T(8,128)(2,1)} %copy-done.15, ...), custom_call_target="tpu_custom_call" | custom-call | flops 30000001024 | bytes 31457280 | tf_op jit(solution)/shard_map/pallas_call | solution.py:995
  511.3 18.2 %shard_map.255.refs_4_ = bf16[320,1280]{1,0:T(8,128)(2,1)} custom-call(bf16[320,1280]{1,0:T(8,128)(2,1)} %reduce-scatter.9.cloned.1.call-done.part_ref.refs_1_), custom_call_target="tpu_custom_call" | custom-call | flops 10000000000 | bytes 10485760 | tf_op jit(solution)/shard_map/pallas_call | solution.py:1240
  529.6 42.7 %shard_map.256 = (bf16[1280,640]{1,0:T(8,128)(2,1)}, bf16[256,1280]{1,0:T(8,128)(2,1)}, f32[8,1280]{1,0:T(8,128)}) custom-call(bf16[1024,960]{1,0:T(8,128)(2,1)} %get-tuple-element.144.refs_0_, bf16[1280,320]{1,0:T(8,128)(2,1)} %get-tuple-element.145.refs_1_, f32[256,1280]{1,0:T(8,128)} %get-tuple-element.146.refs_2_, ...), custom_call_target="tpu_custom_call" | custom-call | flops 30000001024 | bytes 31457280 | tf_op jit(solution)/shard_map/pallas_call | solution.py:995
  572.4 45.0 %shard_map.257 = (bf16[2,320,1024]{2,1,0:T(8,128)(2,1)}, f32[16,320]{1,0:T(8,128)}, bf16[320,1280]{1,0:T(8,128)(2,1)}, bf16[320,640]{1,0:T(8,128)(2,1)}, bf16[320,640]{1,0:T(8,128)(2,1)}) custom-call(bf16[320,1280]{1,0:T(8,128)(2,1)} %reduce-scatter.7.cloned.1.call-done.late_ref.refs_0_, ...), custom_call_target="tpu_custom_call" | custom-call | flops 30000001024 | bytes 31457280 | tf_op jit(solution)/shard_map/pallas_call | solution.py:1226
  617.3 1.4 slice_bitcast_fusion.1
  618.7 1.8 convert_bitcast_fusion
  620.5 0.6 slice_bitcast_fusion.5
  621.1 0.6 fusion.5
  621.7 0.7 reshape.45
  622.4 11.5 %shard_map.258.refs_9_ = bf16[320,640]{1,0:T(8,128)(2,1)} custom-call(bf16[320,640]{1,0:T(8,128)(2,1)} %reduce-scatter.17.cloned.1.call-done.part_ref.refs_6_), custom_call_target="tpu_custom_call" | custom-call | flops 10000000000 | bytes 10485760 | tf_op jit(solution)/shard_map/pallas_call | solution.py:1240
  633.9 4.5 shard_map.259
  638.5 2.0 copy.42
  (81 shorter events, 3.2 us)
Async XLA Ops:
  7.2 65.7 %all-gather.7.cloned.1.call-start = ((), (), s32[]{:S(2)}) async-start(), calls=%async_computation.6 | async-start | bytes 2048000 | tf_op jit(solution)/shard_map/all_gather | solution.py:1335
  9.8 4.3 copy-start.7
  9.9 4.4 copy-start.3
  11.2 12.6 %collective-permute-start = (bf16[320,640]{1,0:T(8,128)(2,1)}, bf16[320,640]{1,0:T(8,128)(2,1)S(1)}, u32[]{:S(2)}, u32[]{:S(2)}) collective-permute-start(bf16[320,640]{1,0:T(8,128)(2,1)} %get-tuple-element.198), channel_id=1, source_target_pairs={{0,16},{16,0},{1,17},{17,1},{2,18},{18,2},{3,19},{19,3},{4,20},{20... | collective-permute-start | bytes 1228808 | tf_op jit(solution)/shard_map/ppermute | solution.py:1268
  15.8 2.7 copy-start.8
  15.8 2.7 copy-start.9
  15.8 2.7 copy-start.10
  15.8 2.7 copy-start.11
  15.8 2.7 copy-start.12
  15.8 2.7 copy-start.13
  15.8 2.7 copy-start.14
  15.8 3.3 copy-start
  24.8 83.9 %all-gather.9.cloned.1.call-start = ((), (), s32[]{:S(2)}) async-start(), calls=%async_computation.7 | async-start | bytes 2048000 | tf_op jit(solution)/shard_map/all_gather | solution.py:1335
  68.4 2.2 copy-start.1
  68.5 2.2 copy-start.2
  70.6 2.2 copy-start.5
  70.6 80.4 %all-gather.11.cloned.1.call-start = ((), (), s32[]{:S(2)}) async-start(), calls=%async_computation.8 | async-start | bytes 2048000 | tf_op jit(solution)/shard_map/all_gather | solution.py:1335
  71.5 117.5 %all-gather.13.cloned.1.call-start = ((), (), s32[]{:S(2)}) async-start(), calls=%async_computation.9 | async-start | bytes 2048000 | tf_op jit(solution)/shard_map/all_gather | solution.py:1335
  72.1 158.8 %all-gather.15.cloned.1.call-start = ((), (), s32[]{:S(2)}) async-start(), calls=%async_computation.10 | async-start | bytes 2048000 | tf_op jit(solution)/shard_map/all_gather | solution.py:1335
  72.7 225.9 %all-gather.17.cloned.1.call-start = ((), (), s32[]{:S(2)}) async-start(), calls=%async_computation.11 | async-start | bytes 4096000 | tf_op jit(solution)/shard_map/all_gather | solution.py:1335
  72.9 38.7 %collective-permute-start.1 = (bf16[1280,640]{1,0:T(8,128)(2,1)}, bf16[1280,640]{1,0:T(8,128)(2,1)S(1)}, u32[]{:S(2)}, u32[]{:S(2)}) collective-permute-start(bf16[1280,640]{1,0:T(8,128)(2,1)} %all-gather.7.cloned.1.call-done.refs_1_.refs_4_), channel_id=1, source_target_pairs={{0,16},{16,0},{1,17},{17,1},{2,18},{18,2},{3,19},{19,3},{4,20},{20... | collective-permute-start | bytes 4915208 | tf_op jit(solution)/shard_map/ppermute | solution.py:1268
  77.3 322.3 %reduce-scatter.11.cloned.1.call-start = ((), (), s32[]{:S(2)}) async-start(), calls=%async_computation.14 | async-start | bytes 4096000 | tf_op jit(solution)/shard_map/reduce_scatter | solution.py:1387
  111.7 1.2 copy-start.15
  298.2 172.6 %reduce-scatter.9.cloned.1.call-start = ((), (), s32[]{:S(2)}) async-start(), calls=%async_computation.13 | async-start | bytes 4096000 | tf_op jit(solution)/shard_map/reduce_scatter | solution.py:1387
  339.9 171.4 %reduce-scatter.7.cloned.1.call-start = ((), (), s32[]{:S(2)}) async-start(), calls=%async_computation.12 | async-start | bytes 4096000 | tf_op jit(solution)/shard_map/reduce_scatter | solution.py:1387
  397.4 132.2 %reduce-scatter.13.cloned.1.call-start = ((), (), s32[]{:S(2)}) async-start(), calls=%async_computation.15 | async-start | bytes 2048000 | tf_op jit(solution)/shard_map/reduce_scatter | solution.py:1387
  465.8 1.3 copy-start.4
  465.9 106.5 %reduce-scatter.15.cloned.1.call-start = ((), (), s32[]{:S(2)}) async-start(), calls=%async_computation.16 | async-start | bytes 2048000 | tf_op jit(solution)/shard_map/reduce_scatter | solution.py:1387
  511.3 109.3 %reduce-scatter.17.cloned.1.call-start = ((), (), s32[]{:S(2)}) async-start(), calls=%async_computation.17 | async-start | bytes 2048000 | tf_op jit(solution)/shard_map/reduce_scatter | solution.py:1387
  618.7 1.8 copy-start.6
Sparse Core Ops, SparseCore 0:
  24.9 39.6 all-gather.6
  70.7 37.9 all-gather.8
  110.8 37.0 all-gather.10
  149.9 37.0 all-gather.12
  188.9 37.0 all-gather.14
  228.0 64.5 all-gather.16
  298.4 62.5 reduce-scatter.10
  363.3 62.3 reduce-scatter.8
  428.0 62.4 reduce-scatter.6
  492.7 36.4 reduce-scatter.12
  531.5 35.3 reduce-scatter.14
  572.4 35.8 reduce-scatter.16

commit v14 on v13

--- a/solution.py
+++ b/solution.py
@@ -386,16 +386,17 @@
     for gather, load in zip(gathers, (loads[0], loads[2], loads[1])):
         load.wait()
         gather.start()
-    for gather in gathers:
+    width = x4.shape[2]
+    for gather, blocks4, full_ref in ((gathers[0], x4, x_ref), (gathers[1], None, None), (gathers[2], g4, g_ref)):
         gather.sibling()
         gather.relay()
         gather.diagonal()
-    swap = push(s4, other4, s_sems, 3 * PARTS, 1 - section, "section")
-    swap.start()
-    width = x4.shape[2]
-    for c in range(x4.shape[0]):
-        x_ref[:, c * width : (c + 1) * width] = x4[c]
-        g_ref[:, c * width : (c + 1) * width] = g4[c]
+        if blocks4 is None:
+            swap = push(s4, other4, s_sems, 3 * PARTS, 1 - section, "section")
+            swap.start()
+        else:
+            for c in range(blocks4.shape[0]):
+                full_ref[:, c * width : (c + 1) * width] = blocks4[c]
     swap.wait()
     for block in blocks:
         block.wait()
@@ -811,26 +812,42 @@
 
 
 def finish_kernel(
-    late_ref, early1_ref, early2_ref, near_ref, far_ref, a0, n0, a1, n1,
+    late_ref, early1_ref, early2_ref, near_hbm, far_hbm, a0_hbm, n0_hbm, a1_hbm, n1_hbm,
     grads_ref, sums_ref, got_late, got_early1, got_early2,
-    mine, stage4, block, land_col, land_x, land_z, land,
-    deliver_sems, col_sems, x_sems, z_sems, part_sems,
+    near_ref, far_ref, a0, n0, a1, n1, mine, stage4, block, land_col, land_x, land_z, send,
+    deliver_sems, col_sems, x_sems, z_sems, part_sems, local_sems,
 ):
     section, row = lax.axis_index("section"), lax.axis_index("row")
     away = 1 - section
     group = Group(near_ref.shape[0])
-    length, width = far_ref.shape
+    width = far_ref.shape[1]
     others = [lax.rem(row + d, land_z.shape[0]) for d in range(1, land_z.shape[0])]
+    loads = [
+        pltpu.make_async_copy(source, into, local_sems.at[n])
+        for n, (source, into) in enumerate(
+            (
+                (near_hbm, near_ref), (far_hbm, far_ref),
+                (a0_hbm, a0), (n0_hbm, n0), (a1_hbm, a1), (n1_hbm, n1),
+            )
+        )
+    ]
+    for copy in loads:
+        copy.start()
     group.greet(True, True, others)
-    gradient_up = OneWay([(far_ref, land)], [], x_sems.at[:, pl.ds(1, 1)])
-    gradient_down = OneWay([], [(mine, land)], x_sems.at[:, pl.ds(2, 1)])
     parts = OneWay(
         [(late_ref, got_late)], [(early1_ref, got_early1), (early2_ref, got_early2)], part_sems
     )
+    parts.start()
+    for copy in loads:
+        copy.wait()
     deliver = Deliver(group, stage4, mine, deliver_sems)
     deliver.start(near_ref)
-    gradient_up.start()
-    parts.start()
+    gradients = push(send, grads_ref.at[section], x_sems, 1, away, "section")
+
+    @pl.when(section == 0)
+    def _():
+        send[...] = turned(far_ref[...]).astype(LOW)
+        gradients.start()
 
     block[...] = jnp.zeros_like(block)
     for layer, (attn, narrow) in enumerate(((a0, n0), (a1, n1))):
@@ -856,7 +873,6 @@
     swap = push(block.at[me, away], land_x, x_sems, 0, away, "section")
     swap.start()
     deliver.done()
-    gradient_down.start()
 
     @pl.when(section == 0)
     def _():
@@ -864,6 +880,8 @@
 
     @pl.when(section == 1)
     def _():
+        send[...] = turned(mine[...]).astype(LOW)
+        gradients.start()
         grads_ref[section] = turned(far_ref[...]).astype(LOW)
 
     swap.wait()
@@ -880,9 +898,7 @@
     for n in range(1, land_z.shape[0]):
         result = result + land_z[n]
     sums_ref[...] = result
-    gradient_up.wait()
-    gradient_down.wait()
-    grads_ref[away] = turned(land[...]).astype(LOW)
+    gradients.wait()
     parts.wait()
 
 
@@ -902,13 +918,11 @@
 
 
 def write_kernel(*refs):
-    (late, far_late, early, far_early), (attend_ref, output_ref, expand_ref, contract_ref) = (
-        [refs[n : n + 3] for n in (0, 3, 6, 9)],
-        refs[12:16],
-    )
-    own, far, sems = refs[16:]
+    late, far_late, early, far_early = [refs[n : n + 3] for n in (0, 3, 6, 9)]
+    sums_ref, attend_ref, output_ref, expand_ref, contract_ref, *vector_refs = refs[12:-3]
+    own, far, sems = refs[-3:]
     half = early[0].shape[1]
-    width = output_ref.shape[1]
+    width = output_ref.shape[0]
     section = lax.axis_index("section")
 
     def load(firsts, seconds):
@@ -936,9 +950,16 @@
     first = own[0].astype(WIDE) + far[0].astype(WIDE)
     for j in range(3):
         attend_ref[j] = first[:, j * width : (j + 1) * width]
-    output_ref[...] = first[:, 3 * width :]
+    corner = first[:, 3 * width :]
+    high = corner.astype(LOW)
+    output_ref[...] = turned(high) + turned((corner - high.astype(WIDE)).astype(LOW))
     expand_ref[...] = own[1].astype(WIDE) + far[1].astype(WIDE)
     contract_ref[...] = own[2].astype(WIDE) + far[2].astype(WIDE)
+    for n in range(6):
+        vector_refs[n][...] = sums_ref[n : n + 1, :]
+    vector_refs[6][...] = sums_ref[8:10, :][None]
+    for n in range(vector_refs[7].shape[1] // width):
+        vector_refs[7][:, n * width : (n + 1) * width] = sums_ref[10 + n : 11 + n, :]
 
 
 VM = pl.BlockSpec(memory_space=pltpu.VMEM)
@@ -1210,23 +1231,27 @@
         *[shape(part.shape) for part in parts],
     )
     scratch = [
+        pltpu.VMEM(near.shape, LOW),
+        pltpu.VMEM(far.shape, LOW),
+        *[pltpu.VMEM(s.shape, WIDE) for s in sums],
         pltpu.VMEM((length, width), LOW),
         pltpu.VMEM((columns, rows, width), LOW),
         pltpu.VMEM((columns, 2, 16, width), WIDE),
         pltpu.VMEM((3, 2, 8, width), WIDE),
         pltpu.VMEM((16, width), WIDE),
         pltpu.VMEM((row_count, 16, width), WIDE),
-        pltpu.VMEM((length, width), LOW),
+        pltpu.VMEM((width, length), LOW),
         pltpu.SemaphoreType.DMA((2, 3)),
         pltpu.SemaphoreType.DMA((2, 3)),
-        pltpu.SemaphoreType.DMA((2, 3)),
+        pltpu.SemaphoreType.DMA((2, 2)),
         pltpu.SemaphoreType.DMA((2, row_count)),
         pltpu.SemaphoreType.DMA((2, 3)),
+        pltpu.SemaphoreType.DMA((6,)),
     ]
     return pl.pallas_call(
         finish_kernel,
         out_shape=outs,
-        in_specs=[ANY] * 3 + [VM] * 6,
+        in_specs=[ANY] * 9,
         out_specs=(VM, VM) + (ANY,) * 3,
         scratch_shapes=scratch,
         compiler_params=pltpu.CompilerParams(
@@ -1250,18 +1275,20 @@
     )(part)
 
 
-def write_call(width, late, far_late, early, far_early):
+def write_call(late, far_late, early, far_early, sums, wide):
     rows, size = late[0].shape
+    width = sums.shape[1]
     return pl.pallas_call(
         write_kernel,
         out_shape=(
-            shape((3, rows, width), WIDE), shape((rows, width), WIDE), shape((rows, size), WIDE), shape((rows, size), WIDE)
+            shape((3, rows, width), WIDE), shape((width, rows), WIDE), shape((rows, size), WIDE), shape((rows, size), WIDE),
+            *[shape((1, width), WIDE)] * 6, shape((1, 2, width), WIDE), shape((1, wide), WIDE),
         ),
-        in_specs=[ANY] * 12,
-        out_specs=(VM,) * 4,
+        in_specs=[ANY] * 12 + [VM],
+        out_specs=(VM,) * 12,
         scratch_shapes=[pltpu.VMEM((3, rows, size), LOW)] * 2 + [pltpu.SemaphoreType.DMA((6,))],
         compiler_params=pltpu.CompilerParams(vmem_limit_bytes=GRANT),
-    )(*late, *far_late, *early, *far_early)
+    )(*late, *far_late, *early, *far_early, sums)
 
 
 def swap_sections(value):
@@ -1425,28 +1452,29 @@
 
     part_w0, small_grads = tie(scatter(total_w0), small_grads)
     far_w0 = cross_call(17, False, part_w0)
-    attend_part, output_part, expand_part, contract_part = write_call(
-        width,
+    attend_part, output_part, expand_part, contract_part, *vector_grads = write_call(
         (part_w1, part_e1, part_c1),
         (far_w1, far_e1, far_c1),
         (part_w0, part_e0, part_c0),
         (far_w0, far_e0, far_c0),
+        small_grads,
+        expand_bias.shape[1],
     )
     return (
         jnp.concatenate([layer_outputs[0], layer_outputs[1]], 1).T[None],
         jnp.concatenate([input_grads[0], input_grads[1]], 1).astype(WIDE).T[None],
-        small_grads[0:1],
-        small_grads[1:2],
+        vector_grads[0],
+        vector_grads[1],
         jnp.swapaxes(attend_part, 0, 1)[None],
-        small_grads[8:10][None],
-        output_part.T[None],
-        small_grads[2:3],
-        small_grads[3:4],
-        small_grads[4:5],
+        vector_grads[6],
+        output_part[None],
+        vector_grads[2],
+        vector_grads[3],
+        vector_grads[4],
         expand_part[None],
-        small_grads[10 : 10 + expand_bias.shape[1] // width].reshape(1, -1),
+        vector_grads[7],
         contract_part.T[None],
-        small_grads[5:6],
+        vector_grads[5],
     )
 
 

time: 657 us -> 647 us (0.985)
  no operation moved by 1% of the time
where the time goes in v14:
time: 647 us; the launch traced here: 638 us
  Pallas kernels  548 us (85%)
  waiting for transfers between devices  37.9 us (6%)
  local copies, waits for them, and re-layouts  22.2 us (3%)
  between operations  14.8 us (2%)
  other arithmetic  9.76 us (2%)
    pallas_call x10, Pallas kernels, launch(): pl.pallas_call(kernel, out_shape=(*outs, *[shape(s.shape, s.dtype) for s...  431 us
    pallas_call x1, Pallas kernels, start_call(): pl.pallas_call(start_kernel, out_shape=outs, in_specs=[ANY] * 5, out_spec...  41.2 us
    pallas_call x1, Pallas kernels, finish_call(): pl.pallas_call(finish_kernel, out_shape=outs, in_specs=[ANY] * 9, out_spe...  40.2 us
    all_gather x6, waiting for transfers between devices, gather_blocks(): return lax.all_gather(block, 'row', axis=0, tiled=True)  31 us
    pallas_call x2, Pallas kernels, cross_call(): pl.pallas_call(functools.partial(cross_kernel, up), out_shape=shape(part....  29.9 us
  transfers between devices with their start and end apart: 14, of which 3 were waited for; matrix products, arithmetic and copies ran while one was open for 4% of the time, Pallas kernels for 83%

profile of v14, /device:TPU:0, one launch (start us, length us, event | category | flops | bytes accessed | tf_op | source)
XLA Modules:
  0.0 638.5 jit_solution(11503099517796291471)
XLA Ops:
  7.2 1.1 copy.34
  8.4 1.5 copy.33
  9.9 0.3 copy.35
  10.2 1.0 broadcast_select_fusion.8
  11.2 2.9 collective-permute-start
  14.2 1.5 copy.37.tokens_ref
  15.8 2.6 copy.38.cotangent_ref
  18.6 0.6 pad.8.small_ref
  19.2 0.8 broadcast_select_fusion.7.expand_ref
  20.0 3.8 collective-permute-done
  23.8 1.0 broadcast_select_fusion.1
  24.8 41.2 %shard_map.245 = (bf16[1024,1280]{1,0:T(8,128)(2,1)}, bf16[1024,1280]{1,0:T(8,128)(2,1)}, bf16[2,4,16,320]{3,2,1,0:T(8,128)(2,1)}, bf16[320,640]{1,0:T(8,128)(2,1)}, bf16[320,1280]{1,0:T(8,128)(2,1)}) custom-call(bf16[2048,320]{1,0:T(8,128)(2,1)} %copy.37.tokens_ref, bf16[2048,320]{1,0:T(8,128)(2,1)} %copy.38.cotangent_ref, bf16[16,320]{1,0:T(8,128)(2,1)} %pad.8.small_ref, ...), custom_call_target="tpu_custom_call" | custom-call | flops 30000001024 | bytes 31457280 | tf_op jit(solution)/shard_map/pallas_call | solution.py:1044
  66.1 2.1 broadcast_select_fusion.2
  68.3 0.8 fusion
  69.2 0.5 all-gather.13.cloned.1.call-update
  69.8 0.5 all-gather.15.cloned.1.call-update
  70.6 1.6 collective-permute-start.1
  72.1 0.7 squeeze.60.refs_3_
  72.8 0.7 squeeze.57.refs_3_
  73.6 0.7 squeeze.59.refs_4_
  74.2 0.7 squeeze.56.refs_4_
  75.0 1.0 broadcast_select_fusion
  76.1 0.6 fusion.2
  76.7 30.9 %all-gather.9.cloned.1.call-done.refs_5_.refs_1_.refs_3_ = bf16[1280,640]{1,0:T(8,128)(2,1)} async-done(((bf16[320,640]{1,0:T(8,128)(2,1)}), bf16[1280,640]{1,0:T(8,128)(2,1)}) %all-gather.9.cloned.1.call-update) | async-done | bytes 1638416 | tf_op jit(solution)/shard_map/all_gather | solution.py:1362
  107.6 1.8 collective-permute-done.1.refs_2_.refs_5_
  109.4 1.2 copy-done.14
  110.6 38.5 %shard_map.246 = (bf16[1024,1280]{1,0:T(8,128)(2,1)}, bf16[15,1024,64]{2,1,0:T(8,128)(2,1)}, bf16[1024,320]{1,0:T(8,128)(2,1)}, f32[8,1024]{1,0:T(8,128)}, f32[2...) custom-call(bf16[1024,1280]{1,0:T(8,128)(2,1)} %get-tuple-element.101.refs_0_, ...), custom_call_target="tpu_custom_call" | custom-call | flops 30000001024 | bytes 31457280 | tf_op jit(solution)/shard_map/pallas_call | solution.py:1016
  149.1 38.4 %shard_map.247 = (bf16[1024,1280]{1,0:T(8,128)(2,1)}, bf16[1024,1280]{1,0:T(8,128)(2,1)}, bf16[1024,1280]{1,0:T(8,128)(2,1)}, bf16[1280,640]{1,0:T(8,128)(2,1)}) custom-call(bf16[256,1280]{1,0:T(8,128)(2,1)} %get-tuple-element.105.refs_0_, bf16[1280,640]{1,0:T(8,128)(2,1)} %all-gather.9.cloned.1.call-done.refs_5_.refs_1_.refs_3_, ...), custom_call_target="tpu_custom_call" | custom-call | flops 30000001024 | bytes 31457280 | tf_op jit(solution)/shard_map/pallas_call | solution.py:1016
  187.5 41.9 %shard_map.248 = (bf16[256,1280]{1,0:T(8,128)(2,1)}, bf16[1024,1280]{1,0:T(8,128)(2,1)}, bf16[1280,640]{1,0:T(8,128)(2,1)}) custom-call(bf16[1024,1280]{1,0:T(8,128)(2,1)} %get-tuple-element.108.refs_0_.refs_6_, f32[256,1280]{1,0:T(8,128)} %get-tuple-element.109.refs_1_.refs_8_, bf16[1280,640]{1,0:T(8,128)(2,1)} %all-gather.11.cloned.1.call-done.refs_4_.refs_2_.refs_1_, ...), custom_call_target="tpu_custom_call" | custom-call | flops 30000001024 | bytes 31457280 | tf_op jit(solution)/shard_map/pallas_call | solution.py:1016
  229.5 38.7 %shard_map.249 = (bf16[1024,1280]{1,0:T(8,128)(2,1)}, bf16[15,1024,64]{2,1,0:T(8,128)(2,1)}, bf16[1024,320]{1,0:T(8,128)(2,1)}, f32[8,1024]{1,0:T(8,128)}, f32[2...) custom-call(bf16[1024,1280]{1,0:T(8,128)(2,1)} %get-tuple-element.111.refs_0_, ...), custom_call_target="tpu_custom_call" | custom-call | flops 30000001024 | bytes 31457280 | tf_op jit(solution)/shard_map/pallas_call | solution.py:1016
  268.2 28.1 %shard_map.250 = (bf16[1024,1280]{1,0:T(8,128)(2,1)}, bf16[1024,1280]{1,0:T(8,128)(2,1)}, bf16[1024,1280]{1,0:T(8,128)(2,1)}, bf16[1280,1280]{1,0:T(8,128)(2,1)}) custom-call(bf16[256,1280]{1,0:T(8,128)(2,1)} %get-tuple-element.113.refs_0_, bf16[1280,640]{1,0:T(8,128)(2,1)} %all-gather.15.cloned.1.call-done.refs_5_.refs_1_.refs_4_, ...), custom_call_target="tpu_custom_call" | custom-call | flops 30000001024 | bytes 31457280 | tf_op jit(solution)/shard_map/pallas_call | solution.py:1016
  296.5 41.8 %shard_map.251 = (f32[256,1280]{1,0:T(8,128)}, bf16[256,1280]{1,0:T(8,128)(2,1)}, f32[8,1280]{1,0:T(8,128)}, bf16[1280,1280]{1,0:T(8,128)(2,1)}, bf16[256,1280]{1,0:T(8,128)(2,1)}) custom-call(bf16[1024,1280]{1,0:T(8,128)(2,1)} %get-tuple-element.116.refs_0_, f32[256,1280]{1,0:T(8,128)} %get-tuple-element.117.refs_1_, ...), custom_call_target="tpu_custom_call" | custom-call | flops 30000001024 | bytes 31457280 | tf_op jit(solution)/shard_map/pallas_call | solution.py:1016
  338.4 2.5 constant_dynamic-slice_fusion.2.refs_11_
  340.9 55.2 %shard_map.252 = (bf16[256,1280]{1,0:T(8,128)(2,1)}, f32[8,1280]{1,0:T(8,128)}, bf16[2,320,1024]{2,1,0:T(8,128)(2,1)}, bf16[1280,1280]{1,0:T(8,128)(2,1)}) custom-call(bf16[256,1280]{1,0:T(8,128)(2,1)} %get-tuple-element.120.refs_0_, f32[256,1280]{1,0:T(8,128)} %get-tuple-element.121.refs_1_, bf16[256,1280]{1,0:T(8,128)(2,1)} %get-tuple-element.122.refs_2_, ...), custom_call_target="tpu_custom_call" | custom-call | flops 30000001024 | bytes 31457280 | tf_op jit(solution)/shard_map/pallas_call | solution.py:1016
  396.1 0.2 reduce-scatter.13.cloned.1.call-start
  396.3 2.0 constant_dynamic-slice_fusion.1.refs_3_
  398.3 66.2 %shard_map.253 = (f32[256,1280]{1,0:T(8,128)}, bf16[256,1280]{1,0:T(8,128)(2,1)}, f32[8,1280]{1,0:T(8,128)}, bf16[1280,640]{1,0:T(8,128)(2,1)}, bf16[1280,640]{1...) custom-call(bf16[256,1280]{1,0:T(8,128)(2,1)} %get-tuple-element.131.refs_0_, ...), custom_call_target="tpu_custom_call" | custom-call | flops 30000001024 | bytes 31457280 | tf_op jit(solution)/shard_map/pallas_call | solution.py:1016
  464.6 1.2 copy-done.4
  465.9 1.2 maximum_bitcast_fusion
  467.1 2.4 constant_dynamic-slice_fusion.far_hbm
  469.5 39.9 %shard_map.254 = (bf16[1024,960]{1,0:T(8,128)(2,1)}, bf16[1280,320]{1,0:T(8,128)(2,1)}, bf16[1280,640]{1,0:T(8,128)(2,1)}) custom-call(bf16[256,1280]{1,0:T(8,128)(2,1)} %get-tuple-element.136.refs_0_, bf16[1280,640]{1,0:T(8,128)(2,1)} %all-gather.7.cloned.1.call-done.refs_1_.refs_4_, bf16[1280,640]{1,0:T(8,128)(2,1)} %copy-done.14, ...), custom_call_target="tpu_custom_call" | custom-call | flops 30000001024 | bytes 31457280 | tf_op jit(solution)/shard_map/pallas_call | solution.py:1016
  509.5 18.8 %shard_map.255.refs_4_ = bf16[320,1280]{1,0:T(8,128)(2,1)} custom-call(bf16[320,1280]{1,0:T(8,128)(2,1)} %reduce-scatter.9.cloned.1.call-done.part_ref.refs_1_), custom_call_target="tpu_custom_call" | custom-call | flops 10000000000 | bytes 10485760 | tf_op jit(solution)/shard_map/pallas_call | solution.py:1265
  528.3 42.8 %shard_map.256 = (bf16[1280,640]{1,0:T(8,128)(2,1)}, bf16[256,1280]{1,0:T(8,128)(2,1)}, f32[8,1280]{1,0:T(8,128)}) custom-call(bf16[1024,960]{1,0:T(8,128)(2,1)} %get-tuple-element.152.refs_0_, bf16[1280,320]{1,0:T(8,128)(2,1)} %get-tuple-element.153.refs_1_, f32[256,1280]{1,0:T(8,128)} %get-tuple-element.154.refs_2_, ...), custom_call_target="tpu_custom_call" | custom-call | flops 30000001024 | bytes 31457280 | tf_op jit(solution)/shard_map/pallas_call | solution.py:1016
  571.2 40.2 %shard_map.257 = (bf16[2,320,1024]{2,1,0:T(8,128)(2,1)}, f32[16,320]{1,0:T(8,128)}, bf16[320,1280]{1,0:T(8,128)(2,1)}, bf16[320,640]{1,0:T(8,128)(2,1)}, bf16[320,640]{1,0:T(8,128)(2,1)}) custom-call(bf16[320,1280]{1,0:T(8,128)(2,1)} %reduce-scatter.7.cloned.1.call-done.late_ref.refs_0_, ...), custom_call_target="tpu_custom_call" | custom-call | flops 30000001024 | bytes 31457280 | tf_op jit(solution)/shard_map/pallas_call | solution.py:1251
  611.5 1.4 slice_bitcast_fusion.1
  612.8 1.8 convert_bitcast_fusion
  614.6 11.1 %shard_map.258.refs_9_ = bf16[320,640]{1,0:T(8,128)(2,1)} custom-call(bf16[320,640]{1,0:T(8,128)(2,1)} %reduce-scatter.17.cloned.1.call-done.part_ref.refs_6_), custom_call_target="tpu_custom_call" | custom-call | flops 10000000000 | bytes 10485760 | tf_op jit(solution)/shard_map/pallas_call | solution.py:1265
  625.7 5.7 shard_map.259
  (74 shorter events, 1.6 us)
Async XLA Ops:
  7.2 63.4 %all-gather.7.cloned.1.call-start = ((), (), s32[]{:S(2)}) async-start(), calls=%async_computation.6 | async-start | bytes 2048000 | tf_op jit(solution)/shard_map/all_gather | solution.py:1362
  9.8 4.3 copy-start.6
  9.9 4.4 copy-start.3
  11.2 12.6 %collective-permute-start = (bf16[320,640]{1,0:T(8,128)(2,1)}, bf16[320,640]{1,0:T(8,128)(2,1)S(1)}, u32[]{:S(2)}, u32[]{:S(2)}) collective-permute-start(bf16[320,640]{1,0:T(8,128)(2,1)} %get-tuple-element.186), channel_id=1, source_target_pairs={{0,16},{16,0},{1,17},{17,1},{2,18},{18,2},{3,19},{19,3},{4,20},{20... | collective-permute-start | bytes 1228808 | tf_op jit(solution)/shard_map/ppermute | solution.py:1295
  15.8 2.7 copy-start.7
  15.8 2.7 copy-start.8
  15.8 2.7 copy-start.9
  15.8 2.7 copy-start.10
  15.8 2.7 copy-start.11
  15.8 2.7 copy-start.12
  15.8 2.7 copy-start.13
  15.8 3.3 copy-start
  24.8 82.8 %all-gather.9.cloned.1.call-start = ((), (), s32[]{:S(2)}) async-start(), calls=%async_computation.7 | async-start | bytes 2048000 | tf_op jit(solution)/shard_map/all_gather | solution.py:1362
  66.1 2.2 copy-start.1
  66.1 2.2 copy-start.2
  68.2 2.2 copy-start.5
  68.2 80.9 %all-gather.11.cloned.1.call-start = ((), (), s32[]{:S(2)}) async-start(), calls=%async_computation.8 | async-start | bytes 2048000 | tf_op jit(solution)/shard_map/all_gather | solution.py:1362
  69.2 118.4 %all-gather.13.cloned.1.call-start = ((), (), s32[]{:S(2)}) async-start(), calls=%async_computation.9 | async-start | bytes 2048000 | tf_op jit(solution)/shard_map/all_gather | solution.py:1362
  69.7 159.7 %all-gather.15.cloned.1.call-start = ((), (), s32[]{:S(2)}) async-start(), calls=%async_computation.10 | async-start | bytes 2048000 | tf_op jit(solution)/shard_map/all_gather | solution.py:1362
  70.3 226.2 %all-gather.17.cloned.1.call-start = ((), (), s32[]{:S(2)}) async-start(), calls=%async_computation.11 | async-start | bytes 4096000 | tf_op jit(solution)/shard_map/all_gather | solution.py:1362
  70.6 38.8 %collective-permute-start.1 = (bf16[1280,640]{1,0:T(8,128)(2,1)}, bf16[1280,640]{1,0:T(8,128)(2,1)S(1)}, u32[]{:S(2)}, u32[]{:S(2)}) collective-permute-start(bf16[1280,640]{1,0:T(8,128)(2,1)} %all-gather.7.cloned.1.call-done.refs_1_.refs_4_), channel_id=1, source_target_pairs={{0,16},{16,0},{1,17},{17,1},{2,18},{18,2},{3,19},{19,3},{4,20},{20... | collective-permute-start | bytes 4915208 | tf_op jit(solution)/shard_map/ppermute | solution.py:1295
  76.0 322.3 %reduce-scatter.11.cloned.1.call-start = ((), (), s32[]{:S(2)}) async-start(), calls=%async_computation.14 | async-start | bytes 4096000 | tf_op jit(solution)/shard_map/reduce_scatter | solution.py:1414
  109.4 1.2 copy-start.14
  296.3 173.2 %reduce-scatter.9.cloned.1.call-start = ((), (), s32[]{:S(2)}) async-start(), calls=%async_computation.13 | async-start | bytes 4096000 | tf_op jit(solution)/shard_map/reduce_scatter | solution.py:1414
  338.3 171.0 %reduce-scatter.7.cloned.1.call-start = ((), (), s32[]{:S(2)}) async-start(), calls=%async_computation.12 | async-start | bytes 4096000 | tf_op jit(solution)/shard_map/reduce_scatter | solution.py:1414
  396.1 132.2 %reduce-scatter.13.cloned.1.call-start = ((), (), s32[]{:S(2)}) async-start(), calls=%async_computation.15 | async-start | bytes 2048000 | tf_op jit(solution)/shard_map/reduce_scatter | solution.py:1414
  464.5 1.3 copy-start.4
  464.5 106.7 %reduce-scatter.15.cloned.1.call-start = ((), (), s32[]{:S(2)}) async-start(), calls=%async_computation.16 | async-start | bytes 2048000 | tf_op jit(solution)/shard_map/reduce_scatter | solution.py:1414
  509.4 105.2 %reduce-scatter.17.cloned.1.call-start = ((), (), s32[]{:S(2)}) async-start(), calls=%async_computation.17 | async-start | bytes 2048000 | tf_op jit(solution)/shard_map/reduce_scatter | solution.py:1414
Sparse Core Ops, SparseCore 0:
  24.9 39.6 all-gather.6
  68.4 39.1 all-gather.8
  109.8 37.0 all-gather.10
  148.8 37.0 all-gather.12
  187.9 37.0 all-gather.14
  227.0 64.5 all-gather.16
  296.4 62.5 reduce-scatter.10
  361.4 62.3 reduce-scatter.8
  426.1 62.3 reduce-scatter.6
  490.7 36.4 reduce-scatter.12
  529.6 35.3 reduce-scatter.14
  571.3 35.7 reduce-scatter.16

commit v15 on v14

--- a/solution.py
+++ b/solution.py
@@ -37,6 +37,14 @@
         lax.broadcasted_iota(jnp.int32, (width, width), 0) == lax.broadcasted_iota(jnp.int32, (width, width), 1)
     ).astype(LOW)
     return nt(unit, values)
+
+
+def turned_back(values):
+    height = values.shape[0]
+    unit = (
+        lax.broadcasted_iota(jnp.int32, (height, height), 0) == lax.broadcasted_iota(jnp.int32, (height, height), 1)
+    ).astype(LOW)
+    return tn(values, unit)
 
 
 def normalise(values):
@@ -106,6 +114,7 @@
 class Gather:
     def __init__(self, group, full, sems, blocks=False):
         self.group, self.full, self.sems, self.blocks = group, full, sems, blocks
+        self.over, self.near, self.relayed = [], [], []
 
     def piece(self, owner, j):
         if not self.blocks:
@@ -113,17 +122,17 @@
         part = self.full.shape[1] // PARTS
         return self.full.at[owner, pl.ds(j * part, part)]
 
+    def start_part(self, j):
+        g = self.group
+        piece = self.piece(g.me, j)
+        self.over.append(push(piece, piece, self.sems, j, g.peer))
+        self.near.append(push(piece, piece, self.sems, PARTS + j, g.sib))
+        self.over[-1].start()
+        self.near[-1].start()
+
     def start(self):
-        g = self.group
-        self.over, self.near, self.relayed = [], [], []
         for j in range(PARTS):
-            piece = self.piece(g.me, j)
-            self.over.append(push(piece, piece, self.sems, j, g.peer))
-            self.over[-1].start()
-        for j in range(PARTS):
-            piece = self.piece(g.me, j)
-            self.near.append(push(piece, piece, self.sems, PARTS + j, g.sib))
-            self.near[-1].start()
+            self.start_part(j)
 
     def sibling(self):
         for copy in self.near:
@@ -147,7 +156,8 @@
 
     def each(self, body, first=None):
         g = self.group
-        self.start()
+        if not self.over:
+            self.start()
         if first is not None:
             first()
         body(g.me)
@@ -363,8 +373,8 @@
 
 
 def start_kernel(
-    tokens_ref, cotangent_ref, small_ref, expand_ref, contract_ref,
-    x_ref, g_ref, vectors_ref, got_expand_ref, got_contract_ref,
+    tokens_ref, cotangent_ref, small_ref, contract_ref,
+    x_ref, g_ref, vectors_ref, got_contract_ref,
     x4, g4, s4, other4, x_sems, g_sems, s_sems, local_sems,
 ):
     section = lax.axis_index("section")
@@ -372,34 +382,30 @@
     length = x_ref.shape[0]
     loads = []
     rows = pl.ds(pl.multiple_of(section * length, length), length)
-    for n, (source, into) in enumerate(((tokens_ref.at[rows], x4), (cotangent_ref.at[rows], g4), (small_ref, s4))):
+    sources = ((tokens_ref.at[:, rows], x4), (cotangent_ref.at[:, rows], g4), (small_ref, s4))
+    for n, (source, into) in enumerate(sources):
         loads.append(pltpu.make_async_copy(source, into.at[group.me], local_sems.at[n]))
         loads[-1].start()
     group.greet(True, False)
-    blocks = [
-        push(source, into, s_sems, 3 * PARTS + 1 + n, 1 - section, "section")
-        for n, (source, into) in enumerate(((expand_ref, got_expand_ref), (contract_ref, got_contract_ref)))
-    ]
-    for block in blocks:
-        block.start()
-    gathers = [Gather(group, x4, x_sems, True), Gather(group, s4, s_sems, True), Gather(group, g4, g_sems, True)]
-    for gather, load in zip(gathers, (loads[0], loads[2], loads[1])):
+    blocks = push(contract_ref, got_contract_ref, s_sems, 3 * PARTS + 1, 1 - section, "section")
+    gathers = [Gather(group, s4, s_sems, True), Gather(group, x4, x_sems, True), Gather(group, g4, g_sems, True)]
+    for gather, load in zip(gathers, (loads[2], loads[0], loads[1])):
         load.wait()
         gather.start()
-    width = x4.shape[2]
-    for gather, blocks4, full_ref in ((gathers[0], x4, x_ref), (gathers[1], None, None), (gathers[2], g4, g_ref)):
+    width = x4.shape[1]
+    for gather, blocks4, full_ref in ((gathers[0], None, None), (gathers[1], x4, x_ref), (gathers[2], g4, g_ref)):
         gather.sibling()
         gather.relay()
         gather.diagonal()
         if blocks4 is None:
             swap = push(s4, other4, s_sems, 3 * PARTS, 1 - section, "section")
             swap.start()
+            blocks.start()
         else:
             for c in range(blocks4.shape[0]):
-                full_ref[:, c * width : (c + 1) * width] = blocks4[c]
+                full_ref[:, c * width : (c + 1) * width] = turned_back(blocks4[c]).astype(LOW)
     swap.wait()
-    for block in blocks:
-        block.wait()
+    blocks.wait()
     vectors_ref[section] = s4[...]
     vectors_ref[1 - section] = other4[...]
     for gather in gathers:
@@ -511,12 +517,14 @@
     scatter = Scatter(group, stage, land, total, scatter_sems)
     scatter.start(lambda owner: nt(active_ref[group.chunk(owner), :], contract[...]))
     group.need(1)
+    gather = Gather(group, full_ref, gather_sems)
     for j in range(PARTS):
         rows = slice(j * group.part, (j + 1) * group.part)
         result = (hidden_ref[rows, :] + scatter.take(j) + vec_ref[5:6, :]).astype(LOW)
         result_ref[rows, :] = result
         full_ref[group.slab(group.me, j), :] = result
-    Gather(group, full_ref, gather_sems).each(lambda owner: None)
+        gather.start_part(j)
+    gather.each(lambda owner: None)
     scatter.done()
 
 
@@ -919,8 +927,16 @@
 
 def write_kernel(*refs):
     late, far_late, early, far_early = [refs[n : n + 3] for n in (0, 3, 6, 9)]
-    sums_ref, attend_ref, output_ref, expand_ref, contract_ref, *vector_refs = refs[12:-3]
-    own, far, sems = refs[-3:]
+    sums_ref, results_ref, grads_ref, attend_ref, output_ref, expand_ref, contract_ref, *vector_refs = refs[12:-4]
+    *vector_refs, outputs_ref, inputs_ref = vector_refs
+    own, far, low, sems = refs[-4:]
+    length = low.shape[2]
+    moves = [pltpu.make_async_copy(grads_ref, low, sems.at[6])] + [
+        pltpu.make_async_copy(results_ref.at[n], outputs_ref.at[:, pl.ds(n * length, length)], sems.at[7 + n])
+        for n in range(2)
+    ]
+    for move in moves:
+        move.start()
     half = early[0].shape[1]
     width = output_ref.shape[0]
     section = lax.axis_index("section")
@@ -947,6 +963,9 @@
     def _():
         load([(late[n], own.at[n]) for n in range(3)], [(far_late[n], far.at[n]) for n in range(3)])
 
+    moves[0].wait()
+    for n in range(2):
+        inputs_ref[:, n * length : (n + 1) * length] = low[n].astype(WIDE)
     first = own[0].astype(WIDE) + far[0].astype(WIDE)
     for j in range(3):
         attend_ref[j] = first[:, j * width : (j + 1) * width]
@@ -960,6 +979,8 @@
     vector_refs[6][...] = sums_ref[8:10, :][None]
     for n in range(vector_refs[7].shape[1] // width):
         vector_refs[7][:, n * width : (n + 1) * width] = sums_ref[10 + n : 11 + n, :]
+    for move in moves[1:]:
+        move.wait()
 
 
 VM = pl.BlockSpec(memory_space=pltpu.VMEM)
@@ -1034,27 +1055,27 @@
     return results[:n_out], results[n_out:]
 
 
-def start_call(number, tokens, cotangent, small, expand, contract, columns):
-    width = tokens.shape[1]
+def start_call(number, tokens, cotangent, small, contract, columns):
+    width = tokens.shape[0]
     size = width * columns
     kinds = small.shape[0]
-    outs = (shape((LENGTH, size)), shape((LENGTH, size)), shape((2, columns, kinds, width)), shape(expand.shape), shape(contract.shape))
-    blocks = pltpu.VMEM((columns, LENGTH, width), LOW)
+    outs = (shape((LENGTH, size)), shape((LENGTH, size)), shape((2, columns, kinds, width)), shape(contract.shape))
+    blocks = pltpu.VMEM((columns, width, LENGTH), LOW)
     vectors = pltpu.VMEM((columns, kinds, width), LOW)
     return pl.pallas_call(
         start_kernel,
         out_shape=outs,
-        in_specs=[ANY] * 5,
-        out_specs=(VM, VM, VM, ANY, ANY),
+        in_specs=[ANY] * 4,
+        out_specs=(VM, VM, VM, ANY),
         scratch_shapes=[
             blocks, blocks, vectors, vectors, PAIRS, PAIRS,
-            pltpu.SemaphoreType.DMA((2, 3 * PARTS + 3)), LOCAL,
+            pltpu.SemaphoreType.DMA((2, 3 * PARTS + 2)), LOCAL,
         ],
         compiler_params=pltpu.CompilerParams(
             collective_id=number, has_side_effects=True, vmem_limit_bytes=GRANT
         ),
         cost_estimate=pl.CostEstimate(flops=int(3e10), bytes_accessed=30 * MEBI, transcendentals=0),
-    )(tokens, cotangent, small, expand, contract)
+    )(tokens, cotangent, small, contract)
 
 
 def attend_call(number, x, pair, vec, bias, rows, width, swaps):
@@ -1275,20 +1296,22 @@
     )(part)
 
 
-def write_call(late, far_late, early, far_early, sums, wide):
+def write_call(late, far_late, early, far_early, sums, wide, results, grads):
     rows, size = late[0].shape
-    width = sums.shape[1]
+    _, width, length = grads.shape
     return pl.pallas_call(
         write_kernel,
         out_shape=(
             shape((3, rows, width), WIDE), shape((width, rows), WIDE), shape((rows, size), WIDE), shape((rows, size), WIDE),
             *[shape((1, width), WIDE)] * 6, shape((1, 2, width), WIDE), shape((1, wide), WIDE),
+            shape((width, 2 * length)), shape((width, 2 * length), WIDE),
         ),
-        in_specs=[ANY] * 12 + [VM],
-        out_specs=(VM,) * 12,
-        scratch_shapes=[pltpu.VMEM((3, rows, size), LOW)] * 2 + [pltpu.SemaphoreType.DMA((6,))],
+        in_specs=[ANY] * 12 + [VM, ANY, ANY],
+        out_specs=(VM,) * 12 + (ANY, VM),
+        scratch_shapes=[pltpu.VMEM((3, rows, size), LOW)] * 2
+        + [pltpu.VMEM(grads.shape, LOW), pltpu.SemaphoreType.DMA((9,))],
         compiler_params=pltpu.CompilerParams(vmem_limit_bytes=GRANT),
-    )(*late, *far_late, *early, *far_early, sums)
+    )(*late, *far_late, *early, *far_early, sums, results, grads)
 
 
 def swap_sections(value):
@@ -1351,11 +1374,12 @@
         0,
     )
     filled = small.shape[0]
-    small = jnp.pad(small, ((0, -filled % 16), (0, 0)))
+    small = jnp.pad(small, ((0, -filled % (16 * PARTS)), (0, 0)))
     got_attend = swap_sections(sent_blocks[0])
-    got_attend, sent_expand = lax.optimization_barrier((got_attend, sent_blocks[1]))
-    x0_full, gy_full, vectors, got_expand, got_contract = start_call(
-        1, tokens, cotangent, small, sent_expand, units[2], columns
+    got_expand = swap_sections(sent_blocks[1])
+    got_attend, got_expand, sent_contract = lax.optimization_barrier((got_attend, got_expand, units[2]))
+    x0_full, gy_full, vectors, got_contract = start_call(
+        1, tokens.T, cotangent.T, small, sent_contract, columns
     )
 
     def gather_blocks(block):
@@ -1452,17 +1476,19 @@
 
     part_w0, small_grads = tie(scatter(total_w0), small_grads)
     far_w0 = cross_call(17, False, part_w0)
-    attend_part, output_part, expand_part, contract_part, *vector_grads = write_call(
+    attend_part, output_part, expand_part, contract_part, *vector_grads, layer_outputs, input_grads = write_call(
         (part_w1, part_e1, part_c1),
         (far_w1, far_e1, far_c1),
         (part_w0, part_e0, part_c0),
         (far_w0, far_e0, far_c0),
         small_grads,
         expand_bias.shape[1],
+        layer_outputs,
+        input_grads,
     )
     return (
-        jnp.concatenate([layer_outputs[0], layer_outputs[1]], 1).T[None],
-        jnp.concatenate([input_grads[0], input_grads[1]], 1).astype(WIDE).T[None],
+        layer_outputs.T[None],
+        input_grads.T[None],
         vector_grads[0],
         vector_grads[1],
         jnp.swapaxes(attend_part, 0, 1)[None],

time: 647 us -> 688 us (1.063)
  Pallas kernels: 548 us -> 580 us
  waiting for transfers between devices: 37.9 us -> 54.1 us
  local copies, waits for them, and re-layouts: 22.2 us -> 14.3 us
    pallas_call x1, Pallas kernels: 5.69 us -> 44.9 us  [write_call(): pl.pallas_call(write_kernel, out_shape=(shape((3, rows, width), WIDE), sh...]
    ppermute x2 -> x3, waiting for transfers between devices: 5.59 us -> 17.3 us  [swap_sections(): return lax.ppermute(value, 'section', [(0, 1), (1, 0)])]
  transfers between devices with their start and end apart: 14 -> 15, of which waited for: 3 -> 5; matrix products, arithmetic and copies ran while one was open for 4% -> 3% of each run, Pallas kernels for 83% -> 78%
where the time goes in v15:
time: 688 us; the launch traced here: 675 us
  Pallas kernels  580 us (84%)
  waiting for transfers between devices  54.1 us (8%)
  between operations  14.8 us (2%)
  local copies, waits for them, and re-layouts  14.3 us (2%)
    pallas_call x10, Pallas kernels, launch(): pl.pallas_call(kernel, out_shape=(*outs, *[shape(s.shape, s.dtype) for s...  430 us
    pallas_call x1, Pallas kernels, write_call(): pl.pallas_call(write_kernel, out_shape=(shape((3, rows, width), WIDE), sh...  44.9 us
    pallas_call x1, Pallas kernels, finish_call(): pl.pallas_call(finish_kernel, out_shape=outs, in_specs=[ANY] * 9, out_spe...  39.7 us
    pallas_call x1, Pallas kernels, start_call(): pl.pallas_call(start_kernel, out_shape=outs, in_specs=[ANY] * 4, out_spec...  36.6 us
    all_gather x6, waiting for transfers between devices, gather_blocks(): return lax.all_gather(block, 'row', axis=0, tiled=True)  31 us
    pallas_call x2, Pallas kernels, cross_call(): pl.pallas_call(functools.partial(cross_kernel, up), out_shape=shape(part....  29 us
    ppermute x3, waiting for transfers between devices, swap_sections(): return lax.ppermute(value, 'section', [(0, 1), (1, 0)])  17.3 us
  transfers between devices with their start and end apart: 15, of which 5 were waited for; matrix products, arithmetic and copies ran while one was open for 3% of the time, Pallas kernels for 78%

profile of v15, /device:TPU:0, one launch (start us, length us, event | category | flops | bytes accessed | tf_op | source)
XLA Modules:
  0.0 675.5 jit_solution(1500560859577607808)
XLA Ops:
  7.2 1.2 broadcast_select_fusion.7
  8.5 3.0 collective-permute-start.1
  11.5 1.1 copy.32
  12.6 0.4 copy.31
  13.0 0.3 copy.33
  13.3 0.3 broadcast_select_fusion.8
  13.7 0.1 collective-permute-start
  13.7 8.0 %collective-permute-done.1 = bf16[320,640]{1,0:T(8,128)(2,1)S(1)} collective-permute-done((bf16[320,640]{1,0:T(8,128)(2,1)S(1)}, bf16[320,640]{1,0:T(8,128)(2,1)S(1)}, u32[]{:S(2)}, u32[]{:S(2)}) %collective-permute-start.1) | collective-permute-done | bytes 409632 | tf_op jit(solution)/shard_map/ppermute | solution.py:1318
  21.8 7.9 %collective-permute-done = bf16[320,640]{1,0:T(8,128)(2,1)S(1)} collective-permute-done((bf16[320,640]{1,0:T(8,128)(2,1)S(1)}, bf16[320,640]{1,0:T(8,128)(2,1)S(1)}, u32[]{:S(2)}, u32[]{:S(2)}) %collective-permute-start) | collective-permute-done | bytes 409632 | tf_op jit(solution)/shard_map/ppermute | solution.py:1318
  29.7 1.0 broadcast_select_fusion.1
  30.9 0.1 reshape_squeeze.6
  31.1 0.6 pad.8.small_ref
  31.7 1.0 broadcast_select_fusion.2
  32.7 36.6 %shard_map.245 = (bf16[1024,1280]{1,0:T(8,128)(2,1)}, bf16[1024,1280]{1,0:T(8,128)(2,1)}, bf16[2,4,32,320]{3,2,1,0:T(8,128)(2,1)}, bf16[320,1280]{1,0:T(8,128)(2,1)}) custom-call(bf16[320,2048]{1,0:T(8,128)(2,1)} %bitcast.46, bf16[320,2048]{1,0:T(8,128)(2,1)} %bitcast.47, bf16[32,320]{1,0:T(8,128)(2,1)} %pad.8.small_ref, bf16[320,1280]{1,0:T(8,128)(2,1)} %bitcast.37), custom_call_target="tpu_custom_call" | custom-call | flops 30000001024 | bytes 31457280 | tf_op jit(solution)/shard_map/pallas_call | solution.py:1065
  69.4 1.9 fusion
  71.3 0.5 all-gather.13.cloned.1.call-update
  71.9 0.5 all-gather.15.cloned.1.call-update
  72.7 1.6 collective-permute-start.2
  74.3 0.7 squeeze.48.refs_3_
  75.0 0.7 squeeze.45.refs_3_
  75.7 0.7 squeeze.47.refs_4_
  76.4 0.7 squeeze.44.refs_4_
  77.1 0.1 reshape.42
  77.2 1.0 broadcast_select_fusion
  78.2 0.6 fusion.2
  78.9 30.9 %all-gather.9.cloned.1.call-done.refs_5_.refs_1_.refs_3_ = bf16[1280,640]{1,0:T(8,128)(2,1)} async-done(((bf16[320,640]{1,0:T(8,128)(2,1)}), bf16[1280,640]{1,0:T(8,128)(2,1)}) %all-gather.9.cloned.1.call-update) | async-done | bytes 1638416 | tf_op jit(solution)/shard_map/all_gather | solution.py:1386
  109.8 1.3 collective-permute-done.2.refs_2_.refs_5_
  111.1 1.2 copy-done.13
  112.2 38.7 %shard_map.246 = (bf16[1024,1280]{1,0:T(8,128)(2,1)}, bf16[15,1024,64]{2,1,0:T(8,128)(2,1)}, bf16[1024,320]{1,0:T(8,128)(2,1)}, f32[8,1024]{1,0:T(8,128)}, f32[2...) custom-call(bf16[1024,1280]{1,0:T(8,128)(2,1)} %get-tuple-element.103.refs_0_, ...), custom_call_target="tpu_custom_call" | custom-call | flops 30000001024 | bytes 31457280 | tf_op jit(solution)/shard_map/pallas_call | solution.py:1037
  151.0 38.5 %shard_map.247 = (bf16[1024,1280]{1,0:T(8,128)(2,1)}, bf16[1024,1280]{1,0:T(8,128)(2,1)}, bf16[1024,1280]{1,0:T(8,128)(2,1)}, bf16[1280,640]{1,0:T(8,128)(2,1)}) custom-call(bf16[256,1280]{1,0:T(8,128)(2,1)} %get-tuple-element.107.refs_0_, bf16[1280,640]{1,0:T(8,128)(2,1)} %all-gather.9.cloned.1.call-done.refs_5_.refs_1_.refs_3_, ...), custom_call_target="tpu_custom_call" | custom-call | flops 30000001024 | bytes 31457280 | tf_op jit(solution)/shard_map/pallas_call | solution.py:1037
  189.6 39.9 %shard_map.248 = (bf16[256,1280]{1,0:T(8,128)(2,1)}, bf16[1024,1280]{1,0:T(8,128)(2,1)}, bf16[1280,640]{1,0:T(8,128)(2,1)}) custom-call(bf16[1024,1280]{1,0:T(8,128)(2,1)} %get-tuple-element.110.refs_0_.refs_6_, f32[256,1280]{1,0:T(8,128)} %get-tuple-element.111.refs_1_.refs_8_, bf16[1280,640]{1,0:T(8,128)(2,1)} %all-gather.11.cloned.1.call-done.refs_4_.refs_2_.refs_1_, ...), custom_call_target="tpu_custom_call" | custom-call | flops 30000001024 | bytes 31457280 | tf_op jit(solution)/shard_map/pallas_call | solution.py:1037
  229.5 38.7 %shard_map.249 = (bf16[1024,1280]{1,0:T(8,128)(2,1)}, bf16[15,1024,64]{2,1,0:T(8,128)(2,1)}, bf16[1024,320]{1,0:T(8,128)(2,1)}, f32[8,1024]{1,0:T(8,128)}, f32[2...) custom-call(bf16[1024,1280]{1,0:T(8,128)(2,1)} %get-tuple-element.113.refs_0_, ...), custom_call_target="tpu_custom_call" | custom-call | flops 30000001024 | bytes 31457280 | tf_op jit(solution)/shard_map/pallas_call | solution.py:1037
  268.2 28.5 %shard_map.250 = (bf16[1024,1280]{1,0:T(8,128)(2,1)}, bf16[1024,1280]{1,0:T(8,128)(2,1)}, bf16[1024,1280]{1,0:T(8,128)(2,1)}, bf16[1280,1280]{1,0:T(8,128)(2,1)}) custom-call(bf16[256,1280]{1,0:T(8,128)(2,1)} %get-tuple-element.115.refs_0_, bf16[1280,640]{1,0:T(8,128)(2,1)} %all-gather.15.cloned.1.call-done.refs_5_.refs_1_.refs_4_, ...), custom_call_target="tpu_custom_call" | custom-call | flops 30000001024 | bytes 31457280 | tf_op jit(solution)/shard_map/pallas_call | solution.py:1037
  296.7 0.3 reduce-scatter.9.cloned.1.call-start
  297.0 41.3 %shard_map.251 = (f32[256,1280]{1,0:T(8,128)}, bf16[256,1280]{1,0:T(8,128)(2,1)}, f32[8,1280]{1,0:T(8,128)}, bf16[1280,1280]{1,0:T(8,128)(2,1)}, bf16[256,1280]{1,0:T(8,128)(2,1)}) custom-call(bf16[1024,1280]{1,0:T(8,128)(2,1)} %get-tuple-element.118.refs_0_, f32[256,1280]{1,0:T(8,128)} %get-tuple-element.119.refs_1_, ...), custom_call_target="tpu_custom_call" | custom-call | flops 30000001024 | bytes 31457280 | tf_op jit(solution)/shard_map/pallas_call | solution.py:1037
  338.5 2.5 constant_dynamic-slice_fusion.2.refs_11_
  340.9 54.9 %shard_map.252 = (bf16[256,1280]{1,0:T(8,128)(2,1)}, f32[8,1280]{1,0:T(8,128)}, bf16[2,320,1024]{2,1,0:T(8,128)(2,1)}, bf16[1280,1280]{1,0:T(8,128)(2,1)}) custom-call(bf16[256,1280]{1,0:T(8,128)(2,1)} %get-tuple-element.122.refs_0_, f32[256,1280]{1,0:T(8,128)} %get-tuple-element.123.refs_1_, bf16[256,1280]{1,0:T(8,128)(2,1)} %get-tuple-element.124.refs_2_, ...), custom_call_target="tpu_custom_call" | custom-call | flops 30000001024 | bytes 31457280 | tf_op jit(solution)/shard_map/pallas_call | solution.py:1037
  395.9 0.3 reduce-scatter.13.cloned.1.call-start
  396.2 66.2 %shard_map.253 = (f32[256,1280]{1,0:T(8,128)}, bf16[256,1280]{1,0:T(8,128)(2,1)}, f32[8,1280]{1,0:T(8,128)}, bf16[1280,640]{1,0:T(8,128)(2,1)}, bf16[1280,640]{1...) custom-call(bf16[256,1280]{1,0:T(8,128)(2,1)} %get-tuple-element.132.refs_0_, ...), custom_call_target="tpu_custom_call" | custom-call | flops 30000001024 | bytes 31457280 | tf_op jit(solution)/shard_map/pallas_call | solution.py:1037
  462.5 2.0 constant_dynamic-slice_fusion.1.refs_3_
  464.5 40.3 %shard_map.254 = (bf16[1024,960]{1,0:T(8,128)(2,1)}, bf16[1280,320]{1,0:T(8,128)(2,1)}, bf16[1280,640]{1,0:T(8,128)(2,1)}) custom-call(bf16[256,1280]{1,0:T(8,128)(2,1)} %get-tuple-element.137.refs_0_, bf16[1280,640]{1,0:T(8,128)(2,1)} %all-gather.7.cloned.1.call-done.refs_1_.refs_4_, bf16[1280,640]{1,0:T(8,128)(2,1)} %copy-done.13, ...), custom_call_target="tpu_custom_call" | custom-call | flops 30000001024 | bytes 31457280 | tf_op jit(solution)/shard_map/pallas_call | solution.py:1037
  504.9 18.2 %shard_map.255.refs_4_ = bf16[320,1280]{1,0:T(8,128)(2,1)} custom-call(bf16[320,1280]{1,0:T(8,128)(2,1)} %reduce-scatter.9.cloned.1.call-done.part_ref.refs_1_), custom_call_target="tpu_custom_call" | custom-call | flops 10000000000 | bytes 10485760 | tf_op jit(solution)/shard_map/pallas_call | solution.py:1286
  523.1 4.5 reduce-scatter.13.cloned.1.call-done.early1_ref.refs_8_
  527.6 42.9 %shard_map.256 = (bf16[1280,640]{1,0:T(8,128)(2,1)}, bf16[256,1280]{1,0:T(8,128)(2,1)}, f32[8,1280]{1,0:T(8,128)}) custom-call(bf16[1024,960]{1,0:T(8,128)(2,1)} %get-tuple-element.153.refs_0_, bf16[1280,320]{1,0:T(8,128)(2,1)} %get-tuple-element.154.refs_1_, f32[256,1280]{1,0:T(8,128)} %get-tuple-element.155.refs_2_, ...), custom_call_target="tpu_custom_call" | custom-call | flops 30000001024 | bytes 31457280 | tf_op jit(solution)/shard_map/pallas_call | solution.py:1037
  570.5 2.4 constant_dynamic-slice_fusion.far_hbm
  573.0 39.7 %shard_map.257 = (bf16[2,320,1024]{2,1,0:T(8,128)(2,1)}, f32[16,320]{1,0:T(8,128)}, bf16[320,1280]{1,0:T(8,128)(2,1)}, bf16[320,640]{1,0:T(8,128)(2,1)}, bf16[320,640]{1,0:T(8,128)(2,1)}) custom-call(bf16[320,1280]{1,0:T(8,128)(2,1)} %reduce-scatter.7.cloned.1.call-done.late_ref.refs_0_, ...), custom_call_target="tpu_custom_call" | custom-call | flops 30000001024 | bytes 31457280 | tf_op jit(solution)/shard_map/pallas_call | solution.py:1272
  612.7 10.8 %shard_map.258.refs_9_ = bf16[320,640]{1,0:T(8,128)(2,1)} custom-call(bf16[320,640]{1,0:T(8,128)(2,1)} %reduce-scatter.17.cloned.1.call-done.part_ref.refs_6_), custom_call_target="tpu_custom_call" | custom-call | flops 10000000000 | bytes 10485760 | tf_op jit(solution)/shard_map/pallas_call | solution.py:1286
  623.5 44.9 %shard_map.259 = (f32[3,320,320]{2,1,0:T(8,128)}, f32[320,320]{1,0:T(8,128)}, f32[320,1280]{1,0:T(8,128)}, f32[320,1280]{1,0:T(8,128)}, f32[1,320]{1,0:T(1,128)}...) custom-call(bf16[320,1280]{1,0:T(8,128)(2,1)} %reduce-scatter.7.clon, ...), custom_call_target="tpu_custom_call" | custom-call | tf_op jit(solution)/shard_map/pallas_call | solution.py:1302
  (68 shorter events, 1.1 us)
Async XLA Ops:
  7.2 5.4 copy-start.3
  7.2 65.5 %all-gather.7.cloned.1.call-start = ((), (), s32[]{:S(2)}) async-start(), calls=%async_computation.6 | async-start | bytes 2048000 | tf_op jit(solution)/shard_map/all_gather | solution.py:1386
  8.5 13.3 %collective-permute-start.1 = (bf16[320,640]{1,0:T(8,128)(2,1)S(1)}, bf16[320,640]{1,0:T(8,128)(2,1)S(1)}, u32[]{:S(2)}, u32[]{:S(2)}) collective-permute-start(bf16[320,640]{1,0:T(8,128)(2,1)S(1)} %broadcast_select_fusion.7), channel_id=1, source_target_pairs={{0,16},{16,0},{1,17},{17,1},{2,18},{18,2},{3,19},{19,3},{4,20},{20... | collective-permute-start | bytes 1228808 | tf_op jit(solution)/shard_map/ppermute | solution.py:1318
  13.5 17.3 %copy-start.5 = (bf16[1,1280]{1,0:T(2,128)(2,1)S(1)}, bf16[1,1280]{1,0:T(2,128)(2,1)}, u32[]{:S(2)}) copy-start(bf16[1,1280]{1,0:T(2,128)(2,1)} %param.25) | copy-start | bytes 7684
  13.6 17.4 %copy-start.6 = (bf16[1,320]{1,0:T(2,128)(2,1)S(1)}, bf16[1,320]{1,0:T(2,128)(2,1)}, u32[]{:S(2)}) copy-start(bf16[1,320]{1,0:T(2,128)(2,1)} %param.16) | copy-start | bytes 1924
  13.6 17.4 %copy-start.7 = (bf16[1,320]{1,0:T(2,128)(2,1)S(1)}, bf16[1,320]{1,0:T(2,128)(2,1)}, u32[]{:S(2)}) copy-start(bf16[1,320]{1,0:T(2,128)(2,1)} %param.17) | copy-start | bytes 1924
  13.6 17.4 %copy-start.8 = (bf16[1,320]{1,0:T(2,128)(2,1)S(1)}, bf16[1,320]{1,0:T(2,128)(2,1)}, u32[]{:S(2)}) copy-start(bf16[1,320]{1,0:T(2,128)(2,1)} %param.21) | copy-start | bytes 1924
  13.6 17.4 %copy-start.9 = (bf16[1,320]{1,0:T(2,128)(2,1)S(1)}, bf16[1,320]{1,0:T(2,128)(2,1)}, u32[]{:S(2)}) copy-start(bf16[1,320]{1,0:T(2,128)(2,1)} %param.22) | copy-start | bytes 1924
  13.6 17.4 %copy-start.10 = (bf16[1,320]{1,0:T(2,128)(2,1)S(1)}, bf16[1,320]{1,0:T(2,128)(2,1)}, u32[]{:S(2)}) copy-start(bf16[1,320]{1,0:T(2,128)(2,1)} %param.23) | copy-start | bytes 1924
  13.6 17.4 %copy-start.11 = (bf16[1,320]{1,0:T(2,128)(2,1)S(1)}, bf16[1,320]{1,0:T(2,128)(2,1)}, u32[]{:S(2)}) copy-start(bf16[1,320]{1,0:T(2,128)(2,1)} %param.27) | copy-start | bytes 1924
  13.6 17.4 %copy-start.12 = (bf16[1,2,320]{2,1,0:T(2,128)(2,1)S(1)}, bf16[1,2,320]{2,1,0:T(2,128)(2,1)}, u32[]{:S(2)}) copy-start(bf16[1,2,320]{2,1,0:T(2,128)(2,1)} %param.19) | copy-start | bytes 3844
  13.6 18.0 %copy-start = (bf16[1,320,1280]{2,1,0:T(8,128)(2,1)S(1)}, bf16[1,320,1280]{2,1,0:T(8,128)(2,1)}, u32[]{:S(2)}) copy-start(bf16[1,320,1280]{2,1,0:T(8,128)(2,1)} %param.24) | copy-start | bytes 2457604
  13.7 16.1 %collective-permute-start = (bf16[320,640]{1,0:T(8,128)(2,1)S(1)}, bf16[320,640]{1,0:T(8,128)(2,1)S(1)}, u32[]{:S(2)}, u32[]{:S(2)}) collective-permute-start(bf16[320,640]{1,0:T(8,128)(2,1)S(1)} %get-tuple-element.190), channel_id=1, source_target_pairs={{0,16},{16,0},{1,17},{17,1},{2,18},{18,2},{3,19},{19,3},{4,20},{20... | collective-permute-start | bytes 1228808 | tf_op jit(solution)/shard_map/ppermute | solution.py:1318
  30.8 79.0 %all-gather.9.cloned.1.call-start = ((), (), s32[]{:S(2)}) async-start(), calls=%async_computation.7 | async-start | bytes 2048000 | tf_op jit(solution)/shard_map/all_gather | solution.py:1386
  32.7 118.3 %all-gather.11.cloned.1.call-start = ((), (), s32[]{:S(2)}) async-start(), calls=%async_computation.8 | async-start | bytes 2048000 | tf_op jit(solution)/shard_map/all_gather | solution.py:1386
  32.7 36.7 %copy-start.1 = (bf16[1,1280,320]{1,2,0:T(8,128)(2,1)S(1)}, bf16[1,1280,320]{1,2,0:T(8,128)(2,1)}, u32[]{:S(2)}) copy-start(bf16[1,1280,320]{1,2,0:T(8,128)(2,1)} %param.26) | copy-start | bytes 2457604
  69.4 3.2 copy-start.4
  71.3 5.9 copy-start.2
  71.3 118.2 %all-gather.13.cloned.1.call-start = ((), (), s32[]{:S(2)}) async-start(), calls=%async_computation.9 | async-start | bytes 2048000 | tf_op jit(solution)/shard_map/all_gather | solution.py:1386
  71.9 157.6 %all-gather.15.cloned.1.call-start = ((), (), s32[]{:S(2)}) async-start(), calls=%async_computation.10 | async-start | bytes 2048000 | tf_op jit(solution)/shard_map/all_gather | solution.py:1386
  72.5 224.6 %all-gather.17.cloned.1.call-start = ((), (), s32[]{:S(2)}) async-start(), calls=%async_computation.11 | async-start | bytes 4096000 | tf_op jit(solution)/shard_map/all_gather | solution.py:1386
  72.7 38.3 %collective-permute-start.2 = (bf16[1280,640]{1,0:T(8,128)(2,1)}, bf16[1280,640]{1,0:T(8,128)(2,1)S(1)}, u32[]{:S(2)}, u32[]{:S(2)}) collective-permute-start(bf16[1280,640]{1,0:T(8,128)(2,1)} %all-gather.7.cloned.1.call-done.refs_1_.refs_4_), channel_id=1, source_target_pairs={{0,16},{16,0},{1,17},{17,1},{2,18},{18,2},{3,19},{19,3},{4,20},{20... | collective-permute-start | bytes 4915208 | tf_op jit(solution)/shard_map/ppermute | solution.py:1318
  78.2 318.0 %reduce-scatter.11.cloned.1.call-start = ((), (), s32[]{:S(2)}) async-start(), calls=%async_computation.14 | async-start | bytes 4096000 | tf_op jit(solution)/shard_map/reduce_scatter | solution.py:1438
  111.1 1.2 copy-start.13
  296.7 167.7 %reduce-scatter.9.cloned.1.call-start = ((), (), s32[]{:S(2)}) async-start(), calls=%async_computation.13 | async-start | bytes 4096000 | tf_op jit(solution)/shard_map/reduce_scatter | solution.py:1438
  338.4 166.4 %reduce-scatter.7.cloned.1.call-start = ((), (), s32[]{:S(2)}) async-start(), calls=%async_computation.12 | async-start | bytes 4096000 | tf_op jit(solution)/shard_map/reduce_scatter | solution.py:1438
  395.9 131.7 %reduce-scatter.13.cloned.1.call-start = ((), (), s32[]{:S(2)}) async-start(), calls=%async_computation.15 | async-start | bytes 2048000 | tf_op jit(solution)/shard_map/reduce_scatter | solution.py:1438
  462.5 110.5 %reduce-scatter.15.cloned.1.call-start = ((), (), s32[]{:S(2)}) async-start(), calls=%async_computation.16 | async-start | bytes 2048000 | tf_op jit(solution)/shard_map/reduce_scatter | solution.py:1438
  504.9 107.8 %reduce-scatter.17.cloned.1.call-start = ((), (), s32[]{:S(2)}) async-start(), calls=%async_computation.17 | async-start | bytes 2048000 | tf_op jit(solution)/shard_map/reduce_scatter | solution.py:1438
Sparse Core Ops, SparseCore 0:
  30.9 39.6 all-gather.6
  72.7 37.0 all-gather.8
  111.9 37.0 all-gather.10
  151.0 37.0 all-gather.12
  190.0 37.0 all-gather.14
  229.1 64.5 all-gather.16
  296.9 62.5 reduce-scatter.10
  361.8 62.3 reduce-scatter.8
  426.5 62.4 reduce-scatter.6
  491.1 36.4 reduce-scatter.12
  530.0 35.3 reduce-scatter.14
  570.6 34.6 reduce-scatter.16

commit v16 on v15

--- a/solution.py
+++ b/solution.py
@@ -373,8 +373,8 @@
 
 
 def start_kernel(
-    tokens_ref, cotangent_ref, small_ref, contract_ref,
-    x_ref, g_ref, vectors_ref, got_contract_ref,
+    tokens_ref, cotangent_ref, small_ref, expand_ref, contract_ref,
+    x_ref, g_ref, vectors_ref, got_expand_ref, got_contract_ref,
     x4, g4, s4, other4, x_sems, g_sems, s_sems, local_sems,
 ):
     section = lax.axis_index("section")
@@ -382,17 +382,21 @@
     length = x_ref.shape[0]
     loads = []
     rows = pl.ds(pl.multiple_of(section * length, length), length)
-    sources = ((tokens_ref.at[:, rows], x4), (cotangent_ref.at[:, rows], g4), (small_ref, s4))
+    sources = ((tokens_ref.at[:, rows], x4), (cotangent_ref.at[rows], g4), (small_ref, s4))
     for n, (source, into) in enumerate(sources):
         loads.append(pltpu.make_async_copy(source, into.at[group.me], local_sems.at[n]))
         loads[-1].start()
     group.greet(True, False)
-    blocks = push(contract_ref, got_contract_ref, s_sems, 3 * PARTS + 1, 1 - section, "section")
+    blocks = [
+        push(source, into, s_sems, 3 * PARTS + 1 + n, 1 - section, "section")
+        for n, (source, into) in enumerate(((expand_ref, got_expand_ref), (contract_ref, got_contract_ref)))
+    ]
+    blocks[0].start()
     gathers = [Gather(group, s4, s_sems, True), Gather(group, x4, x_sems, True), Gather(group, g4, g_sems, True)]
     for gather, load in zip(gathers, (loads[2], loads[0], loads[1])):
         load.wait()
         gather.start()
-    width = x4.shape[1]
+    width = x_ref.shape[1] // 4
     for gather, blocks4, full_ref in ((gathers[0], None, None), (gathers[1], x4, x_ref), (gathers[2], g4, g_ref)):
         gather.sibling()
         gather.relay()
@@ -400,12 +404,16 @@
         if blocks4 is None:
             swap = push(s4, other4, s_sems, 3 * PARTS, 1 - section, "section")
             swap.start()
-            blocks.start()
+            blocks[1].start()
         else:
             for c in range(blocks4.shape[0]):
-                full_ref[:, c * width : (c + 1) * width] = turned_back(blocks4[c]).astype(LOW)
+                block = blocks4[c]
+                if block.shape[0] == width:
+                    block = turned_back(block).astype(LOW)
+                full_ref[:, c * width : (c + 1) * width] = block
     swap.wait()
-    blocks.wait()
+    for block in blocks:
+        block.wait()
     vectors_ref[section] = s4[...]
     vectors_ref[1 - section] = other4[...]
     for gather in gathers:
@@ -927,60 +935,80 @@
 
 def write_kernel(*refs):
     late, far_late, early, far_early = [refs[n : n + 3] for n in (0, 3, 6, 9)]
-    sums_ref, results_ref, grads_ref, attend_ref, output_ref, expand_ref, contract_ref, *vector_refs = refs[12:-4]
-    *vector_refs, outputs_ref, inputs_ref = vector_refs
-    own, far, low, sems = refs[-4:]
-    length = low.shape[2]
-    moves = [pltpu.make_async_copy(grads_ref, low, sems.at[6])] + [
-        pltpu.make_async_copy(results_ref.at[n], outputs_ref.at[:, pl.ds(n * length, length)], sems.at[7 + n])
-        for n in range(2)
+    sums_ref, results_ref, grads_ref, output_ref, *vector_refs = refs[12:24]
+    homes, (own, far, low, results, *held, sems, out_sems) = refs[24:29], refs[29:]
+    attend, expand, contract, outputs, inputs = held
+    stores = [pltpu.make_async_copy(held[n], homes[n], out_sems.at[n]) for n in range(5)]
+    length, width = low.shape[2], output_ref.shape[0]
+    moves = [
+        pltpu.make_async_copy(grads_ref, low, sems.at[6]),
+        pltpu.make_async_copy(results_ref, results, sems.at[7]),
     ]
     for move in moves:
         move.start()
     half = early[0].shape[1]
-    width = output_ref.shape[0]
     section = lax.axis_index("section")
 
-    def load(firsts, seconds):
-        copies = [
+    def pairs(which):
+        if which == 0:
+            firsts = [(early[n], own.at[n, :, pl.ds(0, half)]) for n in range(3)]
+            seconds = [(far_early[n], own.at[n, :, pl.ds(half, half)]) for n in range(3)]
+        else:
+            firsts = [(late[n], own.at[n]) for n in range(3)]
+            seconds = [(far_late[n], far.at[n]) for n in range(3)]
+        return [
             pltpu.make_async_copy(source, into, sems.at[n])
             for n, (source, into) in enumerate((*firsts, *seconds))
         ]
-        for copy in copies:
-            copy.start()
-        for copy in copies:
-            copy.wait()
 
     @pl.when(section == 0)
     def _():
-        load(
-            [(early[n], own.at[n, :, pl.ds(0, half)]) for n in range(3)],
-            [(far_early[n], own.at[n, :, pl.ds(half, half)]) for n in range(3)],
-        )
+        for copy in pairs(0):
+            copy.start()
         far[...] = jnp.zeros_like(far)
 
     @pl.when(section == 1)
     def _():
-        load([(late[n], own.at[n]) for n in range(3)], [(far_late[n], far.at[n]) for n in range(3)])
+        for copy in pairs(1):
+            copy.start()
 
     moves[0].wait()
     for n in range(2):
-        inputs_ref[:, n * length : (n + 1) * length] = low[n].astype(WIDE)
+        inputs[:, n * length : (n + 1) * length] = low[n].astype(WIDE)
+    stores[4].start()
+    moves[1].wait()
+    for n in range(2):
+        outputs[:, n * length : (n + 1) * length] = results[n]
+    stores[3].start()
+
+    @pl.when(section == 0)
+    def _():
+        for copy in pairs(0):
+            copy.wait()
+
+    @pl.when(section == 1)
+    def _():
+        for copy in pairs(1):
+            copy.wait()
+
+    contract[...] = own[2].astype(WIDE) + far[2].astype(WIDE)
+    stores[2].start()
+    expand[...] = own[1].astype(WIDE) + far[1].astype(WIDE)
+    stores[1].start()
     first = own[0].astype(WIDE) + far[0].astype(WIDE)
     for j in range(3):
-        attend_ref[j] = first[:, j * width : (j + 1) * width]
+        attend[j] = first[:, j * width : (j + 1) * width]
+    stores[0].start()
     corner = first[:, 3 * width :]
     high = corner.astype(LOW)
     output_ref[...] = turned(high) + turned((corner - high.astype(WIDE)).astype(LOW))
-    expand_ref[...] = own[1].astype(WIDE) + far[1].astype(WIDE)
-    contract_ref[...] = own[2].astype(WIDE) + far[2].astype(WIDE)
     for n in range(6):
         vector_refs[n][...] = sums_ref[n : n + 1, :]
     vector_refs[6][...] = sums_ref[8:10, :][None]
     for n in range(vector_refs[7].shape[1] // width):
         vector_refs[7][:, n * width : (n + 1) * width] = sums_ref[10 + n : 11 + n, :]
-    for move in moves[1:]:
-        move.wait()
+    for store in stores:
+        store.wait()
 
 
 VM = pl.BlockSpec(memory_space=pltpu.VMEM)
@@ -1055,27 +1083,28 @@
     return results[:n_out], results[n_out:]
 
 
-def start_call(number, tokens, cotangent, small, contract, columns):
-    width = tokens.shape[0]
+def start_call(number, tokens, cotangent, small, expand, contract, columns):
+    width = small.shape[1]
     size = width * columns
     kinds = small.shape[0]
-    outs = (shape((LENGTH, size)), shape((LENGTH, size)), shape((2, columns, kinds, width)), shape(contract.shape))
-    blocks = pltpu.VMEM((columns, width, LENGTH), LOW)
+    outs = (shape((LENGTH, size)), shape((LENGTH, size)), shape((2, columns, kinds, width)), shape(expand.shape), shape(contract.shape))
+    low = pltpu.VMEM((columns, width, LENGTH), LOW)
+    high = pltpu.VMEM((columns, LENGTH, width), LOW)
     vectors = pltpu.VMEM((columns, kinds, width), LOW)
     return pl.pallas_call(
         start_kernel,
         out_shape=outs,
-        in_specs=[ANY] * 4,
-        out_specs=(VM, VM, VM, ANY),
+        in_specs=[ANY] * 5,
+        out_specs=(VM, VM, VM, ANY, ANY),
         scratch_shapes=[
-            blocks, blocks, vectors, vectors, PAIRS, PAIRS,
-            pltpu.SemaphoreType.DMA((2, 3 * PARTS + 2)), LOCAL,
+            low, high, vectors, vectors, PAIRS, PAIRS,
+            pltpu.SemaphoreType.DMA((2, 3 * PARTS + 3)), LOCAL,
         ],
         compiler_params=pltpu.CompilerParams(
             collective_id=number, has_side_effects=True, vmem_limit_bytes=GRANT
         ),
         cost_estimate=pl.CostEstimate(flops=int(3e10), bytes_accessed=30 * MEBI, transcendentals=0),
-    )(tokens, cotangent, small, contract)
+    )(tokens, cotangent, small, expand, contract)
 
 
 def attend_call(number, x, pair, vec, bias, rows, width, swaps):
@@ -1299,17 +1328,22 @@
 def write_call(late, far_late, early, far_early, sums, wide, results, grads):
     rows, size = late[0].shape
     _, width, length = grads.shape
+    large = (
+        shape((3, rows, width), WIDE), shape((rows, size), WIDE), shape((rows, size), WIDE),
+        shape((width, 2 * length)), shape((width, 2 * length), WIDE),
+    )
     return pl.pallas_call(
         write_kernel,
         out_shape=(
-            shape((3, rows, width), WIDE), shape((width, rows), WIDE), shape((rows, size), WIDE), shape((rows, size), WIDE),
-            *[shape((1, width), WIDE)] * 6, shape((1, 2, width), WIDE), shape((1, wide), WIDE),
-            shape((width, 2 * length)), shape((width, 2 * length), WIDE),
+            shape((width, rows), WIDE),
+            *[shape((1, width), WIDE)] * 6, shape((1, 2, width), WIDE), shape((1, wide), WIDE), *large,
         ),
         in_specs=[ANY] * 12 + [VM, ANY, ANY],
-        out_specs=(VM,) * 12 + (ANY, VM),
+        out_specs=(VM,) * 9 + (ANY,) * 5,
         scratch_shapes=[pltpu.VMEM((3, rows, size), LOW)] * 2
-        + [pltpu.VMEM(grads.shape, LOW), pltpu.SemaphoreType.DMA((9,))],
+        + [pltpu.VMEM(grads.shape, LOW), pltpu.VMEM(results.shape, LOW)]
+        + [pltpu.VMEM(s.shape, s.dtype) for s in large]
+        + [pltpu.SemaphoreType.DMA((8,)), pltpu.SemaphoreType.DMA((5,))],
         compiler_params=pltpu.CompilerParams(vmem_limit_bytes=GRANT),
     )(*late, *far_late, *early, *far_early, sums, results, grads)
 
@@ -1376,10 +1410,9 @@
     filled = small.shape[0]
     small = jnp.pad(small, ((0, -filled % (16 * PARTS)), (0, 0)))
     got_attend = swap_sections(sent_blocks[0])
-    got_expand = swap_sections(sent_blocks[1])
-    got_attend, got_expand, sent_contract = lax.optimization_barrier((got_attend, got_expand, units[2]))
-    x0_full, gy_full, vectors, got_contract = start_call(
-        1, tokens.T, cotangent.T, small, sent_contract, columns
+    got_attend, sent_expand = lax.optimization_barrier((got_attend, sent_blocks[1]))
+    x0_full, gy_full, vectors, got_expand, got_contract = start_call(
+        1, tokens.T, cotangent, small, sent_expand, units[2], columns
     )
 
     def gather_blocks(block):
@@ -1476,7 +1509,7 @@
 
     part_w0, small_grads = tie(scatter(total_w0), small_grads)
     far_w0 = cross_call(17, False, part_w0)
-    attend_part, output_part, expand_part, contract_part, *vector_grads, layer_outputs, input_grads = write_call(
+    output_part, *vector_grads, attend_part, expand_part, contract_part, layer_outputs, input_grads = write_call(
         (part_w1, part_e1, part_c1),
         (far_w1, far_e1, far_c1),
         (part_w0, part_e0, part_c0),

time: 688 us -> 642 us (0.933)
  Pallas kernels: 580 us -> 545 us
  waiting for transfers between devices: 54.1 us -> 44.8 us
    pallas_call x2, Pallas kernels: 81.5 us -> 45.9 us  [the longest x1 38.7 us: start_call(): pl.pallas_call(start_kernel, out_shape=outs, in_specs=[ANY] * 5, out_spec...]
    ppermute x3 -> x2, waiting for transfers between devices: 17.3 us -> 8.46 us  [swap_sections(): return lax.ppermute(value, 'section', [(0, 1), (1, 0)])]
  transfers between devices with their start and end apart: 15 -> 14, of which waited for: 5 -> 4; matrix products, arithmetic and copies ran while one was open for 3% -> 3% of each run, Pallas kernels for 78% -> 83%
where the time goes in v16:
time: 642 us; the launch traced here: 633 us
  Pallas kernels  545 us (85%)
  waiting for transfers between devices  44.8 us (7%)
  local copies, waits for them, and re-layouts  15.7 us (2%)
  between operations  14.8 us (2%)
  other arithmetic  7.82 us (1%)
    pallas_call x10, Pallas kernels, launch(): pl.pallas_call(kernel, out_shape=(*outs, *[shape(s.shape, s.dtype) for s...  430 us
    pallas_call x1, Pallas kernels, finish_call(): pl.pallas_call(finish_kernel, out_shape=outs, in_specs=[ANY] * 9, out_spe...  39.7 us
    pallas_call x1, Pallas kernels, start_call(): pl.pallas_call(start_kernel, out_shape=outs, in_specs=[ANY] * 5, out_spec...  38.7 us
    all_gather x6, waiting for transfers between devices, gather_blocks(): return lax.all_gather(block, 'row', axis=0, tiled=True)  31 us
    pallas_call x2, Pallas kernels, cross_call(): pl.pallas_call(functools.partial(cross_kernel, up), out_shape=shape(part....  28.7 us
  transfers between devices with their start and end apart: 14, of which 4 were waited for; matrix products, arithmetic and copies ran while one was open for 3% of the time, Pallas kernels for 83%

profile of v16, /device:TPU:0, one launch (start us, length us, event | category | flops | bytes accessed | tf_op | source)
XLA Modules:
  0.0 633.3 jit_solution(8472492438497164428)
XLA Ops:
  7.2 1.1 copy.33
  8.4 1.5 copy.32
  9.9 0.3 copy.34
  10.2 1.0 broadcast_select_fusion.8
  11.2 3.0 collective-permute-start
  14.3 0.1 reshape_squeeze.6
  14.3 1.5 copy.36.cotangent_ref
  16.0 0.6 pad.8.small_ref
  16.6 0.8 broadcast_select_fusion.7.expand_ref
  17.4 6.6 %collective-permute-done = bf16[320,640]{1,0:T(8,128)(2,1)} collective-permute-done((bf16[320,640]{1,0:T(8,128)(2,1)}, bf16[320,640]{1,0:T(8,128)(2,1)}, u32[]{:S(2)}, u32[]{:S(2)}) %collective-permute-start) | collective-permute-done | bytes 409632 | tf_op jit(solution)/shard_map/ppermute | solution.py:1352
  24.0 2.0 broadcast_select_fusion.1
  26.1 38.7 %shard_map.245 = (bf16[1024,1280]{1,0:T(8,128)(2,1)}, bf16[1024,1280]{1,0:T(8,128)(2,1)}, bf16[2,4,32,320]{3,2,1,0:T(8,128)(2,1)}, bf16[320,640]{1,0:T(8,128)(2,1)}, bf16[320,1280]{1,0:T(8,128)(2,1)}) custom-call(bf16[320,2048]{1,0:T(8,128)(2,1)} %bitcast.45, bf16[2048,320]{1,0:T(8,128)(2,1)} %copy.36.cotangent_ref, bf16[32,320]{1,0:T(8,128)(2,1)} %pad.8.small_ref, ...), custom_call_target="tpu_custom_call" | custom-call | flops 30000001024 | bytes 31457280 | tf_op jit(solution)/shard_map/pallas_call | solution.py:1094
  64.8 2.1 broadcast_select_fusion.2
  67.0 0.8 fusion
  67.9 0.5 all-gather.13.cloned.1.call-update
  68.5 0.5 all-gather.15.cloned.1.call-update
  69.1 0.1 pad.11.clone
  69.3 1.6 collective-permute-start.1
  70.8 0.7 squeeze.48.refs_3_
  71.5 0.7 squeeze.45.refs_3_
  72.2 0.1 pad_maximum_fusion.1
  72.3 0.7 squeeze.47.refs_4_
  73.0 0.7 squeeze.44.refs_4_
  73.6 0.1 reshape.42
  73.7 1.0 broadcast_select_fusion
  74.8 0.6 fusion.2
  75.4 30.9 %all-gather.9.cloned.1.call-done.refs_5_.refs_1_.refs_3_ = bf16[1280,640]{1,0:T(8,128)(2,1)} async-done(((bf16[320,640]{1,0:T(8,128)(2,1)}), bf16[1280,640]{1,0:T(8,128)(2,1)}) %all-gather.9.cloned.1.call-update) | async-done | bytes 1638416 | tf_op jit(solution)/shard_map/all_gather | solution.py:1419
  106.3 1.9 collective-permute-done.1.refs_2_.refs_5_
  108.2 38.5 %shard_map.246 = (bf16[1024,1280]{1,0:T(8,128)(2,1)}, bf16[15,1024,64]{2,1,0:T(8,128)(2,1)}, bf16[1024,320]{1,0:T(8,128)(2,1)}, f32[8,1024]{1,0:T(8,128)}, f32[2...) custom-call(bf16[1024,1280]{1,0:T(8,128)(2,1)} %get-tuple-element.103.refs_0_, ...), custom_call_target="tpu_custom_call" | custom-call | flops 30000001024 | bytes 31457280 | tf_op jit(solution)/shard_map/pallas_call | solution.py:1065
  146.8 38.4 %shard_map.247 = (bf16[1024,1280]{1,0:T(8,128)(2,1)}, bf16[1024,1280]{1,0:T(8,128)(2,1)}, bf16[1024,1280]{1,0:T(8,128)(2,1)}, bf16[1280,640]{1,0:T(8,128)(2,1)}) custom-call(bf16[256,1280]{1,0:T(8,128)(2,1)} %get-tuple-element.107.refs_0_, bf16[1280,640]{1,0:T(8,128)(2,1)} %all-gather.9.cloned.1.call-done.refs_5_.refs_1_.refs_3_, ...), custom_call_target="tpu_custom_call" | custom-call | flops 30000001024 | bytes 31457280 | tf_op jit(solution)/shard_map/pallas_call | solution.py:1065
  185.2 39.9 %shard_map.248 = (bf16[256,1280]{1,0:T(8,128)(2,1)}, bf16[1024,1280]{1,0:T(8,128)(2,1)}, bf16[1280,640]{1,0:T(8,128)(2,1)}) custom-call(bf16[1024,1280]{1,0:T(8,128)(2,1)} %get-tuple-element.110.refs_0_.refs_6_, f32[256,1280]{1,0:T(8,128)} %get-tuple-element.111.refs_1_.refs_8_, bf16[1280,640]{1,0:T(8,128)(2,1)} %all-gather.11.cloned.1.call-done.refs_4_.refs_2_.refs_1_, ...), custom_call_target="tpu_custom_call" | custom-call | flops 30000001024 | bytes 31457280 | tf_op jit(solution)/shard_map/pallas_call | solution.py:1065
  225.1 38.7 %shard_map.249 = (bf16[1024,1280]{1,0:T(8,128)(2,1)}, bf16[15,1024,64]{2,1,0:T(8,128)(2,1)}, bf16[1024,320]{1,0:T(8,128)(2,1)}, f32[8,1024]{1,0:T(8,128)}, f32[2...) custom-call(bf16[1024,1280]{1,0:T(8,128)(2,1)} %get-tuple-element.113.refs_0_, ...), custom_call_target="tpu_custom_call" | custom-call | flops 30000001024 | bytes 31457280 | tf_op jit(solution)/shard_map/pallas_call | solution.py:1065
  263.8 28.9 %shard_map.250 = (bf16[1024,1280]{1,0:T(8,128)(2,1)}, bf16[1024,1280]{1,0:T(8,128)(2,1)}, bf16[1024,1280]{1,0:T(8,128)(2,1)}, bf16[1280,1280]{1,0:T(8,128)(2,1)}) custom-call(bf16[256,1280]{1,0:T(8,128)(2,1)} %get-tuple-element.115.refs_0_, bf16[1280,640]{1,0:T(8,128)(2,1)} %all-gather.15.cloned.1.call-done.refs_5_.refs_1_.refs_4_, ...), custom_call_target="tpu_custom_call" | custom-call | flops 30000001024 | bytes 31457280 | tf_op jit(solution)/shard_map/pallas_call | solution.py:1065
  292.7 0.3 reduce-scatter.9.cloned.1.call-start
  293.0 41.1 %shard_map.251 = (f32[256,1280]{1,0:T(8,128)}, bf16[256,1280]{1,0:T(8,128)(2,1)}, f32[8,1280]{1,0:T(8,128)}, bf16[1280,1280]{1,0:T(8,128)(2,1)}, bf16[256,1280]{1,0:T(8,128)(2,1)}) custom-call(bf16[1024,1280]{1,0:T(8,128)(2,1)} %get-tuple-element.118.refs_0_, f32[256,1280]{1,0:T(8,128)} %get-tuple-element.119.refs_1_, ...), custom_call_target="tpu_custom_call" | custom-call | flops 30000001024 | bytes 31457280 | tf_op jit(solution)/shard_map/pallas_call | solution.py:1065
  334.2 2.5 constant_dynamic-slice_fusion.2.refs_11_
  336.6 55.2 %shard_map.252 = (bf16[256,1280]{1,0:T(8,128)(2,1)}, f32[8,1280]{1,0:T(8,128)}, bf16[2,320,1024]{2,1,0:T(8,128)(2,1)}, bf16[1280,1280]{1,0:T(8,128)(2,1)}) custom-call(bf16[256,1280]{1,0:T(8,128)(2,1)} %get-tuple-element.122.refs_0_, f32[256,1280]{1,0:T(8,128)} %get-tuple-element.123.refs_1_, bf16[256,1280]{1,0:T(8,128)(2,1)} %get-tuple-element.124.refs_2_, ...), custom_call_target="tpu_custom_call" | custom-call | flops 30000001024 | bytes 31457280 | tf_op jit(solution)/shard_map/pallas_call | solution.py:1065
  391.9 0.3 reduce-scatter.13.cloned.1.call-start
  392.1 65.9 %shard_map.253 = (f32[256,1280]{1,0:T(8,128)}, bf16[256,1280]{1,0:T(8,128)(2,1)}, f32[8,1280]{1,0:T(8,128)}, bf16[1280,640]{1,0:T(8,128)(2,1)}, bf16[1280,640]{1...) custom-call(bf16[256,1280]{1,0:T(8,128)(2,1)} %get-tuple-element.132.refs_0_, ...), custom_call_target="tpu_custom_call" | custom-call | flops 30000001024 | bytes 31457280 | tf_op jit(solution)/shard_map/pallas_call | solution.py:1065
  458.2 2.0 constant_dynamic-slice_fusion.1.refs_3_
  460.1 41.0 %shard_map.254 = (bf16[1024,960]{1,0:T(8,128)(2,1)}, bf16[1280,320]{1,0:T(8,128)(2,1)}, bf16[1280,640]{1,0:T(8,128)(2,1)}) custom-call(bf16[256,1280]{1,0:T(8,128)(2,1)} %get-tuple-element.137.refs_0_, bf16[1280,640]{1,0:T(8,128)(2,1)} %all-gather.7.cloned.1.call-done.refs_1_.refs_4_, bf16[1280,640]{1,0:T(8,128)(2,1)} %collective-permute-done.1.refs_2_.refs_5_, ...), custom_call_target="tpu_custom_call" | custom-call | flops 30000001024 | bytes 31457280 | tf_op jit(solution)/shard_map/pallas_call | solution.py:1065
  501.2 17.9 %shard_map.255.refs_4_ = bf16[320,1280]{1,0:T(8,128)(2,1)} custom-call(bf16[320,1280]{1,0:T(8,128)(2,1)} %reduce-scatter.9.cloned.1.call-done.part_ref.refs_1_), custom_call_target="tpu_custom_call" | custom-call | flops 10000000000 | bytes 10485760 | tf_op jit(solution)/shard_map/pallas_call | solution.py:1315
  519.1 4.0 reduce-scatter.13.cloned.1.call-done.early1_ref.refs_8_
  523.2 42.9 %shard_map.256 = (bf16[1280,640]{1,0:T(8,128)(2,1)}, bf16[256,1280]{1,0:T(8,128)(2,1)}, f32[8,1280]{1,0:T(8,128)}) custom-call(bf16[1024,960]{1,0:T(8,128)(2,1)} %get-tuple-element.153.refs_0_, bf16[1280,320]{1,0:T(8,128)(2,1)} %get-tuple-element.154.refs_1_, f32[256,1280]{1,0:T(8,128)} %get-tuple-element.155.refs_2_, ...), custom_call_target="tpu_custom_call" | custom-call | flops 30000001024 | bytes 31457280 | tf_op jit(solution)/shard_map/pallas_call | solution.py:1065
  566.1 2.4 constant_dynamic-slice_fusion.far_hbm
  568.6 39.7 %shard_map.257 = (bf16[2,320,1024]{2,1,0:T(8,128)(2,1)}, f32[16,320]{1,0:T(8,128)}, bf16[320,1280]{1,0:T(8,128)(2,1)}, bf16[320,640]{1,0:T(8,128)(2,1)}, bf16[320,640]{1,0:T(8,128)(2,1)}) custom-call(bf16[320,1280]{1,0:T(8,128)(2,1)} %reduce-scatter.7.cloned.1.call-done.late_ref.refs_0_, ...), custom_call_target="tpu_custom_call" | custom-call | flops 30000001024 | bytes 31457280 | tf_op jit(solution)/shard_map/pallas_call | solution.py:1301
  608.3 10.8 %shard_map.258.refs_9_ = bf16[320,640]{1,0:T(8,128)(2,1)} custom-call(bf16[320,640]{1,0:T(8,128)(2,1)} %reduce-scatter.17.cloned.1.call-done.part_ref.refs_6_), custom_call_target="tpu_custom_call" | custom-call | flops 10000000000 | bytes 10485760 | tf_op jit(solution)/shard_map/pallas_call | solution.py:1315
  619.1 7.2 %shard_map.259 = (f32[320,320]{1,0:T(8,128)}, f32[1,320]{1,0:T(1,128)}, f32[1,320]{1,0:T(1,128)}, f32[1,320]{1,0:T(1,128)}, f32[1,320]{1,0:T(1,128)}, /*index=5*...) custom-call(bf16[320,1280]{1,0:T(8,128)(2,1)} %reduce-scatter.7.clon, ...), custom_call_target="tpu_custom_call" | custom-call | tf_op jit(solution)/shard_map/pallas_call | solution.py:1335
  (65 shorter events, 1.0 us)
Async XLA Ops:
  7.2 62.1 %all-gather.7.cloned.1.call-start = ((), (), s32[]{:S(2)}) async-start(), calls=%async_computation.6 | async-start | bytes 2048000 | tf_op jit(solution)/shard_map/all_gather | solution.py:1419
  9.9 4.4 copy-start.5
  9.9 4.5 copy-start.3
  11.2 4.7 copy-start.6
  11.2 4.7 copy-start.7
  11.2 4.7 copy-start.8
  11.2 4.7 copy-start.9
  11.2 4.7 copy-start.10
  11.2 4.7 copy-start.11
  11.2 4.7 copy-start.12
  11.2 5.4 copy-start
  11.2 12.8 %collective-permute-start = (bf16[320,640]{1,0:T(8,128)(2,1)}, bf16[320,640]{1,0:T(8,128)(2,1)}, u32[]{:S(2)}, u32[]{:S(2)}) collective-permute-start(bf16[320,640]{1,0:T(8,128)(2,1)} %get-tuple-element.190), channel_id=1, source_target_pairs={{0,16},{16,0},{1,17},{17,1},{2,18},{18,2},{3,19},{19,3},{4,20},{20... | collective-permute-start | bytes 1228808 | tf_op jit(solution)/shard_map/ppermute | solution.py:1352
  26.0 80.3 %all-gather.9.cloned.1.call-start = ((), (), s32[]{:S(2)}) async-start(), calls=%async_computation.7 | async-start | bytes 2048000 | tf_op jit(solution)/shard_map/all_gather | solution.py:1419
  64.8 2.2 copy-start.1
  64.8 2.2 copy-start.2
  66.9 2.2 copy-start.4
  66.9 79.8 %all-gather.11.cloned.1.call-start = ((), (), s32[]{:S(2)}) async-start(), calls=%async_computation.8 | async-start | bytes 2048000 | tf_op jit(solution)/shard_map/all_gather | solution.py:1419
  67.9 117.3 %all-gather.13.cloned.1.call-start = ((), (), s32[]{:S(2)}) async-start(), calls=%async_computation.9 | async-start | bytes 2048000 | tf_op jit(solution)/shard_map/all_gather | solution.py:1419
  68.4 156.6 %all-gather.15.cloned.1.call-start = ((), (), s32[]{:S(2)}) async-start(), calls=%async_computation.10 | async-start | bytes 2048000 | tf_op jit(solution)/shard_map/all_gather | solution.py:1419
  69.0 224.0 %all-gather.17.cloned.1.call-start = ((), (), s32[]{:S(2)}) async-start(), calls=%async_computation.11 | async-start | bytes 4096000 | tf_op jit(solution)/shard_map/all_gather | solution.py:1419
  69.3 38.9 %collective-permute-start.1 = (bf16[1280,640]{1,0:T(8,128)(2,1)}, bf16[1280,640]{1,0:T(8,128)(2,1)}, u32[]{:S(2)}, u32[]{:S(2)}) collective-permute-start(bf16[1280,640]{1,0:T(8,128)(2,1)} %all-gather.7.cloned.1.call-done.refs_1_.refs_4_), channel_id=1, source_target_pairs={{0,16},{16,0},{1,17},{17,1},{2,18},{18,2},{3,19},{19,3},{4,20},{20... | collective-permute-start | bytes 4915208 | tf_op jit(solution)/shard_map/ppermute | solution.py:1352
  74.7 317.4 %reduce-scatter.11.cloned.1.call-start = ((), (), s32[]{:S(2)}) async-start(), calls=%async_computation.14 | async-start | bytes 4096000 | tf_op jit(solution)/shard_map/reduce_scatter | solution.py:1471
  292.7 167.4 %reduce-scatter.9.cloned.1.call-start = ((), (), s32[]{:S(2)}) async-start(), calls=%async_computation.13 | async-start | bytes 4096000 | tf_op jit(solution)/shard_map/reduce_scatter | solution.py:1471
  334.1 167.0 %reduce-scatter.7.cloned.1.call-start = ((), (), s32[]{:S(2)}) async-start(), calls=%async_computation.12 | async-start | bytes 4096000 | tf_op jit(solution)/shard_map/reduce_scatter | solution.py:1471
  391.9 131.3 %reduce-scatter.13.cloned.1.call-start = ((), (), s32[]{:S(2)}) async-start(), calls=%async_computation.15 | async-start | bytes 2048000 | tf_op jit(solution)/shard_map/reduce_scatter | solution.py:1471
  458.1 110.5 %reduce-scatter.15.cloned.1.call-start = ((), (), s32[]{:S(2)}) async-start(), calls=%async_computation.16 | async-start | bytes 2048000 | tf_op jit(solution)/shard_map/reduce_scatter | solution.py:1471
  501.2 107.1 %reduce-scatter.17.cloned.1.call-start = ((), (), s32[]{:S(2)}) async-start(), calls=%async_computation.17 | async-start | bytes 2048000 | tf_op jit(solution)/shard_map/reduce_scatter | solution.py:1471
Sparse Core Ops, SparseCore 0:
  26.1 39.6 all-gather.6
  68.0 38.2 all-gather.8
  108.5 37.0 all-gather.10
  147.5 37.0 all-gather.12
  186.6 37.0 all-gather.14
  225.6 64.5 all-gather.16
  292.8 62.1 reduce-scatter.10
  357.4 62.4 reduce-scatter.8
  422.2 62.3 reduce-scatter.6
  486.7 36.4 reduce-scatter.12
  525.6 35.3 reduce-scatter.14
  566.2 34.6 reduce-scatter.16

commit v17 on v16

--- a/solution.py
+++ b/solution.py
@@ -1491,7 +1491,7 @@
     part_e1, low = tie(scatter(e1), low)
     mixed, outer, total_e0 = scores_back_call(14, low, attn, heads, o, lse, ek0, es0)
     part_w1, mixed = tie(scatter(w1), mixed)
-    part_e1, mixed = tie(part_e1, mixed)
+    gx1_columns, part_e1, mixed = lax.optimization_barrier((own_features(gx1_full), part_e1, mixed))
     far_e1, mixed = tie(cross_call(18, True, part_e1), mixed)
     part_c0, mixed = tie(scatter(total_c0), mixed)
     total_w0, gx0_own, attend_sums0 = attend_back_call(
@@ -1502,7 +1502,7 @@
         16,
         (part_w1, part_c0, part_e0),
         gx0_own,
-        own_features(gx1_full),
+        gx1_columns,
         (attend_sums0, expand_sums0, attend_sums1, expand_sums1),
         lax.axis_size("row"),
     )

time: 642 us -> 640 us (level)
  no operation moved by 1% of the time
where the time goes in v17:
time: 640 us; the launch traced here: 631 us
  Pallas kernels  545 us (85%)
  waiting for transfers between devices  42.4 us (7%)
  local copies, waits for them, and re-layouts  15.7 us (2%)
  between operations  14.8 us (2%)
  other arithmetic  7.82 us (1%)
    pallas_call x10, Pallas kernels, launch(): pl.pallas_call(kernel, out_shape=(*outs, *[shape(s.shape, s.dtype) for s...  430 us
    pallas_call x1, Pallas kernels, finish_call(): pl.pallas_call(finish_kernel, out_shape=outs, in_specs=[ANY] * 9, out_spe...  39.8 us
    pallas_call x1, Pallas kernels, start_call(): pl.pallas_call(start_kernel, out_shape=outs, in_specs=[ANY] * 5, out_spec...  38.7 us
    all_gather x6, waiting for transfers between devices, gather_blocks(): return lax.all_gather(block, 'row', axis=0, tiled=True)  31 us
    pallas_call x2, Pallas kernels, cross_call(): pl.pallas_call(functools.partial(cross_kernel, up), out_shape=shape(part....  28.7 us
  transfers between devices with their start and end apart: 14, of which 4 were waited for; matrix products, arithmetic and copies ran while one was open for 3% of the time, Pallas kernels for 83%

profile of v17, /device:TPU:0, one launch (start us, length us, event | category | flops | bytes accessed | tf_op | source)
XLA Modules:
  0.0 631.1 jit_solution(8887334829955538658)
XLA Ops:
  7.2 1.1 copy.33
  8.4 1.5 copy.32
  9.9 0.3 copy.34
  10.2 1.0 broadcast_select_fusion.8
  11.2 3.0 collective-permute-start
  14.3 0.1 reshape_squeeze.6
  14.3 1.5 copy.36.cotangent_ref
  16.0 0.6 pad.8.small_ref
  16.6 0.8 broadcast_select_fusion.7.expand_ref
  17.4 6.6 %collective-permute-done = bf16[320,640]{1,0:T(8,128)(2,1)} collective-permute-done((bf16[320,640]{1,0:T(8,128)(2,1)}, bf16[320,640]{1,0:T(8,128)(2,1)}, u32[]{:S(2)}, u32[]{:S(2)}) %collective-permute-start) | collective-permute-done | bytes 409632 | tf_op jit(solution)/shard_map/ppermute | solution.py:1352
  24.0 2.0 broadcast_select_fusion.1
  26.1 38.7 %shard_map.245 = (bf16[1024,1280]{1,0:T(8,128)(2,1)}, bf16[1024,1280]{1,0:T(8,128)(2,1)}, bf16[2,4,32,320]{3,2,1,0:T(8,128)(2,1)}, bf16[320,640]{1,0:T(8,128)(2,1)}, bf16[320,1280]{1,0:T(8,128)(2,1)}) custom-call(bf16[320,2048]{1,0:T(8,128)(2,1)} %bitcast.45, bf16[2048,320]{1,0:T(8,128)(2,1)} %copy.36.cotangent_ref, bf16[32,320]{1,0:T(8,128)(2,1)} %pad.8.small_ref, ...), custom_call_target="tpu_custom_call" | custom-call | flops 30000001024 | bytes 31457280 | tf_op jit(solution)/shard_map/pallas_call | solution.py:1094
  64.8 2.1 broadcast_select_fusion.2
  67.0 0.8 fusion
  67.9 0.5 all-gather.13.cloned.1.call-update
  68.5 0.5 all-gather.15.cloned.1.call-update
  69.1 0.1 pad.11.clone
  69.3 1.6 collective-permute-start.1
  70.8 0.7 squeeze.48.refs_3_
  71.5 0.7 squeeze.45.refs_3_
  72.2 0.1 pad_maximum_fusion.1
  72.3 0.7 squeeze.47.refs_4_
  73.0 0.7 squeeze.44.refs_4_
  73.6 0.1 reshape.42
  73.7 1.0 broadcast_select_fusion
  74.8 0.6 fusion.2
  75.4 30.9 %all-gather.9.cloned.1.call-done.refs_5_.refs_1_.refs_3_ = bf16[1280,640]{1,0:T(8,128)(2,1)} async-done(((bf16[320,640]{1,0:T(8,128)(2,1)}), bf16[1280,640]{1,0:T(8,128)(2,1)}) %all-gather.9.cloned.1.call-update) | async-done | bytes 1638416 | tf_op jit(solution)/shard_map/all_gather | solution.py:1419
  106.3 1.9 collective-permute-done.1.refs_2_.refs_5_
  108.2 38.5 %shard_map.246 = (bf16[1024,1280]{1,0:T(8,128)(2,1)}, bf16[15,1024,64]{2,1,0:T(8,128)(2,1)}, bf16[1024,320]{1,0:T(8,128)(2,1)}, f32[8,1024]{1,0:T(8,128)}, f32[2...) custom-call(bf16[1024,1280]{1,0:T(8,128)(2,1)} %get-tuple-element.104.refs_0_, ...), custom_call_target="tpu_custom_call" | custom-call | flops 30000001024 | bytes 31457280 | tf_op jit(solution)/shard_map/pallas_call | solution.py:1065
  146.8 38.4 %shard_map.247 = (bf16[1024,1280]{1,0:T(8,128)(2,1)}, bf16[1024,1280]{1,0:T(8,128)(2,1)}, bf16[1024,1280]{1,0:T(8,128)(2,1)}, bf16[1280,640]{1,0:T(8,128)(2,1)}) custom-call(bf16[256,1280]{1,0:T(8,128)(2,1)} %get-tuple-element.108.refs_0_, bf16[1280,640]{1,0:T(8,128)(2,1)} %all-gather.9.cloned.1.call-done.refs_5_.refs_1_.refs_3_, ...), custom_call_target="tpu_custom_call" | custom-call | flops 30000001024 | bytes 31457280 | tf_op jit(solution)/shard_map/pallas_call | solution.py:1065
  185.2 39.9 %shard_map.248 = (bf16[256,1280]{1,0:T(8,128)(2,1)}, bf16[1024,1280]{1,0:T(8,128)(2,1)}, bf16[1280,640]{1,0:T(8,128)(2,1)}) custom-call(bf16[1024,1280]{1,0:T(8,128)(2,1)} %get-tuple-element.111.refs_0_.refs_6_, f32[256,1280]{1,0:T(8,128)} %get-tuple-element.112.refs_1_.refs_8_, bf16[1280,640]{1,0:T(8,128)(2,1)} %all-gather.11.cloned.1.call-done.refs_4_.refs_2_.refs_1_, ...), custom_call_target="tpu_custom_call" | custom-call | flops 30000001024 | bytes 31457280 | tf_op jit(solution)/shard_map/pallas_call | solution.py:1065
  225.1 38.7 %shard_map.249 = (bf16[1024,1280]{1,0:T(8,128)(2,1)}, bf16[15,1024,64]{2,1,0:T(8,128)(2,1)}, bf16[1024,320]{1,0:T(8,128)(2,1)}, f32[8,1024]{1,0:T(8,128)}, f32[2...) custom-call(bf16[1024,1280]{1,0:T(8,128)(2,1)} %get-tuple-element.114.refs_0_, ...), custom_call_target="tpu_custom_call" | custom-call | flops 30000001024 | bytes 31457280 | tf_op jit(solution)/shard_map/pallas_call | solution.py:1065
  263.8 28.9 %shard_map.250 = (bf16[1024,1280]{1,0:T(8,128)(2,1)}, bf16[1024,1280]{1,0:T(8,128)(2,1)}, bf16[1024,1280]{1,0:T(8,128)(2,1)}, bf16[1280,1280]{1,0:T(8,128)(2,1)}) custom-call(bf16[256,1280]{1,0:T(8,128)(2,1)} %get-tuple-element.116.refs_0_, bf16[1280,640]{1,0:T(8,128)(2,1)} %all-gather.15.cloned.1.call-done.refs_5_.refs_1_.refs_4_, ...), custom_call_target="tpu_custom_call" | custom-call | flops 30000001024 | bytes 31457280 | tf_op jit(solution)/shard_map/pallas_call | solution.py:1065
  292.7 0.3 reduce-scatter.9.cloned.1.call-start
  293.0 41.1 %shard_map.251 = (f32[256,1280]{1,0:T(8,128)}, bf16[256,1280]{1,0:T(8,128)(2,1)}, f32[8,1280]{1,0:T(8,128)}, bf16[1280,1280]{1,0:T(8,128)(2,1)}, bf16[256,1280]{1,0:T(8,128)(2,1)}) custom-call(bf16[1024,1280]{1,0:T(8,128)(2,1)} %get-tuple-element.119.refs_0_, f32[256,1280]{1,0:T(8,128)} %get-tuple-element.120.refs_1_, ...), custom_call_target="tpu_custom_call" | custom-call | flops 30000001024 | bytes 31457280 | tf_op jit(solution)/shard_map/pallas_call | solution.py:1065
  334.2 2.5 constant_dynamic-slice_fusion.2.refs_11_
  336.6 55.2 %shard_map.252 = (bf16[256,1280]{1,0:T(8,128)(2,1)}, f32[8,1280]{1,0:T(8,128)}, bf16[2,320,1024]{2,1,0:T(8,128)(2,1)}, bf16[1280,1280]{1,0:T(8,128)(2,1)}) custom-call(bf16[256,1280]{1,0:T(8,128)(2,1)} %get-tuple-element.123.refs_0_, f32[256,1280]{1,0:T(8,128)} %get-tuple-element.124.refs_1_, bf16[256,1280]{1,0:T(8,128)(2,1)} %get-tuple-element.125.refs_2_, ...), custom_call_target="tpu_custom_call" | custom-call | flops 30000001024 | bytes 31457280 | tf_op jit(solution)/shard_map/pallas_call | solution.py:1065
  391.8 0.3 reduce-scatter.13.cloned.1.call-start
  392.1 65.9 %shard_map.253 = (f32[256,1280]{1,0:T(8,128)}, bf16[256,1280]{1,0:T(8,128)(2,1)}, f32[8,1280]{1,0:T(8,128)}, bf16[1280,640]{1,0:T(8,128)(2,1)}, bf16[1280,640]{1...) custom-call(bf16[256,1280]{1,0:T(8,128)(2,1)} %get-tuple-element.133.refs_0_, ...), custom_call_target="tpu_custom_call" | custom-call | flops 30000001024 | bytes 31457280 | tf_op jit(solution)/shard_map/pallas_call | solution.py:1065
  458.2 2.0 constant_dynamic-slice_fusion.refs_3_
  460.1 2.4 constant_dynamic-slice_fusion.1.far_hbm
  462.6 41.0 %shard_map.254 = (bf16[1024,960]{1,0:T(8,128)(2,1)}, bf16[1280,320]{1,0:T(8,128)(2,1)}, bf16[1280,640]{1,0:T(8,128)(2,1)}) custom-call(bf16[256,1280]{1,0:T(8,128)(2,1)} %get-tuple-element.138.refs_0_, bf16[1280,640]{1,0:T(8,128)(2,1)} %all-gather.7.cloned.1.call-done.refs_1_.refs_4_, bf16[1280,640]{1,0:T(8,128)(2,1)} %collective-permute-done.1.refs_2_.refs_5_, ...), custom_call_target="tpu_custom_call" | custom-call | flops 30000001024 | bytes 31457280 | tf_op jit(solution)/shard_map/pallas_call | solution.py:1065
  503.7 17.9 %shard_map.255.refs_4_ = bf16[320,1280]{1,0:T(8,128)(2,1)} custom-call(bf16[320,1280]{1,0:T(8,128)(2,1)} %reduce-scatter.9.cloned.1.call-done.part_ref.refs_1_), custom_call_target="tpu_custom_call" | custom-call | flops 10000000000 | bytes 10485760 | tf_op jit(solution)/shard_map/pallas_call | solution.py:1315
  521.6 1.7 reduce-scatter.13.cloned.1.call-done.early1_ref.refs_8_
  523.3 42.9 %shard_map.256 = (bf16[1280,640]{1,0:T(8,128)(2,1)}, bf16[256,1280]{1,0:T(8,128)(2,1)}, f32[8,1280]{1,0:T(8,128)}) custom-call(bf16[1024,960]{1,0:T(8,128)(2,1)} %get-tuple-element.155.refs_0_, bf16[1280,320]{1,0:T(8,128)(2,1)} %get-tuple-element.156.refs_1_, f32[256,1280]{1,0:T(8,128)} %get-tuple-element.157.refs_2_, ...), custom_call_target="tpu_custom_call" | custom-call | flops 30000001024 | bytes 31457280 | tf_op jit(solution)/shard_map/pallas_call | solution.py:1065
  566.2 39.8 %shard_map.257 = (bf16[2,320,1024]{2,1,0:T(8,128)(2,1)}, f32[16,320]{1,0:T(8,128)}, bf16[320,1280]{1,0:T(8,128)(2,1)}, bf16[320,640]{1,0:T(8,128)(2,1)}, bf16[320,640]{1,0:T(8,128)(2,1)}) custom-call(bf16[320,1280]{1,0:T(8,128)(2,1)} %reduce-scatter.7.cloned.1.call-done.late_ref.refs_0_, ...), custom_call_target="tpu_custom_call" | custom-call | flops 30000001024 | bytes 31457280 | tf_op jit(solution)/shard_map/pallas_call | solution.py:1301
  606.0 10.8 %shard_map.258.refs_9_ = bf16[320,640]{1,0:T(8,128)(2,1)} custom-call(bf16[320,640]{1,0:T(8,128)(2,1)} %reduce-scatter.17.cloned.1.call-done.part_ref.refs_6_), custom_call_target="tpu_custom_call" | custom-call | flops 10000000000 | bytes 10485760 | tf_op jit(solution)/shard_map/pallas_call | solution.py:1315
  616.9 7.2 %shard_map.259 = (f32[320,320]{1,0:T(8,128)}, f32[1,320]{1,0:T(1,128)}, f32[1,320]{1,0:T(1,128)}, f32[1,320]{1,0:T(1,128)}, f32[1,320]{1,0:T(1,128)}, /*index=5*...) custom-call(bf16[320,1280]{1,0:T(8,128)(2,1)} %reduce-scatter.7.clon, ...), custom_call_target="tpu_custom_call" | custom-call | tf_op jit(solution)/shard_map/pallas_call | solution.py:1335
  (65 shorter events, 1.0 us)
Async XLA Ops:
  7.2 62.1 %all-gather.7.cloned.1.call-start = ((), (), s32[]{:S(2)}) async-start(), calls=%async_computation.6 | async-start | bytes 2048000 | tf_op jit(solution)/shard_map/all_gather | solution.py:1419
  9.9 4.4 copy-start.5
  9.9 4.5 copy-start.3
  11.2 4.7 copy-start.6
  11.2 4.7 copy-start.7
  11.2 4.7 copy-start.8
  11.2 4.7 copy-start.9
  11.2 4.7 copy-start.10
  11.2 4.7 copy-start.11
  11.2 4.7 copy-start.12
  11.2 5.4 copy-start
  11.2 12.8 %collective-permute-start = (bf16[320,640]{1,0:T(8,128)(2,1)}, bf16[320,640]{1,0:T(8,128)(2,1)}, u32[]{:S(2)}, u32[]{:S(2)}) collective-permute-start(bf16[320,640]{1,0:T(8,128)(2,1)} %get-tuple-element.192), channel_id=1, source_target_pairs={{0,16},{16,0},{1,17},{17,1},{2,18},{18,2},{3,19},{19,3},{4,20},{20... | collective-permute-start | bytes 1228808 | tf_op jit(solution)/shard_map/ppermute | solution.py:1352
  26.0 80.3 %all-gather.9.cloned.1.call-start = ((), (), s32[]{:S(2)}) async-start(), calls=%async_computation.7 | async-start | bytes 2048000 | tf_op jit(solution)/shard_map/all_gather | solution.py:1419
  64.8 2.2 copy-start.1
  64.8 2.2 copy-start.2
  66.9 2.2 copy-start.4
  66.9 79.8 %all-gather.11.cloned.1.call-start = ((), (), s32[]{:S(2)}) async-start(), calls=%async_computation.8 | async-start | bytes 2048000 | tf_op jit(solution)/shard_map/all_gather | solution.py:1419
  67.9 117.3 %all-gather.13.cloned.1.call-start = ((), (), s32[]{:S(2)}) async-start(), calls=%async_computation.9 | async-start | bytes 2048000 | tf_op jit(solution)/shard_map/all_gather | solution.py:1419
  68.4 156.6 %all-gather.15.cloned.1.call-start = ((), (), s32[]{:S(2)}) async-start(), calls=%async_computation.10 | async-start | bytes 2048000 | tf_op jit(solution)/shard_map/all_gather | solution.py:1419
  69.0 224.0 %all-gather.17.cloned.1.call-start = ((), (), s32[]{:S(2)}) async-start(), calls=%async_computation.11 | async-start | bytes 4096000 | tf_op jit(solution)/shard_map/all_gather | solution.py:1419
  69.3 38.9 %collective-permute-start.1 = (bf16[1280,640]{1,0:T(8,128)(2,1)}, bf16[1280,640]{1,0:T(8,128)(2,1)}, u32[]{:S(2)}, u32[]{:S(2)}) collective-permute-start(bf16[1280,640]{1,0:T(8,128)(2,1)} %all-gather.7.cloned.1.call-done.refs_1_.refs_4_), channel_id=1, source_target_pairs={{0,16},{16,0},{1,17},{17,1},{2,18},{18,2},{3,19},{19,3},{4,20},{20... | collective-permute-start | bytes 4915208 | tf_op jit(solution)/shard_map/ppermute | solution.py:1352
  74.7 317.4 %reduce-scatter.11.cloned.1.call-start = ((), (), s32[]{:S(2)}) async-start(), calls=%async_computation.14 | async-start | bytes 4096000 | tf_op jit(solution)/shard_map/reduce_scatter | solution.py:1471
  292.7 169.9 %reduce-scatter.9.cloned.1.call-start = ((), (), s32[]{:S(2)}) async-start(), calls=%async_computation.13 | async-start | bytes 4096000 | tf_op jit(solution)/shard_map/reduce_scatter | solution.py:1471
  334.1 169.5 %reduce-scatter.7.cloned.1.call-start = ((), (), s32[]{:S(2)}) async-start(), calls=%async_computation.12 | async-start | bytes 4096000 | tf_op jit(solution)/shard_map/reduce_scatter | solution.py:1471
  391.8 131.5 %reduce-scatter.13.cloned.1.call-start = ((), (), s32[]{:S(2)}) async-start(), calls=%async_computation.15 | async-start | bytes 2048000 | tf_op jit(solution)/shard_map/reduce_scatter | solution.py:1471
  458.1 108.1 %reduce-scatter.15.cloned.1.call-start = ((), (), s32[]{:S(2)}) async-start(), calls=%async_computation.16 | async-start | bytes 2048000 | tf_op jit(solution)/shard_map/reduce_scatter | solution.py:1471
  503.7 102.4 %reduce-scatter.17.cloned.1.call-start = ((), (), s32[]{:S(2)}) async-start(), calls=%async_computation.17 | async-start | bytes 2048000 | tf_op jit(solution)/shard_map/reduce_scatter | solution.py:1471
Sparse Core Ops, SparseCore 0:
  26.1 39.6 all-gather.6
  68.0 38.2 all-gather.8
  108.5 37.0 all-gather.10
  147.5 37.0 all-gather.12
  186.6 37.0 all-gather.14
  225.6 64.5 all-gather.16
  292.8 62.2 reduce-scatter.10
  357.4 62.3 reduce-scatter.8
  422.2 62.3 reduce-scatter.6
  486.8 36.4 reduce-scatter.12
  525.7 35.3 reduce-scatter.14
  566.3 34.6 reduce-scatter.16
